TPU v7x, 32 devices: a whole 2x2x4 slice. The times are simulated.
32 devices in a mesh: seq: 8 (over z, core), mem: 4 (over y, x).
Axes of the slice: x: 2, y: 2, z: 4, core: 2. Of those that a mesh axis runs over, the one named last changes fastest.
Arguments:
- inputs: bfloat16 [2, 8, 4, 256, 1472], P(None, 'seq', 'mem'), may hold values from -6 to 6
- memory: bfloat16 [2, 8, 4, 1024, 1472], P(None, 'seq', None, 'mem'), may hold values from -6 to 6
- memory_lengths: int32 [2, 8, 4], P(None, 'seq'), may hold values from 1 to 1024, 2048 in all within a row
- keep_mask: int32 [2, 8, 4, 1024], P(None, 'seq', None, 'mem'), may hold values 0 or 1
- norm_self: bfloat16 [1472], replicated, may hold values from 0.099609375 to 1.8984375
- query_self: bfloat16 [1472, 384], P(None, 'seq'), may hold values from -0.0390625 to 0.0390625
- key_self: bfloat16 [1472, 384], P(None, 'seq'), may hold values from -0.15625 to 0.15625
- value_self: bfloat16 [1472, 384], P(None, 'seq'), may hold values from -0.15625 to 0.15625
- output_self: bfloat16 [384, 1472], P('seq'), may hold values from -1.25 to 1.25
- bias_table: bfloat16 [32, 6], replicated, may hold values from -4 to 4
- norm_cross: bfloat16 [1472], replicated, may hold values from 0.099609375 to 1.8984375
- query_cross: bfloat16 [1472, 384], P(None, 'seq'), may hold values from -0.0390625 to 0.0390625
- key_cross: bfloat16 [1472, 384], P(None, 'seq'), may hold values from -0.15625 to 0.15625
- value_cross: bfloat16 [1472, 384], P(None, 'seq'), may hold values from -0.15625 to 0.15625
- output_cross: bfloat16 [384, 1472], P('seq'), may hold values from -2.5 to 2.5
- norm_feed: bfloat16 [1472], replicated, may hold values from 0.099609375 to 1.8984375
- gate_feed: bfloat16 [1472, 3584], P(None, 'seq'), may hold values from -0.15625 to 0.15625
- linear_feed: bfloat16 [1472, 3584], P(None, 'seq'), may hold values from -0.15625 to 0.15625
- down_feed: bfloat16 [3584, 1472], P('seq'), may hold values from -0.09375 to 0.09375
- output_grad: bfloat16 [2, 8, 4, 256, 1472], P(None, 'seq', 'mem'), may hold values from -6 to 6
Outputs:
- result: float32 [2, 8, 4, 256, 1472], P(None, 'seq', 'mem')
- input_grad: float32 [2, 8, 4, 256, 1472], P(None, 'seq', 'mem')
- memory_grad: float32 [2, 8, 4, 1024, 1472], P(None, 'seq', None, 'mem')
- norm_self_grad: float32 [1472], replicated
- query_self_grad: float32 [1472, 384], P(None, 'seq')
- key_self_grad: float32 [1472, 384], P(None, 'seq')
- value_self_grad: float32 [1472, 384], P(None, 'seq')
- output_self_grad: float32 [384, 1472], P('seq')
- bias_table_grad: float32 [32, 6], replicated
- norm_cross_grad: float32 [1472], replicated
- query_cross_grad: float32 [1472, 384], P(None, 'seq')
- key_cross_grad: float32 [1472, 384], P(None, 'seq')
- value_cross_grad: float32 [1472, 384], P(None, 'seq')
- output_cross_grad: float32 [384, 1472], P('seq')
- norm_feed_grad: float32 [1472], replicated
- gate_feed_grad: float32 [1472, 3584], P(None, 'seq')
- linear_feed_grad: float32 [1472, 3584], P(None, 'seq')
- down_feed_grad: float32 [3584, 1472], P('seq')
Inputs may be any that keep to these rules, and one draw needn't show every extreme that they name: `memory_lengths`: each encoder length of a group; in every group of 4 pairs the longest has exactly 1024 and their sum is 2048.
All inputs are finite; a program needn't handle non-finite values. No bound on the sum of `keep_mask` on one device may be relied on, other than what follows from the above.
Results may differ from a plain program's by a relative error of at most 0.03.
The roundings to bfloat16 on the way count: a program that leaves them out, or rounds other values in their place, can miss the bound.
Values may be sent and summed in bfloat16 or wider, within the bound.
No kernel may reach another device: no remote copies, remote signals or barrier semaphores. Data moves between devices by JAX's collectives and lax.ppermute only.
A program may use at most 320 MiB of HBM per device.

v0:
```python
import math

import jax
import jax.numpy as jnp
from jax import lax
from jax.sharding import PartitionSpec as P

norm_eps = 1e-06
masked_score = -1e30


def merged(value, axis, join):
    pieces = jax.tree.map(lambda part: lax.all_gather(part, axis), value)
    head = jax.tree.map(lambda part: part[0], pieces)
    tail = jax.tree.map(lambda part: part[1:], pieces)
    so_far, _ = lax.scan(lambda so_far, section: (join(so_far, section), None), head, tail)
    return so_far


def bucket_edges():
    return [math.ceil(16 * 8 ** ((number - 16) / 16)) for number in range(17, 32)]


def position_buckets(length):
    row_index = jnp.arange(length, dtype=jnp.int32)
    offset = jnp.maximum(row_index[:, None] - row_index[None, :], 0)
    bucket = jnp.minimum(offset, 16)
    for threshold in bucket_edges():
        bucket = bucket + (offset >= threshold).astype(jnp.int32)
    return bucket


def rms_norm(value, gain):
    scale = lax.rsqrt(jnp.mean(value * value, axis=-1, keepdims=True) + norm_eps)
    return value * scale * gain


def norm_back(value, gain, upstream):
    unused, pullback = jax.vjp(rms_norm, value, gain)
    return pullback(upstream)


def gelu_gate(gate_act, linear):
    return jax.nn.gelu(gate_act, approximate=True) * linear


def matmul(left, right):
    return jnp.dot(left, right, preferred_element_type=jnp.float32)


def contract_rows(left, right):
    return lax.dot_general(
        left, right, (((0,), (0,)), ((), ())), preferred_element_type=jnp.float32
    )


def contract_cols(left, right):
    return lax.dot_general(
        left, right, (((1,), (1,)), ((), ())), preferred_element_type=jnp.float32
    )


def merge_stats(first_part, second_part):
    row_peak = jnp.maximum(first_part[0], second_part[0])
    row_total = first_part[1] * jnp.exp(first_part[0] - row_peak) + second_part[1] * jnp.exp(
        second_part[0] - row_peak
    )
    return (row_peak, row_total)


def fetch_weights(columns, row_parts):
    whole_columns = (
        lax.all_gather(columns[0], "seq", axis=1, tiled=True),
        lax.all_gather(columns[1], "seq", axis=1, tiled=True),
        lax.all_gather(columns[2], "seq", axis=1, tiled=True),
        lax.all_gather(columns[3], "seq", axis=1, tiled=True),
        lax.all_gather(columns[4], "seq", axis=1, tiled=True),
        lax.all_gather(columns[5], "seq", axis=1, tiled=True),
        lax.all_gather(columns[6], "seq", axis=1, tiled=True),
        lax.all_gather(columns[7], "seq", axis=1, tiled=True),
    )
    whole_rows = (
        lax.all_gather(row_parts[0], "seq", axis=0, tiled=True),
        lax.all_gather(row_parts[1], "seq", axis=0, tiled=True),
        lax.all_gather(row_parts[2], "seq", axis=0, tiled=True),
    )
    return (whole_columns, whole_rows)


def self_scores(query_heads, key_heads, position_bias, causal):
    scores = (
        jnp.einsum("ihd,jhd->hij", query_heads, key_heads, preferred_element_type=jnp.float32)
        + position_bias
    )
    return jnp.where(causal[None], scores, masked_score)


def cross_logits(queries_all, key_heads, valid):
    scores = jnp.einsum(
        "pihd,pjhd->phij", queries_all, key_heads, preferred_element_type=jnp.float32
    )
    return jnp.where(valid[:, None, None, :], scores, masked_score)


def per_device(
    inputs,
    memory,
    memory_lengths,
    keep_mask,
    norm_self,
    query_self,
    key_self,
    value_self,
    output_self,
    bias_table,
    norm_cross,
    query_cross,
    key_cross,
    value_cross,
    output_cross,
    norm_feed,
    gate_feed,
    linear_feed,
    down_feed,
    output_grad,
):
    micro_count = inputs.shape[0]
    length = inputs.shape[3]
    model_width = inputs.shape[4]
    pair_count = memory.shape[2]
    slot_count = memory.shape[3]
    head_count = bias_table.shape[1]
    bucket_count = bias_table.shape[0]
    seq_count = lax.axis_size("seq")
    inner_width = query_self.shape[1] * seq_count
    head_depth = inner_width // head_count
    feed_width = gate_feed.shape[1] * seq_count
    mem_index = lax.axis_index("mem")
    gain_self = norm_self.astype(jnp.float32)
    gain_cross = norm_cross.astype(jnp.float32)
    gain_feed = norm_feed.astype(jnp.float32)
    onehot = (
        position_buckets(length).reshape(length * length, 1)
        == jnp.arange(bucket_count, dtype=jnp.int32)[None, :]
    ).astype(jnp.bfloat16)
    position_bias = (
        jnp.dot(onehot, bias_table, preferred_element_type=jnp.float32)
        .reshape(length, length, head_count)
        .transpose(2, 0, 1)
    )
    row_index = jnp.arange(length, dtype=jnp.int32)
    causal = row_index[:, None] >= row_index[None, :]
    spots = mem_index * slot_count + jnp.arange(slot_count, dtype=jnp.int32)
    column_shards = (
        query_self,
        key_self,
        value_self,
        query_cross,
        key_cross,
        value_cross,
        gate_feed,
        linear_feed,
    )
    row_shards = (output_self, output_cross, down_feed)
    inner_zero = jnp.zeros((model_width, inner_width), jnp.float32)
    grad_query_self = inner_zero
    grad_key_self = inner_zero
    grad_value_self = inner_zero
    grad_query_cross = inner_zero
    grad_key_cross = inner_zero
    grad_value_cross = inner_zero
    grad_output_self = jnp.zeros((inner_width, model_width), jnp.float32)
    grad_output_cross = jnp.zeros((inner_width, model_width), jnp.float32)
    grad_gate = jnp.zeros((model_width, feed_width), jnp.float32)
    grad_linear = jnp.zeros((model_width, feed_width), jnp.float32)
    grad_down = jnp.zeros((feed_width, model_width), jnp.float32)
    grad_gain_self = jnp.zeros((model_width,), jnp.float32)
    grad_gain_cross = jnp.zeros((model_width,), jnp.float32)
    grad_gain_feed = jnp.zeros((model_width,), jnp.float32)
    grad_table = jnp.zeros((bucket_count, head_count), jnp.float32)
    results = []
    input_grads = []
    memory_grads = []
    for micro_index in range(micro_count):
        weights_now = fetch_weights(column_shards, row_shards)
        (
            query_full,
            key_full,
            value_full,
            cross_query,
            cross_key,
            cross_value,
            gate_full,
            linear_full,
        ), (output_full, cross_output, down_full) = weights_now
        tokens = inputs[micro_index, 0, 0].astype(jnp.float32)
        source = memory[micro_index, 0].reshape(pair_count * slot_count, model_width)
        lengths_now = memory_lengths[micro_index, 0]
        keep_now = keep_mask[micro_index, 0]
        normed = rms_norm(tokens, gain_self).astype(jnp.bfloat16)
        query_low = matmul(normed, query_full).astype(jnp.bfloat16)
        keys_low = matmul(normed, key_full).astype(jnp.bfloat16)
        values_low = matmul(normed, value_full).astype(jnp.bfloat16)
        query_heads = query_low.reshape(length, head_count, head_depth)
        key_heads = keys_low.reshape(length, head_count, head_depth)
        value_heads = values_low.reshape(length, head_count, head_depth)
        scores = self_scores(query_heads, key_heads, position_bias, causal)
        self_peak = jnp.max(scores, axis=-1, keepdims=True)
        expo = jnp.exp(scores - self_peak)
        self_total = jnp.sum(expo, axis=-1, keepdims=True)
        attend = expo / self_total
        attend_low = attend.astype(jnp.bfloat16)
        mixed = (
            jnp.einsum("hij,jhd->ihd", attend_low, value_heads, preferred_element_type=jnp.float32)
            .astype(jnp.bfloat16)
            .reshape(length, inner_width)
        )
        first_sum = tokens + matmul(mixed, output_full)
        normed_cross = rms_norm(first_sum, gain_cross).astype(jnp.bfloat16)
        cross_query_low = matmul(normed_cross, cross_query).astype(jnp.bfloat16)
        cross_keys_low = matmul(source, cross_key).astype(jnp.bfloat16)
        cross_values_low = matmul(source, cross_value).astype(jnp.bfloat16)
        valid = (spots[None, :] < lengths_now[:, None]) & ((keep_now == 1) | (spots[None, :] == 0))
        local_keys = cross_keys_low.reshape(pair_count, slot_count, head_count, head_depth)
        local_values = cross_values_low.reshape(pair_count, slot_count, head_count, head_depth)
        queries_all = lax.all_gather(cross_query_low[None], "mem", axis=0, tiled=True).reshape(
            pair_count, length, head_count, head_depth
        )
        cross_scores = cross_logits(queries_all, local_keys, valid)
        local_peak = jnp.max(cross_scores, axis=-1)
        local_total = jnp.sum(
            jnp.where(valid[:, None, None, :], jnp.exp(cross_scores - local_peak[..., None]), 0.0),
            axis=-1,
        )
        cross_peak, cross_total = merged((local_peak, local_total), "mem", merge_stats)
        cross_attend = (
            jnp.where(valid[:, None, None, :], jnp.exp(cross_scores - cross_peak[..., None]), 0.0)
            / cross_total[..., None]
        )
        cross_low = cross_attend.astype(jnp.bfloat16)
        partial_out = jnp.einsum(
            "phij,pjhd->pihd", cross_low, local_values, preferred_element_type=jnp.float32
        ).reshape(pair_count, length, inner_width)
        cross_mixed = lax.psum_scatter(partial_out, "mem", scatter_dimension=0, tiled=True)[
            0
        ].astype(jnp.bfloat16)
        second_sum = first_sum + matmul(cross_mixed, cross_output)
        normed_feed = rms_norm(second_sum, gain_feed).astype(jnp.bfloat16)
        gate_act = matmul(normed_feed, gate_full)
        linear = matmul(normed_feed, linear_full)
        hidden = gelu_gate(gate_act, linear).astype(jnp.bfloat16)
        results.append(second_sum + matmul(hidden, down_full))
        upstream_low = output_grad[micro_index, 0, 0]
        upstream = upstream_low.astype(jnp.float32)
        grad_down = grad_down + contract_rows(hidden, upstream_low)
        hidden_grad = contract_cols(upstream_low, down_full)
        unused, gelu_pullback = jax.vjp(gelu_gate, gate_act, linear)
        gate_grad, linear_grad = gelu_pullback(hidden_grad)
        gate_low = gate_grad.astype(jnp.bfloat16)
        linear_low = linear_grad.astype(jnp.bfloat16)
        grad_gate = grad_gate + contract_rows(normed_feed, gate_low)
        grad_linear = grad_linear + contract_rows(normed_feed, linear_low)
        normed_feed_grad = contract_cols(gate_low, gate_full) + contract_cols(
            linear_low, linear_full
        )
        second_part, gain_part = norm_back(second_sum, gain_feed, normed_feed_grad)
        second_grad = upstream + second_part
        grad_gain_feed = grad_gain_feed + gain_part
        cross_out_low = second_grad.astype(jnp.bfloat16)
        grad_output_cross = grad_output_cross + contract_rows(cross_mixed, cross_out_low)
        cross_mixed_grad = contract_cols(cross_out_low, cross_output).astype(jnp.bfloat16)
        grads_all = lax.all_gather(cross_mixed_grad[None], "mem", axis=0, tiled=True).reshape(
            pair_count, length, head_count, head_depth
        )
        cross_scores = cross_logits(queries_all, local_keys, valid)
        cross_attend = (
            jnp.where(valid[:, None, None, :], jnp.exp(cross_scores - cross_peak[..., None]), 0.0)
            / cross_total[..., None]
        )
        attend_grad = jnp.einsum(
            "pihd,pjhd->phij", grads_all, local_values, preferred_element_type=jnp.float32
        )
        local_dots = jnp.sum(cross_attend * attend_grad, axis=-1)
        row_dots = lax.psum(local_dots, "mem")
        score_grad = (cross_attend * (attend_grad - row_dots[..., None])).astype(jnp.bfloat16)
        query_part = jnp.einsum(
            "phij,pjhd->pihd", score_grad, local_keys, preferred_element_type=jnp.float32
        ).reshape(pair_count, length, inner_width)
        query_grad = (
            lax.psum_scatter(
                query_part.astype(jnp.bfloat16), "mem", scatter_dimension=0, tiled=True
            )
            .astype(jnp.float32)[0]
            .astype(jnp.bfloat16)
        )
        key_grad = (
            jnp.einsum(
                "phij,pihd->pjhd", score_grad, queries_all, preferred_element_type=jnp.float32
            )
            .astype(jnp.bfloat16)
            .reshape(pair_count * slot_count, inner_width)
        )
        value_grad = (
            jnp.einsum("phij,pihd->pjhd", cross_low, grads_all, preferred_element_type=jnp.float32)
            .astype(jnp.bfloat16)
            .reshape(pair_count * slot_count, inner_width)
        )
        grad_key_cross = grad_key_cross + contract_rows(source, key_grad)
        grad_value_cross = grad_value_cross + contract_rows(source, value_grad)
        grad_query_cross = grad_query_cross + contract_rows(normed_cross, query_grad)
        memory_part = contract_cols(key_grad, cross_key) + contract_cols(value_grad, cross_value)
        memory_grads.append(memory_part.reshape(pair_count, slot_count, model_width))
        normed_cross_grad = contract_cols(query_grad, cross_query)
        first_part, gain_part = norm_back(first_sum, gain_cross, normed_cross_grad)
        first_grad = second_grad + first_part
        grad_gain_cross = grad_gain_cross + gain_part
        self_out_low = first_grad.astype(jnp.bfloat16)
        grad_output_self = grad_output_self + contract_rows(mixed, self_out_low)
        mixed_grad = (
            contract_cols(self_out_low, output_full)
            .astype(jnp.bfloat16)
            .reshape(length, head_count, head_depth)
        )
        scores = self_scores(query_heads, key_heads, position_bias, causal)
        attend = jnp.exp(scores - self_peak) / self_total
        attend_grad = jnp.einsum(
            "ihd,jhd->hij", mixed_grad, value_heads, preferred_element_type=jnp.float32
        )
        row_dots_self = jnp.sum(attend * attend_grad, axis=-1, keepdims=True)
        score_grad_self = (attend * (attend_grad - row_dots_self)).astype(jnp.bfloat16)
        grad_table = grad_table + contract_rows(
            onehot, score_grad_self.reshape(head_count, length * length).T
        )
        query_grad_self = (
            jnp.einsum(
                "hij,jhd->ihd", score_grad_self, key_heads, preferred_element_type=jnp.float32
            )
            .astype(jnp.bfloat16)
            .reshape(length, inner_width)
        )
        key_grad_self = (
            jnp.einsum(
                "hij,ihd->jhd", score_grad_self, query_heads, preferred_element_type=jnp.float32
            )
            .astype(jnp.bfloat16)
            .reshape(length, inner_width)
        )
        value_grad_self = (
            jnp.einsum("hij,ihd->jhd", attend_low, mixed_grad, preferred_element_type=jnp.float32)
            .astype(jnp.bfloat16)
            .reshape(length, inner_width)
        )
        grad_query_self = grad_query_self + contract_rows(normed, query_grad_self)
        grad_key_self = grad_key_self + contract_rows(normed, key_grad_self)
        grad_value_self = grad_value_self + contract_rows(normed, value_grad_self)
        normed_grad = (
            contract_cols(query_grad_self, query_full)
            + contract_cols(key_grad_self, key_full)
            + contract_cols(value_grad_self, value_full)
        )
        token_part, gain_part = norm_back(tokens, gain_self, normed_grad)
        input_grads.append(first_grad + token_part)
        grad_gain_self = grad_gain_self + gain_part
    column_sums = (
        lax.psum_scatter(
            grad_query_self.astype(jnp.bfloat16), "seq", scatter_dimension=1, tiled=True
        ).astype(jnp.float32),
        lax.psum_scatter(
            grad_key_self.astype(jnp.bfloat16), "seq", scatter_dimension=1, tiled=True
        ).astype(jnp.float32),
        lax.psum_scatter(
            grad_value_self.astype(jnp.bfloat16), "seq", scatter_dimension=1, tiled=True
        ).astype(jnp.float32),
        lax.psum_scatter(
            grad_query_cross.astype(jnp.bfloat16), "seq", scatter_dimension=1, tiled=True
        ).astype(jnp.float32),
        lax.psum_scatter(
            grad_key_cross.astype(jnp.bfloat16), "seq", scatter_dimension=1, tiled=True
        ).astype(jnp.float32),
        lax.psum_scatter(
            grad_value_cross.astype(jnp.bfloat16), "seq", scatter_dimension=1, tiled=True
        ).astype(jnp.float32),
        lax.psum_scatter(
            grad_gate.astype(jnp.bfloat16), "seq", scatter_dimension=1, tiled=True
        ).astype(jnp.float32),
        lax.psum_scatter(
            grad_linear.astype(jnp.bfloat16), "seq", scatter_dimension=1, tiled=True
        ).astype(jnp.float32),
    )
    row_sums = (
        lax.psum_scatter(
            grad_output_self.astype(jnp.bfloat16), "seq", scatter_dimension=0, tiled=True
        ).astype(jnp.float32),
        lax.psum_scatter(
            grad_output_cross.astype(jnp.bfloat16), "seq", scatter_dimension=0, tiled=True
        ).astype(jnp.float32),
        lax.psum_scatter(
            grad_down.astype(jnp.bfloat16), "seq", scatter_dimension=0, tiled=True
        ).astype(jnp.float32),
    )
    shard_sums = (
        lax.psum(column_sums[0].astype(jnp.bfloat16), "mem").astype(jnp.float32),
        lax.psum(column_sums[1].astype(jnp.bfloat16), "mem").astype(jnp.float32),
        lax.psum(column_sums[2].astype(jnp.bfloat16), "mem").astype(jnp.float32),
        lax.psum(column_sums[3].astype(jnp.bfloat16), "mem").astype(jnp.float32),
        lax.psum(column_sums[4].astype(jnp.bfloat16), "mem").astype(jnp.float32),
        lax.psum(column_sums[5].astype(jnp.bfloat16), "mem").astype(jnp.float32),
        lax.psum(column_sums[6].astype(jnp.bfloat16), "mem").astype(jnp.float32),
        lax.psum(column_sums[7].astype(jnp.bfloat16), "mem").astype(jnp.float32),
        lax.psum(row_sums[0].astype(jnp.bfloat16), "mem").astype(jnp.float32),
        lax.psum(row_sums[1].astype(jnp.bfloat16), "mem").astype(jnp.float32),
        lax.psum(row_sums[2].astype(jnp.bfloat16), "mem").astype(jnp.float32),
    )
    small_sums = lax.psum(
        (grad_gain_self, grad_gain_cross, grad_gain_feed, grad_table), ("seq", "mem")
    )
    result_out = jnp.stack(results)[:, None, None]
    input_out = jnp.stack(input_grads)[:, None, None]
    memory_out = jnp.stack(memory_grads)[:, None]
    return (
        result_out,
        input_out,
        memory_out,
        small_sums[0],
        shard_sums[0],
        shard_sums[1],
        shard_sums[2],
        shard_sums[8],
        small_sums[3],
        small_sums[1],
        shard_sums[3],
        shard_sums[4],
        shard_sums[5],
        shard_sums[9],
        small_sums[2],
        shard_sums[6],
        shard_sums[7],
        shard_sums[10],
    )


def solution(mesh):
    return jax.shard_map(
        per_device,
        mesh=mesh,
        in_specs=(
            P(None, "seq", "mem", None, None),
            P(None, "seq", None, "mem", None),
            P(None, "seq", None),
            P(None, "seq", None, "mem"),
            P(),
            P(None, "seq"),
            P(None, "seq"),
            P(None, "seq"),
            P("seq", None),
            P(),
            P(),
            P(None, "seq"),
            P(None, "seq"),
            P(None, "seq"),
            P("seq", None),
            P(),
            P(None, "seq"),
            P(None, "seq"),
            P("seq", None),
            P(None, "seq", "mem", None, None),
        ),
        out_specs=(
            P(None, "seq", "mem", None, None),
            P(None, "seq", "mem", None, None),
            P(None, "seq", None, "mem", None),
            P(),
            P(None, "seq"),
            P(None, "seq"),
            P(None, "seq"),
            P("seq", None),
            P(),
            P(),
            P(None, "seq"),
            P(None, "seq"),
            P(None, "seq"),
            P("seq", None),
            P(),
            P(None, "seq"),
            P(None, "seq"),
            P("seq", None),
        ),
        check_vma=False,
    )
```

profile of v0, /device:TPU:8, one launch (start us, length us, event | category | flops | bytes accessed | tf_op | source)
XLA Modules:
  0.0 1592.1 jit_solution(6043531605904725958)
XLA Ops:
  19.8 6.3 fusion.204
  26.2 4.9 copy.235
  40.0 17.6 %all-gather.22.cloned.1.call-done = bf16[1472,384]{0,1:T(8,128)(2,1)} async-done(((bf16[1472,48]{0,1:T(8,128)(2,1)}), bf16[1472,384]{0,1:T(8,128)(2,1)}) %all-gather.22.cloned.1.call-update) | async-done | bytes 1130512 | tf_op jit(solution)/shard_map/all_gather | solution.py:73
  60.0 21.7 %all-gather.24.cloned.1.call-done = bf16[1472,384]{0,1:T(8,128)(2,1)} async-done(((bf16[1472,48]{0,1:T(8,128)(2,1)}), bf16[1472,384]{0,1:T(8,128)(2,1)}) %all-gather.24.cloned.1.call-update) | async-done | bytes 1130512 | tf_op jit(solution)/shard_map/all_gather | solution.py:74
  90.5 15.2 all-gather.26.cloned.1.call-done
  120.6 9.0 all-gather.32.cloned.1.call-done
  129.6 4.9 convolution_convert_fusion.6
  145.6 8.0 all-gather.30.cloned.1.call-done
  156.3 13.6 all-gather
  184.6 5.1 convolution_convert_fusion.7
  190.6 7.7 all-gather.1
  198.3 8.4 all-gather.2
  211.1 11.5 all-gather.3
  232.8 5.9 fusion.60
  241.8 8.9 all-gather.4
  252.4 7.8 all-gather.5
  266.0 6.0 fusion.56
  277.6 26.1 %reduce-scatter.52.cloned.1.call-done = f32[1,256,384]{1,2,0:T(8,128)} async-done(((f32[4,256,384]{1,2,0:T(8,128)}), f32[1,256,384]{1,2,0:T(8,128)}) %reduce-scatter.52.cloned.1.call-update) | async-done | bytes 393232
  307.2 99.1 %all-gather.36.cloned.1.call-done = bf16[1472,3584]{0,1:T(8,128)(2,1)} async-done(((bf16[1472,448]{0,1:T(8,128)(2,1)}), bf16[1472,3584]{0,1:T(8,128)(2,1)}) %all-gather.36.cloned.1.call-update) | async-done | bytes 10551312 | tf_op jit(solution)/shard_map/all_gather | solution.py:79
  406.3 9.0 fusion.207
  415.3 94.6 %all-gather.38.cloned.1.call-done = bf16[1472,3584]{0,1:T(8,128)(2,1)} async-done(((bf16[1472,448]{0,1:T(8,128)(2,1)}), bf16[1472,3584]{0,1:T(8,128)(2,1)}) %all-gather.38.cloned.1.call-update) | async-done | bytes 10551312 | tf_op jit(solution)/shard_map/all_gather | solution.py:80
  509.9 9.1 fusion.208
  518.9 94.7 %all-gather.40.cloned.1.call-done = bf16[3584,1472]{1,0:T(8,128)(2,1)} async-done(((bf16[448,1472]{1,0:T(8,128)(2,1)}), bf16[3584,1472]{1,0:T(8,128)(2,1)}) %all-gather.40.cloned.1.call-update) | async-done | bytes 10551312 | tf_op jit(solution)/shard_map/all_gather | solution.py:85
  613.6 11.1 multiply_convert_fusion.3
  624.8 10.9 fusion.211
  635.7 10.8 multiply_reduce_fusion.5
  646.5 6.1 fusion.209
  652.7 9.1 fusion.210
  661.8 9.6 multiply_convert_fusion.2
  671.4 8.7 fusion.213
  680.2 10.6 multiply_reduce_fusion.4
  694.8 13.8 all-gather.7
  711.5 8.3 multiply_reduce_fusion
  720.4 10.4 all-gather.6
  731.9 6.5 multiply_reduce_fusion.1
  738.4 16.7 %all-reduce.5 = (f32[4,6,256]{2,1,0:T(8,128)S(1)}, f32[4,6,256]{2,1,0:T(8,128)S(1)}) all-reduce(f32[4,6,256]{2,1,0:T(8,128)S(1)} %get-tuple-element.246, f32[4,6,256]{2,1,0:T(8,128)S(1)} %get-tuple-element.248), channel_id=1, replica_groups=mesh['seq'=8,'mem'=4] {'mem'}, use_global_device_ids=true, to_apply=%region_22.23 | all-reduce | flops 12288 | bytes 98304 | tf_op jit(solution)/shard_map/psum | solution.py:284
  755.2 5.8 multiply_convert_fusion
  762.6 5.8 multiply_convert_fusion.1
  785.5 4.9 fusion.90
  791.5 4.8 fusion.93
  812.6 5.1 reduce-scatter.54.cloned.1.call-done
  858.4 10.8 fusion.219
  869.2 13.3 add_convert_fusion.2
  882.6 10.7 fusion.220
  893.3 13.4 add_convert_fusion.1
  908.1 10.7 fusion.104
  918.8 13.4 add_convert_fusion
  944.5 9.9 fusion.34
  954.4 10.0 fusion.35
  968.1 13.7 reduce-scatter.30.cloned.1.call-done
  981.8 33.1 %reduce-scatter.32.cloned.1.call-done = bf16[1472,48]{0,1:T(8,128)(2,1)} async-done(((bf16[1472,384]{0,1:T(8,128)(2,1)}), bf16[1472,48]{0,1:T(8,128)(2,1)}) %reduce-scatter.32.cloned.1.call-update) | async-done | bytes 141328 | tf_op jit(solution)/shard_map/reduce_scatter | solution.py:371
  1014.9 33.3 %reduce-scatter.34.cloned.1.call-done = bf16[48,1472]{1,0:T(8,128)(2,1)} async-done(((bf16[384,1472]{1,0:T(8,128)(2,1)}), bf16[48,1472]{1,0:T(8,128)(2,1)}) %reduce-scatter.34.cloned.1.call-update) | async-done | bytes 141328 | tf_op jit(solution)/shard_map/reduce_scatter | solution.py:391
  1048.2 33.4 %reduce-scatter.36.cloned.1.call-done = bf16[1472,48]{0,1:T(8,128)(2,1)} async-done(((bf16[1472,384]{0,1:T(8,128)(2,1)}), bf16[1472,48]{0,1:T(8,128)(2,1)}) %reduce-scatter.36.cloned.1.call-update) | async-done | bytes 141328 | tf_op jit(solution)/shard_map/reduce_scatter | solution.py:374
  1081.6 116.2 %reduce-scatter.40.cloned.1.call-done = bf16[1472,448]{0,1:T(8,128)(2,1)} async-done(((bf16[1472,3584]{0,1:T(8,128)(2,1)}), bf16[1472,448]{0,1:T(8,128)(2,1)}) %reduce-scatter.40.cloned.1.call-update) | async-done | bytes 1318928 | tf_op jit(solution)/shard_map/reduce_scatter | solution.py:383
  1197.8 115.1 %reduce-scatter.42.cloned.1.call-done = bf16[1472,448]{0,1:T(8,128)(2,1)} async-done(((bf16[1472,3584]{0,1:T(8,128)(2,1)}), bf16[1472,448]{0,1:T(8,128)(2,1)}) %reduce-scatter.42.cloned.1.call-update) | async-done | bytes 1318928 | tf_op jit(solution)/shard_map/reduce_scatter | solution.py:386
  1312.9 114.9 %reduce-scatter.44.cloned.1.call-done = bf16[448,1472]{1,0:T(8,128)(2,1)} async-done(((bf16[3584,1472]{1,0:T(8,128)(2,1)}), bf16[448,1472]{1,0:T(8,128)(2,1)}) %reduce-scatter.44.cloned.1.call-update) | async-done | bytes 1318928 | tf_op jit(solution)/shard_map/reduce_scatter | solution.py:397
  1428.9 7.0 convolution_add_fusion.1
  1435.9 8.0 stack_reshape.7
  1444.0 6.5 copy.274
  1450.4 8.2 stack_reshape.6
  1458.7 6.9 copy.273
  1467.5 10.1 maximum_bitcast_fusion
  1492.5 43.2 %all-reduce.4 = (f32[1472]{0:T(1024)}, f32[32,6]{0,1:T(8,128)}, f32[1472]{0:T(1024)}, f32[1472]{0:T(1024)}) all-reduce(f32[1472]{0:T(1024)S(1)} %add.502, f32[32,6]{0,1:T(8,128)S(1)} %fusion.98, f32[1472]{0:T(1024)S(1)} %add.508, f32[1472]{0:T(1024)S(1)} %add.513), channel_id=1, replica_groups=mesh['seq'=8,'mem'=4] {'seq','mem'}, use_global_device_ids=true, to_apply=%region_36.37 | all-reduce | flops 4608 | bytes 36864 | tf_op jit(solution)/shard_map/psum | solution.py:414
  1541.1 28.0 %all-reduce.9.cloned.1.call-done = (bf16[1472,48]{1,0:T(8,128)(2,1)}, bf16[1472,48]{1,0:T(8,128)(2,1)}, bf16[1472,48]{0,1:T(8,128)(2,1)}, bf16[1472,48]{0,1:T(8,...) async-done(((bf16[1472,48]{1,0:T(8,128)(2,1)}, ...) | async-done | bytes 5087248 | tf_op jit(solution)/shard_map/psum | solution.py:406
  (599 shorter events, 251.3 us)
Async XLA Ops:
  7.2 29.7 %all-gather.20.cloned.1.call-start = ((), (), s32[]{:S(2)}) async-start(), calls=%async_computation.15 | async-start | bytes 1327104 | tf_op jit(solution)/shard_map/all_gather | solution.py:75
  8.0 49.7 %all-gather.22.cloned.1.call-start = ((), (), s32[]{:S(2)}) async-start(), calls=%async_computation.16 | async-start | bytes 1327104 | tf_op jit(solution)/shard_map/all_gather | solution.py:73
  8.7 73.0 %all-gather.24.cloned.1.call-start = ((), (), s32[]{:S(2)}) async-start(), calls=%async_computation.17 | async-start | bytes 1327104 | tf_op jit(solution)/shard_map/all_gather | solution.py:74
  9.4 96.2 %all-gather.26.cloned.1.call-start = ((), (), s32[]{:S(2)}) async-start(), calls=%async_computation.18 | async-start | bytes 1327104 | tf_op jit(solution)/shard_map/all_gather | solution.py:83
  10.0 119.6 %all-gather.32.cloned.1.call-start = ((), (), s32[]{:S(2)}) async-start(), calls=%async_computation.21 | async-start | bytes 1327104 | tf_op jit(solution)/shard_map/all_gather | solution.py:77
  10.6 143.0 %all-gather.30.cloned.1.call-start = ((), (), s32[]{:S(2)}) async-start(), calls=%async_computation.20 | async-start | bytes 1327104 | tf_op jit(solution)/shard_map/all_gather | solution.py:76
  11.2 173.4 %all-gather.28.cloned.1.call-start = ((), (), s32[]{:S(2)}) async-start(), calls=%async_computation.19 | async-start | bytes 1327104 | tf_op jit(solution)/shard_map/all_gather | solution.py:78
  11.9 262.4 %all-gather.34.cloned.1.call-start = ((), (), s32[]{:S(2)}) async-start(), calls=%async_computation.22 | async-start | bytes 1327104 | tf_op jit(solution)/shard_map/all_gather | solution.py:84
  12.7 261.7 %reduce-scatter.50.cloned.1.call-start = ((), (), s32[]{:S(2)}) async-start(), calls=%async_computation.37 | async-start | bytes 1966080
  13.5 18.1 %copy-start.160 = (f32[256]{0:T(256)}, f32[256]{0:T(256)S(1)}, u32[]{:S(2)}) copy-start(f32[256]{0:T(256)S(1)} %get-tuple-element.164) | copy-start | bytes 3076
  14.1 67.6 %copy-start.150 = (f32[256]{0:T(256)}, f32[256]{0:T(256)S(1)}, u32[]{:S(2)}) copy-start(f32[256]{0:T(256)S(1)} %fusion.186) | copy-start | bytes 3076
  14.1 97.8 %copy-start.127 = (f32[1472]{0:T(1024)}, f32[1472]{0:T(1024)S(1)}, u32[]{:S(2)}) copy-start(f32[1472]{0:T(1024)S(1)} %convert_element_type.650) | copy-start | bytes 17668
  19.8 65.9 %copy-start.26 = (f32[256,256,6]{0,1,2:T(8,128)}, f32[256,256,6]{0,1,2:T(8,128)S(1)}, u32[]{:S(2)}) copy-start(f32[256,256,6]{0,1,2:T(8,128)S(1)} %copy.221) | copy-start | bytes 4718596
  31.6 80.3 %copy-start.152 = (f32[256]{0:T(256)}, f32[256]{0:T(256)S(1)}, u32[]{:S(2)}) copy-start(f32[256]{0:T(256)S(1)} %fusion.183) | copy-start | bytes 3076
  60.0 25.7 %copy-start.88 = (bf16[256,384]{0,1:T(8,128)(2,1)}, bf16[256,384]{0,1:T(8,128)(2,1)S(1)}, u32[]{:S(2)}) copy-start(bf16[256,384]{0,1:T(8,128)(2,1)S(1)} %copy.232) | copy-start | bytes 589828
  90.4 17.3 %copy-start.115 = (bf16[6,64,256]{2,1,0:T(8,128)(2,1)}, bf16[6,64,256]{2,1,0:T(8,128)(2,1)S(1)}, u32[]{:S(2)}) copy-start(bf16[6,64,256]{2,1,0:T(8,128)(2,1)S(1)} %convolution_convert_fusion.26) | copy-start | bytes 589828
  107.8 196.0 %copy-start.6 = (f32[256,1472]{0,1:T(8,128)}, f32[256,1472]{0,1:T(8,128)S(1)}, u32[]{:S(2)}) copy-start(f32[256,1472]{0,1:T(8,128)S(1)} %get-tuple-element.231) | copy-start | bytes 4521988
  107.8 81.9 %copy-start.156 = (f32[256]{0:T(256)}, f32[256]{0:T(256)S(1)}, u32[]{:S(2)}) copy-start(f32[256]{0:T(256)S(1)} %fusion.187) | copy-start | bytes 3076
  120.6 19.3 %copy-start.146 = (f32[6,256]{1,0:T(8,128)}, f32[6,256]{1,0:T(8,128)S(1)}, u32[]{:S(2)}) copy-start(f32[6,256]{1,0:T(8,128)S(1)} %get-tuple-element.234) | copy-start | bytes 18436
  142.4 11.2 copy-start.129
  145.6 24.2 %copy-start.166 = (f32[256]{0:T(256)}, f32[256]{0:T(256)S(1)}, u32[]{:S(2)}) copy-start(f32[256]{0:T(256)S(1)} %get-tuple-element.236) | copy-start | bytes 3076
  145.6 24.2 %copy-start.154 = (f32[256]{0:T(256)}, f32[256]{0:T(256)S(1)}, u32[]{:S(2)}) copy-start(f32[256]{0:T(256)S(1)} %fusion.184) | copy-start | bytes 3076
  198.3 12.7 copy-start.123
  211.1 27.7 %copy-start.37 = (bf16[4,256,6,64]{1,0,3,2:T(4,128)(2,1)}, bf16[4,256,6,64]{1,0,3,2:T(4,128)(2,1)S(1)}, u32[]{:S(2)}) copy-start(bf16[4,256,6,64]{1,0,3,2:T(4,128)(2,1)S(1)} %reshape.610) | copy-start | bytes 2359300
  238.7 65.0 %reduce-scatter.52.cloned.1.call-start = ((), (), s32[]{:S(2)}) async-start(), calls=%async_computation.38 | async-start | bytes 1966080
  241.8 10.5 copy-start.3
  250.8 9.4 copy-start.57
  250.8 9.4 copy-start.68
  272.0 134.3 %all-gather.36.cloned.1.call-start = ((), (), s32[]{:S(2)}) async-start(), calls=%async_computation.23 | async-start | bytes 12386304 | tf_op jit(solution)/shard_map/all_gather | solution.py:79
  272.7 237.1 %all-gather.38.cloned.1.call-start = ((), (), s32[]{:S(2)}) async-start(), calls=%async_computation.24 | async-start | bytes 12386304 | tf_op jit(solution)/shard_map/all_gather | solution.py:80
  273.3 340.3 %all-gather.40.cloned.1.call-start = ((), (), s32[]{:S(2)}) async-start(), calls=%async_computation.25 | async-start | bytes 12386304 | tf_op jit(solution)/shard_map/all_gather | solution.py:85
  274.1 535.2 %reduce-scatter.56.cloned.1.call-start = ((), (), s32[]{:S(2)}) async-start(), calls=%async_computation.40 | async-start | bytes 983040
  277.6 29.3 %copy-start.28 = (f32[256,1472]{0,1:T(8,128)S(1)}, f32[256,1472]{0,1:T(8,128)}, u32[]{:S(2)}) copy-start(f32[256,1472]{0,1:T(8,128)} %get-tuple-element.241) | copy-start | bytes 4521988
  307.2 202.7 %copy-start.39 = (bf16[256,1472]{0,1:T(8,128)(2,1)}, bf16[256,1472]{0,1:T(8,128)(2,1)S(1)}, u32[]{:S(2)}) copy-start(bf16[256,1472]{0,1:T(8,128)(2,1)S(1)} %multiply_convert_fusion.10) | copy-start | bytes 2260996
  624.8 11.0 copy-start.79
  624.8 11.0 copy-start.78
  624.8 11.0 copy-start.47
  680.2 10.6 copy-start.29
  680.2 10.6 copy-start.106
  693.0 26.7 %copy-start.16 = (f32[256,1472]{0,1:T(8,128)}, f32[256,1472]{0,1:T(8,128)S(1)}, u32[]{:S(2)}) copy-start(f32[256,1472]{0,1:T(8,128)S(1)} %get-tuple-element.217) | copy-start | bytes 4521988
  731.9 23.3 %copy-start.99 = (f32[4,6,256]{2,1,0:T(8,128)S(1)}, f32[4,6,256]{2,1,0:T(8,128)}, u32[]{:S(2)}) copy-start(f32[4,6,256]{2,1,0:T(8,128)} %copy-done.98) | copy-start | bytes 73732
  731.9 23.3 %copy-start.101 = (f32[4,6,256]{2,1,0:T(8,128)S(1)}, f32[4,6,256]{2,1,0:T(8,128)}, u32[]{:S(2)}) copy-start(f32[4,6,256]{2,1,0:T(8,128)} %copy-done.100) | copy-start | bytes 73732
  762.5 55.1 %reduce-scatter.54.cloned.1.call-start = ((), (), s32[]{:S(2)}) async-start(), calls=%async_computation.39 | async-start | bytes 983040
  770.4 194.0 %reduce-scatter.46.cloned.1.call-start = ((), (), s32[]{:S(2)}) async-start(), calls=%async_computation.35 | async-start | bytes 1327104
  785.3 180.9 %reduce-scatter.48.cloned.1.call-start = ((), (), s32[]{:S(2)}) async-start(), calls=%async_computation.36 | async-start | bytes 1327104
  805.8 162.3 %reduce-scatter.38.cloned.1.call-start = ((), (), s32[]{:S(2)}) async-start(), calls=%async_computation.31 | async-start | bytes 1327104 | tf_op jit(solution)/shard_map/reduce_scatter | solution.py:394
  809.0 159.1 %reduce-scatter.28.cloned.1.call-start = ((), (), s32[]{:S(2)}) async-start(), calls=%async_computation.26 | async-start | bytes 1327104 | tf_op jit(solution)/shard_map/reduce_scatter | solution.py:365
  812.6 9.2 copy-start.167
  812.6 9.2 copy-start.165
  836.6 145.2 %reduce-scatter.30.cloned.1.call-start = ((), (), s32[]{:S(2)}) async-start(), calls=%async_computation.27 | async-start | bytes 1327104 | tf_op jit(solution)/shard_map/reduce_scatter | solution.py:368
  842.1 172.8 %reduce-scatter.32.cloned.1.call-start = ((), (), s32[]{:S(2)}) async-start(), calls=%async_computation.28 | async-start | bytes 1327104 | tf_op jit(solution)/shard_map/reduce_scatter | solution.py:371
  849.5 198.7 %reduce-scatter.34.cloned.1.call-start = ((), (), s32[]{:S(2)}) async-start(), calls=%async_computation.29 | async-start | bytes 1327104 | tf_op jit(solution)/shard_map/reduce_scatter | solution.py:391
  853.2 228.4 %reduce-scatter.36.cloned.1.call-start = ((), (), s32[]{:S(2)}) async-start(), calls=%async_computation.30 | async-start | bytes 1327104 | tf_op jit(solution)/shard_map/reduce_scatter | solution.py:374
  857.3 11.9 copy-start.52
  857.3 340.5 %reduce-scatter.40.cloned.1.call-start = ((), (), s32[]{:S(2)}) async-start(), calls=%async_computation.32 | async-start | bytes 12386304 | tf_op jit(solution)/shard_map/reduce_scatter | solution.py:383
  882.5 430.4 %reduce-scatter.42.cloned.1.call-start = ((), (), s32[]{:S(2)}) async-start(), calls=%async_computation.33 | async-start | bytes 12386304 | tf_op jit(solution)/shard_map/reduce_scatter | solution.py:386
  906.7 521.1 %reduce-scatter.44.cloned.1.call-start = ((), (), s32[]{:S(2)}) async-start(), calls=%async_computation.34 | async-start | bytes 12386304 | tf_op jit(solution)/shard_map/reduce_scatter | solution.py:397
  932.2 636.9 %all-reduce.9.cloned.1.call-start = ((), (), s32[]{:S(2)}) async-start(), calls=%async_computation.41 | async-start | bytes 11534336 | tf_op jit(solution)/shard_map/psum | solution.py:406
  944.5 9.9 copy-start.30
  944.5 9.9 copy-start.64
  1467.5 10.1 copy-start.32
  1491.1 44.6 %copy-start.161 = (f32[256]{0:T(256)S(1)}, f32[256]{0:T(256)}, u32[]{:S(2)}) copy-start(f32[256]{0:T(256)} %copy-done.160) | copy-start | bytes 3076
  1491.1 44.6 %copy-start.163 = (f32[256]{0:T(256)S(1)}, f32[256]{0:T(256)}, u32[]{:S(2)}) copy-start(f32[256]{0:T(256)} %copy-done.162) | copy-start | bytes 3076
  1491.1 44.6 %copy-start.13 = (f32[256,1472]{0,1:T(8,128)S(1)}, f32[256,1472]{0,1:T(8,128)}, u32[]{:S(2)}) copy-start(f32[256,1472]{0,1:T(8,128)} %get-tuple-element.221) | copy-start | bytes 4521988
  (142 other events, 462.1 us)
Sparse Core Ops, SparseCore 0:
  9.7 23.7 all-gather.19
  35.2 22.4 all-gather.21
  59.3 22.4 all-gather.23
  83.2 22.4 all-gather.25
  107.2 22.4 all-gather.31
  131.1 22.4 all-gather.29
  155.2 22.4 all-gather.27
  179.4 22.2 all-gather.33
  238.9 30.4 reduce-scatter.49
  272.8 30.8 reduce-scatter.51
  305.4 100.8 all-gather.35
  407.8 102.0 all-gather.37
  511.5 102.0 all-gather.39
  762.6 26.0 reduce-scatter.55
  791.5 26.1 reduce-scatter.53
  819.8 29.0 reduce-scatter.45
  851.0 30.9 reduce-scatter.47
  884.1 30.9 reduce-scatter.37
  917.4 31.0 reduce-scatter.27
  950.6 31.0 reduce-scatter.29
  984.1 30.7 reduce-scatter.31
  1017.2 30.9 reduce-scatter.33
  1050.5 31.0 reduce-scatter.35
  1084.3 113.4 reduce-scatter.39
  1200.1 112.7 reduce-scatter.41
  1315.0 112.7 reduce-scatter.43
  1433.7 135.3 all-reduce.8
where the time goes:
time: 1600 us; the launch traced here: 1590 us
  waiting for transfers between devices  886 us (55%)
  matrix products  361 us (23%)
  blocking collectives  142 us (9%)
  local copies, waits for them, and re-layouts  125 us (8%)
  other arithmetic  58.4 us (4%)
  between operations  17.1 us (1%)
    reduce_scatter x1, waiting for transfers between devices, per_device(): lax.psum_scatter(grad_gate.astype(jnp.bfloat16), 'seq', scatter_dimension...  116 us
    reduce_scatter x1, waiting for transfers between devices, per_device(): lax.psum_scatter(grad_linear.astype(jnp.bfloat16), 'seq', scatter_dimensi...  115 us
    reduce_scatter x1, waiting for transfers between devices, per_device(): lax.psum_scatter(grad_down.astype(jnp.bfloat16), 'seq', scatter_dimension...  115 us
    dot_general x24, matrix products, contract_rows(): lax.dot_general(left, right, (((0,), (0,)), ((), ())), preferred_element_...  100 us
    all_gather x1, waiting for transfers between devices, fetch_weights(): lax.all_gather(columns[6], 'seq', axis=1, tiled=True)  99.1 us
    dot_general x22, matrix products, matmul(): return jnp.dot(left, right, preferred_element_type=jnp.float32)  97.3 us
    dot_general x22, matrix products, contract_cols(): lax.dot_general(left, right, (((1,), (1,)), ((), ())), preferred_element_...  94.9 us
    all_gather x1, waiting for transfers between devices, fetch_weights(): lax.all_gather(row_parts[2], 'seq', axis=0, tiled=True)  94.7 us
  transfers between devices with their start and end apart: 27, of which 18 were waited for; matrix products, arithmetic and copies ran while one was open for 25% of the time, Pallas kernels for 0%

commit v1 on v0

v1 whole, which is shorter than its diff:
```python
import functools
import math

import jax
import jax.numpy as jnp
from jax import lax
from jax.experimental import pallas as pl
from jax.experimental.pallas import tpu as pltpu
from jax.sharding import PartitionSpec as P

norm_eps = 1e-06
masked_score = -1e30
bf16 = jnp.bfloat16
f32 = jnp.float32


def bucket_edges():
    return [math.ceil(16 * 8 ** ((number - 16) / 16)) for number in range(17, 32)]


def position_buckets(length):
    row_index = jnp.arange(length, dtype=jnp.int32)
    offset = jnp.maximum(row_index[:, None] - row_index[None, :], 0)
    bucket = jnp.minimum(offset, 16)
    for threshold in bucket_edges():
        bucket = bucket + (offset >= threshold).astype(jnp.int32)
    return bucket


def matmul(left, right):
    return jnp.dot(left, right, preferred_element_type=f32)


def contract_rows(left, right):
    return lax.dot_general(left, right, (((0,), (0,)), ((), ())), preferred_element_type=f32)


def contract_cols(left, right):
    return lax.dot_general(left, right, (((1,), (1,)), ((), ())), preferred_element_type=f32)


def add_low(left, right):
    return (left.astype(f32) + right.astype(f32)).astype(bf16)


def to_core(value):
    count = lax.axis_size("seq")
    return lax.ppermute(value, "seq", [(i, i ^ 1) for i in range(count)])


def to_next(value):
    count = lax.axis_size("seq")
    return lax.ppermute(value, "seq", [(i, (i + 2) % count) for i in range(count)])


def to_mem(value, mask):
    count = lax.axis_size("mem")
    return lax.ppermute(value, "mem", [(i, i ^ mask) for i in range(count)])


def mem_bits():
    return [1 << b for b in range((lax.axis_size("mem") - 1).bit_length())]


def to_step(value, step):
    count = lax.axis_size("seq")
    return lax.ppermute(value, "seq", [(i, (i + 2 * step) % count) for i in range(count)])


def to_seq(value, mask):
    count = lax.axis_size("seq")
    return lax.ppermute(value, "seq", [(i, i ^ mask) for i in range(count)])


def after(value, *others):
    return lax.optimization_barrier((value, *others))[0]


def ring_gather(value):
    pieces = [value]
    for _ in range(lax.axis_size("seq") // 2 - 1):
        pieces.append(to_next(pieces[-1]))
    return pieces


def ring_sum(pieces):
    total = pieces[1]
    for piece in pieces[2:]:
        total = add_low(to_next(total), piece)
    return add_low(to_next(total), pieces[0])


def spread_gather(value, bits):
    held, order = value[None], [0]
    for bit in bits:
        held = jnp.concatenate([held, to_mem(held, bit)], axis=0)
        order = order + [k | bit for k in order]
    return [held[order.index(k)] for k in range(len(order))]


def fold(held, bits):
    order = list(range(held.shape[0]))
    for bit in bits:
        keep = [i for i, k in enumerate(order) if not k & bit]
        send = [order.index(order[i] | bit) for i in keep]
        moved = to_mem(jnp.stack([held[i] for i in send]), bit)
        held = jnp.stack([add_low(held[i], moved[n]) for n, i in enumerate(keep)])
        order = [order[i] for i in keep]
    return held[0]


def sum_low(pieces):
    total = pieces[0].astype(f32)
    for piece in pieces[1:]:
        total = total + piece.astype(f32)
    return total.astype(bf16)


def direct_fold(pieces):
    return sum_low([to_mem(p, k) if k else p for k, p in enumerate(pieces)])


def natural(pieces, mem_index):
    stacked = jnp.stack(pieces)
    return jnp.stack(
        [
            lax.dynamic_index_in_dim(stacked, mem_index ^ k, 0, keepdims=False)
            for k in range(len(pieces))
        ]
    )


def back_to_mem(value, mem_index):
    pieces = [to_mem(value, k) if k else value for k in range(lax.axis_size("mem"))]
    return natural(pieces, mem_index).astype(f32)


def assemble_kernel(spot, own, other, out):
    chips = own.shape[0]
    core, chip = spot[0], spot[1]
    for j in range(chips):
        at = lax.rem(chip - j + chips, chips) * 2
        out[0, at + core] = own[j, 0]
        out[0, at + 1 - core] = other[j, 0]


def assemble(spot, own, other):
    chips, mems, share, width = own.shape
    block = pl.BlockSpec((chips, 1, share, width), lambda q, spot: (0, spot[2 + q], 0, 0))
    return pl.pallas_call(
        assemble_kernel,
        grid_spec=pltpu.PrefetchScalarGridSpec(
            num_scalar_prefetch=1,
            grid=(mems,),
            in_specs=[block, block],
            out_specs=pl.BlockSpec((1, 2 * chips, share, width), lambda q, spot: (q, 0, 0, 0)),
        ),
        out_shape=jax.ShapeDtypeStruct((mems, 2 * chips, share, width), bf16),
        compiler_params=params(32),
        name="assemble",
    )(spot, own, other)

def params(limit_mb=56):
    return pltpu.CompilerParams(vmem_limit_bytes=limit_mb * 1024 * 1024)


def row_norm(value):
    return lax.rsqrt(jnp.mean(value * value, axis=-1, keepdims=True) + norm_eps)


def norm_back_rows(value, gain, upstream):
    scale = row_norm(value)
    weighted = upstream * gain
    mean_dot = jnp.mean(weighted * value, axis=-1, keepdims=True)
    gain_grad = jnp.sum(upstream * value * scale, axis=0, keepdims=True)
    return weighted * scale - value * (scale * scale * scale * mean_dot), gain_grad


def lane_head(length, depth):
    return lax.broadcasted_iota(jnp.int32, (length, 128), 1) // depth


def self_fwd_kernel(depth, length, tok, g1, qw, kw, vw, ow, bias, g2, cw, normed_o, q_o, k_o, v_o, mixed_o, first_o, nc_o, cq_o):
    x = tok[...].astype(f32)
    normed = (x * row_norm(x) * g1[...]).astype(bf16)
    normed_o[...] = normed
    q_o[...] = contract_cols(normed, qw[...]).astype(bf16)
    k_o[...] = contract_cols(normed, kw[...]).astype(bf16)
    v_o[...] = contract_cols(normed, vw[...]).astype(bf16)
    inner = qw.shape[0]
    groups, share = inner // 128, 128 // depth
    lanes = lane_head(length, depth)

    def body(step, carry):
        micro, group = step // groups, step % groups
        rows = pl.ds(pl.multiple_of(micro * length, length), length)
        cols = pl.ds(pl.multiple_of(group * 128, 128), 128)
        q, k, v = q_o[rows, cols], k_o[rows, cols], v_o[rows, cols]
        out = jnp.zeros((length, 128), f32)
        for a in range(share):
            s = contract_cols(jnp.where(lanes == a, q, 0), k) + bias[group * share + a]
            e = jnp.exp(s - jnp.max(s, axis=-1, keepdims=True))
            p = (e / jnp.sum(e, axis=-1, keepdims=True)).astype(bf16)
            out = jnp.where(lanes == a, matmul(p, v), out)
        mixed_o[rows, cols] = out.astype(bf16)
        return carry

    lax.fori_loop(0, x.shape[0] // length * groups, body, 0)
    first = tok[...].astype(f32) + matmul(mixed_o[...], ow[...])
    first_o[...] = first
    nc = (first * row_norm(first) * g2[...]).astype(bf16)
    nc_o[...] = nc
    cq_o[...] = contract_cols(nc, cw[...]).astype(bf16)


def self_fwd(depth, length, tok, g1, qw, kw, vw, ow, bias, g2, cw):
    rows, width = tok.shape
    inner = qw.shape[0]
    low, slim = jax.ShapeDtypeStruct((rows, width), bf16), jax.ShapeDtypeStruct((rows, inner), bf16)
    return pl.pallas_call(
        functools.partial(self_fwd_kernel, depth, length),
        out_shape=(low, slim, slim, slim, slim, jax.ShapeDtypeStruct((rows, width), f32), low, slim),
        compiler_params=params(),
        name="self_fwd",
    )(tok, g1, qw, kw, vw, ow, bias, g2, cw)


def cross_fwd_kernel(depth, length, parts, cq, mask, ow, first, g3, *refs):
    kvs, (mixed_o, second_o, nf_o) = refs[:parts], refs[parts:]
    inner = ow.shape[0]
    groups, share = inner // 128, 128 // depth
    lanes = lane_head(length, depth)

    def body(step, carry):
        micro, group = step // groups, step % groups
        rows = pl.ds(pl.multiple_of(micro * length, length), length)
        cols = pl.ds(pl.multiple_of(group * 128, 128), 128)
        vcols = pl.ds(pl.multiple_of(inner + group * 128, 128), 128)
        q = cq[rows, cols]
        k = jnp.concatenate([kv[micro, :, cols] for kv in kvs], axis=0)
        v = jnp.concatenate([kv[micro, :, vcols] for kv in kvs], axis=0)
        out = jnp.zeros((length, 128), f32)
        for a in range(share):
            s = contract_cols(jnp.where(lanes == a, q, 0), k)
            s = jnp.where(mask[micro] > 0, s, masked_score)
            e = jnp.exp(s - jnp.max(s, axis=-1, keepdims=True))
            p = (e / jnp.sum(e, axis=-1, keepdims=True)).astype(bf16)
            out = jnp.where(lanes == a, matmul(p, v), out)
        mixed_o[rows, cols] = out.astype(bf16)
        return carry

    lax.fori_loop(0, cq.shape[0] // length * groups, body, 0)
    second = first[...] + matmul(mixed_o[...], ow[...])
    second_o[...] = second
    nf_o[...] = (second * row_norm(second) * g3[...]).astype(bf16)


def cross_fwd(depth, length, cq, mask, ow, first, g3, kvs):
    rows, width = first.shape
    return pl.pallas_call(
        functools.partial(cross_fwd_kernel, depth, length, len(kvs)),
        out_shape=(
            jax.ShapeDtypeStruct(cq.shape, bf16),
            jax.ShapeDtypeStruct((rows, width), f32),
            jax.ShapeDtypeStruct((rows, width), bf16),
        ),
        compiler_params=params(),
        name="cross_fwd",
    )(cq, mask, ow, first, g3, *kvs)


def cross_bwd_kernel(depth, length, parts, og, nf_own, nf_more, second, g3, mixed, cq, mask, ow, first, g2, nc, qw, *refs):
    kvs = refs[:parts]
    kvg = refs[parts : 2 * parts]
    g3_o, dow_o, dqw_o, firstg_o, g2_o, mixg, dq = refs[2 * parts :]
    inner = ow.shape[0]
    slots = kvs[0].shape[1]
    groups, share = inner // 128, 128 // depth
    lanes = lane_head(length, depth)
    part, gain = norm_back_rows(second[...], g3[...], nf_own[...] + nf_more[...].astype(f32))
    g3_o[...] = gain
    second_grad = og[...].astype(f32) + part
    firstg_o[...] = second_grad
    low = second_grad.astype(bf16)
    dow_o[...] = contract_rows(mixed[...], low).astype(bf16)
    mixg[...] = contract_cols(low, ow[...]).astype(bf16)

    def body(step, carry):
        micro, group = step // groups, step % groups
        rows = pl.ds(pl.multiple_of(micro * length, length), length)
        cols = pl.ds(pl.multiple_of(group * 128, 128), 128)
        vcols = pl.ds(pl.multiple_of(inner + group * 128, 128), 128)
        q, o = cq[rows, cols], mixg[rows, cols]
        k = jnp.concatenate([kv[micro, :, cols] for kv in kvs], axis=0)
        v = jnp.concatenate([kv[micro, :, vcols] for kv in kvs], axis=0)
        q_grad = jnp.zeros((length, 128), f32)
        k_grad = jnp.zeros((parts * slots, 128), f32)
        v_grad = jnp.zeros((parts * slots, 128), f32)
        for a in range(share):
            qa, oa = jnp.where(lanes == a, q, 0), jnp.where(lanes == a, o, 0)
            s = contract_cols(qa, k)
            s = jnp.where(mask[micro] > 0, s, masked_score)
            e = jnp.exp(s - jnp.max(s, axis=-1, keepdims=True))
            p = e / jnp.sum(e, axis=-1, keepdims=True)
            v_grad += contract_rows(p.astype(bf16), oa)
            dp = contract_cols(oa, v)
            ds = (p * (dp - jnp.sum(p * dp, axis=-1, keepdims=True))).astype(bf16)
            q_grad = jnp.where(lanes == a, matmul(ds, k), q_grad)
            k_grad += contract_rows(ds, qa)
        dq[rows, cols] = q_grad.astype(bf16)
        for t in range(parts):
            kvg[t][micro, :, cols] = k_grad[t * slots : (t + 1) * slots].astype(bf16)
            kvg[t][micro, :, vcols] = v_grad[t * slots : (t + 1) * slots].astype(bf16)
        return carry

    lax.fori_loop(0, cq.shape[0] // length * groups, body, 0)
    dqw_o[...] = contract_rows(dq[...], nc[...]).astype(bf16)
    part, gain = norm_back_rows(first[...], g2[...], matmul(dq[...], qw[...]))
    g2_o[...] = gain
    firstg_o[...] = firstg_o[...] + part


def cross_bwd(depth, length, og, nf_own, nf_more, second, g3, mixed, cq, mask, ow, first, g2, nc, qw, kvs):
    rows, width = first.shape
    gain = jax.ShapeDtypeStruct((1, width), f32)
    weight = jax.ShapeDtypeStruct(ow.shape, bf16)
    out = pl.pallas_call(
        functools.partial(cross_bwd_kernel, depth, length, len(kvs)),
        out_shape=(
            *[jax.ShapeDtypeStruct(kv.shape, bf16) for kv in kvs],
            gain,
            weight,
            weight,
            jax.ShapeDtypeStruct((rows, width), f32),
            gain,
        ),
        scratch_shapes=[pltpu.VMEM(cq.shape, bf16), pltpu.VMEM(cq.shape, bf16)],
        compiler_params=params(),
        name="cross_bwd",
    )(og, nf_own, nf_more, second, g3, mixed, cq, mask, ow, first, g2, nc, qw, *kvs)
    return out[: len(kvs)], out[len(kvs) :]


def self_bwd_kernel(depth, length, first_grad, mixed, q, k, v, bias, ow, qw, kw, vw, normed, tok, g1, dow_o, dqw_o, dkw_o, dvw_o, ing_o, g1_o, ds_o, mixg, dq, dk, dv):
    inner = ow.shape[0]
    groups, share = inner // 128, 128 // depth
    lanes = lane_head(length, depth)
    low = first_grad[...].astype(bf16)
    dow_o[...] = contract_rows(mixed[...], low).astype(bf16)
    mixg[...] = contract_cols(low, ow[...]).astype(bf16)

    def body(group, carry):
        cols = pl.ds(pl.multiple_of(group * 128, 128), 128)
        total = [jnp.zeros((length, length), f32) for _ in range(share)]
        for micro in range(tok.shape[0] // length):
            rows = slice(micro * length, (micro + 1) * length)
            qs, ks, vs, o = q[rows, cols], k[rows, cols], v[rows, cols], mixg[rows, cols]
            q_grad = jnp.zeros((length, 128), f32)
            k_grad = jnp.zeros((length, 128), f32)
            v_grad = jnp.zeros((length, 128), f32)
            for a in range(share):
                qa, oa = jnp.where(lanes == a, qs, 0), jnp.where(lanes == a, o, 0)
                s = contract_cols(qa, ks) + bias[group * share + a]
                e = jnp.exp(s - jnp.max(s, axis=-1, keepdims=True))
                p = e / jnp.sum(e, axis=-1, keepdims=True)
                v_grad += contract_rows(p.astype(bf16), oa)
                dp = contract_cols(oa, vs)
                ds = (p * (dp - jnp.sum(p * dp, axis=-1, keepdims=True))).astype(bf16)
                total[a] = total[a] + ds.astype(f32)
                q_grad = jnp.where(lanes == a, matmul(ds, ks), q_grad)
                k_grad += contract_rows(ds, qa)
            dq[rows, cols] = q_grad.astype(bf16)
            dk[rows, cols] = k_grad.astype(bf16)
            dv[rows, cols] = v_grad.astype(bf16)
        for a in range(share):
            ds_o[group * share + a] = total[a]
        return carry

    lax.fori_loop(0, groups, body, 0)
    dqw_o[...] = contract_rows(dq[...], normed[...]).astype(bf16)
    dkw_o[...] = contract_rows(dk[...], normed[...]).astype(bf16)
    dvw_o[...] = contract_rows(dv[...], normed[...]).astype(bf16)
    up = matmul(dq[...], qw[...]) + matmul(dk[...], kw[...]) + matmul(dv[...], vw[...])
    part, gain = norm_back_rows(tok[...].astype(f32), g1[...], up)
    g1_o[...] = gain
    ing_o[...] = first_grad[...] + part


def self_bwd(depth, length, first_grad, mixed, q, k, v, bias, ow, qw, kw, vw, normed, tok, g1):
    rows, width = tok.shape
    weight = jax.ShapeDtypeStruct(ow.shape, bf16)
    return pl.pallas_call(
        functools.partial(self_bwd_kernel, depth, length),
        out_shape=(
            weight,
            weight,
            weight,
            weight,
            jax.ShapeDtypeStruct((rows, width), f32),
            jax.ShapeDtypeStruct((1, width), f32),
            jax.ShapeDtypeStruct(bias.shape, f32),
        ),
        scratch_shapes=[pltpu.VMEM(q.shape, bf16)] * 4,
        compiler_params=params(),
        name="self_bwd",
    )(first_grad, mixed, q, k, v, bias, ow, qw, kw, vw, normed, tok, g1)


def kv_fwd_kernel(place, source, kw, vw, out):
    inner = kw.shape[0]
    rows = source[0, 0]
    out[0, 0, :, :inner] = contract_cols(rows, kw[...]).astype(bf16)
    out[0, 0, :, inner:] = contract_cols(rows, vw[...]).astype(bf16)


def kv_fwd(place, memory, kw, vw):
    micros, pairs, slots, width = memory.shape
    inner = kw.shape[0]
    whole = pl.BlockSpec((inner, width), lambda s, m, place: (0, 0))
    return pl.pallas_call(
        kv_fwd_kernel,
        grid_spec=pltpu.PrefetchScalarGridSpec(
            num_scalar_prefetch=1,
            grid=(pairs, micros),
            in_specs=[
                pl.BlockSpec((1, 1, slots, width), lambda s, m, place: (m, place[s], 0, 0)),
                whole,
                whole,
            ],
            out_specs=pl.BlockSpec((1, 1, slots, 2 * inner), lambda s, m, place: (s, m, 0, 0)),
        ),
        out_shape=jax.ShapeDtypeStruct((pairs, micros, slots, 2 * inner), bf16),
        compiler_params=params(32),
        name="kv_fwd",
    )(place, memory, kw, vw)


def kv_bwd_kernel(place, source, kw, vw, kvg, out, dkw_o, dvw_o, acc):
    inner = kw.shape[0]
    step = pl.program_id(0) * pl.num_programs(1) + pl.program_id(1)
    grads = kvg[0, 0]

    @pl.when(step == 0)
    def clear():
        acc[...] = jnp.zeros_like(acc)

    out[0, 0] = matmul(grads[:, :inner], kw[...]) + matmul(grads[:, inner:], vw[...])
    acc[...] += contract_rows(grads, source[0, 0])

    @pl.when(step == pl.num_programs(0) * pl.num_programs(1) - 1)
    def write():
        dkw_o[...] = acc[:inner].astype(bf16)
        dvw_o[...] = acc[inner:].astype(bf16)


def kv_bwd(place, memory, kw, vw, kvg):
    micros, pairs, slots, width = memory.shape
    inner = kw.shape[0]
    whole = pl.BlockSpec((inner, width), lambda s, m, place: (0, 0))
    weight = jax.ShapeDtypeStruct((inner, width), bf16)
    block = pl.BlockSpec((1, 1, slots, width), lambda s, m, place: (m, place[s], 0, 0))
    return pl.pallas_call(
        kv_bwd_kernel,
        grid_spec=pltpu.PrefetchScalarGridSpec(
            num_scalar_prefetch=1,
            grid=(pairs, micros),
            in_specs=[
                block,
                whole,
                whole,
                pl.BlockSpec((1, 1, slots, 2 * inner), lambda s, m, place: (s, m, 0, 0)),
            ],
            out_specs=(block, whole, whole),
            scratch_shapes=[pltpu.VMEM((2 * inner, width), f32)],
        ),
        out_shape=(jax.ShapeDtypeStruct(memory.shape, f32), weight, weight),
        compiler_params=params(48),
        name="kv_bwd",
    )(place, memory, kw, vw, kvg)


gelu_c = math.sqrt(2 / math.pi)


def feed_kernel(nf_a, nf_b, og_a, og_b, gw, lw, dw, dgw_o, dlw_o, ddw_o, res_o, res_b, nfg_o, nfg_b, nf, og, res_t, nfg_t, sems):
    step = pl.program_id(0)
    rows = nf_a.shape[0]

    @pl.when(step == 0)
    def load():
        copies = [
            pltpu.make_async_copy(src, dst.at[pl.ds(at, rows)], sems.at[i])
            for i, (src, dst, at) in enumerate([(nf_a, nf, 0), (nf_b, nf, rows), (og_a, og, 0), (og_b, og, rows)])
        ]
        for copy in copies:
            copy.start()
        for copy in copies:
            copy.wait()

    x, up = nf[...], og[...]
    g = contract_cols(x, gw[...])
    lin = contract_cols(x, lw[...])
    hg = contract_cols(up, dw[...])
    t = jnp.tanh(gelu_c * (g + 0.044715 * (g * g * g)))
    act = 0.5 * g * (1.0 + t)
    slope = 0.5 * (1.0 + t) + 0.5 * g * (1.0 - t * t) * (gelu_c * (1.0 + 3 * 0.044715 * (g * g)))
    hidden = (act * lin).astype(bf16)
    gl = (hg * lin * slope).astype(bf16)
    ll = (hg * act).astype(bf16)
    ddw_o[...] = contract_rows(hidden, up).astype(bf16)
    dgw_o[...] = contract_rows(gl, x).astype(bf16)
    dlw_o[...] = contract_rows(ll, x).astype(bf16)
    res = matmul(hidden, dw[...])
    nfg = matmul(gl, gw[...]) + matmul(ll, lw[...])

    @pl.when(step == 0)
    def first():
        res_o[...] = res[:rows]
        res_t[...] = res[rows:]
        nfg_o[...] = nfg[:rows]
        nfg_t[...] = nfg[rows:]

    @pl.when(step > 0)
    def later():
        res_o[...] += res[:rows]
        res_t[...] += res[rows:]
        nfg_o[...] += nfg[:rows]
        nfg_t[...] += nfg[rows:]

    @pl.when(step == pl.num_programs(0) - 1)
    def last():
        res_b[...] = res_t[...].astype(bf16)
        nfg_b[...] = nfg_t[...].astype(bf16)


def feed_layer(nf_a, nf_b, og_a, og_b, gw, lw, dw, block):
    rows, width = nf_a.shape
    hidden = gw.shape[0]
    any_spec = pl.BlockSpec(memory_space=pl.ANY)
    tile = pl.BlockSpec((block, width), lambda i: (i, 0))
    whole = pl.BlockSpec((rows, width), lambda i: (0, 0))
    weight = jax.ShapeDtypeStruct((hidden, width), bf16)
    wide, low = jax.ShapeDtypeStruct((rows, width), f32), jax.ShapeDtypeStruct((rows, width), bf16)
    return pl.pallas_call(
        feed_kernel,
        grid=(hidden // block,),
        in_specs=[any_spec] * 4 + [tile] * 3,
        out_specs=(tile, tile, tile, whole, whole, whole, whole),
        out_shape=(weight, weight, weight, wide, low, wide, low),
        scratch_shapes=[
            pltpu.VMEM((2 * rows, width), bf16),
            pltpu.VMEM((2 * rows, width), bf16),
            pltpu.VMEM((rows, width), f32),
            pltpu.VMEM((rows, width), f32),
            pltpu.SemaphoreType.DMA((4,)),
        ],
        compiler_params=params(60),
        name="feed",
    )(nf_a, nf_b, og_a, og_b, gw, lw, dw)


def per_device(
    inputs,
    memory,
    memory_lengths,
    keep_mask,
    norm_self,
    query_self,
    key_self,
    value_self,
    output_self,
    bias_table,
    norm_cross,
    query_cross,
    key_cross,
    value_cross,
    output_cross,
    norm_feed,
    gate_feed,
    linear_feed,
    down_feed,
    output_grad,
):
    micros = inputs.shape[0]
    length = inputs.shape[3]
    width = inputs.shape[4]
    pairs = memory.shape[2]
    slots = memory.shape[3]
    heads = bias_table.shape[1]
    buckets = bias_table.shape[0]
    seqs = lax.axis_size("seq")
    mems = lax.axis_size("mem")
    chips = seqs // 2
    slim = query_self.shape[1]
    inner = slim * seqs
    depth = inner // heads
    feed = gate_feed.shape[1]
    part = feed // mems
    rows = micros * length
    seq_index = lax.axis_index("seq")
    core = seq_index % 2
    chip = seq_index // 2
    mem_index = lax.axis_index("mem")
    gain_self = norm_self.astype(f32)
    gain_cross = norm_cross.astype(f32)
    gain_feed = norm_feed.astype(f32)


    bits = mem_bits()
    spot = jnp.stack([core, chip] + [mem_index ^ q for q in range(mems)]).astype(jnp.int32)

    def quarters(shard):
        shard = shard.reshape(mems, shard.shape[0] // mems, width)
        return jnp.stack(
            [lax.dynamic_index_in_dim(shard, mem_index ^ k, 0, keepdims=False) for k in range(mems)]
        )

    first_pack = quarters(jnp.concatenate([key_cross.T, value_cross.T, query_self.T, key_self.T], axis=0))
    second_pack = jnp.concatenate([value_self.T, output_self, query_cross.T, output_cross], axis=0)
    ring = ring_gather(first_pack[0])
    others = jnp.stack(ring[1:])
    spread = jnp.stack([to_mem(others, k) if k else others for k in range(mems)], axis=1)
    held = jnp.concatenate([first_pack[None], spread], axis=0)
    first_mats = assemble(spot, held, to_core(held))
    first_mats = (
        first_mats.reshape(4, mems // 4, seqs, -1, width).transpose(0, 2, 1, 3, 4).reshape(4, inner, width)
    )
    second_mats = lax.all_gather(second_pack, "seq", axis=0).reshape(seqs, 4, slim, width)
    kc_full, vc_full, qs_full, ks_full = [first_mats[i] for i in range(4)]
    vs_full, os_full, qc_full, oc_full = [second_mats[:, i].reshape(inner, width) for i in range(4)]

    gate_own, linear_own, down_own = quarters(gate_feed.T), quarters(linear_feed.T), quarters(down_feed)
    start = after(jnp.stack([gate_own[0], linear_own[0]]), ring[-1])
    both_ring = jnp.stack(ring_gather(start)[1:])
    gate_spread = spread_gather(both_ring[:, 0], bits)
    linear_spread = spread_gather(both_ring[:, 1], bits[::-1])
    down_ring = ring_gather(after(down_own, both_ring))
    gate_full = jnp.stack([jnp.concatenate([gate_own[k][None], gate_spread[k]]) for k in range(mems)])
    linear_full = jnp.stack([jnp.concatenate([linear_own[k][None], linear_spread[k]]) for k in range(mems)])
    down_full = jnp.stack(down_ring, axis=1)
    hidden_all = mems * chips * part
    gate_full = gate_full.reshape(hidden_all, width)
    linear_full = linear_full.reshape(hidden_all, width)
    down_full = down_full.reshape(hidden_all, width)

    onehot = (
        position_buckets(length).reshape(length * length, 1)
        == jnp.arange(buckets, dtype=jnp.int32)[None, :]
    ).astype(bf16)
    position_bias = (
        jnp.dot(onehot, bias_table, preferred_element_type=f32)
        .reshape(length, length, heads)
        .transpose(2, 0, 1)
    )
    row_index = jnp.arange(length, dtype=jnp.int32)
    causal = row_index[:, None] >= row_index[None, :]
    position_bias = jnp.where(causal[None], position_bias, masked_score)
    tokens = inputs.reshape(rows, width)
    og_low = output_grad.reshape(rows, width)
    og_other = to_core(og_low)
    source = memory.reshape(micros, pairs, slots, width)
    gain_self, gain_cross, gain_feed = [g.reshape(1, width) for g in (gain_self, gain_cross, gain_feed)]
    keep_all = lax.all_gather(keep_mask[:, 0], "mem", axis=0)
    keep_own = lax.dynamic_index_in_dim(keep_all, mem_index, 2, keepdims=False)
    keep_own = jnp.stack(
        [lax.dynamic_index_in_dim(keep_own, mem_index ^ s, 0, keepdims=False) for s in range(mems)], 1
    )
    spots = jnp.stack(
        [(mem_index ^ s) * slots + jnp.arange(slots, dtype=jnp.int32) for s in range(mems)], 0
    )
    len_own = lax.dynamic_index_in_dim(memory_lengths[:, 0], mem_index, 1, keepdims=False)
    valid = (spots[None] < len_own[:, None, None]) & ((keep_own == 1) | (spots[None] == 0))
    valid = valid.reshape(micros, 1, mems * slots).astype(f32)
    place = spot[2:]

    kv_local = kv_fwd(place, source, kc_full, vc_full)
    kvs = [to_mem(kv_local[s], s) if s else kv_local[s] for s in range(mems)]
    normed, q, k, v, mixed, first_sum, normed_cross, cq = self_fwd(
        depth, length, tokens, gain_self, qs_full, ks_full, vs_full, os_full, position_bias, gain_cross, qc_full
    )
    cmixed, second_sum, normed_feed = cross_fwd(depth, length, cq, valid, oc_full, first_sum, gain_feed, kvs)
    nf_other = to_core(normed_feed)
    block = 256 if hidden_all % 256 == 0 else part
    grad_gate, grad_linear, grad_down, res_own, res_send, nfg_own, nfg_send = feed_layer(
        normed_feed, nf_other, og_low, og_other, gate_full, linear_full, down_full, block
    )
    nfg_more = to_core(nfg_send)
    result = second_sum + res_own + to_core(res_send).astype(f32)

    split = (mems, chips, part, width)
    gate_sum = fold(grad_gate.reshape(split), bits[::-1])
    linear_sum = fold(grad_linear.reshape(split), bits)
    both_sum = ring_sum([jnp.stack([gate_sum[j], linear_sum[j]]) for j in range(chips)])
    grad_down = grad_down.reshape(split)
    down_sum = ring_sum([grad_down[:, j] for j in range(chips)])
    down_sum = direct_fold([down_sum[s] for s in range(mems)])
    feed_out = back_to_mem(jnp.concatenate([both_sum, down_sum[None]]), mem_index)
    gate_out, linear_out, down_out = [feed_out[:, i].reshape(feed, width) for i in range(3)]

    kvg, (grad_gain_feed, grad_co, grad_cq, first_grad, grad_gain_cross) = cross_bwd(
        depth, length, og_low, nfg_own, nfg_more, second_sum, gain_feed, cmixed, cq, valid, oc_full,
        first_sum, gain_cross, normed_cross, qc_full, kvs,
    )
    kvg = jnp.stack([to_mem(kvg[s], s) if s else kvg[s] for s in range(mems)])
    memory_grad, grad_kc, grad_vc = kv_bwd(place, source, kc_full, vc_full, kvg)
    grad_os, grad_qs, grad_ks, grad_vs, input_grad, grad_gain_self, score_sum = self_bwd(
        depth, length, first_grad, mixed, q, k, v, position_bias, os_full, qs_full, ks_full, vs_full,
        normed, tokens, gain_self,
    )

    cross_stack = jnp.stack([g.reshape(seqs, slim, width) for g in (grad_kc, grad_vc, grad_cq, grad_co)], axis=1)
    cross_sum = lax.psum_scatter(cross_stack.reshape(seqs, 4 * slim, width), "seq", scatter_dimension=0)
    cross_sum = direct_fold([cross_sum] * mems).astype(f32).reshape(4, slim, width)

    self_stack = jnp.stack(
        [g.reshape(chips, 2, slim, width) for g in (grad_qs, grad_ks, grad_vs, grad_os)], axis=2
    )
    kept = lax.dynamic_index_in_dim(self_stack, core, 1, keepdims=False)
    sent = lax.dynamic_index_in_dim(self_stack, 1 - core, 1, keepdims=False)
    total = add_low(kept, to_core(sent)).reshape(chips, mems, 4 * slim // mems, width)
    total = direct_fold(
        [lax.dynamic_index_in_dim(total, mem_index ^ s, 1, keepdims=False) for s in range(mems)]
    )
    pieces = [
        lax.dynamic_index_in_dim(total, (chip + j) % chips, 0, keepdims=False) for j in range(chips)
    ]
    total = sum_low([to_step(p, j) if j else p for j, p in enumerate(pieces)])
    self_sum = back_to_mem(total, mem_index).reshape(4, slim, width)

    grad_table = lax.dot_general(
        onehot.astype(f32),
        score_sum.reshape(heads, length * length),
        (((0,), (1,)), ((), ())),
        preferred_element_type=f32,
    )
    table_row = jnp.pad(grad_table.reshape(1, buckets * heads), ((0, 0), (0, width - buckets * heads)))
    small = jnp.concatenate([grad_gain_self, grad_gain_cross, grad_gain_feed, table_row], axis=0)
    for bit in bits:
        small = small + to_mem(small, bit)
    for bit in [1 << b for b in range((seqs - 1).bit_length())]:
        small = small + to_seq(small, bit)
    return (
        result.reshape(inputs.shape),
        input_grad.reshape(inputs.shape),
        memory_grad.reshape(memory.shape),
        small[0],
        self_sum[0].T,
        self_sum[1].T,
        self_sum[2].T,
        self_sum[3],
        small[3, : buckets * heads].reshape(buckets, heads),
        small[1],
        cross_sum[2].T,
        cross_sum[0].T,
        cross_sum[1].T,
        cross_sum[3],
        small[2],
        gate_out.T,
        linear_out.T,
        down_out,
    )


def solution(mesh):
    tokens_at = P(None, "seq", "mem", None, None)
    memory_at = P(None, "seq", None, "mem", None)
    columns, row_cut = P(None, "seq"), P("seq", None)
    return jax.shard_map(
        per_device,
        mesh=mesh,
        in_specs=(
            tokens_at,
            memory_at,
            P(None, "seq", None),
            P(None, "seq", None, "mem"),
            P(),
            columns,
            columns,
            columns,
            row_cut,
            P(),
            P(),
            columns,
            columns,
            columns,
            row_cut,
            P(),
            columns,
            columns,
            row_cut,
            tokens_at,
        ),
        out_specs=(
            tokens_at,
            tokens_at,
            memory_at,
            P(),
            columns,
            columns,
            columns,
            row_cut,
            P(),
            P(),
            columns,
            columns,
            columns,
            row_cut,
            P(),
            columns,
            columns,
            row_cut,
        ),
        check_vma=False,
    )
```

time: 1600 us -> 783 us (0.49)
  waiting for transfers between devices: 886 us -> 301 us
  matrix products: 361 us -> 2.62 us
  Pallas kernels: 0 us -> 184 us
  blocking collectives: 142 us -> 8.07 us
  starting transfers between devices: 2.25 us -> 81.3 us
  local copies, waits for them, and re-layouts: 125 us -> 103 us
  other arithmetic: 58.4 us -> 77.4 us
    reduce_scatter x9 -> x1, waiting for transfers between devices: 460 us -> 0.01 us  [per_device(): lax.psum_scatter(cross_stack.reshape(seqs, 4 * slim, width), 'seq', scatt...]
    all_gather x11 -> x1, waiting for transfers between devices: 360 us -> 0.01 us  [per_device(): lax.all_gather(second_pack, 'seq', axis=0).reshape(seqs, 4, slim, width)]
    dot_general x93 -> x2, matrix products: 361 us -> 2.62 us  [the longest x1 1.33 us: per_device(): jnp.dot(onehot, bias_table, preferred_element_type=f32)]
    ppermute x0 -> x61, waiting for transfers between devices: none -> 301 us  [the longest x34 143 us: to_mem(): return lax.ppermute(value, 'mem', [(i, i ^ mask) for i in range(count)])]
    pallas_call x0 -> x8, Pallas kernels: none -> 184 us  [the longest x1 72.7 us: feed_layer(): pl.pallas_call(feed_kernel, grid=(hidden // block,), in_specs=[any_spec]...]
    ppermute x0 -> x61, starting transfers between devices: none -> 81.3 us  [the longest x34 40.7 us: to_mem(): return lax.ppermute(value, 'mem', [(i, i ^ mask) for i in range(count)])]
    all_gather x8 -> x1, blocking collectives: 82.1 us -> 8.07 us  [per_device(): keep_all = lax.all_gather(keep_mask[:, 0], 'mem', axis=0)]
    psum x2 -> x0, blocking collectives: 59.9 us -> none  [the longest x1 43.2 us: per_device(): lax.psum((grad_gain_self, grad_gain_cross, grad_gain_feed, grad_table), (...]
  transfers between devices with their start and end apart: 27 -> 63, of which waited for: 18 -> 27; matrix products, arithmetic and copies ran while one was open for 25% -> 22% of each run, Pallas kernels for 0% -> 14%
where the time goes in v1:
time: 783 us; the launch traced here: 772 us
  waiting for transfers between devices  301 us (38%)
  Pallas kernels  184 us (23%)
  local copies, waits for them, and re-layouts  103 us (13%)
  starting transfers between devices  81.3 us (10%)
  other arithmetic  77.4 us (10%)
  between operations  15.5 us (2%)
  blocking collectives  8.07 us (1%)
    ppermute x34, waiting for transfers between devices, to_mem(): return lax.ppermute(value, 'mem', [(i, i ^ mask) for i in range(count)])  143 us
    ppermute x15, waiting for transfers between devices, to_next(): lax.ppermute(value, 'seq', [(i, (i + 2) % count) for i in range(count)])  136 us
    pallas_call x1, Pallas kernels, feed_layer(): pl.pallas_call(feed_kernel, grid=(hidden // block,), in_specs=[any_spec]...  72.7 us
    ppermute x34, starting transfers between devices, to_mem(): return lax.ppermute(value, 'mem', [(i, i ^ mask) for i in range(count)])  40.7 us
    unnamed x128, local copies, waits for them, and re-layouts  38.8 us
    pallas_call x1, Pallas kernels, cross_bwd(): pl.pallas_call(functools.partial(cross_bwd_kernel, depth, length, len(kvs...  31.2 us
    ppermute x15, starting transfers between devices, to_next(): lax.ppermute(value, 'seq', [(i, (i + 2) % count) for i in range(count)])  29.9 us
    ppermute x3, waiting for transfers between devices, to_step(): lax.ppermute(value, 'seq', [(i, (i + 2 * step) % count) for i in range(co...  21.6 us
  transfers between devices with their start and end apart: 63, of which 27 were waited for; matrix products, arithmetic and copies ran while one was open for 22% of the time, Pallas kernels for 14%

profile of v1, /device:TPU:8, one launch (start us, length us, event | category | flops | bytes accessed | tf_op | source)
XLA Modules:
  0.0 772.1 jit_solution(5551957675975628134)
XLA Ops:
  20.6 9.4 %collective-permute-done.1 = bf16[48,1472]{1,0:T(8,128)(2,1)S(1)} collective-permute-done((bf16[48,1472]{1,0:T(8,128)(2,1)}, bf16[48,1472]{1,0:T(8,128)(2,1)S(1)}, u32[]{:S(2)}, u32[]{:S(2)}) %collective-permute-start.1) | collective-permute-done | bytes 141344 | tf_op jit(solution)/shard_map/ppermute | solution.py:53
  32.4 8.1 %all-gather.1 = s32[8,1,4,256]{3,2,1,0:T(4,128)S(1)} all-gather(s32[2,1,4,256]{3,2,1,0:T(4,128)S(1)} %copy-done.48), channel_id=3, replica_groups=mesh['seq'=8,'mem'=4] {'mem'}, dimensions={0}, use_global_device_ids=true | all-gather | bytes 40960 | tf_op jit(solution)/shard_map/all_gather | solution.py:663
  46.1 33.3 %collective-permute-done.12 = bf16[2,112,1472]{2,1,0:T(8,128)(2,1)S(1)} collective-permute-done((bf16[2,112,1472]{2,1,0:T(8,128)(2,1)S(1)}, bf16[2,112,1472]{2,1,0:T(8,128)(2,1)S(1)}, u32[]{:S(2)}, u32[]{:S(2)}) %collective-permute-start.12) | collective-permute-done | bytes 659488 | tf_op jit(solution)/shard_map/ppermute | solution.py:53
  87.7 8.9 %collective-permute-done.13 = bf16[2,112,1472]{2,1,0:T(8,128)(2,1)} collective-permute-done((bf16[2,112,1472]{2,1,0:T(8,128)(2,1)S(1)}, bf16[2,112,1472]{2,1,0:T(8,128)(2,1)}, u32[]{:S(2)}, u32[]{:S(2)}) %collective-permute-start.13) | collective-permute-done | bytes 659488 | tf_op jit(solution)/shard_map/ppermute | solution.py:53
  96.6 2.6 collective-permute-start.14
  100.8 5.8 collective-permute-done.4
  109.2 4.4 collective-permute-done.14
  125.1 8.5 %copy.171 = bf16[2,1,4,256,1472]{4,3,2,0,1:T(8,128)(2,1)} copy(bf16[2,1,4,256,1472]{3,4,2,1,0:T(8,128)(2,1)} %param.21) | data formatting | bytes 12058624 | tf_op args[1]
  133.6 2.6 copy.161
  138.2 2.6 copy.179.og_b
  145.6 3.2 assemble.1
  155.3 8.4 %kv_fwd.1 = bf16[4,2,256,768]{3,2,1,0:T(8,128)(2,1)S(1)} custom-call(s32[4]{0:T(128)S(1)} %pad_add_fusion.place, bf16[2,4,256,1472]{3,2,1,0:T(8,128)(2,1)S(1)} %bitcast.304, bf16[384,1472]{1,0:T(8,128)(2,1)S(1)} %bitcast.307, bf16[384,1472]{1,0:T(8,128)(2,1)S(1)} %bitcast.305), custom_call_target="tpu_custom_call" | custom-call | tf_op jit(solution)/shard_map/kv_fwd/pallas_call | solution.py:420
  169.8 14.5 %collective-permute-done.20 = bf16[4,112,1472]{2,1,0:T(8,128)(2,1)} collective-permute-done((bf16[4,112,1472]{2,1,0:T(8,128)(2,1)}, bf16[4,112,1472]{2,1,0:T(8,128)(2,1)}, u32[]{:S(2)}, u32[]{:S(2)}) %collective-permute-start.20) | collective-permute-done | bytes 1318944 | tf_op jit(solution)/shard_map/ppermute | solution.py:53
  185.7 5.9 collective-permute-done.18
  193.5 5.2 collective-permute-done.16
  198.8 3.6 pad_maximum_fusion.1
  203.7 4.5 fusion.54
  208.2 15.5 %self_fwd.1 = (bf16[512,1472]{1,0:T(8,128)(2,1)}, bf16[512,384]{1,0:T(8,128)(2,1)}, bf16[512,384]{1,0:T(8,128)(2,1)}, bf16[512,384]{1,0:T(8,128)(2,1)}, bf16[512...) custom-call(bf16[512,1472]{1,0:T(8,128)(2,1)} %bitcast.321, ...), custom_call_target="tpu_custom_call" | custom-call | tf_op jit(solution)/shard_map/self_fwd/pallas_call | solution.py:220
  223.7 4.8 collective-permute-done.8.refs_2_
  228.5 15.0 %cross_fwd.1 = (bf16[512,384]{1,0:T(8,128)(2,1)}, f32[512,1472]{1,0:T(8,128)}, bf16[512,1472]{1,0:T(8,128)(2,1)}) custom-call(bf16[512,384]{1,0:T(8,128)(2,1)} %get-tuple-element.57.cq, f32[2,1,1024]{2,1,0:T(1,128)} %and_convert_fusion.mask, bf16[384,1472]{1,0:T(8,128)(2,1)} %bitcast.325, f32[512,1472]{1,0:T(8,128)} %get-tuple-element.58.first, ...), custom_call_target="tpu_custom_call" | custom-call | tf_op jit(solution)/shard_map/cross_fwd/pallas_call | solution.py:260
  243.4 2.6 copy.172
  247.9 4.7 pad_maximum_fusion
  252.6 6.5 pad_maximum_fusion.2
  259.1 2.6 copy.178.nf_b
  261.7 72.7 %feed.1 = (bf16[1792,1472]{1,0:T(8,128)(2,1)}, bf16[1792,1472]{1,0:T(8,128)(2,1)}, bf16[1792,1472]{1,0:T(8,128)(2,1)}, f32[512,1472]{1,0:T(8,128)}, bf16[512,147...) custom-call(bf16[512,1472]{1,0:T(8,128)(2,1)} %get-tuple-element.60.nf_a, ...), custom_call_target="tpu_custom_call" | custom-call | tf_op jit(solution)/shard_map/feed/pallas_call | solution.py:544
  334.4 2.6 copy.182
  337.0 4.7 fusion.51
  344.8 2.7 copy.183.nf_more
  347.5 31.2 %cross_bwd.1 = (bf16[2,256,768]{2,1,0:T(8,128)(2,1)}, bf16[2,256,768]{2,1,0:T(8,128)(2,1)}, bf16[2,256,768]{2,1,0:T(8,128)(2,1)}, bf16[2,256,768]{2,1,0:T(8,128)...) custom-call(bf16[512,1472]{1,0:T(8,128)(2,1)} %bitcast.313, ...), custom_call_target="tpu_custom_call" | custom-call | tf_op jit(solution)/shard_map/cross_bwd/pallas_call | solution.py:327
  378.8 20.6 %self_bwd.1 = (bf16[384,1472]{1,0:T(8,128)(2,1)}, bf16[384,1472]{1,0:T(8,128)(2,1)}, bf16[384,1472]{1,0:T(8,128)(2,1)}, bf16[384,1472]{1,0:T(8,128)(2,1)}, f32[5...) custom-call(f32[512,1472]{1,0:T(8,128)} %get-tuple-element.69.first_grad, ...), custom_call_target="tpu_custom_call" | custom-call | tf_op jit(solution)/shard_map/self_bwd/pallas_call | solution.py:392
  404.0 2.5 slice_bitcast_fusion.3
  407.8 2.6 copy.180
  411.0 4.7 fusion.52
  421.1 19.3 %collective-permute-done.52 = bf16[4,112,1472]{2,1,0:T(8,128)(2,1)} collective-permute-done((bf16[4,112,1472]{2,1,0:T(8,128)(2,1)}, bf16[4,112,1472]{2,1,0:T(8,128)(2,1)}, u32[]{:S(2)}, u32[]{:S(2)}) %collective-permute-start.52) | collective-permute-done | bytes 1318944 | tf_op jit(solution)/shard_map/ppermute | solution.py:53
  440.4 3.2 fusion.7
  445.6 2.6 copy.181
  448.2 2.6 collective-permute-start.31
  450.9 5.9 convert_add_fusion.1
  460.7 3.5 copy.194
  464.2 3.5 copy.193
  467.7 3.4 dynamic-slice_bitcast_fusion
  472.5 24.9 %collective-permute-done.24 = bf16[2,256,768]{2,1,0:T(8,128)(2,1)} collective-permute-done((bf16[2,256,768]{2,1,0:T(8,128)(2,1)}, bf16[2,256,768]{2,1,0:T(8,128)(2,1)}, u32[]{:S(2)}, u32[]{:S(2)}) %collective-permute-start.24) | collective-permute-done | bytes 786464 | tf_op jit(solution)/shard_map/ppermute | solution.py:58
  497.4 4.1 collective-permute-start.53
  501.5 13.1 %collective-permute-done.26 = bf16[2,256,768]{2,1,0:T(8,128)(2,1)} collective-permute-done((bf16[2,256,768]{2,1,0:T(8,128)(2,1)}, bf16[2,256,768]{2,1,0:T(8,128)(2,1)}, u32[]{:S(2)}, u32[]{:S(2)}) %collective-permute-start.26) | collective-permute-done | bytes 786464 | tf_op jit(solution)/shard_map/ppermute | solution.py:58
  514.6 3.4 pad_maximum_fusion.6.kvg
  518.1 17.3 %kv_bwd.1 = (f32[2,4,256,1472]{3,2,1,0:T(8,128)}, bf16[384,1472]{1,0:T(8,128)(2,1)S(1)}, bf16[384,1472]{1,0:T(8,128)(2,1)S(1)}) custom-call(s32[4]{0:T(128)S(1)} %pad_add_fusion.place, bf16[2,4,256,1472]{3,2,1,0:T(8,128)(2,1)} %bitcast.301, bf16[384,1472]{1,0:T(8,128)(2,1)S(1)} %bitcast.308, bf16[384,1472]{1,0:T(8,128)(2,1)S(1)} %bitcast.306, ...), custom_call_target="tpu_custom_call" | custom-call | tf_op jit(solution)/shard_map/kv_bwd/pallas_call | solution.py:462
  538.5 12.5 %copy.195 = f32[2,1,4,256,1472]{3,4,2,1,0:T(8,128)} copy(f32[2,1,4,256,1472]{4,3,2,0,1:T(8,128)} %bitcast.323) | data formatting | bytes 24117248
  559.3 3.1 collective-permute-start.54
  562.4 2.5 fusion.2
  567.1 19.1 %collective-permute-done.46 = bf16[1,4,112,1472]{3,2,1,0:T(8,128)(2,1)S(1)} collective-permute-done((bf16[1,4,112,1472]{3,2,1,0:T(8,128)(2,1)S(1)}, bf16[1,4,112,1472]{3,2,1,0:T(8,128)(2,1)S(1)}, u32[]{:S(2)}, u32[]{:S(2)}) %collective-permute-start.46) | collective-permute-done | bytes 1318944 | tf_op jit(solution)/shard_map/ppermute | solution.py:58
  592.0 3.1 collective-permute-start.49
  595.1 26.5 %collective-permute-done.54 = bf16[4,112,1472]{2,1,0:T(8,128)(2,1)S(1)} collective-permute-done((bf16[4,112,1472]{2,1,0:T(8,128)(2,1)S(1)}, bf16[4,112,1472]{2,1,0:T(8,128)(2,1)S(1)}, u32[]{:S(2)}, u32[]{:S(2)}) %collective-permute-start.54) | collective-permute-done | bytes 1318944 | tf_op jit(solution)/shard_map/ppermute | solution.py:53
  625.6 4.1 collective-permute-start.37
  629.7 6.7 collective-permute-done.49
  640.0 5.0 collective-permute-done.36
  650.7 14.4 %collective-permute-done.38 = bf16[48,1472]{1,0:T(8,128)(2,1)S(1)} collective-permute-done((bf16[48,1472]{1,0:T(8,128)(2,1)S(1)}, bf16[48,1472]{1,0:T(8,128)(2,1)S(1)}, u32[]{:S(2)}, u32[]{:S(2)}) %collective-permute-start.38) | collective-permute-done | bytes 141344 | tf_op jit(solution)/shard_map/ppermute | solution.py:67
  671.6 3.9 collective-permute-done.40
  675.6 10.1 %collective-permute-done.51 = bf16[2,112,1472]{2,1,0:T(8,128)(2,1)S(1)} collective-permute-done((bf16[2,112,1472]{2,1,0:T(8,128)(2,1)S(1)}, bf16[2,112,1472]{2,1,0:T(8,128)(2,1)S(1)}, u32[]{:S(2)}, u32[]{:S(2)}) %collective-permute-start.51) | collective-permute-done | bytes 659488 | tf_op jit(solution)/shard_map/ppermute | solution.py:53
  690.8 21.1 %collective-permute-done.58 = bf16[3,112,1472]{2,1,0:T(8,128)(2,1)S(1)} collective-permute-done((bf16[3,112,1472]{2,1,0:T(8,128)(2,1)S(1)}, bf16[3,112,1472]{2,1,0:T(8,128)(2,1)S(1)}, u32[]{:S(2)}, u32[]{:S(2)}) %collective-permute-start.58) | collective-permute-done | bytes 989216 | tf_op jit(solution)/shard_map/ppermute | solution.py:58
  711.8 20.6 %collective-permute-done.59 = bf16[3,112,1472]{2,1,0:T(8,128)(2,1)S(1)} collective-permute-done((bf16[3,112,1472]{2,1,0:T(8,128)(2,1)S(1)}, bf16[3,112,1472]{2,1,0:T(8,128)(2,1)S(1)}, u32[]{:S(2)}, u32[]{:S(2)}) %collective-permute-start.59) | collective-permute-done | bytes 989216 | tf_op jit(solution)/shard_map/ppermute | solution.py:58
  733.3 3.7 maximum_convert_fusion
  740.5 7.0 fusion.50
  747.5 6.0 collective-permute-done.42
  753.5 10.0 %collective-permute-done.43 = bf16[192,1472]{1,0:T(8,128)(2,1)S(1)} collective-permute-done((bf16[192,1472]{1,0:T(8,128)(2,1)}, bf16[192,1472]{1,0:T(8,128)(2,1)S(1)}, u32[]{:S(2)}, u32[]{:S(2)}) %collective-permute-start.43) | collective-permute-done | bytes 565280 | tf_op jit(solution)/shard_map/ppermute | solution.py:58
  (320 shorter events, 143.0 us)
Async XLA Ops:
  7.2 92.2 %copy-start = (bf16[32,6]{0,1:T(8,128)(2,1)S(1)}, bf16[32,6]{0,1:T(8,128)(2,1)}, u32[]{:S(2)}) copy-start(bf16[32,6]{0,1:T(8,128)(2,1)} %param.29) | copy-start | bytes 1156
  7.2 196.4 %all-gather.4.cloned.1.call-start = ((), (), s32[]{:S(2)}) async-start(), calls=%async_computation.2 | async-start | bytes 5308416 | tf_op jit(solution)/shard_map/all_gather | solution.py:628
  9.4 8.6 %collective-permute-start = (bf16[48,1472]{1,0:T(8,128)(2,1)}, bf16[48,1472]{1,0:T(8,128)(2,1)}, u32[]{:S(2)}, u32[]{:S(2)}) collective-permute-start(bf16[48,1472]{1,0:T(8,128)(2,1)} %bitcast.13), channel_id=1, source_target_pairs={{0,8},{4,12},{8,16},{12,20},{16,24},{20,28},{24,0},{28,4},{1,9},{5... | collective-permute-start | bytes 423944 | tf_op jit(solution)/shard_map/ppermute | solution.py:53
  11.9 725.2 %reduce-scatter.2.cloned.1.call-start = ((), (), s32[]{:S(2)}) async-start(), calls=%async_computation.1 | async-start | bytes 5308416 | tf_op jit(solution)/shard_map/reduce_scatter | solution.py:712
  14.3 123.9 %collective-permute-start.11 = (bf16[512,1472]{0,1:T(8,128)(2,1)}, bf16[512,1472]{0,1:T(8,128)(2,1)}, u32[]{:S(2)}, u32[]{:S(2)}) collective-permute-start(bf16[512,1472]{0,1:T(8,128)(2,1)} %copy.174), channel_id=1, source_target_pairs={{0,4},{4,0},{8,12},{12,8},{16,20},{20,16},{24,28},{28,24},{1,5},{5... | collective-permute-start | bytes 4521992 | tf_op jit(solution)/shard_map/ppermute | solution.py:48
  17.9 12.0 %collective-permute-start.1 = (bf16[48,1472]{1,0:T(8,128)(2,1)}, bf16[48,1472]{1,0:T(8,128)(2,1)S(1)}, u32[]{:S(2)}, u32[]{:S(2)}) collective-permute-start(bf16[48,1472]{1,0:T(8,128)(2,1)} %collective-permute-done), channel_id=1, source_target_pairs={{0,8},{4,12},{8,16},{12,20},{16,24},{20,28},{24,0},{28,4},{1,9},{5... | collective-permute-start | bytes 423944 | tf_op jit(solution)/shard_map/ppermute | solution.py:53
  29.9 12.5 %collective-permute-start.2 = (bf16[48,1472]{1,0:T(8,128)(2,1)S(1)}, bf16[48,1472]{1,0:T(8,128)(2,1)S(1)}, u32[]{:S(2)}, u32[]{:S(2)}) collective-permute-start(bf16[48,1472]{1,0:T(8,128)(2,1)S(1)} %collective-permute-done.1), channel_id=1, source_target_pairs={{0,8},{4,12},{8,16},{12,20},{16,24},{20,28},{24,0},{28,4},{1,9},{5... | collective-permute-start | bytes 423944 | tf_op jit(solution)/shard_map/ppermute | solution.py:53
  42.5 36.9 %collective-permute-start.12 = (bf16[2,112,1472]{2,1,0:T(8,128)(2,1)S(1)}, bf16[2,112,1472]{2,1,0:T(8,128)(2,1)S(1)}, u32[]{:S(2)}, u32[]{:S(2)}) collective-permute-start(bf16[2,112,1472]{2,1,0:T(8,128)(2,1)S(1)} %pad_maximum_fusion.14), channel_id=1, source_target_pairs={{0,8},{4,12},{8,16},{12,20},{16,24},{20,28},{24,0},{28,4},{1,9},{5... | collective-permute-start | bytes 1978376 | tf_op jit(solution)/shard_map/ppermute | solution.py:53
  79.3 17.2 %collective-permute-start.13 = (bf16[2,112,1472]{2,1,0:T(8,128)(2,1)S(1)}, bf16[2,112,1472]{2,1,0:T(8,128)(2,1)}, u32[]{:S(2)}, u32[]{:S(2)}) collective-permute-start(bf16[2,112,1472]{2,1,0:T(8,128)(2,1)S(1)} %collective-permute-done.12), channel_id=1, source_target_pairs={{0,8},{4,12},{8,16},{12,20},{16,24},{20,28},{24,0},{28,4},{1,9},{5... | collective-permute-start | bytes 1978376 | tf_op jit(solution)/shard_map/ppermute | solution.py:53
  84.1 16.7 %collective-permute-start.3 = (bf16[3,48,1472]{2,1,0:T(8,128)(2,1)S(1)}, bf16[3,48,1472]{2,1,0:T(8,128)(2,1)S(1)}, u32[]{:S(2)}, u32[]{:S(2)}) collective-permute-start(bf16[3,48,1472]{2,1,0:T(8,128)(2,1)S(1)} %get-tuple-element.272), channel_id=1, source_target_pairs={{0,1},{1,0},{2,3},{3,2},{4,5},{5,4},{6,7},{7,6},{8,9},{9,8},{10,11... | collective-permute-start | bytes 1271816 | tf_op jit(solution)/shard_map/ppermute | solution.py:58
  85.6 20.9 %collective-permute-start.4 = (bf16[3,48,1472]{2,1,0:T(8,128)(2,1)S(1)}, bf16[3,48,1472]{2,1,0:T(8,128)(2,1)S(1)}, u32[]{:S(2)}, u32[]{:S(2)}) collective-permute-start(bf16[3,48,1472]{2,1,0:T(8,128)(2,1)S(1)} %get-tuple-element.272), channel_id=1, source_target_pairs={{0,2},{1,3},{2,0},{3,1},{4,6},{5,7},{6,4},{7,5},{8,10},{9,11},{10,... | collective-permute-start | bytes 1271816 | tf_op jit(solution)/shard_map/ppermute | solution.py:58
  87.1 19.4 %collective-permute-start.5 = (bf16[3,48,1472]{2,1,0:T(8,128)(2,1)S(1)}, bf16[3,48,1472]{2,1,0:T(8,128)(2,1)S(1)}, u32[]{:S(2)}, u32[]{:S(2)}) collective-permute-start(bf16[3,48,1472]{2,1,0:T(8,128)(2,1)S(1)} %get-tuple-element.272), channel_id=1, source_target_pairs={{0,3},{1,2},{2,1},{3,0},{4,7},{5,6},{6,5},{7,4},{8,11},{9,10},{10,... | collective-permute-start | bytes 1271816 | tf_op jit(solution)/shard_map/ppermute | solution.py:58
  96.6 17.1 %collective-permute-start.14 = (bf16[2,112,1472]{2,1,0:T(8,128)(2,1)}, bf16[2,112,1472]{2,1,0:T(8,128)(2,1)}, u32[]{:S(2)}, u32[]{:S(2)}) collective-permute-start(bf16[2,112,1472]{2,1,0:T(8,128)(2,1)} %collective-permute-done.13), channel_id=1, source_target_pairs={{0,8},{4,12},{8,16},{12,20},{16,24},{20,28},{24,0},{28,4},{1,9},{5... | collective-permute-start | bytes 1978376 | tf_op jit(solution)/shard_map/ppermute | solution.py:53
  109.1 36.5 %collective-permute-start.6 = (bf16[4,4,48,1472]{3,2,1,0:T(8,128)(2,1)S(1)}, bf16[4,4,48,1472]{3,2,1,0:T(8,128)(2,1)}, u32[]{:S(2)}, u32[]{:S(2)}) collective-permute-start(bf16[4,4,48,1472]{3,2,1,0:T(8,128)(2,1)S(1)} %maximum_maximum_fusion.own), channel_id=1, source_target_pairs={{0,4},{4,0},{8,12},{12,8},{16,20},{20,16},{24,28},{28,24},{1,5},{5... | collective-permute-start | bytes 6782984 | tf_op jit(solution)/shard_map/ppermute | solution.py:48
  117.4 24.8 %collective-permute-start.17 = (bf16[1,3,112,1472]{3,2,1,0:T(8,128)(2,1)}, bf16[1,3,112,1472]{3,2,1,0:T(8,128)(2,1)S(1)}, u32[]{:S(2)}, u32[]{:S(2)}) collective-permute-start(bf16[1,3,112,1472]{3,2,1,0:T(8,128)(2,1)} %get-tuple-element.221), channel_id=1, source_target_pairs={{0,2},{1,3},{2,0},{3,1},{4,6},{5,7},{6,4},{7,5},{8,10},{9,11},{10,... | collective-permute-start | bytes 2967560 | tf_op jit(solution)/shard_map/ppermute | solution.py:58
  120.7 32.2 %collective-permute-start.19 = (bf16[4,112,1472]{2,1,0:T(8,128)(2,1)}, bf16[4,112,1472]{2,1,0:T(8,128)(2,1)}, u32[]{:S(2)}, u32[]{:S(2)}) collective-permute-start(bf16[4,112,1472]{2,1,0:T(8,128)(2,1)} %pad_maximum_fusion.12), channel_id=1, source_target_pairs={{0,8},{4,12},{8,16},{12,20},{16,24},{20,28},{24,0},{28,4},{1,9},{5... | collective-permute-start | bytes 3956744 | tf_op jit(solution)/shard_map/ppermute | solution.py:53
  122.9 25.9 %collective-permute-start.15 = (bf16[1,3,112,1472]{3,2,1,0:T(8,128)(2,1)}, bf16[1,3,112,1472]{3,2,1,0:T(8,128)(2,1)}, u32[]{:S(2)}, u32[]{:S(2)}) collective-permute-start(bf16[1,3,112,1472]{3,2,1,0:T(8,128)(2,1)} %get-tuple-element.220), channel_id=1, source_target_pairs={{0,1},{1,0},{2,3},{3,2},{4,5},{5,4},{6,7},{7,6},{8,9},{9,8},{10,11... | collective-permute-start | bytes 2967560 | tf_op jit(solution)/shard_map/ppermute | solution.py:58
  143.7 47.9 %collective-permute-start.18 = (bf16[2,3,112,1472]{3,2,1,0:T(8,128)(2,1)S(1)}, bf16[2,3,112,1472]{3,2,1,0:T(8,128)(2,1)S(1)}, u32[]{:S(2)}, u32[]{:S(2)}) collective-permute-start(bf16[2,3,112,1472]{3,2,1,0:T(8,128)(2,1)S(1)} %pad_maximum_fusion.11), channel_id=1, source_target_pairs={{0,1},{1,0},{2,3},{3,2},{4,5},{5,4},{6,7},{7,6},{8,9},{9,8},{10,11... | collective-permute-start | bytes 5935112 | tf_op jit(solution)/shard_map/ppermute | solution.py:58
  150.7 47.9 %collective-permute-start.16 = (bf16[2,3,112,1472]{3,2,1,0:T(8,128)(2,1)S(1)}, bf16[2,3,112,1472]{3,2,1,0:T(8,128)(2,1)S(1)}, u32[]{:S(2)}, u32[]{:S(2)}) collective-permute-start(bf16[2,3,112,1472]{3,2,1,0:T(8,128)(2,1)S(1)} %pad_maximum_fusion.10), channel_id=1, source_target_pairs={{0,2},{1,3},{2,0},{3,1},{4,6},{5,7},{6,4},{7,5},{8,10},{9,11},{10,... | collective-permute-start | bytes 5935112 | tf_op jit(solution)/shard_map/ppermute | solution.py:58
  152.9 31.3 %collective-permute-start.20 = (bf16[4,112,1472]{2,1,0:T(8,128)(2,1)}, bf16[4,112,1472]{2,1,0:T(8,128)(2,1)}, u32[]{:S(2)}, u32[]{:S(2)}) collective-permute-start(bf16[4,112,1472]{2,1,0:T(8,128)(2,1)} %collective-permute-done.19), channel_id=1, source_target_pairs={{0,8},{4,12},{8,16},{12,20},{16,24},{20,28},{24,0},{28,4},{1,9},{5... | collective-permute-start | bytes 3956744 | tf_op jit(solution)/shard_map/ppermute | solution.py:53
  165.5 58.1 %collective-permute-start.7 = (bf16[2,256,768]{2,1,0:T(8,128)(2,1)}, bf16[2,256,768]{2,1,0:T(8,128)(2,1)}, u32[]{:S(2)}, u32[]{:S(2)}) collective-permute-start(bf16[2,256,768]{2,1,0:T(8,128)(2,1)} %get-tuple-element.214), channel_id=1, source_target_pairs={{0,1},{1,0},{2,3},{3,2},{4,5},{5,4},{6,7},{7,6},{8,9},{9,8},{10,11... | collective-permute-start | bytes 2359304 | tf_op jit(solution)/shard_map/ppermute | solution.py:58
  166.6 61.9 %collective-permute-start.8 = (bf16[2,256,768]{2,1,0:T(8,128)(2,1)}, bf16[2,256,768]{2,1,0:T(8,128)(2,1)}, u32[]{:S(2)}, u32[]{:S(2)}) collective-permute-start(bf16[2,256,768]{2,1,0:T(8,128)(2,1)} %get-tuple-element.213), channel_id=1, source_target_pairs={{0,2},{1,3},{2,0},{3,1},{4,6},{5,7},{6,4},{7,5},{8,10},{9,11},{10,... | collective-permute-start | bytes 2359304 | tf_op jit(solution)/shard_map/ppermute | solution.py:58
  184.3 44.2 %collective-permute-start.9 = (bf16[2,256,768]{2,1,0:T(8,128)(2,1)}, bf16[2,256,768]{2,1,0:T(8,128)(2,1)}, u32[]{:S(2)}, u32[]{:S(2)}) collective-permute-start(bf16[2,256,768]{2,1,0:T(8,128)(2,1)} %get-tuple-element.212), channel_id=1, source_target_pairs={{0,3},{1,2},{2,1},{3,0},{4,7},{5,6},{6,5},{7,4},{8,11},{9,10},{10,... | collective-permute-start | bytes 2359304 | tf_op jit(solution)/shard_map/ppermute | solution.py:58
  191.7 60.9 %collective-permute-start.21 = (bf16[4,112,1472]{2,1,0:T(8,128)(2,1)}, bf16[4,112,1472]{2,1,0:T(8,128)(2,1)}, u32[]{:S(2)}, u32[]{:S(2)}) collective-permute-start(bf16[4,112,1472]{2,1,0:T(8,128)(2,1)} %collective-permute-done.20), channel_id=1, source_target_pairs={{0,8},{4,12},{8,16},{12,20},{16,24},{20,28},{24,0},{28,4},{1,9},{5... | collective-permute-start | bytes 3956744 | tf_op jit(solution)/shard_map/ppermute | solution.py:53
  246.0 13.1 %collective-permute-start.10 = (bf16[512,1472]{0,1:T(8,128)(2,1)}, bf16[512,1472]{0,1:T(8,128)(2,1)}, u32[]{:S(2)}, u32[]{:S(2)}) collective-permute-start(bf16[512,1472]{0,1:T(8,128)(2,1)} %copy.172), channel_id=1, source_target_pairs={{0,4},{4,0},{8,12},{12,8},{16,20},{20,16},{24,28},{28,24},{1,5},{5... | collective-permute-start | bytes 4521992 | tf_op jit(solution)/shard_map/ppermute | solution.py:48
  337.0 7.7 %collective-permute-start.23 = (bf16[512,1472]{0,1:T(8,128)(2,1)}, bf16[512,1472]{0,1:T(8,128)(2,1)}, u32[]{:S(2)}, u32[]{:S(2)}) collective-permute-start(bf16[512,1472]{0,1:T(8,128)(2,1)} %copy.182), channel_id=1, source_target_pairs={{0,4},{4,0},{8,12},{12,8},{16,20},{20,16},{24,28},{28,24},{1,5},{5... | collective-permute-start | bytes 4521992 | tf_op jit(solution)/shard_map/ppermute | solution.py:48
  343.5 207.5 %collective-permute-start.45 = (bf16[2,4,112,1472]{3,2,1,0:T(8,128)(2,1)}, bf16[2,4,112,1472]{3,2,1,0:T(8,128)(2,1)}, u32[]{:S(2)}, u32[]{:S(2)}) collective-permute-start(bf16[2,4,112,1472]{3,2,1,0:T(8,128)(2,1)} %pad_maximum_fusion.7), channel_id=1, source_target_pairs={{0,2},{1,3},{2,0},{3,1},{4,6},{5,7},{6,4},{7,5},{8,10},{9,11},{10,... | collective-permute-start | bytes 7913480 | tf_op jit(solution)/shard_map/ppermute | solution.py:58
  403.2 7.2 collective-permute-start.27
  406.5 33.9 %collective-permute-start.52 = (bf16[4,112,1472]{2,1,0:T(8,128)(2,1)}, bf16[4,112,1472]{2,1,0:T(8,128)(2,1)}, u32[]{:S(2)}, u32[]{:S(2)}) collective-permute-start(bf16[4,112,1472]{2,1,0:T(8,128)(2,1)} %slice_bitcast_fusion.3), channel_id=1, source_target_pairs={{0,8},{4,12},{8,16},{12,20},{16,24},{20,28},{24,0},{28,4},{1,9},{5... | collective-permute-start | bytes 3956744 | tf_op jit(solution)/shard_map/ppermute | solution.py:53
  410.4 34.6 %collective-permute-start.22 = (bf16[512,1472]{0,1:T(8,128)(2,1)}, bf16[512,1472]{0,1:T(8,128)(2,1)}, u32[]{:S(2)}, u32[]{:S(2)}) collective-permute-start(bf16[512,1472]{0,1:T(8,128)(2,1)} %copy.180), channel_id=1, source_target_pairs={{0,4},{4,0},{8,12},{12,8},{16,20},{20,16},{24,28},{28,24},{1,5},{5... | collective-permute-start | bytes 4521992 | tf_op jit(solution)/shard_map/ppermute | solution.py:48
  410.4 5.2 collective-permute-start.28
  415.7 3.7 collective-permute-start.29
  417.8 136.9 %collective-permute-start.47 = (bf16[2,4,112,1472]{3,2,1,0:T(8,128)(2,1)}, bf16[2,4,112,1472]{3,2,1,0:T(8,128)(2,1)}, u32[]{:S(2)}, u32[]{:S(2)}) collective-permute-start(bf16[2,4,112,1472]{3,2,1,0:T(8,128)(2,1)} %pad_maximum_fusion.8), channel_id=1, source_target_pairs={{0,1},{1,0},{2,3},{3,2},{4,5},{5,4},{6,7},{7,6},{8,9},{9,8},{10,11... | collective-permute-start | bytes 7913480 | tf_op jit(solution)/shard_map/ppermute | solution.py:58
  419.4 28.9 %collective-permute-start.30 = (f32[4,1472]{1,0:T(4,128)S(1)}, f32[4,1472]{1,0:T(4,128)S(1)}, u32[]{:S(2)}, u32[]{:S(2)}) collective-permute-start(f32[4,1472]{1,0:T(4,128)S(1)} %add.476), channel_id=1, source_target_pairs={{0,8},{4,12},{8,0},{12,4},{16,24},{20,28},{24,16},{28,20},{1,9},{5... | collective-permute-start | bytes 70664 | tf_op jit(solution)/shard_map/ppermute | solution.py:72
  443.6 53.8 %collective-permute-start.24 = (bf16[2,256,768]{2,1,0:T(8,128)(2,1)}, bf16[2,256,768]{2,1,0:T(8,128)(2,1)}, u32[]{:S(2)}, u32[]{:S(2)}) collective-permute-start(bf16[2,256,768]{2,1,0:T(8,128)(2,1)} %get-tuple-element.77), channel_id=1, source_target_pairs={{0,1},{1,0},{2,3},{3,2},{4,5},{5,4},{6,7},{7,6},{8,9},{9,8},{10,11... | collective-permute-start | bytes 2359304 | tf_op jit(solution)/shard_map/ppermute | solution.py:58
  445.0 56.5 %collective-permute-start.25 = (bf16[2,256,768]{2,1,0:T(8,128)(2,1)}, bf16[2,256,768]{2,1,0:T(8,128)(2,1)}, u32[]{:S(2)}, u32[]{:S(2)}) collective-permute-start(bf16[2,256,768]{2,1,0:T(8,128)(2,1)} %get-tuple-element.78), channel_id=1, source_target_pairs={{0,2},{1,3},{2,0},{3,1},{4,6},{5,7},{6,4},{7,5},{8,10},{9,11},{10,... | collective-permute-start | bytes 2359304 | tf_op jit(solution)/shard_map/ppermute | solution.py:58
  448.2 8.6 %collective-permute-start.31 = (f32[4,1472]{1,0:T(4,128)S(1)}, f32[4,1472]{1,0:T(4,128)S(1)}, u32[]{:S(2)}, u32[]{:S(2)}) collective-permute-start(f32[4,1472]{1,0:T(4,128)S(1)} %add.477), channel_id=1, source_target_pairs={{0,16},{4,20},{8,24},{12,28},{16,0},{20,4},{24,8},{28,12},{1,17},{... | collective-permute-start | bytes 70664 | tf_op jit(solution)/shard_map/ppermute | solution.py:72
  456.8 57.8 %collective-permute-start.26 = (bf16[2,256,768]{2,1,0:T(8,128)(2,1)}, bf16[2,256,768]{2,1,0:T(8,128)(2,1)}, u32[]{:S(2)}, u32[]{:S(2)}) collective-permute-start(bf16[2,256,768]{2,1,0:T(8,128)(2,1)} %get-tuple-element.79), channel_id=1, source_target_pairs={{0,3},{1,2},{2,1},{3,0},{4,7},{5,6},{6,5},{7,4},{8,11},{9,10},{10,... | collective-permute-start | bytes 2359304 | tf_op jit(solution)/shard_map/ppermute | solution.py:58
  497.4 59.8 %collective-permute-start.53 = (bf16[4,112,1472]{2,1,0:T(8,128)(2,1)}, bf16[4,112,1472]{2,1,0:T(8,128)(2,1)}, u32[]{:S(2)}, u32[]{:S(2)}) collective-permute-start(bf16[4,112,1472]{2,1,0:T(8,128)(2,1)} %fusion.7), channel_id=1, source_target_pairs={{0,8},{4,12},{8,16},{12,20},{16,24},{20,28},{24,0},{28,4},{1,9},{5... | collective-permute-start | bytes 3956744 | tf_op jit(solution)/shard_map/ppermute | solution.py:53
  501.5 60.9 %collective-permute-start.32 = (bf16[4,4,48,1472]{3,2,0,1:T(8,128)(2,1)}, bf16[4,4,48,1472]{3,2,0,1:T(8,128)(2,1)}, u32[]{:S(2)}, u32[]{:S(2)}) collective-permute-start(bf16[4,4,48,1472]{3,2,0,1:T(8,128)(2,1)} %dynamic-slice_bitcast_fusion), channel_id=1, source_target_pairs={{0,4},{4,0},{8,12},{12,8},{16,20},{20,16},{24,28},{28,24},{1,5},{5... | collective-permute-start | bytes 6782984 | tf_op jit(solution)/shard_map/ppermute | solution.py:48
  553.0 33.2 %collective-permute-start.46 = (bf16[1,4,112,1472]{3,2,1,0:T(8,128)(2,1)S(1)}, bf16[1,4,112,1472]{3,2,1,0:T(8,128)(2,1)S(1)}, u32[]{:S(2)}, u32[]{:S(2)}) collective-permute-start(bf16[1,4,112,1472]{3,2,1,0:T(8,128)(2,1)S(1)} %fusion.12), channel_id=1, source_target_pairs={{0,1},{1,0},{2,3},{3,2},{4,5},{5,4},{6,7},{7,6},{8,9},{9,8},{10,11... | collective-permute-start | bytes 3956744 | tf_op jit(solution)/shard_map/ppermute | solution.py:58
  556.5 33.3 %collective-permute-start.48 = (bf16[1,4,112,1472]{3,2,1,0:T(8,128)(2,1)S(1)}, bf16[1,4,112,1472]{3,2,1,0:T(8,128)(2,1)S(1)}, u32[]{:S(2)}, u32[]{:S(2)}) collective-permute-start(bf16[1,4,112,1472]{3,2,1,0:T(8,128)(2,1)S(1)} %fusion.9), channel_id=1, source_target_pairs={{0,2},{1,3},{2,0},{3,1},{4,6},{5,7},{6,4},{7,5},{8,10},{9,11},{10,... | collective-permute-start | bytes 3956744 | tf_op jit(solution)/shard_map/ppermute | solution.py:58
  559.3 62.3 %collective-permute-start.54 = (bf16[4,112,1472]{2,1,0:T(8,128)(2,1)S(1)}, bf16[4,112,1472]{2,1,0:T(8,128)(2,1)S(1)}, u32[]{:S(2)}, u32[]{:S(2)}) collective-permute-start(bf16[4,112,1472]{2,1,0:T(8,128)(2,1)S(1)} %fusion.6), channel_id=1, source_target_pairs={{0,8},{4,12},{8,16},{12,20},{16,24},{20,28},{24,0},{28,4},{1,9},{5... | collective-permute-start | bytes 3956744 | tf_op jit(solution)/shard_map/ppermute | solution.py:53
  565.0 58.3 %collective-permute-start.33 = (bf16[4,48,1472]{2,1,0:T(8,128)(2,1)S(1)}, bf16[4,48,1472]{2,1,0:T(8,128)(2,1)S(1)}, u32[]{:S(2)}, u32[]{:S(2)}) collective-permute-start(bf16[4,48,1472]{2,1,0:T(8,128)(2,1)S(1)} %get-tuple-element.216), channel_id=1, source_target_pairs={{0,1},{1,0},{2,3},{3,2},{4,5},{5,4},{6,7},{7,6},{8,9},{9,8},{10,11... | collective-permute-start | bytes 1695752 | tf_op jit(solution)/shard_map/ppermute | solution.py:58
  566.6 56.8 %collective-permute-start.34 = (bf16[4,48,1472]{2,1,0:T(8,128)(2,1)S(1)}, bf16[4,48,1472]{2,1,0:T(8,128)(2,1)S(1)}, u32[]{:S(2)}, u32[]{:S(2)}) collective-permute-start(bf16[4,48,1472]{2,1,0:T(8,128)(2,1)S(1)} %get-tuple-element.218), channel_id=1, source_target_pairs={{0,2},{1,3},{2,0},{3,1},{4,6},{5,7},{6,4},{7,5},{8,10},{9,11},{10,... | collective-permute-start | bytes 1695752 | tf_op jit(solution)/shard_map/ppermute | solution.py:58
  586.2 37.2 %collective-permute-start.35 = (bf16[4,48,1472]{2,1,0:T(8,128)(2,1)S(1)}, bf16[4,48,1472]{2,1,0:T(8,128)(2,1)S(1)}, u32[]{:S(2)}, u32[]{:S(2)}) collective-permute-start(bf16[4,48,1472]{2,1,0:T(8,128)(2,1)S(1)} %get-tuple-element.217), channel_id=1, source_target_pairs={{0,3},{1,2},{2,1},{3,0},{4,7},{5,6},{6,5},{7,4},{8,11},{9,10},{10,... | collective-permute-start | bytes 1695752 | tf_op jit(solution)/shard_map/ppermute | solution.py:58
  592.0 44.3 %collective-permute-start.49 = (bf16[2,112,1472]{2,1,0:T(8,128)(2,1)S(1)}, bf16[2,112,1472]{2,1,0:T(8,128)(2,1)S(1)}, u32[]{:S(2)}, u32[]{:S(2)}) collective-permute-start(bf16[2,112,1472]{2,1,0:T(8,128)(2,1)S(1)} %pad_maximum_fusion.15), channel_id=1, source_target_pairs={{0,8},{4,12},{8,16},{12,20},{16,24},{20,28},{24,0},{28,4},{1,9},{5... | collective-permute-start | bytes 1978376 | tf_op jit(solution)/shard_map/ppermute | solution.py:53
  623.8 21.2 %collective-permute-start.36 = (bf16[48,1472]{1,0:T(8,128)(2,1)S(1)}, bf16[48,1472]{1,0:T(8,128)(2,1)S(1)}, u32[]{:S(2)}, u32[]{:S(2)}) collective-permute-start(bf16[48,1472]{1,0:T(8,128)(2,1)S(1)} %get-tuple-element.264), channel_id=1, source_target_pairs={{0,8},{4,12},{8,16},{12,20},{16,24},{20,28},{24,0},{28,4},{1,9},{5... | collective-permute-start | bytes 423944 | tf_op jit(solution)/shard_map/ppermute | solution.py:67
  625.6 22.7 %collective-permute-start.37 = (bf16[48,1472]{1,0:T(8,128)(2,1)S(1)}, bf16[48,1472]{1,0:T(8,128)(2,1)S(1)}, u32[]{:S(2)}, u32[]{:S(2)}) collective-permute-start(bf16[48,1472]{1,0:T(8,128)(2,1)S(1)} %get-tuple-element.266), channel_id=1, source_target_pairs={{0,16},{4,20},{8,24},{12,28},{16,0},{20,4},{24,8},{28,12},{1,17},{... | collective-permute-start | bytes 423944 | tf_op jit(solution)/shard_map/ppermute | solution.py:67
  629.7 35.5 %collective-permute-start.38 = (bf16[48,1472]{1,0:T(8,128)(2,1)S(1)}, bf16[48,1472]{1,0:T(8,128)(2,1)S(1)}, u32[]{:S(2)}, u32[]{:S(2)}) collective-permute-start(bf16[48,1472]{1,0:T(8,128)(2,1)S(1)} %get-tuple-element.265), channel_id=1, source_target_pairs={{0,24},{4,28},{8,0},{12,4},{16,8},{20,12},{24,16},{28,20},{1,25},{... | collective-permute-start | bytes 423944 | tf_op jit(solution)/shard_map/ppermute | solution.py:67
  636.5 30.2 %collective-permute-start.50 = (bf16[2,112,1472]{2,1,0:T(8,128)(2,1)S(1)}, bf16[2,112,1472]{2,1,0:T(8,128)(2,1)S(1)}, u32[]{:S(2)}, u32[]{:S(2)}) collective-permute-start(bf16[2,112,1472]{2,1,0:T(8,128)(2,1)S(1)} %add_convert_fusion.2), channel_id=1, source_target_pairs={{0,8},{4,12},{8,16},{12,20},{16,24},{20,28},{24,0},{28,4},{1,9},{5... | collective-permute-start | bytes 1978376 | tf_op jit(solution)/shard_map/ppermute | solution.py:53
  638.5 30.0 %collective-permute-start.55 = (bf16[112,1472]{1,0:T(8,128)(2,1)S(1)}, bf16[112,1472]{1,0:T(8,128)(2,1)S(1)}, u32[]{:S(2)}, u32[]{:S(2)}) collective-permute-start(bf16[112,1472]{1,0:T(8,128)(2,1)S(1)} %get-tuple-element.235), channel_id=1, source_target_pairs={{0,1},{1,0},{2,3},{3,2},{4,5},{5,4},{6,7},{7,6},{8,9},{9,8},{10,11... | collective-permute-start | bytes 989192 | tf_op jit(solution)/shard_map/ppermute | solution.py:58
  645.0 24.0 %collective-permute-start.56 = (bf16[112,1472]{1,0:T(8,128)(2,1)S(1)}, bf16[112,1472]{1,0:T(8,128)(2,1)S(1)}, u32[]{:S(2)}, u32[]{:S(2)}) collective-permute-start(bf16[112,1472]{1,0:T(8,128)(2,1)S(1)} %get-tuple-element.237), channel_id=1, source_target_pairs={{0,2},{1,3},{2,0},{3,1},{4,6},{5,7},{6,4},{7,5},{8,10},{9,11},{10,... | collective-permute-start | bytes 989192 | tf_op jit(solution)/shard_map/ppermute | solution.py:58
  648.4 20.7 %collective-permute-start.57 = (bf16[112,1472]{1,0:T(8,128)(2,1)S(1)}, bf16[112,1472]{1,0:T(8,128)(2,1)S(1)}, u32[]{:S(2)}, u32[]{:S(2)}) collective-permute-start(bf16[112,1472]{1,0:T(8,128)(2,1)S(1)} %get-tuple-element.236), channel_id=1, source_target_pairs={{0,3},{1,2},{2,1},{3,0},{4,7},{5,6},{6,5},{7,4},{8,11},{9,10},{10,... | collective-permute-start | bytes 989192 | tf_op jit(solution)/shard_map/ppermute | solution.py:58
  665.2 6.4 collective-permute-start.39
  666.8 8.7 %collective-permute-start.40 = (bf16[48,1472]{1,0:T(8,128)(2,1)S(1)}, bf16[48,1472]{1,0:T(8,128)(2,1)S(1)}, u32[]{:S(2)}, u32[]{:S(2)}) collective-permute-start(bf16[48,1472]{1,0:T(8,128)(2,1)S(1)} %fusion.25), channel_id=1, source_target_pairs={{0,2},{1,3},{2,0},{3,1},{4,6},{5,7},{6,4},{7,5},{8,10},{9,11},{10,... | collective-permute-start | bytes 423944 | tf_op jit(solution)/shard_map/ppermute | solution.py:58
  668.5 7.1 collective-permute-start.41
  669.1 16.6 %collective-permute-start.51 = (bf16[2,112,1472]{2,1,0:T(8,128)(2,1)S(1)}, bf16[2,112,1472]{2,1,0:T(8,128)(2,1)S(1)}, u32[]{:S(2)}, u32[]{:S(2)}) collective-permute-start(bf16[2,112,1472]{2,1,0:T(8,128)(2,1)S(1)} %add_convert_fusion.1), channel_id=1, source_target_pairs={{0,8},{4,12},{8,16},{12,20},{16,24},{20,28},{24,0},{28,4},{1,9},{5... | collective-permute-start | bytes 1978376 | tf_op jit(solution)/shard_map/ppermute | solution.py:53
  686.0 25.8 %collective-permute-start.58 = (bf16[3,112,1472]{2,1,0:T(8,128)(2,1)S(1)}, bf16[3,112,1472]{2,1,0:T(8,128)(2,1)S(1)}, u32[]{:S(2)}, u32[]{:S(2)}) collective-permute-start(bf16[3,112,1472]{2,1,0:T(8,128)(2,1)S(1)} %get-tuple-element.259), channel_id=1, source_target_pairs={{0,1},{1,0},{2,3},{3,2},{4,5},{5,4},{6,7},{7,6},{8,9},{9,8},{10,11... | collective-permute-start | bytes 2967560 | tf_op jit(solution)/shard_map/ppermute | solution.py:58
  687.6 44.9 %collective-permute-start.59 = (bf16[3,112,1472]{2,1,0:T(8,128)(2,1)S(1)}, bf16[3,112,1472]{2,1,0:T(8,128)(2,1)S(1)}, u32[]{:S(2)}, u32[]{:S(2)}) collective-permute-start(bf16[3,112,1472]{2,1,0:T(8,128)(2,1)S(1)} %get-tuple-element.259), channel_id=1, source_target_pairs={{0,2},{1,3},{2,0},{3,1},{4,6},{5,7},{6,4},{7,5},{8,10},{9,11},{10,... | collective-permute-start | bytes 2967560 | tf_op jit(solution)/shard_map/ppermute | solution.py:58
  689.0 43.4 %collective-permute-start.60 = (bf16[3,112,1472]{2,1,0:T(8,128)(2,1)S(1)}, bf16[3,112,1472]{2,1,0:T(8,128)(2,1)S(1)}, u32[]{:S(2)}, u32[]{:S(2)}) collective-permute-start(bf16[3,112,1472]{2,1,0:T(8,128)(2,1)S(1)} %get-tuple-element.259), channel_id=1, source_target_pairs={{0,3},{1,2},{2,1},{3,0},{4,7},{5,6},{6,5},{7,4},{8,11},{9,10},{10,... | collective-permute-start | bytes 2967560 | tf_op jit(solution)/shard_map/ppermute | solution.py:58
  737.0 16.5 %collective-permute-start.42 = (bf16[192,1472]{1,0:T(8,128)(2,1)}, bf16[192,1472]{1,0:T(8,128)(2,1)S(1)}, u32[]{:S(2)}, u32[]{:S(2)}) collective-permute-start(bf16[192,1472]{1,0:T(8,128)(2,1)} %bitcast.378), channel_id=1, source_target_pairs={{0,1},{1,0},{2,3},{3,2},{4,5},{5,4},{6,7},{7,6},{8,9},{9,8},{10,11... | collective-permute-start | bytes 1695752 | tf_op jit(solution)/shard_map/ppermute | solution.py:58
  738.2 25.2 %collective-permute-start.43 = (bf16[192,1472]{1,0:T(8,128)(2,1)}, bf16[192,1472]{1,0:T(8,128)(2,1)S(1)}, u32[]{:S(2)}, u32[]{:S(2)}) collective-permute-start(bf16[192,1472]{1,0:T(8,128)(2,1)} %bitcast.379), channel_id=1, source_target_pairs={{0,2},{1,3},{2,0},{3,1},{4,6},{5,7},{6,4},{7,5},{8,10},{9,11},{10,... | collective-permute-start | bytes 1695752 | tf_op jit(solution)/shard_map/ppermute | solution.py:58
  739.1 24.4 %collective-permute-start.44 = (bf16[192,1472]{1,0:T(8,128)(2,1)}, bf16[192,1472]{1,0:T(8,128)(2,1)S(1)}, u32[]{:S(2)}, u32[]{:S(2)}) collective-permute-start(bf16[192,1472]{1,0:T(8,128)(2,1)} %bitcast.380), channel_id=1, source_target_pairs={{0,3},{1,2},{2,1},{3,0},{4,7},{5,6},{6,5},{7,4},{8,11},{9,10},{10,... | collective-permute-start | bytes 1695752 | tf_op jit(solution)/shard_map/ppermute | solution.py:58
  (56 other events, 540.9 us)
Sparse Core Ops, SparseCore 0:
  12.0 69.9 all-gather.3
  538.6 82.5 reduce-scatter.1

commit v2 on v1

--- a/solution.py
+++ b/solution.py
@@ -46,6 +46,10 @@
 def to_core(value):
     count = lax.axis_size("seq")
     return lax.ppermute(value, "seq", [(i, i ^ 1) for i in range(count)])
+
+
+def rows_to_core(value):
+    return to_core(value.reshape(-1, 64, value.shape[-1])).reshape(value.shape)
 
 
 def to_next(value):
@@ -157,11 +161,18 @@
         ),
         out_shape=jax.ShapeDtypeStruct((mems, 2 * chips, share, width), bf16),
         compiler_params=params(32),
+        cost_estimate=cost(3),
         name="assemble",
     )(spot, own, other)
 
 def params(limit_mb=56):
     return pltpu.CompilerParams(vmem_limit_bytes=limit_mb * 1024 * 1024)
+
+
+def cost(micro_seconds):
+    return pl.CostEstimate(
+        flops=micro_seconds * 10**9, bytes_accessed=micro_seconds * 3 * 10**6, transcendentals=0
+    )
 
 
 def row_norm(value):
@@ -221,6 +232,7 @@
         functools.partial(self_fwd_kernel, depth, length),
         out_shape=(low, slim, slim, slim, slim, jax.ShapeDtypeStruct((rows, width), f32), low, slim),
         compiler_params=params(),
+        cost_estimate=cost(16),
         name="self_fwd",
     )(tok, g1, qw, kw, vw, ow, bias, g2, cw)
 
@@ -265,6 +277,7 @@
             jax.ShapeDtypeStruct((rows, width), bf16),
         ),
         compiler_params=params(),
+        cost_estimate=cost(15),
         name="cross_fwd",
     )(cq, mask, ow, first, g3, *kvs)
 
@@ -336,6 +349,7 @@
         ),
         scratch_shapes=[pltpu.VMEM(cq.shape, bf16), pltpu.VMEM(cq.shape, bf16)],
         compiler_params=params(),
+        cost_estimate=cost(31),
         name="cross_bwd",
     )(og, nf_own, nf_more, second, g3, mixed, cq, mask, ow, first, g2, nc, qw, *kvs)
     return out[: len(kvs)], out[len(kvs) :]
@@ -402,6 +416,7 @@
         ),
         scratch_shapes=[pltpu.VMEM(q.shape, bf16)] * 4,
         compiler_params=params(),
+        cost_estimate=cost(21),
         name="self_bwd",
     )(first_grad, mixed, q, k, v, bias, ow, qw, kw, vw, normed, tok, g1)
 
@@ -409,12 +424,14 @@
 def kv_fwd_kernel(place, source, kw, vw, out):
     inner = kw.shape[0]
     rows = source[0, 0]
-    out[0, 0, :, :inner] = contract_cols(rows, kw[...]).astype(bf16)
-    out[0, 0, :, inner:] = contract_cols(rows, vw[...]).astype(bf16)
+    for n, w in enumerate((kw, vw)):
+        out[0, 0, :, n * inner : (n + 1) * inner] = lax.dot_general(
+            rows, w[...], (((0,), (1,)), ((), ())), preferred_element_type=f32
+        ).astype(bf16)
 
 
 def kv_fwd(place, memory, kw, vw):
-    micros, pairs, slots, width = memory.shape
+    micros, pairs, width, slots = memory.shape
     inner = kw.shape[0]
     whole = pl.BlockSpec((inner, width), lambda s, m, place: (0, 0))
     return pl.pallas_call(
@@ -423,7 +440,7 @@
             num_scalar_prefetch=1,
             grid=(pairs, micros),
             in_specs=[
-                pl.BlockSpec((1, 1, slots, width), lambda s, m, place: (m, place[s], 0, 0)),
+                pl.BlockSpec((1, 1, width, slots), lambda s, m, place: (m, place[s], 0, 0)),
                 whole,
                 whole,
             ],
@@ -431,6 +448,7 @@
         ),
         out_shape=jax.ShapeDtypeStruct((pairs, micros, slots, 2 * inner), bf16),
         compiler_params=params(32),
+        cost_estimate=cost(9),
         name="kv_fwd",
     )(place, memory, kw, vw)
 
@@ -444,8 +462,14 @@
     def clear():
         acc[...] = jnp.zeros_like(acc)
 
-    out[0, 0] = matmul(grads[:, :inner], kw[...]) + matmul(grads[:, inner:], vw[...])
-    acc[...] += contract_rows(grads, source[0, 0])
+    out[0, 0] = lax.dot_general(
+        kw[...], grads[:, :inner], (((0,), (1,)), ((), ())), preferred_element_type=f32
+    ) + lax.dot_general(
+        vw[...], grads[:, inner:], (((0,), (1,)), ((), ())), preferred_element_type=f32
+    )
+    acc[...] += lax.dot_general(
+        grads, source[0, 0], (((0,), (1,)), ((), ())), preferred_element_type=f32
+    )
 
     @pl.when(step == pl.num_programs(0) * pl.num_programs(1) - 1)
     def write():
@@ -454,11 +478,11 @@
 
 
 def kv_bwd(place, memory, kw, vw, kvg):
-    micros, pairs, slots, width = memory.shape
+    micros, pairs, width, slots = memory.shape
     inner = kw.shape[0]
     whole = pl.BlockSpec((inner, width), lambda s, m, place: (0, 0))
     weight = jax.ShapeDtypeStruct((inner, width), bf16)
-    block = pl.BlockSpec((1, 1, slots, width), lambda s, m, place: (m, place[s], 0, 0))
+    block = pl.BlockSpec((1, 1, width, slots), lambda s, m, place: (m, place[s], 0, 0))
     return pl.pallas_call(
         kv_bwd_kernel,
         grid_spec=pltpu.PrefetchScalarGridSpec(
@@ -475,6 +499,7 @@
         ),
         out_shape=(jax.ShapeDtypeStruct(memory.shape, f32), weight, weight),
         compiler_params=params(48),
+        cost_estimate=cost(17),
         name="kv_bwd",
     )(place, memory, kw, vw, kvg)
 
@@ -482,36 +507,127 @@
 gelu_c = math.sqrt(2 / math.pi)
 
 
-def feed_kernel(nf_a, nf_b, og_a, og_b, gw, lw, dw, dgw_o, dlw_o, ddw_o, res_o, res_b, nfg_o, nfg_b, nf, og, res_t, nfg_t, sems):
+def plan(steps):
+    arrays, out = [], []
+    for buffers in steps:
+        out.append([])
+        for n, sources in enumerate(buffers):
+            at = 0
+            for array, index, rows in sources:
+                found = [i for i, known in enumerate(arrays) if known is array]
+                if not found:
+                    arrays.append(array)
+                out[-1].append((found[0] if found else len(arrays) - 1, index, n, at, rows))
+                at += rows
+    return arrays, out
+
+
+def fetch(places, refs, hold, sems, step, slot):
+    copies = []
+    for i, (which, index, n, at, rows) in enumerate(places[step]):
+        src = refs[which].at[index] if index else refs[which]
+        copies.append(pltpu.make_async_copy(src, hold.at[slot, n, pl.ds(at, rows)], sems.at[slot, i]))
+    return copies
+
+
+def run_fetch(places, refs, hold, sems):
     step = pl.program_id(0)
+    for i in range(len(places)):
+
+        @pl.when(step == i)
+        def move(i=i):
+            if i == 0:
+                for copy in fetch(places, refs, hold, sems, 0, 0):
+                    copy.start()
+            if i + 1 < len(places):
+                for copy in fetch(places, refs, hold, sems, i + 1, (i + 1) % 2):
+                    copy.start()
+            for copy in fetch(places, refs, hold, sems, i, i % 2):
+                copy.wait()
+
+
+def feed_grad_kernel(places, count, *refs):
+    nf_a, nf_b, og_a, og_b = refs[:4]
+    weights = refs[4 : 4 + count]
+    dgw_o, dlw_o, ddw_o, hid_o, gl_o, ll_o, nf, og, hold, sems, whole_sems = refs[4 + count :]
     rows = nf_a.shape[0]
+    step = pl.program_id(0)
+
+    def loads():
+        return [
+            pltpu.make_async_copy(src, dst.at[pl.ds(at, rows)], whole_sems.at[i])
+            for i, (src, dst, at) in enumerate([(nf_a, nf, 0), (nf_b, nf, rows), (og_a, og, 0), (og_b, og, rows)])
+        ]
 
     @pl.when(step == 0)
     def load():
-        copies = [
-            pltpu.make_async_copy(src, dst.at[pl.ds(at, rows)], sems.at[i])
-            for i, (src, dst, at) in enumerate([(nf_a, nf, 0), (nf_b, nf, rows), (og_a, og, 0), (og_b, og, rows)])
-        ]
-        for copy in copies:
+        for copy in loads():
             copy.start()
-        for copy in copies:
+
+    run_fetch(places, weights, hold, sems)
+
+    @pl.when(step == 0)
+    def loaded():
+        for copy in loads():
             copy.wait()
 
+    slot = lax.rem(step, 2)
     x, up = nf[...], og[...]
-    g = contract_cols(x, gw[...])
-    lin = contract_cols(x, lw[...])
-    hg = contract_cols(up, dw[...])
+    g = contract_cols(x, hold[slot, 0])
+    lin = contract_cols(x, hold[slot, 1])
+    hg = contract_cols(up, hold[slot, 2])
     t = jnp.tanh(gelu_c * (g + 0.044715 * (g * g * g)))
     act = 0.5 * g * (1.0 + t)
     slope = 0.5 * (1.0 + t) + 0.5 * g * (1.0 - t * t) * (gelu_c * (1.0 + 3 * 0.044715 * (g * g)))
     hidden = (act * lin).astype(bf16)
     gl = (hg * lin * slope).astype(bf16)
     ll = (hg * act).astype(bf16)
-    ddw_o[...] = contract_rows(hidden, up).astype(bf16)
-    dgw_o[...] = contract_rows(gl, x).astype(bf16)
-    dlw_o[...] = contract_rows(ll, x).astype(bf16)
-    res = matmul(hidden, dw[...])
-    nfg = matmul(gl, gw[...]) + matmul(ll, lw[...])
+    hid_o[0] = hidden
+    gl_o[0] = gl
+    ll_o[0] = ll
+    dgw_o[0] = contract_rows(gl, x).astype(bf16)
+    dlw_o[0] = contract_rows(ll, x).astype(bf16)
+    ddw_o[0] = contract_rows(hidden, up).astype(bf16)
+
+
+def feed_grad(nf_a, nf_b, og_a, og_b, steps, block):
+    rows, width = nf_a.shape
+    weights, places = plan(steps)
+    n = len(steps)
+    any_spec = pl.BlockSpec(memory_space=pl.ANY)
+    tile = pl.BlockSpec((1, block, width), lambda i: (i, 0, 0))
+    column = pl.BlockSpec((1, 2 * rows, block), lambda i: (i, 0, 0))
+    weight = jax.ShapeDtypeStruct((n, block, width), bf16)
+    act = jax.ShapeDtypeStruct((n, 2 * rows, block), bf16)
+    return pl.pallas_call(
+        functools.partial(feed_grad_kernel, places, len(weights)),
+        grid=(n,),
+        in_specs=[any_spec] * (4 + len(weights)),
+        out_specs=(tile, tile, tile, column, column, column),
+        out_shape=(weight, weight, weight, act, act, act),
+        scratch_shapes=[
+            pltpu.VMEM((2 * rows, width), bf16),
+            pltpu.VMEM((2 * rows, width), bf16),
+            pltpu.VMEM((2, 3, block, width), bf16),
+            pltpu.SemaphoreType.DMA((2, max(len(p) for p in places))),
+            pltpu.SemaphoreType.DMA((4,)),
+        ],
+        compiler_params=params(60),
+        cost_estimate=cost(13 * n),
+        name="feed_grad",
+    )(nf_a, nf_b, og_a, og_b, *weights)
+
+
+def feed_out_kernel(places, act_places, count, act_count, *refs):
+    weights, acts = refs[:count], refs[count : count + act_count]
+    nfg_o, nfg_b, res_o, res_b, res_t, nfg_t, hold, acts_hold, sems, act_sems = refs[count + act_count :]
+    step = pl.program_id(0)
+    rows = nfg_o.shape[0]
+    run_fetch(places, weights, hold, sems)
+    run_fetch(act_places, acts, acts_hold, act_sems)
+    slot = lax.rem(step, 2)
+    nfg = matmul(acts_hold[slot, 0], hold[slot, 0]) + matmul(acts_hold[slot, 1], hold[slot, 1])
+    res = matmul(acts_hold[slot, 2], hold[slot, 2])
 
     @pl.when(step == 0)
     def first():
@@ -533,30 +649,50 @@
         nfg_b[...] = nfg_t[...].astype(bf16)
 
 
-def feed_layer(nf_a, nf_b, og_a, og_b, gw, lw, dw, block):
-    rows, width = nf_a.shape
-    hidden = gw.shape[0]
-    any_spec = pl.BlockSpec(memory_space=pl.ANY)
-    tile = pl.BlockSpec((block, width), lambda i: (i, 0))
+def feed_out(rows, width, steps, act_steps, block):
+    weights, places = plan(steps)
+    acts, act_places = plan(act_steps)
     whole = pl.BlockSpec((rows, width), lambda i: (0, 0))
-    weight = jax.ShapeDtypeStruct((hidden, width), bf16)
     wide, low = jax.ShapeDtypeStruct((rows, width), f32), jax.ShapeDtypeStruct((rows, width), bf16)
     return pl.pallas_call(
-        feed_kernel,
-        grid=(hidden // block,),
-        in_specs=[any_spec] * 4 + [tile] * 3,
-        out_specs=(tile, tile, tile, whole, whole, whole, whole),
-        out_shape=(weight, weight, weight, wide, low, wide, low),
+        functools.partial(feed_out_kernel, places, act_places, len(weights), len(acts)),
+        grid=(len(steps),),
+        in_specs=[pl.BlockSpec(memory_space=pl.ANY)] * (len(weights) + len(acts)),
+        out_specs=(whole, whole, whole, whole),
+        out_shape=(wide, low, wide, low),
         scratch_shapes=[
-            pltpu.VMEM((2 * rows, width), bf16),
-            pltpu.VMEM((2 * rows, width), bf16),
             pltpu.VMEM((rows, width), f32),
             pltpu.VMEM((rows, width), f32),
-            pltpu.SemaphoreType.DMA((4,)),
+            pltpu.VMEM((2, 3, block, width), bf16),
+            pltpu.VMEM((2, 3, 2 * rows, block), bf16),
+            pltpu.SemaphoreType.DMA((2, max(len(p) for p in places))),
+            pltpu.SemaphoreType.DMA((2, max(len(p) for p in act_places))),
         ],
         compiler_params=params(60),
-        name="feed",
-    )(nf_a, nf_b, og_a, og_b, gw, lw, dw)
+        cost_estimate=cost(30),
+        name="feed_out",
+    )(*weights, *acts)
+
+
+def tree_sum(values):
+    while len(values) > 1:
+        values = [left + right for left, right in zip(values[::2], values[1::2])]
+    return values[0]
+
+
+def tie(*values):
+    return lax.optimization_barrier(values)
+
+
+def fold_parts(held, order, bit):
+    keep = [i for i, k in enumerate(order) if not k & bit]
+    send = [order.index(order[i] | bit) for i in keep]
+    return [jnp.stack([held[:, i] for i in at], axis=1) for at in (keep, send)]
+
+
+def fold_step(held, order, bit):
+    kept, sent = fold_parts(held, order, bit)
+    return kept, to_mem(sent, bit), [k for k in order if not k & bit]
 
 
 def per_device(
@@ -615,33 +751,24 @@
             [lax.dynamic_index_in_dim(shard, mem_index ^ k, 0, keepdims=False) for k in range(mems)]
         )
 
+    last = chips - 1
+    early = list(range(1, last))
+
+    def matrices(held, other):
+        full = assemble(spot, held, other)
+        full = full.reshape(4, mems // 4, seqs, -1, width).transpose(0, 2, 1, 3, 4)
+        return full.reshape(4, inner, width)
+
+    def hold_plane(pack, moved):
+        return jnp.concatenate([pack[None], jnp.stack(moved, axis=1)], axis=0)
+
     first_pack = quarters(jnp.concatenate([key_cross.T, value_cross.T, query_self.T, key_self.T], axis=0))
-    second_pack = jnp.concatenate([value_self.T, output_self, query_cross.T, output_cross], axis=0)
-    ring = ring_gather(first_pack[0])
-    others = jnp.stack(ring[1:])
-    spread = jnp.stack([to_mem(others, k) if k else others for k in range(mems)], axis=1)
-    held = jnp.concatenate([first_pack[None], spread], axis=0)
-    first_mats = assemble(spot, held, to_core(held))
-    first_mats = (
-        first_mats.reshape(4, mems // 4, seqs, -1, width).transpose(0, 2, 1, 3, 4).reshape(4, inner, width)
-    )
-    second_mats = lax.all_gather(second_pack, "seq", axis=0).reshape(seqs, 4, slim, width)
-    kc_full, vc_full, qs_full, ks_full = [first_mats[i] for i in range(4)]
-    vs_full, os_full, qc_full, oc_full = [second_mats[:, i].reshape(inner, width) for i in range(4)]
-
+    second_pack = quarters(
+        jnp.concatenate([value_self.T, output_self, query_cross.T, output_cross], axis=0)
+    )
     gate_own, linear_own, down_own = quarters(gate_feed.T), quarters(linear_feed.T), quarters(down_feed)
-    start = after(jnp.stack([gate_own[0], linear_own[0]]), ring[-1])
-    both_ring = jnp.stack(ring_gather(start)[1:])
-    gate_spread = spread_gather(both_ring[:, 0], bits)
-    linear_spread = spread_gather(both_ring[:, 1], bits[::-1])
-    down_ring = ring_gather(after(down_own, both_ring))
-    gate_full = jnp.stack([jnp.concatenate([gate_own[k][None], gate_spread[k]]) for k in range(mems)])
-    linear_full = jnp.stack([jnp.concatenate([linear_own[k][None], linear_spread[k]]) for k in range(mems)])
-    down_full = jnp.stack(down_ring, axis=1)
-    hidden_all = mems * chips * part
-    gate_full = gate_full.reshape(hidden_all, width)
-    linear_full = linear_full.reshape(hidden_all, width)
-    down_full = down_full.reshape(hidden_all, width)
+    both = [jnp.stack([gate_own[0], linear_own[0]])]
+    down = [down_own]
 
     onehot = (
         position_buckets(length).reshape(length * length, 1)
@@ -657,75 +784,216 @@
     position_bias = jnp.where(causal[None], position_bias, masked_score)
     tokens = inputs.reshape(rows, width)
     og_low = output_grad.reshape(rows, width)
-    og_other = to_core(og_low)
-    source = memory.reshape(micros, pairs, slots, width)
     gain_self, gain_cross, gain_feed = [g.reshape(1, width) for g in (gain_self, gain_cross, gain_feed)]
+    spots = jnp.stack(
+        [(mem_index ^ s) * slots + jnp.arange(slots, dtype=jnp.int32) for s in range(mems)], 0
+    )
+    len_own = lax.dynamic_index_in_dim(memory_lengths[:, 0], mem_index, 1, keepdims=False)
+    place = spot[2:]
+    source = memory.reshape(micros, pairs, slots, width).swapaxes(2, 3)
+    both_packs = jnp.stack([first_pack[0], second_pack[0]])
+    moved = [to_step(both_packs, j) for j in range(1, chips)]
+    og_other = rows_to_core(og_low)
     keep_all = lax.all_gather(keep_mask[:, 0], "mem", axis=0)
+    moved, both[0], og_other, keep_all = tie(moved, both[0], og_other, keep_all)
     keep_own = lax.dynamic_index_in_dim(keep_all, mem_index, 2, keepdims=False)
     keep_own = jnp.stack(
         [lax.dynamic_index_in_dim(keep_own, mem_index ^ s, 0, keepdims=False) for s in range(mems)], 1
     )
-    spots = jnp.stack(
-        [(mem_index ^ s) * slots + jnp.arange(slots, dtype=jnp.int32) for s in range(mems)], 0
-    )
-    len_own = lax.dynamic_index_in_dim(memory_lengths[:, 0], mem_index, 1, keepdims=False)
     valid = (spots[None] < len_own[:, None, None]) & ((keep_own == 1) | (spots[None] == 0))
     valid = valid.reshape(micros, 1, mems * slots).astype(f32)
-    place = spot[2:]
-
+
+
+    first_parts, second_parts = [jnp.stack([piece[i] for piece in moved])[None] for i in range(2)]
+    first_order, second_order = [0], [0]
+    for first_bit, second_bit in zip(bits, bits[::-1]):
+        first_more, second_more = to_mem(first_parts, first_bit), to_mem(second_parts, second_bit)
+        first_order = first_order + [k | first_bit for k in first_order]
+        second_order = second_order + [k | second_bit for k in second_order]
+        if len(both) < last:
+            both.append(to_next(both[-1]))
+        first_more, second_more, both[-1] = tie(first_more, second_more, both[-1])
+        first_parts = jnp.concatenate([first_parts, first_more])
+        second_parts = jnp.concatenate([second_parts, second_more])
+    while len(both) < last:
+        both.append(to_next(both[-1]))
+
+    def hold_parts(pack, parts, order):
+        spread = jnp.stack([parts[order.index(k)] for k in range(mems)], axis=1)
+        return jnp.concatenate([pack[None], spread], axis=0)
+
+    first_held = hold_parts(first_pack, first_parts, first_order)
+    first_more = to_core(first_held)
+    gate_early = jnp.stack([both[j][0] for j in early])[None]
+    linear_early = jnp.stack([both[j][1] for j in early])[None]
+    gate_a1 = to_mem(gate_early, bits[0])
+    linear_a1 = to_mem(linear_early, bits[-1])
+    both.append(to_next(both[-1]))
+    second_held = hold_parts(second_pack, second_parts, second_order)
+    first_more, gate_a1, linear_a1, both[last], second_held = tie(
+        first_more, gate_a1, linear_a1, both[last], second_held
+    )
+
+    second_more = to_core(second_held)
+    gate_late, linear_late = both[last][:1], both[last][1:]
+    gate_late_a1 = to_mem(gate_late, bits[0])
+    linear_late_a1 = to_mem(linear_late, bits[-1])
+    first_mats = matrices(first_held, first_more)
+    kc_full, vc_full, qs_full, ks_full = [first_mats[i] for i in range(4)]
     kv_local = kv_fwd(place, source, kc_full, vc_full)
+    gate_early = jnp.concatenate([gate_early, gate_a1])
+    linear_early = jnp.concatenate([linear_early, linear_a1])
+    kv_local, second_more, gate_late_a1, linear_late_a1, down[0], gate_early, linear_early = tie(
+        kv_local, second_more, gate_late_a1, linear_late_a1, down[0], gate_early, linear_early
+    )
+
     kvs = [to_mem(kv_local[s], s) if s else kv_local[s] for s in range(mems)]
+    down.append(to_next(down[0]))
+    second_mats = matrices(second_held, second_more)
+    vs_full, os_full, qc_full, oc_full = [second_mats[i] for i in range(4)]
     normed, q, k, v, mixed, first_sum, normed_cross, cq = self_fwd(
         depth, length, tokens, gain_self, qs_full, ks_full, vs_full, os_full, position_bias, gain_cross, qc_full
     )
+    kvs, down[1], cq, gate_early, linear_early = tie(kvs, down[1], cq, gate_early, linear_early)
+
+    def spread_rest(held, order, over):
+        parts = [held]
+        for bit in over:
+            parts.append(to_mem(jnp.concatenate(parts) if len(parts) > 1 else parts[0], bit))
+            order = order + [k | bit for k in order]
+        return parts, order
+
+    gate_parts, gate_order = spread_rest(gate_early, [0, bits[0]], bits[1:])
+    linear_parts, linear_order = spread_rest(linear_early, [0, bits[-1]], bits[::-1][1:])
+    gate_late = jnp.concatenate([gate_late, gate_late_a1])
+    linear_late = jnp.concatenate([linear_late, linear_late_a1])
+    for _ in early[1:]:
+        down.append(to_next(down[-1]))
     cmixed, second_sum, normed_feed = cross_fwd(depth, length, cq, valid, oc_full, first_sum, gain_feed, kvs)
-    nf_other = to_core(normed_feed)
-    block = 256 if hidden_all % 256 == 0 else part
-    grad_gate, grad_linear, grad_down, res_own, res_send, nfg_own, nfg_send = feed_layer(
-        normed_feed, nf_other, og_low, og_other, gate_full, linear_full, down_full, block
-    )
-    nfg_more = to_core(nfg_send)
-    result = second_sum + res_own + to_core(res_send).astype(f32)
-
-    split = (mems, chips, part, width)
-    gate_sum = fold(grad_gate.reshape(split), bits[::-1])
-    linear_sum = fold(grad_linear.reshape(split), bits)
-    both_sum = ring_sum([jnp.stack([gate_sum[j], linear_sum[j]]) for j in range(chips)])
-    grad_down = grad_down.reshape(split)
-    down_sum = ring_sum([grad_down[:, j] for j in range(chips)])
-    down_sum = direct_fold([down_sum[s] for s in range(mems)])
-    feed_out = back_to_mem(jnp.concatenate([both_sum, down_sum[None]]), mem_index)
-    gate_out, linear_out, down_out = [feed_out[:, i].reshape(feed, width) for i in range(3)]
-
+    gate_parts, linear_parts, gate_late, linear_late, down[1:], normed_feed = tie(
+        gate_parts, linear_parts, gate_late, linear_late, down[1:], normed_feed
+    )
+
+    def sources(parts, order, n):
+        places = {}
+        at = 0
+        for piece in parts:
+            for i in range(piece.shape[0]):
+                places[order[at]] = (piece, (i, n) if piece.ndim == 4 else (i,), part)
+                at += 1
+        return [places[k] for k in range(mems)]
+
+    def whole_source(array, listed):
+        if part % 16 == 0:
+            return listed
+        pieces = []
+        for piece, index, _ in listed:
+            for i in index:
+                piece = piece[i]
+            pieces.append(piece)
+        return [(jnp.concatenate(pieces), (), feed)]
+
+    own_steps = [[(g.reshape(feed, width), (), feed)] for g in (gate_own, linear_own, down_own)]
+    early_steps = [
+        [
+            whole_source(None, sources(gate_parts, gate_order, n)),
+            whole_source(None, sources(linear_parts, linear_order, n)),
+            [(down[j].reshape(feed, width), (), feed)],
+        ]
+        for n, j in enumerate(early)
+    ]
+    nf_other = rows_to_core(normed_feed)
+    gate_late_parts, gate_order = spread_rest(gate_late, [0, bits[0]], bits[1:])
+    linear_late_parts, linear_order = spread_rest(linear_late, [0, bits[-1]], bits[::-1][1:])
+    down.append(to_next(down[-1]))
+    grads_a = feed_grad(normed_feed, nf_other, og_low, og_other, early_steps + [own_steps], feed)
+    grads_a, gate_late_parts, linear_late_parts, down[last], nf_more = tie(
+        grads_a, gate_late_parts, linear_late_parts, down[last], nf_other
+    )
+
+    gate_x = grads_a[0].reshape(last, mems, part, width)
+    linear_x = grads_a[1].reshape(last, mems, part, width)
+    natural_order = list(range(mems))
+    gate_kept, gate_moved, gate_ord = fold_step(gate_x, natural_order, bits[-1])
+    linear_kept, linear_moved, linear_ord = fold_step(linear_x, natural_order, bits[0])
+    down_total = to_next(grads_a[2][0])
+    late_steps = [
+        [
+            whole_source(None, sources(gate_late_parts, gate_order, 0)),
+            whole_source(None, sources(linear_late_parts, linear_order, 0)),
+            [(down[last].reshape(feed, width), (), feed)],
+        ]
+    ]
+    grads_b = feed_grad(normed_feed, nf_more, og_low, og_other, late_steps, feed)
+    act_steps = [
+        [[(grads[i], (n,), 2 * rows)] for i in (4, 5, 3)]
+        for grads, count in ((grads_a, last), (grads_b, 1))
+        for n in range(count)
+    ]
+    nfg_own, nfg_send, res_own, res_send = feed_out(
+        rows, width, early_steps + [own_steps] + late_steps, act_steps, feed
+    )
+    gate_moved, linear_moved, down_total, nfg_send, dg_b, dl_b = tie(
+        gate_moved, linear_moved, down_total, nfg_send, grads_b[0], grads_b[1]
+    )
+
+    def two_folds(fresh, order, bit, older, older_order, older_bit):
+        kept, sent = fold_parts(fresh, order, bit)
+        older_kept, older_sent = fold_parts(older, older_order, older_bit)
+        moved = to_mem(jnp.concatenate([sent.reshape(-1, part, width), older_sent.reshape(-1, part, width)]), bit)
+        count = sent.shape[0] * sent.shape[1]
+        return kept, moved[:count].reshape(sent.shape), older_kept, moved[count:].reshape(older_sent.shape)
+
+    def fold_to_last(held, order, over):
+        for bit in over[:-1]:
+            kept, moved, order = fold_step(held, order, bit)
+            held = add_low(kept, moved)
+        return held, order
+
+    gate_y, gate_yo = fold_to_last(add_low(gate_kept, gate_moved), gate_ord, bits[::-1][1:])
+    linear_y, linear_yo = fold_to_last(add_low(linear_kept, linear_moved), linear_ord, bits[1:])
+    nfg_more = rows_to_core(nfg_send)
+    gate_b, gate_bm, linear_yk, linear_ym = two_folds(
+        dg_b.reshape(1, mems, part, width), natural_order, bits[-1], linear_y, linear_yo, bits[-1]
+    )
+    linear_b, linear_bm, gate_yk, gate_ym = two_folds(
+        dl_b.reshape(1, mems, part, width), natural_order, bits[0], gate_y, gate_yo, bits[0]
+    )
+    for j in early[1:]:
+        down_total = to_next(add_low(down_total, grads_a[2][j - 1]))
     kvg, (grad_gain_feed, grad_co, grad_cq, first_grad, grad_gain_cross) = cross_bwd(
         depth, length, og_low, nfg_own, nfg_more, second_sum, gain_feed, cmixed, cq, valid, oc_full,
         first_sum, gain_cross, normed_cross, qc_full, kvs,
     )
-    kvg = jnp.stack([to_mem(kvg[s], s) if s else kvg[s] for s in range(mems)])
-    memory_grad, grad_kc, grad_vc = kv_bwd(place, source, kc_full, vc_full, kvg)
+    gate_bm, linear_bm, gate_ym, linear_ym, down_total, kvg, grad_gain_cross, res_send = tie(
+        gate_bm, linear_bm, gate_ym, linear_ym, down_total, kvg, grad_gain_cross, res_send
+    )
+
+    kvg = [to_mem(kvg[s], s) if s else kvg[s] for s in range(mems)]
+    gate_y, linear_y = add_low(gate_yk, gate_ym)[:, 0], add_low(linear_yk, linear_ym)[:, 0]
+    down_total = add_low(down_total, grads_b[2][0]).reshape(mems, part, width)
+    ring = to_next(jnp.concatenate([down_total, gate_y[:1], linear_y[:1]]))
+    res_more = rows_to_core(res_send)
     grad_os, grad_qs, grad_ks, grad_vs, input_grad, grad_gain_self, score_sum = self_bwd(
         depth, length, first_grad, mixed, q, k, v, position_bias, os_full, qs_full, ks_full, vs_full,
         normed, tokens, gain_self,
     )
-
-    cross_stack = jnp.stack([g.reshape(seqs, slim, width) for g in (grad_kc, grad_vc, grad_cq, grad_co)], axis=1)
-    cross_sum = lax.psum_scatter(cross_stack.reshape(seqs, 4 * slim, width), "seq", scatter_dimension=0)
-    cross_sum = direct_fold([cross_sum] * mems).astype(f32).reshape(4, slim, width)
+    kvg, ring, grad_qs, res_more, gate_bm, linear_bm = tie(kvg, ring, grad_qs, res_more, gate_bm, linear_bm)
 
     self_stack = jnp.stack(
         [g.reshape(chips, 2, slim, width) for g in (grad_qs, grad_ks, grad_vs, grad_os)], axis=2
     )
     kept = lax.dynamic_index_in_dim(self_stack, core, 1, keepdims=False)
-    sent = lax.dynamic_index_in_dim(self_stack, 1 - core, 1, keepdims=False)
-    total = add_low(kept, to_core(sent)).reshape(chips, mems, 4 * slim // mems, width)
-    total = direct_fold(
-        [lax.dynamic_index_in_dim(total, mem_index ^ s, 1, keepdims=False) for s in range(mems)]
-    )
-    pieces = [
-        lax.dynamic_index_in_dim(total, (chip + j) % chips, 0, keepdims=False) for j in range(chips)
-    ]
-    total = sum_low([to_step(p, j) if j else p for j, p in enumerate(pieces)])
-    self_sum = back_to_mem(total, mem_index).reshape(4, slim, width)
+    sent = to_core(lax.dynamic_index_in_dim(self_stack, 1 - core, 1, keepdims=False))
+    down_total, both_total = ring[:mems], ring[mems:]
+    for j in early[1:]:
+        both_total = to_next(add_low(both_total, jnp.stack([gate_y[j - 1], linear_y[j - 1]])))
+    gate_b, gate_bo = fold_to_last(add_low(gate_b, gate_bm), gate_ord, bits[::-1][1:])
+    linear_b, linear_bo = fold_to_last(add_low(linear_b, linear_bm), linear_ord, bits[1:])
+    gate_bk, gate_bm, _ = fold_step(gate_b, gate_bo, bits[0])
+    linear_bk, linear_bm, _ = fold_step(linear_b, linear_bo, bits[-1])
+    memory_grad, grad_kc, grad_vc = kv_bwd(place, source, kc_full, vc_full, jnp.stack(kvg))
+    sent, both_total, gate_bm, linear_bm, grad_kc = tie(sent, both_total, gate_bm, linear_bm, grad_kc)
 
     grad_table = lax.dot_general(
         onehot.astype(f32),
@@ -735,14 +1003,80 @@
     )
     table_row = jnp.pad(grad_table.reshape(1, buckets * heads), ((0, 0), (0, width - buckets * heads)))
     small = jnp.concatenate([grad_gain_self, grad_gain_cross, grad_gain_feed, table_row], axis=0)
-    for bit in bits:
-        small = small + to_mem(small, bit)
-    for bit in [1 << b for b in range((seqs - 1).bit_length())]:
-        small = small + to_seq(small, bit)
+
+    def to_rows(value):
+        high = value.astype(bf16)
+        rest = (value - high.astype(f32)).astype(bf16)
+        return jnp.concatenate([high, rest, jnp.zeros((16 - 2 * value.shape[0], width), bf16)])
+
+    def from_rows(value, count):
+        return value[:count].astype(f32) + value[count : 2 * count].astype(f32)
+
+    cross_stack = jnp.stack(
+        [g.reshape(seqs, slim, width) for g in (grad_kc, grad_vc, grad_cq, grad_co)], axis=1
+    ).reshape(seqs, 4 * slim, width)
+    cross_sum = lax.psum_scatter(cross_stack, "seq", scatter_dimension=0)
+    total = add_low(kept, sent).reshape(chips, mems, 4 * slim // mems, width)
+    share = 4 * slim // mems
+    down_mine = add_low(down_total, grads_a[2][last - 1].reshape(mems, part, width))
+    columns = []
+    for s in range(mems):
+        column = lax.dynamic_index_in_dim(total, mem_index ^ s, 1, keepdims=False).reshape(-1, width)
+        columns.append(jnp.concatenate([column, down_mine[s], to_rows(small)]))
+    columns = [to_mem(p, s) if s else p for s, p in enumerate(columns)]
+    gate_b, linear_b = add_low(gate_bk, gate_bm)[0, 0], add_low(linear_bk, linear_bm)[0, 0]
+    both_total = to_next(add_low(both_total, jnp.stack([gate_b, linear_b])))
+    columns, both_total = tie(columns, both_total)
+
+    down_sum = sum_low([p[chips * share : chips * share + part] for p in columns])
+    small = tree_sum([from_rows(p[chips * share + part :], 4) for p in columns])
+    total = sum_low([p[: chips * share] for p in columns]).reshape(chips, share, width)
+    pieces = [
+        jnp.concatenate(
+            [lax.dynamic_index_in_dim(total, (chip + j) % chips, 0, keepdims=False), to_rows(small)]
+        )
+        for j in range(chips)
+    ]
+    pieces = [to_step(p, j) if j else p for j, p in enumerate(pieces)]
+    both_sum = add_low(both_total, jnp.stack([gate_y[last - 1], linear_y[last - 1]]))
+    gate_g = [both_sum[:1], to_mem(both_sum[:1], bits[0])]
+    linear_g = [both_sum[1:], to_mem(both_sum[1:], bits[-1])]
+    pieces, gate_g, linear_g, cross_sum = tie(pieces, gate_g, linear_g, cross_sum)
+
+    self_mine = sum_low([p[:share] for p in pieces])
+    small = jnp.stack([from_rows(p[share:], 4) for p in pieces])
+    small = tree_sum(
+        [lax.dynamic_index_in_dim(small, (chip - z) % chips, 0, keepdims=False) for z in range(chips)]
+    )
+    gate_g, gate_order = spread_rest(jnp.concatenate(gate_g), [0, bits[0]], bits[1:])
+    linear_g, linear_order = spread_rest(jnp.concatenate(linear_g), [0, bits[-1]], bits[::-1][1:])
+    cross_parts = [to_mem(p, s) if s else p for s, p in enumerate(quarters(cross_sum))]
+    gate_g, linear_g, cross_parts, small, self_mine = tie(gate_g, linear_g, cross_parts, small, self_mine)
+
+    mine = jnp.concatenate([self_mine, sum_low(cross_parts), down_sum])
+    mine_g = [mine] + [to_mem(mine, k) for k in range(1, mems)]
+    small = small + to_core(small)
+
+    def settle(parts, order):
+        flat = jnp.concatenate(parts)
+        pieces = [flat[order.index(k)] for k in range(mems)]
+        return natural(pieces, mem_index).astype(f32)
+
+    gate_out = settle(gate_g, gate_order).reshape(feed, width)
+    linear_out = settle(linear_g, linear_order).reshape(feed, width)
+    mine_g, gate_out, linear_out = tie(mine_g, gate_out, linear_out)
+    result = second_sum + res_own + res_more.astype(f32)
+
+    def settled(start, rows_of):
+        return natural([p[start : start + rows_of] for p in mine_g], mem_index).astype(f32)
+
+    self_sum = settled(0, share).reshape(4, slim, width)
+    cross_sum = settled(share, share).reshape(4, slim, width)
+    down_out = settled(2 * share, part).reshape(feed, width)
     return (
         result.reshape(inputs.shape),
         input_grad.reshape(inputs.shape),
-        memory_grad.reshape(memory.shape),
+        memory_grad.swapaxes(2, 3).reshape(memory.shape),
         small[0],
         self_sum[0].T,
         self_sum[1].T,

time: 783 us -> 625 us (0.80)
  waiting for transfers between devices: 301 us -> 175 us
  starting transfers between devices: 81.3 us -> 61 us
  local copies, waits for them, and re-layouts: 103 us -> 84.3 us
  Pallas kernels: 184 us -> 198 us
    ppermute x15 -> x11, waiting for transfers between devices: 136 us -> 48.9 us  [to_next(): lax.ppermute(value, 'seq', [(i, (i + 2) % count) for i in range(count)])]
    ppermute x34 -> x37, waiting for transfers between devices: 143 us -> 109 us  [to_mem(): return lax.ppermute(value, 'mem', [(i, i ^ mask) for i in range(count)])]
    another operation x18 -> x16, other arithmetic: 32.5 us -> 10 us  [the longest x1 3.29 us: per_device(): jnp.stack(kvg)]
    ppermute x15 -> x11, starting transfers between devices: 29.9 us -> 9.41 us  [to_next(): lax.ppermute(value, 'seq', [(i, (i + 2) % count) for i in range(count)])]
    concatenate x0 -> x7, local copies, waits for them, and re-layouts: none -> 19.5 us  [the longest x4 19.3 us: per_device(): columns.append(jnp.concatenate([column, down_mine[s], to_rows(small)]))]
    pallas_call x1 -> x3, Pallas kernels: 72.7 us -> 85.9 us  [the longest x2 51.9 us: feed_grad(): pl.pallas_call(functools.partial(feed_grad_kernel, places, len(weights)),...]
    ppermute x4 -> x0, local copies, waits for them, and re-layouts: 10.5 us -> none  [to_core(): return lax.ppermute(value, 'seq', [(i, i ^ 1) for i in range(count)])]
    unnamed x128 -> x187, local copies, waits for them, and re-layouts: 38.8 us -> 28.6 us
  transfers between devices with their start and end apart: 63 -> 63, of which waited for: 27 -> 24; matrix products, arithmetic and copies ran while one was open for 22% -> 18% of each run, Pallas kernels for 14% -> 32%
where the time goes in v2:
time: 625 us; the launch traced here: 615 us
  Pallas kernels  198 us (32%)
  waiting for transfers between devices  175 us (28%)
  local copies, waits for them, and re-layouts  84.3 us (13%)
  other arithmetic  69.7 us (11%)
  starting transfers between devices  61 us (10%)
  between operations  16.4 us (3%)
  blocking collectives  8.16 us (1%)
    ppermute x37, waiting for transfers between devices, to_mem(): return lax.ppermute(value, 'mem', [(i, i ^ mask) for i in range(count)])  109 us
    pallas_call x2, Pallas kernels, feed_grad(): pl.pallas_call(functools.partial(feed_grad_kernel, places, len(weights)),...  51.9 us
    ppermute x11, waiting for transfers between devices, to_next(): lax.ppermute(value, 'seq', [(i, (i + 2) % count) for i in range(count)])  48.9 us
    ppermute x37, starting transfers between devices, to_mem(): return lax.ppermute(value, 'mem', [(i, i ^ mask) for i in range(count)])  40.6 us
    pallas_call x1, Pallas kernels, feed_out(): pl.pallas_call(functools.partial(feed_out_kernel, places, act_places, len...  34 us
    pallas_call x1, Pallas kernels, cross_bwd(): pl.pallas_call(functools.partial(cross_bwd_kernel, depth, length, len(kvs...  31.5 us
    unnamed x187, local copies, waits for them, and re-layouts  28.6 us
    pallas_call x1, Pallas kernels, self_bwd(): pl.pallas_call(functools.partial(self_bwd_kernel, depth, length), out_sha...  20.8 us
  transfers between devices with their start and end apart: 63, of which 24 were waited for; matrix products, arithmetic and copies ran while one was open for 18% of the time, Pallas kernels for 32%

profile of v2, /device:TPU:8, one launch (start us, length us, event | category | flops | bytes accessed | tf_op | source)
XLA Modules:
  0.0 615.0 jit_solution(7137794510235278649)
XLA Ops:
  14.5 2.0 collective-permute-start.2
  21.1 2.4 constant_dynamic-slice_fusion.26
  24.5 8.2 %all-gather = s32[8,1,4,256]{3,2,1,0:T(4,128)S(1)} all-gather(s32[2,1,4,256]{3,2,1,0:T(4,128)S(1)} %copy-done.74), channel_id=2, replica_groups=mesh['seq'=8,'mem'=4] {'mem'}, dimensions={0}, use_global_device_ids=true | all-gather | bytes 40960 | tf_op jit(solution)/shard_map/all_gather | solution.py:797
  39.0 1.8 collective-permute-done.2
  47.8 1.8 fusion.9.bias
  49.6 6.5 %collective-permute-done.5 = bf16[1,3,48,1472]{3,2,1,0:T(8,128)(2,1)S(1)} collective-permute-done((bf16[1,3,48,1472]{3,2,1,0:T(8,128)(2,1)S(1)}, bf16[1,3,48,1472]{3,2,1,0:T(8,128)(2,1)S(1)}, u32[]{:S(2)}, u32[]{:S(2)}) %collective-permute-start.5) | collective-permute-done | bytes 423968 | tf_op jit(solution)/shard_map/ppermute | solution.py:62
  56.0 2.1 collective-permute-done.4
  58.1 4.4 collective-permute-done.6
  66.7 2.6 copy.141
  73.6 13.8 %collective-permute-done.9 = bf16[2,112,1472]{2,1,0:T(8,128)(2,1)} collective-permute-done((bf16[2,112,1472]{2,1,0:T(8,128)(2,1)}, bf16[2,112,1472]{2,1,0:T(8,128)(2,1)}, u32[]{:S(2)}, u32[]{:S(2)}) %collective-permute-start.9) | collective-permute-done | bytes 659488 | tf_op jit(solution)/shard_map/ppermute | solution.py:57
  95.7 13.2 %collective-permute-done.12 = bf16[1,2,112,1472]{3,2,1,0:T(8,128)(2,1)S(1)} collective-permute-done((bf16[1,2,112,1472]{3,2,1,0:T(8,128)(2,1)S(1)}, bf16[1,2,112,1472]{3,2,1,0:T(8,128)(2,1)S(1)}, u32[]{:S(2)}, u32[]{:S(2)}) %collective-permute-start.12) | collective-permute-done | bytes 659488 | tf_op jit(solution)/shard_map/ppermute | solution.py:62
  113.0 1.8 fusion.39
  114.8 8.8 %kv_fwd.1 = bf16[4,2,256,768]{3,2,1,0:T(8,128)(2,1)S(1)} custom-call(s32[4]{0:T(128)S(1)} %pad_add_fusion.place, bf16[2,4,1472,256]{3,2,1,0:T(8,128)(2,1)S(1)} %bitcast.336, bf16[384,1472]{1,0:T(8,128)(2,1)S(1)} %bitcast.329, bf16[384,1472]{1,0:T(8,128)(2,1)S(1)} %bitcast.327), custom_call_target="tpu_custom_call" | custom-call | flops 8999999488 | bytes 27000000 | tf_op jit(solution)/shard_map/kv_fwd/pallas_call | solution.py:437
  125.4 2.3 fusion.38
  132.7 15.5 %self_fwd.1 = (bf16[512,1472]{1,0:T(8,128)(2,1)}, bf16[512,384]{1,0:T(8,128)(2,1)}, bf16[512,384]{1,0:T(8,128)(2,1)}, bf16[512,384]{1,0:T(8,128)(2,1)}, bf16[512...) custom-call(bf16[512,1472]{1,0:T(8,128)(2,1)} %bitcast.360, ...), custom_call_target="tpu_custom_call" | custom-call | flops 16000000000 | bytes 48000000 | tf_op jit(solution)/shard_map/self_fwd/pallas_call | solution.py:231
  148.1 1.9 pad_maximum_fusion.21.refs_6_.refs_11_
  151.0 15.2 %collective-permute-done.18.refs_2_ = bf16[2,256,768]{2,1,0:T(8,128)(2,1)} collective-permute-done((bf16[2,256,768]{2,1,0:T(8,128)(2,1)S(1)}, bf16[2,256,768]{2,1,0:T(8,128)(2,1)}, u32[]{:S(2)}, u32[]{:S(2)}) %collective-permute-start.18) | collective-permute-done | bytes 786464 | tf_op jit(solution)/shard_map/ppermute | solution.py:62
  168.7 15.1 %cross_fwd.1 = (bf16[512,384]{1,0:T(8,128)(2,1)}, f32[512,1472]{1,0:T(8,128)}, bf16[512,1472]{1,0:T(8,128)(2,1)}) custom-call(bf16[512,384]{1,0:T(8,128)(2,1)} %get-tuple-element.199.cq, f32[2,1,1024]{2,1,0:T(1,128)} %and_convert_fusion.mask, bf16[384,1472]{1,0:T(8,128)(2,1)} %bitcast.384, f32[512,1472]{1,0:T(8,128)} %get-tuple-element.201.first, ...), custom_call_target="tpu_custom_call" | custom-call | flops 15000000512 | bytes 45000000 | tf_op jit(solution)/shard_map/cross_fwd/pallas_call | solution.py:272
  183.8 13.4 %collective-permute-done.21.refs_5_.refs_1_ = bf16[2,2,112,1472]{3,2,1,0:T(8,128)(2,1)S(1)} collective-permute-done((bf16[2,2,112,1472]{3,2,1,0:T(8,128)(2,1)S(1)}, bf16[2,2,112,1472]{3,2,1,0:T(8,128)(2,1)S(1)}, u32[]{:S(2)}, u32[]{:S(2)}) %collective-permute-start.21) | collective-permute-done | bytes 1318944 | tf_op jit(solution)/shard_map/ppermute | solution.py:62
  206.2 36.8 %feed_grad.2 = (bf16[3,448,1472]{2,1,0:T(8,128)(2,1)}, bf16[3,448,1472]{2,1,0:T(8,128)(2,1)}, bf16[3,448,1472]{2,1,0:T(8,128)(2,1)}, bf16[3,1024,448]{2,1,0:T(8,...) custom-call(bf16[512,1472]{1,0:T(8,128)(2,1)} %get-tuple-element.219.refs_0_, ...), custom_call_target="tpu_custom_call" | custom-call | flops 38999998464 | bytes 117000000 | tf_op jit(solution)/shard_map/feed_grad/pallas_call | solution.py:602
  243.1 4.0 slice_bitcast_fusion.7
  254.5 2.7 collective-permute-start.30
  257.2 15.1 %feed_grad.3 = (bf16[1,448,1472]{2,1,0:T(8,128)(2,1)}, bf16[1,448,1472]{2,1,0:T(8,128)(2,1)}, bf16[1,448,1472]{2,1,0:T(8,128)(2,1)}, bf16[1,1024,448]{2,1,0:T(8,...) custom-call(bf16[512,1472]{1,0:T(8,128)(2,1)} %get-tuple-element.219.refs_0_, ...), custom_call_target="tpu_custom_call" | custom-call | flops 12999999488 | bytes 39000000 | tf_op jit(solution)/shard_map/feed_grad/pallas_call | solution.py:602
  272.3 34.0 %feed_out.1 = (f32[512,1472]{1,0:T(8,128)}, bf16[512,1472]{1,0:T(8,128)(2,1)}, f32[512,1472]{1,0:T(8,128)}, bf16[512,1472]{1,0:T(8,128)(2,1)}) custom-call(bf16[2,2,112,1472]{3,2,1,0:T(8,128)(2,1)} %copy-done.25, bf16[2,2,112,1472]{3,2,1,0:T(8,128)(2,1)} %copy-done.80, bf16[2,2,112,1472]{3,2,1,0:T(8,128)(2,1)} %copy-done.24, ...), custom_call_target="tpu_custom_call" | custom-call | flops 30000001024 | bytes 90000000 | tf_op jit(solution)/shard_map/feed_out/pallas_call | solution.py:657
  306.5 3.3 fusion.7
  309.7 2.5 collective-permute-start.33
  313.1 2.3 add_convert_fusion
  317.5 2.2 add_convert_fusion.1
  321.8 31.5 %cross_bwd.1 = (bf16[2,256,768]{2,1,0:T(8,128)(2,1)}, bf16[2,256,768]{2,1,0:T(8,128)(2,1)}, bf16[2,256,768]{2,1,0:T(8,128)(2,1)}, bf16[2,256,768]{2,1,0:T(8,128)...) custom-call(bf16[512,1472]{1,0:T(8,128)(2,1)} %bitcast.359, ...), custom_call_target="tpu_custom_call" | custom-call | flops 31000000512 | bytes 93000000 | tf_op jit(solution)/shard_map/cross_bwd/pallas_call | solution.py:340
  353.3 2.3 collective-permute-done.32
  356.7 4.5 collective-permute-done.31
  368.0 1.8 fusion.6
  375.0 20.8 %self_bwd.1 = (bf16[384,1472]{1,0:T(8,128)(2,1)}, bf16[384,1472]{1,0:T(8,128)(2,1)}, bf16[384,1472]{1,0:T(8,128)(2,1)}, bf16[384,1472]{1,0:T(8,128)(2,1)}, f32[5...) custom-call(f32[512,1472]{1,0:T(8,128)} %get-tuple-element.271.first_grad, ...), custom_call_target="tpu_custom_call" | custom-call | flops 20999999488 | bytes 63000000 | tf_op jit(solution)/shard_map/self_bwd/pallas_call | solution.py:406
  395.8 13.9 %collective-permute-done.36 = bf16[2,256,768]{2,1,0:T(8,128)(2,1)S(1)} collective-permute-done((bf16[2,256,768]{2,1,0:T(8,128)(2,1)}, bf16[2,256,768]{2,1,0:T(8,128)(2,1)S(1)}, u32[]{:S(2)}, u32[]{:S(2)}) %collective-permute-start.36) | collective-permute-done | bytes 786464 | tf_op jit(solution)/shard_map/ppermute | solution.py:62
  409.7 8.0 %collective-permute-done.38 = bf16[6,112,1472]{2,1,0:T(8,128)(2,1)} collective-permute-done((bf16[6,112,1472]{2,1,0:T(8,128)(2,1)}, bf16[6,112,1472]{2,1,0:T(8,128)(2,1)}, u32[]{:S(2)}, u32[]{:S(2)}) %collective-permute-start.38) | collective-permute-done | bytes 1978400 | tf_op jit(solution)/shard_map/ppermute | solution.py:57
  423.6 1.9 copy-done.6
  425.6 2.3 add_convert_fusion.6
  428.3 3.3 pad_maximum_fusion.2.kvg
  431.6 17.4 %kv_bwd.1 = (f32[2,4,1472,256]{3,2,1,0:T(8,128)}, bf16[384,1472]{1,0:T(8,128)(2,1)S(1)}, bf16[384,1472]{1,0:T(8,128)(2,1)S(1)}) custom-call(s32[4]{0:T(128)S(1)} %pad_add_fusion.place, bf16[2,4,1472,256]{3,2,1,0:T(8,128)(2,1)} %bitcast.333, bf16[384,1472]{1,0:T(8,128)(2,1)S(1)} %bitcast.330, bf16[384,1472]{1,0:T(8,128)(2,1)S(1)} %bitcast.328, ...), custom_call_target="tpu_custom_call" | custom-call | flops 16999999488 | bytes 51000000 | tf_op jit(solution)/shard_map/kv_bwd/pallas_call | solution.py:486
  449.1 2.7 pad_maximum_fusion.1
  452.5 2.3 copy.176
  456.2 3.5 copy.159
  459.8 1.8 fusion.5
  463.8 2.5 fusion.2
  467.4 5.8 concatenate.104
  474.9 5.8 concatenate.103
  481.3 4.6 concatenate.102
  490.0 3.0 convert_add_fusion.1
  493.0 2.3 copy.158
  495.3 3.0 concatenate.101
  498.2 21.0 %collective-permute-done.47 = bf16[2,112,1472]{2,1,0:T(8,128)(2,1)} collective-permute-done((bf16[2,112,1472]{2,1,0:T(8,128)(2,1)}, bf16[2,112,1472]{2,1,0:T(8,128)(2,1)}, u32[]{:S(2)}, u32[]{:S(2)}) %collective-permute-start.47) | collective-permute-done | bytes 659488 | tf_op jit(solution)/shard_map/ppermute | solution.py:57
  520.7 1.8 collective-permute-start.51
  523.9 1.8 add_convert_fusion.7
  528.3 4.2 collective-permute-start.49
  534.1 1.8 collective-permute-done.48
  535.9 8.5 %collective-permute-done.49 = bf16[64,1472]{1,0:T(8,128)(2,1)S(1)} collective-permute-done((bf16[64,1472]{1,0:T(8,128)(2,1)S(1)}, bf16[64,1472]{1,0:T(8,128)(2,1)S(1)}, u32[]{:S(2)}, u32[]{:S(2)}) %collective-permute-start.49) | collective-permute-done | bytes 188448 | tf_op jit(solution)/shard_map/ppermute | solution.py:71
  544.5 3.6 collective-permute-done.50
  555.6 16.2 %collective-permute-done.55 = bf16[48,1472]{1,0:T(8,128)(2,1)S(1)} collective-permute-done((bf16[48,1472]{1,0:T(8,128)(2,1)S(1)}, bf16[48,1472]{1,0:T(8,128)(2,1)S(1)}, u32[]{:S(2)}, u32[]{:S(2)}) %collective-permute-start.55) | collective-permute-done | bytes 141344 | tf_op jit(solution)/shard_map/ppermute | solution.py:62
  571.8 2.0 collective-permute-done.56
  578.1 2.0 bitcast_convert_fusion.2
  580.6 2.0 bitcast_convert_fusion.3
  584.0 7.3 %collective-permute-done.59 = bf16[208,1472]{1,0:T(8,128)(2,1)S(1)} collective-permute-done((bf16[208,1472]{1,0:T(8,128)(2,1)S(1)}, bf16[208,1472]{1,0:T(8,128)(2,1)S(1)}, u32[]{:S(2)}, u32[]{:S(2)}) %collective-permute-start.59) | collective-permute-done | bytes 612384 | tf_op jit(solution)/shard_map/ppermute | solution.py:62
  591.3 11.1 %collective-permute-done.61 = bf16[208,1472]{1,0:T(8,128)(2,1)S(1)} collective-permute-done((bf16[208,1472]{1,0:T(8,128)(2,1)S(1)}, bf16[208,1472]{1,0:T(8,128)(2,1)S(1)}, u32[]{:S(2)}, u32[]{:S(2)}) %collective-permute-start.61) | collective-permute-done | bytes 612384 | tf_op jit(solution)/shard_map/ppermute | solution.py:62
  603.2 2.0 bitcast_convert_fusion.1
  (431 shorter events, 133.0 us)
Async XLA Ops:
  7.2 541.6 %reduce-scatter.2.cloned.1.call-start = ((), (), s32[]{:S(2)}) async-start(), calls=%async_computation.1 | async-start | bytes 5308416 | tf_op jit(solution)/shard_map/reduce_scatter | solution.py:1018
  11.9 25.8 %collective-permute-start = (bf16[2,48,1472]{2,1,0:T(8,128)(2,1)}, bf16[2,48,1472]{2,1,0:T(8,128)(2,1)}, u32[]{:S(2)}, u32[]{:S(2)}) collective-permute-start(bf16[2,48,1472]{2,1,0:T(8,128)(2,1)} %pad_maximum_fusion.41), channel_id=1, source_target_pairs={{0,8},{4,12},{8,16},{12,20},{16,24},{20,28},{24,0},{28,4},{1,9},{5... | collective-permute-start | bytes 847880 | tf_op jit(solution)/shard_map/ppermute | solution.py:71
  13.5 25.5 %collective-permute-start.1 = (bf16[2,48,1472]{2,1,0:T(8,128)(2,1)}, bf16[2,48,1472]{2,1,0:T(8,128)(2,1)}, u32[]{:S(2)}, u32[]{:S(2)}) collective-permute-start(bf16[2,48,1472]{2,1,0:T(8,128)(2,1)} %pad_maximum_fusion.41), channel_id=1, source_target_pairs={{0,16},{4,20},{8,24},{12,28},{16,0},{20,4},{24,8},{28,12},{1,17},{... | collective-permute-start | bytes 847880 | tf_op jit(solution)/shard_map/ppermute | solution.py:71
  14.5 26.3 %collective-permute-start.2 = (bf16[2,48,1472]{2,1,0:T(8,128)(2,1)}, bf16[2,48,1472]{2,1,0:T(8,128)(2,1)}, u32[]{:S(2)}, u32[]{:S(2)}) collective-permute-start(bf16[2,48,1472]{2,1,0:T(8,128)(2,1)} %pad_maximum_fusion.41), channel_id=1, source_target_pairs={{0,24},{4,28},{8,0},{12,4},{16,8},{20,12},{24,16},{28,20},{1,25},{... | collective-permute-start | bytes 847880 | tf_op jit(solution)/shard_map/ppermute | solution.py:71
  18.2 22.6 %collective-permute-start.3 = (bf16[8,64,1472]{2,1,0:T(8,128)(2,1)S(1)}, bf16[8,64,1472]{2,1,0:T(8,128)(2,1)}, u32[]{:S(2)}, u32[]{:S(2)}) collective-permute-start(bf16[8,64,1472]{2,1,0:T(8,128)(2,1)S(1)} %bitcast.356), channel_id=1, source_target_pairs={{0,4},{4,0},{8,12},{12,8},{16,20},{20,16},{24,28},{28,24},{1,5},{5... | collective-permute-start | bytes 4521992 | tf_op jit(solution)/shard_map/ppermute | solution.py:48
  43.9 12.2 %collective-permute-start.5 = (bf16[1,3,48,1472]{3,2,1,0:T(8,128)(2,1)S(1)}, bf16[1,3,48,1472]{3,2,1,0:T(8,128)(2,1)S(1)}, u32[]{:S(2)}, u32[]{:S(2)}) collective-permute-start(bf16[1,3,48,1472]{3,2,1,0:T(8,128)(2,1)S(1)} %get-tuple-element.552), channel_id=1, source_target_pairs={{0,2},{1,3},{2,0},{3,1},{4,6},{5,7},{6,4},{7,5},{8,10},{9,11},{10,... | collective-permute-start | bytes 1271816 | tf_op jit(solution)/shard_map/ppermute | solution.py:62
  45.5 17.1 %collective-permute-start.6 = (bf16[2,112,1472]{2,1,0:T(8,128)(2,1)S(1)}, bf16[2,112,1472]{2,1,0:T(8,128)(2,1)S(1)}, u32[]{:S(2)}, u32[]{:S(2)}) collective-permute-start(bf16[2,112,1472]{2,1,0:T(8,128)(2,1)S(1)} %pad_maximum_fusion.19), channel_id=1, source_target_pairs={{0,8},{4,12},{8,16},{12,20},{16,24},{20,28},{24,0},{28,4},{1,9},{5... | collective-permute-start | bytes 1978376 | tf_op jit(solution)/shard_map/ppermute | solution.py:57
  46.3 11.8 %collective-permute-start.4 = (bf16[1,3,48,1472]{3,2,1,0:T(8,128)(2,1)S(1)}, bf16[1,3,48,1472]{3,2,1,0:T(8,128)(2,1)S(1)}, u32[]{:S(2)}, u32[]{:S(2)}) collective-permute-start(bf16[1,3,48,1472]{3,2,1,0:T(8,128)(2,1)S(1)} %get-tuple-element.554), channel_id=1, source_target_pairs={{0,1},{1,0},{2,3},{3,2},{4,5},{5,4},{6,7},{7,6},{8,9},{9,8},{10,11... | collective-permute-start | bytes 1271816 | tf_op jit(solution)/shard_map/ppermute | solution.py:62
  63.6 23.8 %collective-permute-start.8 = (bf16[2,3,48,1472]{3,2,1,0:T(8,128)(2,1)}, bf16[2,3,48,1472]{3,2,1,0:T(8,128)(2,1)}, u32[]{:S(2)}, u32[]{:S(2)}) collective-permute-start(bf16[2,3,48,1472]{3,2,1,0:T(8,128)(2,1)} %pad_maximum_fusion.18), channel_id=1, source_target_pairs={{0,1},{1,0},{2,3},{3,2},{4,5},{5,4},{6,7},{7,6},{8,9},{9,8},{10,11... | collective-permute-start | bytes 2543624 | tf_op jit(solution)/shard_map/ppermute | solution.py:62
  66.1 21.3 %collective-permute-start.7 = (bf16[2,3,48,1472]{3,2,1,0:T(8,128)(2,1)}, bf16[2,3,48,1472]{3,2,1,0:T(8,128)(2,1)}, u32[]{:S(2)}, u32[]{:S(2)}) collective-permute-start(bf16[2,3,48,1472]{3,2,1,0:T(8,128)(2,1)} %pad_maximum_fusion.17), channel_id=1, source_target_pairs={{0,2},{1,3},{2,0},{3,1},{4,6},{5,7},{6,4},{7,5},{8,10},{9,11},{10,... | collective-permute-start | bytes 2543624 | tf_op jit(solution)/shard_map/ppermute | solution.py:62
  71.5 16.0 %collective-permute-start.9 = (bf16[2,112,1472]{2,1,0:T(8,128)(2,1)}, bf16[2,112,1472]{2,1,0:T(8,128)(2,1)}, u32[]{:S(2)}, u32[]{:S(2)}) collective-permute-start(bf16[2,112,1472]{2,1,0:T(8,128)(2,1)} %copy-done.57), channel_id=1, source_target_pairs={{0,8},{4,12},{8,16},{12,20},{16,24},{20,28},{24,0},{28,4},{1,9},{5... | collective-permute-start | bytes 1978376 | tf_op jit(solution)/shard_map/ppermute | solution.py:57
  89.1 21.2 %collective-permute-start.10 = (bf16[4,4,48,1472]{3,2,0,1:T(8,128)(2,1)S(1)}, bf16[4,4,48,1472]{3,2,0,1:T(8,128)(2,1)S(1)}, u32[]{:S(2)}, u32[]{:S(2)}) collective-permute-start(bf16[4,4,48,1472]{3,2,0,1:T(8,128)(2,1)S(1)} %maximum_maximum_fusion), channel_id=1, source_target_pairs={{0,4},{4,0},{8,12},{12,8},{16,20},{20,16},{24,28},{28,24},{1,5},{5... | collective-permute-start | bytes 6782984 | tf_op jit(solution)/shard_map/ppermute | solution.py:48
  90.0 20.2 %collective-permute-start.13 = (bf16[2,112,1472]{2,1,0:T(8,128)(2,1)}, bf16[2,112,1472]{2,1,0:T(8,128)(2,1)S(1)}, u32[]{:S(2)}, u32[]{:S(2)}) collective-permute-start(bf16[2,112,1472]{2,1,0:T(8,128)(2,1)} %collective-permute-done.9), channel_id=1, source_target_pairs={{0,8},{4,12},{8,16},{12,20},{16,24},{20,28},{24,0},{28,4},{1,9},{5... | collective-permute-start | bytes 1978376 | tf_op jit(solution)/shard_map/ppermute | solution.py:57
  91.8 17.0 %collective-permute-start.12 = (bf16[1,2,112,1472]{3,2,1,0:T(8,128)(2,1)S(1)}, bf16[1,2,112,1472]{3,2,1,0:T(8,128)(2,1)S(1)}, u32[]{:S(2)}, u32[]{:S(2)}) collective-permute-start(bf16[1,2,112,1472]{3,2,1,0:T(8,128)(2,1)S(1)} %maximum_bitcast_fusion.1), channel_id=1, source_target_pairs={{0,2},{1,3},{2,0},{3,1},{4,6},{5,7},{6,4},{7,5},{8,10},{9,11},{10,... | collective-permute-start | bytes 1978376 | tf_op jit(solution)/shard_map/ppermute | solution.py:62
  93.5 16.7 %collective-permute-start.11 = (bf16[1,2,112,1472]{3,2,1,0:T(8,128)(2,1)S(1)}, bf16[1,2,112,1472]{3,2,1,0:T(8,128)(2,1)S(1)}, u32[]{:S(2)}, u32[]{:S(2)}) collective-permute-start(bf16[1,2,112,1472]{3,2,1,0:T(8,128)(2,1)S(1)} %maximum_bitcast_fusion), channel_id=1, source_target_pairs={{0,1},{1,0},{2,3},{3,2},{4,5},{5,4},{6,7},{7,6},{8,9},{9,8},{10,11... | collective-permute-start | bytes 1978376 | tf_op jit(solution)/shard_map/ppermute | solution.py:62
  110.4 13.6 %collective-permute-start.14 = (bf16[4,4,48,1472]{3,2,1,0:T(8,128)(2,1)S(1)}, bf16[4,4,48,1472]{3,2,1,0:T(8,128)(2,1)S(1)}, u32[]{:S(2)}, u32[]{:S(2)}) collective-permute-start(bf16[4,4,48,1472]{3,2,1,0:T(8,128)(2,1)S(1)} %maximum_maximum_fusion.1.own), channel_id=1, source_target_pairs={{0,4},{4,0},{8,12},{12,8},{16,20},{20,16},{24,28},{28,24},{1,5},{5... | collective-permute-start | bytes 6782984 | tf_op jit(solution)/shard_map/ppermute | solution.py:48
  110.6 13.4 %collective-permute-start.15 = (bf16[1,112,1472]{2,1,0:T(8,128)(2,1)S(1)}, bf16[1,112,1472]{2,1,0:T(8,128)(2,1)S(1)}, u32[]{:S(2)}, u32[]{:S(2)}) collective-permute-start(bf16[1,112,1472]{2,1,0:T(8,128)(2,1)S(1)} %get-tuple-element.514), channel_id=1, source_target_pairs={{0,1},{1,0},{2,3},{3,2},{4,5},{5,4},{6,7},{7,6},{8,9},{9,8},{10,11... | collective-permute-start | bytes 989192 | tf_op jit(solution)/shard_map/ppermute | solution.py:62
  111.2 12.8 %collective-permute-start.16 = (bf16[1,112,1472]{2,1,0:T(8,128)(2,1)S(1)}, bf16[1,112,1472]{2,1,0:T(8,128)(2,1)S(1)}, u32[]{:S(2)}, u32[]{:S(2)}) collective-permute-start(bf16[1,112,1472]{2,1,0:T(8,128)(2,1)S(1)} %get-tuple-element.513), channel_id=1, source_target_pairs={{0,2},{1,3},{2,0},{3,1},{4,6},{5,7},{6,4},{7,5},{8,10},{9,11},{10,... | collective-permute-start | bytes 989192 | tf_op jit(solution)/shard_map/ppermute | solution.py:62
  123.8 44.1 %copy-start.24 = (bf16[2,2,112,1472]{3,2,1,0:T(8,128)(2,1)}, bf16[2,2,112,1472]{3,2,1,0:T(8,128)(2,1)S(1)}, u32[]{:S(2)}) copy-start(bf16[2,2,112,1472]{3,2,1,0:T(8,128)(2,1)S(1)} %pad_maximum_fusion.9.refs_6_.refs_2_) | copy-start | bytes 3956740
  128.7 22.3 %collective-permute-start.17 = (bf16[2,256,768]{2,1,0:T(8,128)(2,1)S(1)}, bf16[2,256,768]{2,1,0:T(8,128)(2,1)}, u32[]{:S(2)}, u32[]{:S(2)}) collective-permute-start(bf16[2,256,768]{2,1,0:T(8,128)(2,1)S(1)} %get-tuple-element.451), channel_id=1, source_target_pairs={{0,1},{1,0},{2,3},{3,2},{4,5},{5,4},{6,7},{7,6},{8,9},{9,8},{10,11... | collective-permute-start | bytes 2359304 | tf_op jit(solution)/shard_map/ppermute | solution.py:62
  130.2 36.0 %collective-permute-start.18 = (bf16[2,256,768]{2,1,0:T(8,128)(2,1)S(1)}, bf16[2,256,768]{2,1,0:T(8,128)(2,1)}, u32[]{:S(2)}, u32[]{:S(2)}) collective-permute-start(bf16[2,256,768]{2,1,0:T(8,128)(2,1)S(1)} %get-tuple-element.450), channel_id=1, source_target_pairs={{0,2},{1,3},{2,0},{3,1},{4,6},{5,7},{6,4},{7,5},{8,10},{9,11},{10,... | collective-permute-start | bytes 2359304 | tf_op jit(solution)/shard_map/ppermute | solution.py:62
  131.7 34.5 %collective-permute-start.19 = (bf16[2,256,768]{2,1,0:T(8,128)(2,1)S(1)}, bf16[2,256,768]{2,1,0:T(8,128)(2,1)}, u32[]{:S(2)}, u32[]{:S(2)}) collective-permute-start(bf16[2,256,768]{2,1,0:T(8,128)(2,1)S(1)} %get-tuple-element.449), channel_id=1, source_target_pairs={{0,3},{1,2},{2,1},{3,0},{4,7},{5,6},{6,5},{7,4},{8,11},{9,10},{10,... | collective-permute-start | bytes 2359304 | tf_op jit(solution)/shard_map/ppermute | solution.py:62
  132.2 34.1 %collective-permute-start.20 = (bf16[4,112,1472]{2,1,0:T(8,128)(2,1)S(1)}, bf16[4,112,1472]{2,1,0:T(8,128)(2,1)}, u32[]{:S(2)}, u32[]{:S(2)}) collective-permute-start(bf16[4,112,1472]{2,1,0:T(8,128)(2,1)S(1)} %copy-done.21), channel_id=1, source_target_pairs={{0,8},{4,12},{8,16},{12,20},{16,24},{20,28},{24,0},{28,4},{1,9},{5... | collective-permute-start | bytes 3956744 | tf_op jit(solution)/shard_map/ppermute | solution.py:57
  166.3 30.9 %collective-permute-start.21 = (bf16[2,2,112,1472]{3,2,1,0:T(8,128)(2,1)S(1)}, bf16[2,2,112,1472]{3,2,1,0:T(8,128)(2,1)S(1)}, u32[]{:S(2)}, u32[]{:S(2)}) collective-permute-start(bf16[2,2,112,1472]{3,2,1,0:T(8,128)(2,1)S(1)} %pad_maximum_fusion.8.refs_4_.refs_0_), channel_id=1, source_target_pairs={{0,2},{1,3},{2,0},{3,1},{4,6},{5,7},{6,4},{7,5},{8,10},{9,11},{10,... | collective-permute-start | bytes 3956744 | tf_op jit(solution)/shard_map/ppermute | solution.py:62
  167.9 29.6 %collective-permute-start.22 = (bf16[2,2,112,1472]{3,2,1,0:T(8,128)(2,1)S(1)}, bf16[2,2,112,1472]{3,2,1,0:T(8,128)(2,1)S(1)}, u32[]{:S(2)}, u32[]{:S(2)}) collective-permute-start(bf16[2,2,112,1472]{3,2,1,0:T(8,128)(2,1)S(1)} %pad_maximum_fusion.9.refs_6_.refs_2_), channel_id=1, source_target_pairs={{0,1},{1,0},{2,3},{3,2},{4,5},{5,4},{6,7},{7,6},{8,9},{9,8},{10,11... | collective-permute-start | bytes 3956744 | tf_op jit(solution)/shard_map/ppermute | solution.py:62
  168.4 30.6 %collective-permute-start.23 = (bf16[4,112,1472]{2,1,0:T(8,128)(2,1)}, bf16[4,112,1472]{2,1,0:T(8,128)(2,1)}, u32[]{:S(2)}, u32[]{:S(2)}) collective-permute-start(bf16[4,112,1472]{2,1,0:T(8,128)(2,1)} %collective-permute-done.20), channel_id=1, source_target_pairs={{0,8},{4,12},{8,16},{12,20},{16,24},{20,28},{24,0},{28,4},{1,9},{5... | collective-permute-start | bytes 3956744 | tf_op jit(solution)/shard_map/ppermute | solution.py:57
  199.0 6.1 collective-permute-start.24
  201.7 41.4 %collective-permute-start.27 = (bf16[4,112,1472]{2,1,0:T(8,128)(2,1)}, bf16[4,112,1472]{2,1,0:T(8,128)(2,1)}, u32[]{:S(2)}, u32[]{:S(2)}) collective-permute-start(bf16[4,112,1472]{2,1,0:T(8,128)(2,1)} %collective-permute-done.23), channel_id=1, source_target_pairs={{0,8},{4,12},{8,16},{12,20},{16,24},{20,28},{24,0},{28,4},{1,9},{5... | collective-permute-start | bytes 3956744 | tf_op jit(solution)/shard_map/ppermute | solution.py:57
  203.0 40.0 %collective-permute-start.25 = (bf16[2,112,1472]{2,1,0:T(8,128)(2,1)S(1)}, bf16[2,112,1472]{2,1,0:T(8,128)(2,1)S(1)}, u32[]{:S(2)}, u32[]{:S(2)}) collective-permute-start(bf16[2,112,1472]{2,1,0:T(8,128)(2,1)S(1)} %copy-done.60), channel_id=1, source_target_pairs={{0,2},{1,3},{2,0},{3,1},{4,6},{5,7},{6,4},{7,5},{8,10},{9,11},{10,... | collective-permute-start | bytes 1978376 | tf_op jit(solution)/shard_map/ppermute | solution.py:62
  204.5 38.5 %collective-permute-start.26 = (bf16[2,112,1472]{2,1,0:T(8,128)(2,1)S(1)}, bf16[2,112,1472]{2,1,0:T(8,128)(2,1)}, u32[]{:S(2)}, u32[]{:S(2)}) collective-permute-start(bf16[2,112,1472]{2,1,0:T(8,128)(2,1)S(1)} %copy-done.59), channel_id=1, source_target_pairs={{0,1},{1,0},{2,3},{3,2},{4,5},{5,4},{6,7},{7,6},{8,9},{9,8},{10,11... | collective-permute-start | bytes 1978376 | tf_op jit(solution)/shard_map/ppermute | solution.py:62
  248.6 57.8 %collective-permute-start.29 = (bf16[3,2,112,1472]{3,2,0,1:T(8,128)(2,1)}, bf16[3,2,112,1472]{3,2,0,1:T(8,128)(2,1)}, u32[]{:S(2)}, u32[]{:S(2)}) collective-permute-start(bf16[3,2,112,1472]{3,2,0,1:T(8,128)(2,1)} %pad_maximum_fusion.3), channel_id=1, source_target_pairs={{0,1},{1,0},{2,3},{3,2},{4,5},{5,4},{6,7},{7,6},{8,9},{9,8},{10,11... | collective-permute-start | bytes 5935112 | tf_op jit(solution)/shard_map/ppermute | solution.py:62
  251.8 54.6 %collective-permute-start.28 = (bf16[3,2,112,1472]{3,2,0,1:T(8,128)(2,1)}, bf16[3,2,112,1472]{3,2,0,1:T(8,128)(2,1)}, u32[]{:S(2)}, u32[]{:S(2)}) collective-permute-start(bf16[3,2,112,1472]{3,2,0,1:T(8,128)(2,1)} %copy.163), channel_id=1, source_target_pairs={{0,2},{1,3},{2,0},{3,1},{4,6},{5,7},{6,4},{7,5},{8,10},{9,11},{10,... | collective-permute-start | bytes 5935112 | tf_op jit(solution)/shard_map/ppermute | solution.py:62
  254.5 51.9 %collective-permute-start.30 = (bf16[448,1472]{1,0:T(8,128)(2,1)}, bf16[448,1472]{1,0:T(8,128)(2,1)}, u32[]{:S(2)}, u32[]{:S(2)}) collective-permute-start(bf16[448,1472]{1,0:T(8,128)(2,1)} %get-tuple-element.442), channel_id=1, source_target_pairs={{0,8},{4,12},{8,16},{12,20},{16,24},{20,28},{24,0},{28,4},{1,9},{5... | collective-permute-start | bytes 3956744 | tf_op jit(solution)/shard_map/ppermute | solution.py:57
  306.4 15.4 %collective-permute-start.34 = (bf16[8,64,1472]{2,1,0:T(8,128)(2,1)}, bf16[8,64,1472]{2,1,0:T(8,128)(2,1)}, u32[]{:S(2)}, u32[]{:S(2)}) collective-permute-start(bf16[8,64,1472]{2,1,0:T(8,128)(2,1)} %bitcast.416), channel_id=1, source_target_pairs={{0,4},{4,0},{8,12},{12,8},{16,20},{20,16},{24,28},{28,24},{1,5},{5... | collective-permute-start | bytes 4521992 | tf_op jit(solution)/shard_map/ppermute | solution.py:48
  309.7 55.2 %collective-permute-start.33 = (bf16[448,1472]{1,0:T(8,128)(2,1)}, bf16[448,1472]{1,0:T(8,128)(2,1)}, u32[]{:S(2)}, u32[]{:S(2)}) collective-permute-start(bf16[448,1472]{1,0:T(8,128)(2,1)} %fusion.7), channel_id=1, source_target_pairs={{0,8},{4,12},{8,16},{12,20},{16,24},{20,28},{24,0},{28,4},{1,9},{5... | collective-permute-start | bytes 3956744 | tf_op jit(solution)/shard_map/ppermute | solution.py:57
  315.8 39.8 %collective-permute-start.32 = (bf16[5,112,1472]{2,1,0:T(8,128)(2,1)S(1)}, bf16[5,112,1472]{2,1,0:T(8,128)(2,1)}, u32[]{:S(2)}, u32[]{:S(2)}) collective-permute-start(bf16[5,112,1472]{2,1,0:T(8,128)(2,1)S(1)} %pad_maximum_fusion.6), channel_id=1, source_target_pairs={{0,1},{1,0},{2,3},{3,2},{4,5},{5,4},{6,7},{7,6},{8,9},{9,8},{10,11... | collective-permute-start | bytes 4945928 | tf_op jit(solution)/shard_map/ppermute | solution.py:62
  321.2 39.9 %collective-permute-start.31 = (bf16[5,112,1472]{2,1,0:T(8,128)(2,1)}, bf16[5,112,1472]{2,1,0:T(8,128)(2,1)}, u32[]{:S(2)}, u32[]{:S(2)}) collective-permute-start(bf16[5,112,1472]{2,1,0:T(8,128)(2,1)} %pad_maximum_fusion.5), channel_id=1, source_target_pairs={{0,2},{1,3},{2,0},{3,1},{4,6},{5,7},{6,4},{7,5},{8,10},{9,11},{10,... | collective-permute-start | bytes 4945928 | tf_op jit(solution)/shard_map/ppermute | solution.py:62
  371.3 46.5 %collective-permute-start.38 = (bf16[6,112,1472]{2,1,0:T(8,128)(2,1)}, bf16[6,112,1472]{2,1,0:T(8,128)(2,1)}, u32[]{:S(2)}, u32[]{:S(2)}) collective-permute-start(bf16[6,112,1472]{2,1,0:T(8,128)(2,1)} %pad_maximum_fusion.4), channel_id=1, source_target_pairs={{0,8},{4,12},{8,16},{12,20},{16,24},{20,28},{24,0},{28,4},{1,9},{5... | collective-permute-start | bytes 5935112 | tf_op jit(solution)/shard_map/ppermute | solution.py:57
  371.5 38.2 %collective-permute-start.39 = (bf16[8,64,1472]{2,1,0:T(8,128)(2,1)}, bf16[8,64,1472]{2,1,0:T(8,128)(2,1)S(1)}, u32[]{:S(2)}, u32[]{:S(2)}) collective-permute-start(bf16[8,64,1472]{2,1,0:T(8,128)(2,1)} %bitcast.412), channel_id=1, source_target_pairs={{0,4},{4,0},{8,12},{12,8},{16,20},{20,16},{24,28},{28,24},{1,5},{5... | collective-permute-start | bytes 4521992 | tf_op jit(solution)/shard_map/ppermute | solution.py:48
  371.6 24.3 %collective-permute-start.35 = (bf16[2,256,768]{2,1,0:T(8,128)(2,1)}, bf16[2,256,768]{2,1,0:T(8,128)(2,1)S(1)}, u32[]{:S(2)}, u32[]{:S(2)}) collective-permute-start(bf16[2,256,768]{2,1,0:T(8,128)(2,1)} %get-tuple-element.264), channel_id=1, source_target_pairs={{0,1},{1,0},{2,3},{3,2},{4,5},{5,4},{6,7},{7,6},{8,9},{9,8},{10,11... | collective-permute-start | bytes 2359304 | tf_op jit(solution)/shard_map/ppermute | solution.py:62
  373.0 36.7 %collective-permute-start.36 = (bf16[2,256,768]{2,1,0:T(8,128)(2,1)}, bf16[2,256,768]{2,1,0:T(8,128)(2,1)S(1)}, u32[]{:S(2)}, u32[]{:S(2)}) collective-permute-start(bf16[2,256,768]{2,1,0:T(8,128)(2,1)} %get-tuple-element.265), channel_id=1, source_target_pairs={{0,2},{1,3},{2,0},{3,1},{4,6},{5,7},{6,4},{7,5},{8,10},{9,11},{10,... | collective-permute-start | bytes 2359304 | tf_op jit(solution)/shard_map/ppermute | solution.py:62
  373.5 36.2 %collective-permute-start.37 = (bf16[2,256,768]{2,1,0:T(8,128)(2,1)}, bf16[2,256,768]{2,1,0:T(8,128)(2,1)}, u32[]{:S(2)}, u32[]{:S(2)}) collective-permute-start(bf16[2,256,768]{2,1,0:T(8,128)(2,1)} %get-tuple-element.266), channel_id=1, source_target_pairs={{0,3},{1,2},{2,1},{3,0},{4,7},{5,6},{6,5},{7,4},{8,11},{9,10},{10,... | collective-permute-start | bytes 2359304 | tf_op jit(solution)/shard_map/ppermute | solution.py:62
  418.7 30.3 %collective-permute-start.43 = (bf16[1,1,112,1472]{3,2,1,0:T(8,128)(2,1)}, bf16[1,1,112,1472]{3,2,1,0:T(8,128)(2,1)S(1)}, u32[]{:S(2)}, u32[]{:S(2)}) collective-permute-start(bf16[1,1,112,1472]{3,2,1,0:T(8,128)(2,1)} %slice.591), channel_id=1, source_target_pairs={{0,2},{1,3},{2,0},{3,1},{4,6},{5,7},{6,4},{7,5},{8,10},{9,11},{10,... | collective-permute-start | bytes 989192 | tf_op jit(solution)/shard_map/ppermute | solution.py:62
  420.2 28.8 %collective-permute-start.42 = (bf16[1,1,112,1472]{3,2,1,0:T(8,128)(2,1)}, bf16[1,1,112,1472]{3,2,1,0:T(8,128)(2,1)}, u32[]{:S(2)}, u32[]{:S(2)}) collective-permute-start(bf16[1,1,112,1472]{3,2,1,0:T(8,128)(2,1)} %slice.588), channel_id=1, source_target_pairs={{0,1},{1,0},{2,3},{3,2},{4,5},{5,4},{6,7},{7,6},{8,9},{9,8},{10,11... | collective-permute-start | bytes 989192 | tf_op jit(solution)/shard_map/ppermute | solution.py:62
  425.5 23.6 %collective-permute-start.40 = (bf16[4,4,48,1472]{3,2,0,1:T(8,128)(2,1)S(1)}, bf16[4,4,48,1472]{3,2,0,1:T(8,128)(2,1)S(1)}, u32[]{:S(2)}, u32[]{:S(2)}) collective-permute-start(bf16[4,4,48,1472]{3,2,0,1:T(8,128)(2,1)S(1)} %dynamic-slice_bitcast_fusion), channel_id=1, source_target_pairs={{0,4},{4,0},{8,12},{12,8},{16,20},{20,16},{24,28},{28,24},{1,5},{5... | collective-permute-start | bytes 6782984 | tf_op jit(solution)/shard_map/ppermute | solution.py:48
  427.8 21.3 %collective-permute-start.41 = (bf16[2,112,1472]{2,1,0:T(8,128)(2,1)}, bf16[2,112,1472]{2,1,0:T(8,128)(2,1)S(1)}, u32[]{:S(2)}, u32[]{:S(2)}) collective-permute-start(bf16[2,112,1472]{2,1,0:T(8,128)(2,1)} %add_convert_fusion.6), channel_id=1, source_target_pairs={{0,8},{4,12},{8,16},{12,20},{16,24},{20,28},{24,0},{28,4},{1,9},{5... | collective-permute-start | bytes 1978376 | tf_op jit(solution)/shard_map/ppermute | solution.py:57
  473.2 46.1 %collective-permute-start.46 = (bf16[320,1472]{1,0:T(8,128)(2,1)}, bf16[320,1472]{1,0:T(8,128)(2,1)}, u32[]{:S(2)}, u32[]{:S(2)}) collective-permute-start(bf16[320,1472]{1,0:T(8,128)(2,1)} %concatenate.104), channel_id=1, source_target_pairs={{0,3},{1,2},{2,1},{3,0},{4,7},{5,6},{6,5},{7,4},{8,11},{9,10},{10,... | collective-permute-start | bytes 2826248 | tf_op jit(solution)/shard_map/ppermute | solution.py:62
  480.8 38.5 %collective-permute-start.45 = (bf16[320,1472]{1,0:T(8,128)(2,1)}, bf16[320,1472]{1,0:T(8,128)(2,1)}, u32[]{:S(2)}, u32[]{:S(2)}) collective-permute-start(bf16[320,1472]{1,0:T(8,128)(2,1)} %concatenate.103), channel_id=1, source_target_pairs={{0,2},{1,3},{2,0},{3,1},{4,6},{5,7},{6,4},{7,5},{8,10},{9,11},{10,... | collective-permute-start | bytes 2826248 | tf_op jit(solution)/shard_map/ppermute | solution.py:62
  486.0 33.3 %collective-permute-start.44 = (bf16[320,1472]{1,0:T(8,128)(2,1)}, bf16[320,1472]{1,0:T(8,128)(2,1)}, u32[]{:S(2)}, u32[]{:S(2)}) collective-permute-start(bf16[320,1472]{1,0:T(8,128)(2,1)} %concatenate.102), channel_id=1, source_target_pairs={{0,1},{1,0},{2,3},{3,2},{4,5},{5,4},{6,7},{7,6},{8,9},{9,8},{10,11... | collective-permute-start | bytes 2826248 | tf_op jit(solution)/shard_map/ppermute | solution.py:62
  489.6 29.7 %collective-permute-start.47 = (bf16[2,112,1472]{2,1,0:T(8,128)(2,1)}, bf16[2,112,1472]{2,1,0:T(8,128)(2,1)}, u32[]{:S(2)}, u32[]{:S(2)}) collective-permute-start(bf16[2,112,1472]{2,1,0:T(8,128)(2,1)} %add_convert_fusion.3), channel_id=1, source_target_pairs={{0,8},{4,12},{8,16},{12,20},{16,24},{20,28},{24,0},{28,4},{1,9},{5... | collective-permute-start | bytes 1978376 | tf_op jit(solution)/shard_map/ppermute | solution.py:57
  520.7 27.4 %collective-permute-start.51 = (bf16[1,112,1472]{2,1,0:T(8,128)(2,1)S(1)}, bf16[1,112,1472]{2,1,0:T(8,128)(2,1)S(1)}, u32[]{:S(2)}, u32[]{:S(2)}) collective-permute-start(bf16[1,112,1472]{2,1,0:T(8,128)(2,1)S(1)} %get-tuple-element.313), channel_id=1, source_target_pairs={{0,1},{1,0},{2,3},{3,2},{4,5},{5,4},{6,7},{7,6},{8,9},{9,8},{10,11... | collective-permute-start | bytes 989192 | tf_op jit(solution)/shard_map/ppermute | solution.py:62
  522.4 26.3 %collective-permute-start.52 = (bf16[1,112,1472]{2,1,0:T(8,128)(2,1)S(1)}, bf16[1,112,1472]{2,1,0:T(8,128)(2,1)S(1)}, u32[]{:S(2)}, u32[]{:S(2)}) collective-permute-start(bf16[1,112,1472]{2,1,0:T(8,128)(2,1)S(1)} %get-tuple-element.315), channel_id=1, source_target_pairs={{0,2},{1,3},{2,0},{3,1},{4,6},{5,7},{6,4},{7,5},{8,10},{9,11},{10,... | collective-permute-start | bytes 989192 | tf_op jit(solution)/shard_map/ppermute | solution.py:62
  526.7 9.2 %collective-permute-start.48 = (bf16[64,1472]{1,0:T(8,128)(2,1)S(1)}, bf16[64,1472]{1,0:T(8,128)(2,1)S(1)}, u32[]{:S(2)}, u32[]{:S(2)}) collective-permute-start(bf16[64,1472]{1,0:T(8,128)(2,1)S(1)} %get-tuple-element.562), channel_id=1, source_target_pairs={{0,8},{4,12},{8,16},{12,20},{16,24},{20,28},{24,0},{28,4},{1,9},{5... | collective-permute-start | bytes 565256 | tf_op jit(solution)/shard_map/ppermute | solution.py:71
  528.3 16.2 %collective-permute-start.49 = (bf16[64,1472]{1,0:T(8,128)(2,1)S(1)}, bf16[64,1472]{1,0:T(8,128)(2,1)S(1)}, u32[]{:S(2)}, u32[]{:S(2)}) collective-permute-start(bf16[64,1472]{1,0:T(8,128)(2,1)S(1)} %get-tuple-element.563), channel_id=1, source_target_pairs={{0,16},{4,20},{8,24},{12,28},{16,0},{20,4},{24,8},{28,12},{1,17},{... | collective-permute-start | bytes 565256 | tf_op jit(solution)/shard_map/ppermute | solution.py:71
  532.5 15.6 %collective-permute-start.50 = (bf16[64,1472]{1,0:T(8,128)(2,1)S(1)}, bf16[64,1472]{1,0:T(8,128)(2,1)S(1)}, u32[]{:S(2)}, u32[]{:S(2)}) collective-permute-start(bf16[64,1472]{1,0:T(8,128)(2,1)S(1)} %get-tuple-element.561), channel_id=1, source_target_pairs={{0,24},{4,28},{8,0},{12,4},{16,8},{20,12},{24,16},{28,20},{1,25},{... | collective-permute-start | bytes 565256 | tf_op jit(solution)/shard_map/ppermute | solution.py:71
  550.6 23.2 %collective-permute-start.54 = (bf16[2,112,1472]{2,1,0:T(8,128)(2,1)S(1)}, bf16[2,112,1472]{2,1,0:T(8,128)(2,1)S(1)}, u32[]{:S(2)}, u32[]{:S(2)}) collective-permute-start(bf16[2,112,1472]{2,1,0:T(8,128)(2,1)S(1)} %constant_dynamic-update-slice_fusion.2), channel_id=1, source_target_pairs={{0,1},{1,0},{2,3},{3,2},{4,5},{5,4},{6,7},{7,6},{8,9},{9,8},{10,11... | collective-permute-start | bytes 1978376 | tf_op jit(solution)/shard_map/ppermute | solution.py:62
  551.2 22.6 %collective-permute-start.53 = (bf16[2,112,1472]{2,1,0:T(8,128)(2,1)S(1)}, bf16[2,112,1472]{2,1,0:T(8,128)(2,1)S(1)}, u32[]{:S(2)}, u32[]{:S(2)}) collective-permute-start(bf16[2,112,1472]{2,1,0:T(8,128)(2,1)S(1)} %constant_dynamic-update-slice_fusion), channel_id=1, source_target_pairs={{0,2},{1,3},{2,0},{3,1},{4,6},{5,7},{6,4},{7,5},{8,10},{9,11},{10,... | collective-permute-start | bytes 1978376 | tf_op jit(solution)/shard_map/ppermute | solution.py:62
  551.9 20.0 %collective-permute-start.55 = (bf16[48,1472]{1,0:T(8,128)(2,1)S(1)}, bf16[48,1472]{1,0:T(8,128)(2,1)S(1)}, u32[]{:S(2)}, u32[]{:S(2)}) collective-permute-start(bf16[48,1472]{1,0:T(8,128)(2,1)S(1)} %get-tuple-element.537), channel_id=1, source_target_pairs={{0,1},{1,0},{2,3},{3,2},{4,5},{5,4},{6,7},{7,6},{8,9},{9,8},{10,11... | collective-permute-start | bytes 423944 | tf_op jit(solution)/shard_map/ppermute | solution.py:62
  553.4 20.4 %collective-permute-start.56 = (bf16[48,1472]{1,0:T(8,128)(2,1)S(1)}, bf16[48,1472]{1,0:T(8,128)(2,1)S(1)}, u32[]{:S(2)}, u32[]{:S(2)}) collective-permute-start(bf16[48,1472]{1,0:T(8,128)(2,1)S(1)} %get-tuple-element.536), channel_id=1, source_target_pairs={{0,2},{1,3},{2,0},{3,1},{4,6},{5,7},{6,4},{7,5},{8,10},{9,11},{10,... | collective-permute-start | bytes 423944 | tf_op jit(solution)/shard_map/ppermute | solution.py:62
  554.9 18.9 %collective-permute-start.57 = (bf16[48,1472]{1,0:T(8,128)(2,1)S(1)}, bf16[48,1472]{1,0:T(8,128)(2,1)S(1)}, u32[]{:S(2)}, u32[]{:S(2)}) collective-permute-start(bf16[48,1472]{1,0:T(8,128)(2,1)S(1)} %get-tuple-element.535), channel_id=1, source_target_pairs={{0,3},{1,2},{2,1},{3,0},{4,7},{5,6},{6,5},{7,4},{8,11},{9,10},{10,... | collective-permute-start | bytes 423944 | tf_op jit(solution)/shard_map/ppermute | solution.py:62
  574.0 17.4 %collective-permute-start.59 = (bf16[208,1472]{1,0:T(8,128)(2,1)S(1)}, bf16[208,1472]{1,0:T(8,128)(2,1)S(1)}, u32[]{:S(2)}, u32[]{:S(2)}) collective-permute-start(bf16[208,1472]{1,0:T(8,128)(2,1)S(1)} %pad_maximum_fusion.22), channel_id=1, source_target_pairs={{0,1},{1,0},{2,3},{3,2},{4,5},{5,4},{6,7},{7,6},{8,9},{9,8},{10,11... | collective-permute-start | bytes 1837064 | tf_op jit(solution)/shard_map/ppermute | solution.py:62
  575.5 15.8 %collective-permute-start.60 = (bf16[208,1472]{1,0:T(8,128)(2,1)S(1)}, bf16[208,1472]{1,0:T(8,128)(2,1)S(1)}, u32[]{:S(2)}, u32[]{:S(2)}) collective-permute-start(bf16[208,1472]{1,0:T(8,128)(2,1)S(1)} %pad_maximum_fusion.22), channel_id=1, source_target_pairs={{0,2},{1,3},{2,0},{3,1},{4,6},{5,7},{6,4},{7,5},{8,10},{9,11},{10,... | collective-permute-start | bytes 1837064 | tf_op jit(solution)/shard_map/ppermute | solution.py:62
  576.1 26.4 %collective-permute-start.61 = (bf16[208,1472]{1,0:T(8,128)(2,1)S(1)}, bf16[208,1472]{1,0:T(8,128)(2,1)S(1)}, u32[]{:S(2)}, u32[]{:S(2)}) collective-permute-start(bf16[208,1472]{1,0:T(8,128)(2,1)S(1)} %pad_maximum_fusion.22), channel_id=1, source_target_pairs={{0,3},{1,2},{2,1},{3,0},{4,7},{5,6},{6,5},{7,4},{8,11},{9,10},{10,... | collective-permute-start | bytes 1837064 | tf_op jit(solution)/shard_map/ppermute | solution.py:62
  580.3 2.2 collective-permute-start.58
  (84 other events, 599.1 us)
Sparse Core Ops, SparseCore 0:
  452.4 64.1 reduce-scatter.1

commit v3 on v2

--- a/solution.py
+++ b/solution.py
@@ -139,31 +139,28 @@
     return natural(pieces, mem_index).astype(f32)
 
 
-def assemble_kernel(spot, own, other, out):
+def assemble_kernel(spot, own, other, *outs):
     chips = own.shape[0]
     core, chip = spot[0], spot[1]
-    for j in range(chips):
-        at = lax.rem(chip - j + chips, chips) * 2
-        out[0, at + core] = own[j, 0]
-        out[0, at + 1 - core] = other[j, 0]
+    for q, out in enumerate(outs):
+        for j in range(chips):
+            at = lax.rem(chip - j + chips, chips) * 2
+            out[at + core] = own[j, spot[2 + q]]
+            out[at + 1 - core] = other[j, spot[2 + q]]
 
 
 def assemble(spot, own, other):
     chips, mems, share, width = own.shape
-    block = pl.BlockSpec((chips, 1, share, width), lambda q, spot: (0, spot[2 + q], 0, 0))
+    vmem = pl.BlockSpec(memory_space=pltpu.VMEM)
     return pl.pallas_call(
         assemble_kernel,
-        grid_spec=pltpu.PrefetchScalarGridSpec(
-            num_scalar_prefetch=1,
-            grid=(mems,),
-            in_specs=[block, block],
-            out_specs=pl.BlockSpec((1, 2 * chips, share, width), lambda q, spot: (q, 0, 0, 0)),
-        ),
-        out_shape=jax.ShapeDtypeStruct((mems, 2 * chips, share, width), bf16),
-        compiler_params=params(32),
+        in_specs=[pl.BlockSpec(memory_space=pltpu.SMEM), vmem, vmem],
+        out_shape=[jax.ShapeDtypeStruct((2 * chips, share, width), bf16)] * mems,
+        compiler_params=params(26),
         cost_estimate=cost(3),
         name="assemble",
     )(spot, own, other)
+
 
 def params(limit_mb=56):
     return pltpu.CompilerParams(vmem_limit_bytes=limit_mb * 1024 * 1024)
@@ -191,8 +188,10 @@
     return lax.broadcasted_iota(jnp.int32, (length, 128), 1) // depth
 
 
-def self_fwd_kernel(depth, length, tok, g1, qw, kw, vw, ow, bias, g2, cw, normed_o, q_o, k_o, v_o, mixed_o, first_o, nc_o, cq_o):
-    x = tok[...].astype(f32)
+def self_fwd_kernel(depth, length, tok, g1, qw, kw, vw, ow, bias, g2, cw, tok_o, normed_o, q_o, k_o, v_o, mixed_o, first_o, nc_o, cq_o):
+    for m in range(tok.shape[0]):
+        tok_o[m * length : (m + 1) * length] = tok[m].astype(f32).T.astype(bf16)
+    x = tok_o[...].astype(f32)
     normed = (x * row_norm(x) * g1[...]).astype(bf16)
     normed_o[...] = normed
     q_o[...] = contract_cols(normed, qw[...]).astype(bf16)
@@ -217,7 +216,7 @@
         return carry
 
     lax.fori_loop(0, x.shape[0] // length * groups, body, 0)
-    first = tok[...].astype(f32) + matmul(mixed_o[...], ow[...])
+    first = tok_o[...].astype(f32) + matmul(mixed_o[...], ow[...])
     first_o[...] = first
     nc = (first * row_norm(first) * g2[...]).astype(bf16)
     nc_o[...] = nc
@@ -225,13 +224,13 @@
 
 
 def self_fwd(depth, length, tok, g1, qw, kw, vw, ow, bias, g2, cw):
-    rows, width = tok.shape
+    rows, width = tok.shape[0] * tok.shape[2], tok.shape[1]
     inner = qw.shape[0]
     low, slim = jax.ShapeDtypeStruct((rows, width), bf16), jax.ShapeDtypeStruct((rows, inner), bf16)
     return pl.pallas_call(
         functools.partial(self_fwd_kernel, depth, length),
-        out_shape=(low, slim, slim, slim, slim, jax.ShapeDtypeStruct((rows, width), f32), low, slim),
-        compiler_params=params(),
+        out_shape=(low, low, slim, slim, slim, slim, jax.ShapeDtypeStruct((rows, width), f32), low, slim),
+        compiler_params=params(40),
         cost_estimate=cost(16),
         name="self_fwd",
     )(tok, g1, qw, kw, vw, ow, bias, g2, cw)
@@ -276,7 +275,7 @@
             jax.ShapeDtypeStruct((rows, width), f32),
             jax.ShapeDtypeStruct((rows, width), bf16),
         ),
-        compiler_params=params(),
+        compiler_params=params(36),
         cost_estimate=cost(15),
         name="cross_fwd",
     )(cq, mask, ow, first, g3, *kvs)
@@ -348,7 +347,7 @@
             gain,
         ),
         scratch_shapes=[pltpu.VMEM(cq.shape, bf16), pltpu.VMEM(cq.shape, bf16)],
-        compiler_params=params(),
+        compiler_params=params(50),
         cost_estimate=cost(31),
         name="cross_bwd",
     )(og, nf_own, nf_more, second, g3, mixed, cq, mask, ow, first, g2, nc, qw, *kvs)
@@ -415,19 +414,23 @@
             jax.ShapeDtypeStruct(bias.shape, f32),
         ),
         scratch_shapes=[pltpu.VMEM(q.shape, bf16)] * 4,
-        compiler_params=params(),
+        compiler_params=params(42),
         cost_estimate=cost(21),
         name="self_bwd",
     )(first_grad, mixed, q, k, v, bias, ow, qw, kw, vw, normed, tok, g1)
 
 
-def kv_fwd_kernel(place, source, kw, vw, out):
-    inner = kw.shape[0]
+def kv_fwd_kernel(place, source, kw, vw, *outs):
     rows = source[0, 0]
-    for n, w in enumerate((kw, vw)):
-        out[0, 0, :, n * inner : (n + 1) * inner] = lax.dot_general(
-            rows, w[...], (((0,), (1,)), ((), ())), preferred_element_type=f32
-        ).astype(bf16)
+    both = [
+        lax.dot_general(rows, w[...], (((0,), (1,)), ((), ())), preferred_element_type=f32).astype(bf16)
+        for w in (kw, vw)
+    ]
+    for s, out in enumerate(outs):
+
+        @pl.when(pl.program_id(0) == s)
+        def write(out=out):
+            out[0] = jnp.concatenate(both, axis=1)
 
 
 def kv_fwd(place, memory, kw, vw):
@@ -444,64 +447,108 @@
                 whole,
                 whole,
             ],
-            out_specs=pl.BlockSpec((1, 1, slots, 2 * inner), lambda s, m, place: (s, m, 0, 0)),
+            out_specs=[
+                pl.BlockSpec(
+                    (1, slots, 2 * inner),
+                    lambda s, m, place, t=t: (jnp.where(s < t, 0, jnp.where(s == t, m, micros - 1)), 0, 0),
+                )
+                for t in range(pairs)
+            ],
         ),
-        out_shape=jax.ShapeDtypeStruct((pairs, micros, slots, 2 * inner), bf16),
-        compiler_params=params(32),
+        out_shape=[jax.ShapeDtypeStruct((micros, slots, 2 * inner), bf16)] * pairs,
+        compiler_params=params(20),
         cost_estimate=cost(9),
         name="kv_fwd",
     )(place, memory, kw, vw)
 
 
-def kv_bwd_kernel(place, source, kw, vw, kvg, out, dkw_o, dvw_o, acc):
-    inner = kw.shape[0]
-    step = pl.program_id(0) * pl.num_programs(1) + pl.program_id(1)
-    grads = kvg[0, 0]
+def kv_weights_kernel(place, source, *refs):
+    kvgs, (dkw_o, dvw_o, acc) = refs[:-3], refs[-3:]
+    inner = dkw_o.shape[0]
+    pair = pl.program_id(0)
+    step = pair * pl.num_programs(1) + pl.program_id(1)
 
     @pl.when(step == 0)
     def clear():
         acc[...] = jnp.zeros_like(acc)
 
+    grads = kvgs[0][0]
+    for t in range(1, len(kvgs)):
+        grads = jnp.where(pair == t, kvgs[t][0], grads)
+    acc[...] += lax.dot_general(
+        grads, source[0, 0], (((0,), (1,)), ((), ())), preferred_element_type=f32
+    )
+
+    @pl.when(step == pl.num_programs(0) * pl.num_programs(1) - 1)
+    def write():
+        dkw_o[...] = acc[:inner].astype(bf16)
+        dvw_o[...] = acc[inner:].astype(bf16)
+
+
+def kv_memory_kernel(place, kw, vw, *refs):
+    kvgs, out = refs[:-1], refs[-1]
+    inner = kw.shape[0]
+    pair = pl.program_id(0)
+    grads = kvgs[0][0]
+    for t in range(1, len(kvgs)):
+        grads = jnp.where(pair == t, kvgs[t][0], grads)
     out[0, 0] = lax.dot_general(
         kw[...], grads[:, :inner], (((0,), (1,)), ((), ())), preferred_element_type=f32
     ) + lax.dot_general(
         vw[...], grads[:, inner:], (((0,), (1,)), ((), ())), preferred_element_type=f32
     )
-    acc[...] += lax.dot_general(
-        grads, source[0, 0], (((0,), (1,)), ((), ())), preferred_element_type=f32
-    )
-
-    @pl.when(step == pl.num_programs(0) * pl.num_programs(1) - 1)
-    def write():
-        dkw_o[...] = acc[:inner].astype(bf16)
-        dvw_o[...] = acc[inner:].astype(bf16)
-
-
-def kv_bwd(place, memory, kw, vw, kvg):
+
+
+def kv_specs(pairs, micros, slots, inner, width):
+    whole = pl.BlockSpec((inner, width), lambda s, m, place: (0, 0))
+    block = pl.BlockSpec((1, 1, width, slots), lambda s, m, place: (m, place[s], 0, 0))
+    pieces = [
+        pl.BlockSpec(
+            (1, slots, 2 * inner),
+            lambda s, m, place, t=t: (jnp.where(s < t, 0, jnp.where(s == t, m, micros - 1)), 0, 0),
+        )
+        for t in range(pairs)
+    ]
+    return whole, block, pieces
+
+
+def kv_weights(place, memory, kvgs, inner):
     micros, pairs, width, slots = memory.shape
-    inner = kw.shape[0]
-    whole = pl.BlockSpec((inner, width), lambda s, m, place: (0, 0))
+    whole, block, pieces = kv_specs(pairs, micros, slots, inner, width)
     weight = jax.ShapeDtypeStruct((inner, width), bf16)
-    block = pl.BlockSpec((1, 1, width, slots), lambda s, m, place: (m, place[s], 0, 0))
     return pl.pallas_call(
-        kv_bwd_kernel,
+        kv_weights_kernel,
         grid_spec=pltpu.PrefetchScalarGridSpec(
             num_scalar_prefetch=1,
             grid=(pairs, micros),
-            in_specs=[
-                block,
-                whole,
-                whole,
-                pl.BlockSpec((1, 1, slots, 2 * inner), lambda s, m, place: (s, m, 0, 0)),
-            ],
-            out_specs=(block, whole, whole),
+            in_specs=[block, *pieces],
+            out_specs=(whole, whole),
             scratch_shapes=[pltpu.VMEM((2 * inner, width), f32)],
         ),
-        out_shape=(jax.ShapeDtypeStruct(memory.shape, f32), weight, weight),
-        compiler_params=params(48),
-        cost_estimate=cost(17),
-        name="kv_bwd",
-    )(place, memory, kw, vw, kvg)
+        out_shape=(weight, weight),
+        compiler_params=params(24),
+        cost_estimate=cost(9),
+        name="kv_weights",
+    )(place, memory, *kvgs)
+
+
+def kv_memory(place, shape, kw, vw, kvgs):
+    micros, pairs, width, slots = shape
+    inner = kw.shape[0]
+    whole, block, pieces = kv_specs(pairs, micros, slots, inner, width)
+    return pl.pallas_call(
+        kv_memory_kernel,
+        grid_spec=pltpu.PrefetchScalarGridSpec(
+            num_scalar_prefetch=1,
+            grid=(pairs, micros),
+            in_specs=[whole, whole, *pieces],
+            out_specs=block,
+        ),
+        out_shape=jax.ShapeDtypeStruct(shape, f32),
+        compiler_params=params(20),
+        cost_estimate=cost(10),
+        name="kv_memory",
+    )(place, kw, vw, *kvgs)
 
 
 gelu_c = math.sqrt(2 / math.pi)
@@ -546,10 +593,14 @@
                 copy.wait()
 
 
-def feed_grad_kernel(places, count, *refs):
+def feed_grad_kernel(places, count, mems, *refs):
     nf_a, nf_b, og_a, og_b = refs[:4]
     weights = refs[4 : 4 + count]
-    dgw_o, dlw_o, ddw_o, hid_o, gl_o, ll_o, nf, og, hold, sems, whole_sems = refs[4 + count :]
+    split = 2 if mems else 1
+    dgw_o, dlw_o = refs[4 + count : 4 + count + split], refs[4 + count + split : 4 + count + 2 * split]
+    steps = len(places)
+    ddw_o = refs[4 + count + 2 * split : 4 + count + 2 * split + steps]
+    hid_o, gl_o, ll_o, nf, og, hold, sems, whole_sems = refs[4 + count + 2 * split + steps :]
     rows = nf_a.shape[0]
     step = pl.program_id(0)
 
@@ -585,12 +636,25 @@
     hid_o[0] = hidden
     gl_o[0] = gl
     ll_o[0] = ll
-    dgw_o[0] = contract_rows(gl, x).astype(bf16)
-    dlw_o[0] = contract_rows(ll, x).astype(bf16)
-    ddw_o[0] = contract_rows(hidden, up).astype(bf16)
-
-
-def feed_grad(nf_a, nf_b, og_a, og_b, steps, block):
+    for outs, upstream, bit in ((dgw_o, gl, mems // 2), (dlw_o, ll, 1)):
+        grad = contract_rows(upstream, x).astype(bf16)
+        if not mems:
+            outs[0][0] = grad
+            continue
+        part = grad.shape[0] // mems
+        for k in range(mems):
+            at = [i for i in range(mems) if (i & bit) == (k & bit)].index(k)
+            outs[1 if k & bit else 0][0, at] = grad[k * part : (k + 1) * part]
+    down_grad = contract_rows(hidden, up).astype(bf16)
+
+    for i, out in enumerate(ddw_o):
+
+        @pl.when(step == i)
+        def write(out=out):
+            out[...] = down_grad
+
+
+def feed_grad(nf_a, nf_b, og_a, og_b, steps, block, mems):
     rows, width = nf_a.shape
     weights, places = plan(steps)
     n = len(steps)
@@ -599,12 +663,29 @@
     column = pl.BlockSpec((1, 2 * rows, block), lambda i: (i, 0, 0))
     weight = jax.ShapeDtypeStruct((n, block, width), bf16)
     act = jax.ShapeDtypeStruct((n, 2 * rows, block), bf16)
+    half_tile, half = tile, weight
+    if mems:
+        half_tile = pl.BlockSpec((1, mems // 2, block // mems, width), lambda i: (i, 0, 0, 0))
+        half = jax.ShapeDtypeStruct((n, mems // 2, block // mems, width), bf16)
+    count = 4 if mems else 2
     return pl.pallas_call(
-        functools.partial(feed_grad_kernel, places, len(weights)),
+        functools.partial(feed_grad_kernel, places, len(weights), mems),
         grid=(n,),
         in_specs=[any_spec] * (4 + len(weights)),
-        out_specs=(tile, tile, tile, column, column, column),
-        out_shape=(weight, weight, weight, act, act, act),
+        out_specs=(
+            *[half_tile] * count,
+            *[pl.BlockSpec((block, width), lambda i: (0, 0))] * n,
+            column,
+            column,
+            column,
+        ),
+        out_shape=(
+            *[half] * count,
+            *[jax.ShapeDtypeStruct((block, width), bf16)] * n,
+            act,
+            act,
+            act,
+        ),
         scratch_shapes=[
             pltpu.VMEM((2 * rows, width), bf16),
             pltpu.VMEM((2 * rows, width), bf16),
@@ -612,7 +693,7 @@
             pltpu.SemaphoreType.DMA((2, max(len(p) for p in places))),
             pltpu.SemaphoreType.DMA((4,)),
         ],
-        compiler_params=params(60),
+        compiler_params=params(54),
         cost_estimate=cost(13 * n),
         name="feed_grad",
     )(nf_a, nf_b, og_a, og_b, *weights)
@@ -668,10 +749,78 @@
             pltpu.SemaphoreType.DMA((2, max(len(p) for p in places))),
             pltpu.SemaphoreType.DMA((2, max(len(p) for p in act_places))),
         ],
-        compiler_params=params(60),
+        compiler_params=params(54),
         cost_estimate=cost(30),
         name="feed_out",
     )(*weights, *acts)
+
+
+def joined(value):
+    return jnp.concatenate(value) if isinstance(value, list) else value
+
+
+def fuse(fn, *arrays, limit=0):
+    shapes = jax.eval_shape(lambda *a: [joined(o) for o in fn(*a)], *arrays)
+    if any(a.shape[-2] % 16 for a in (*arrays, *shapes)):
+        return [joined(o) for o in fn(*arrays)]
+
+    limit = limit or 6 + sum(math.prod(a.shape) for a in (*arrays, *shapes)) * 4 // 2**20
+
+    def kernel(*refs):
+        for out, value in zip(refs[len(arrays) :], fn(*[ref[...] for ref in refs[: len(arrays)]])):
+            at = 0
+            for piece in value if isinstance(value, list) else [value]:
+                out[at : at + piece.shape[0]] = piece
+                at += piece.shape[0]
+
+    return pl.pallas_call(
+        kernel, out_shape=shapes, compiler_params=params(limit), cost_estimate=cost(3), name="fuse"
+    )(*arrays)
+
+
+def core_split_kernel(spot, *refs):
+    grads, (kept, sent) = refs[:-2], refs[-2:]
+    core = spot[0]
+    for i, grad in enumerate(grads):
+        for z in range(grad.shape[0]):
+            kept[z, i] = grad[z, core]
+            sent[z, i] = grad[z, 1 - core]
+
+
+def core_split(spot, grads):
+    chips, _, slim, width = grads[0].shape
+    shape = jax.ShapeDtypeStruct((chips, len(grads), slim, width), bf16)
+    return pl.pallas_call(
+        core_split_kernel,
+        in_specs=[pl.BlockSpec(memory_space=pltpu.SMEM)] + [pl.BlockSpec(memory_space=pltpu.VMEM)] * len(grads),
+        out_shape=(shape, shape),
+        compiler_params=params(60),
+        cost_estimate=cost(4),
+        name="core_split",
+    )(spot, *grads)
+
+
+def columns_kernel(spot, kept, moved, *outs):
+    chips = kept.shape[0]
+    for k, out in enumerate(outs):
+        for z in range(chips):
+            out[z] = add_low(kept[z, spot[2 + k]], moved[z, spot[2 + k]])
+
+
+def columns_of(spot, kept, moved, mems):
+    chips, count, slim, width = kept.shape
+    if count != mems:
+        total = add_low(kept, moved).reshape(chips, mems, -1, width)
+        return [lax.dynamic_index_in_dim(total, spot[2 + k], 1, keepdims=False) for k in range(mems)]
+    vmem = pl.BlockSpec(memory_space=pltpu.VMEM)
+    return pl.pallas_call(
+        columns_kernel,
+        in_specs=[pl.BlockSpec(memory_space=pltpu.SMEM), vmem, vmem],
+        out_shape=[jax.ShapeDtypeStruct((chips, slim, width), bf16)] * mems,
+        compiler_params=params(18),
+        cost_estimate=cost(4),
+        name="columns",
+    )(spot, kept, moved)
 
 
 def tree_sum(values):
@@ -756,8 +905,10 @@
 
     def matrices(held, other):
         full = assemble(spot, held, other)
-        full = full.reshape(4, mems // 4, seqs, -1, width).transpose(0, 2, 1, 3, 4)
-        return full.reshape(4, inner, width)
+        if mems == 4:
+            return [full[i].reshape(inner, width) for i in range(4)]
+        full = jnp.stack(full).reshape(4, mems // 4, seqs, -1, width).transpose(0, 2, 1, 3, 4)
+        return list(full.reshape(4, inner, width))
 
     def hold_plane(pack, moved):
         return jnp.concatenate([pack[None], jnp.stack(moved, axis=1)], axis=0)
@@ -782,7 +933,6 @@
     row_index = jnp.arange(length, dtype=jnp.int32)
     causal = row_index[:, None] >= row_index[None, :]
     position_bias = jnp.where(causal[None], position_bias, masked_score)
-    tokens = inputs.reshape(rows, width)
     og_low = output_grad.reshape(rows, width)
     gain_self, gain_cross, gain_feed = [g.reshape(1, width) for g in (gain_self, gain_cross, gain_feed)]
     spots = jnp.stack(
@@ -804,7 +954,10 @@
     valid = valid.reshape(micros, 1, mems * slots).astype(f32)
 
 
-    first_parts, second_parts = [jnp.stack([piece[i] for piece in moved])[None] for i in range(2)]
+    first_parts, second_parts = fuse(
+        lambda *m: [[p[:1] for p in m], [p[1:] for p in m]], *moved
+    )
+    first_parts, second_parts = first_parts[None], second_parts[None]
     first_order, second_order = [0], [0]
     for first_bit, second_bit in zip(bits, bits[::-1]):
         first_more, second_more = to_mem(first_parts, first_bit), to_mem(second_parts, second_bit)
@@ -839,7 +992,7 @@
     gate_late_a1 = to_mem(gate_late, bits[0])
     linear_late_a1 = to_mem(linear_late, bits[-1])
     first_mats = matrices(first_held, first_more)
-    kc_full, vc_full, qs_full, ks_full = [first_mats[i] for i in range(4)]
+    kc_full, vc_full, qs_full, ks_full = first_mats
     kv_local = kv_fwd(place, source, kc_full, vc_full)
     gate_early = jnp.concatenate([gate_early, gate_a1])
     linear_early = jnp.concatenate([linear_early, linear_a1])
@@ -850,9 +1003,9 @@
     kvs = [to_mem(kv_local[s], s) if s else kv_local[s] for s in range(mems)]
     down.append(to_next(down[0]))
     second_mats = matrices(second_held, second_more)
-    vs_full, os_full, qc_full, oc_full = [second_mats[i] for i in range(4)]
-    normed, q, k, v, mixed, first_sum, normed_cross, cq = self_fwd(
-        depth, length, tokens, gain_self, qs_full, ks_full, vs_full, os_full, position_bias, gain_cross, qc_full
+    vs_full, os_full, qc_full, oc_full = second_mats
+    tokens, normed, q, k, v, mixed, first_sum, normed_cross, cq = self_fwd(
+        depth, length, inputs.reshape(micros, length, width).swapaxes(1, 2), gain_self, qs_full, ks_full, vs_full, os_full, position_bias, gain_cross, qc_full
     )
     kvs, down[1], cq, gate_early, linear_early = tie(kvs, down[1], cq, gate_early, linear_early)
 
@@ -906,17 +1059,31 @@
     gate_late_parts, gate_order = spread_rest(gate_late, [0, bits[0]], bits[1:])
     linear_late_parts, linear_order = spread_rest(linear_late, [0, bits[-1]], bits[::-1][1:])
     down.append(to_next(down[-1]))
-    grads_a = feed_grad(normed_feed, nf_other, og_low, og_other, early_steps + [own_steps], feed)
+    whole_bits = mems if mems == 4 and part % 16 == 0 else 0
+    grads_a = feed_grad(normed_feed, nf_other, og_low, og_other, early_steps + [own_steps], feed, whole_bits)
     grads_a, gate_late_parts, linear_late_parts, down[last], nf_more = tie(
         grads_a, gate_late_parts, linear_late_parts, down[last], nf_other
     )
 
-    gate_x = grads_a[0].reshape(last, mems, part, width)
-    linear_x = grads_a[1].reshape(last, mems, part, width)
     natural_order = list(range(mems))
-    gate_kept, gate_moved, gate_ord = fold_step(gate_x, natural_order, bits[-1])
-    linear_kept, linear_moved, linear_ord = fold_step(linear_x, natural_order, bits[0])
-    down_total = to_next(grads_a[2][0])
+    gate_ord = [k for k in natural_order if not k & bits[-1]]
+    linear_ord = [k for k in natural_order if not k & bits[0]]
+
+    def halves(grads):
+        if whole_bits:
+            return (grads[0:2], grads[2:4], grads[4:-3], *grads[-3:])
+        shape = (-1, mems, part, width)
+        return (
+            fold_parts(grads[0].reshape(shape), natural_order, bits[-1]),
+            fold_parts(grads[1].reshape(shape), natural_order, bits[0]),
+            grads[2:-3],
+            *grads[-3:],
+        )
+
+    (gate_keep, gate_send), (linear_keep, linear_send), grad_down_a, *acts_a = halves(grads_a)
+    down_total = to_next(grad_down_a[0])
+    gate_moved = to_mem(gate_send, bits[-1])
+    linear_moved = to_mem(linear_send, bits[0])
     late_steps = [
         [
             whole_source(None, sources(gate_late_parts, gate_order, 0)),
@@ -924,77 +1091,134 @@
             [(down[last].reshape(feed, width), (), feed)],
         ]
     ]
-    grads_b = feed_grad(normed_feed, nf_more, og_low, og_other, late_steps, feed)
+    grads_b = feed_grad(normed_feed, nf_more, og_low, og_other, late_steps, feed, whole_bits)
+    (gate_b, gate_bs), (linear_b, linear_bs), (grad_down_b,), *acts_b = halves(grads_b)
     act_steps = [
-        [[(grads[i], (n,), 2 * rows)] for i in (4, 5, 3)]
-        for grads, count in ((grads_a, last), (grads_b, 1))
+        [[(acts[i], (n,), 2 * rows)] for i in (1, 2, 0)]
+        for acts, count in ((acts_a, last), (acts_b, 1))
         for n in range(count)
     ]
     nfg_own, nfg_send, res_own, res_send = feed_out(
         rows, width, early_steps + [own_steps] + late_steps, act_steps, feed
     )
-    gate_moved, linear_moved, down_total, nfg_send, dg_b, dl_b = tie(
-        gate_moved, linear_moved, down_total, nfg_send, grads_b[0], grads_b[1]
-    )
-
-    def two_folds(fresh, order, bit, older, older_order, older_bit):
-        kept, sent = fold_parts(fresh, order, bit)
-        older_kept, older_sent = fold_parts(older, older_order, older_bit)
-        moved = to_mem(jnp.concatenate([sent.reshape(-1, part, width), older_sent.reshape(-1, part, width)]), bit)
-        count = sent.shape[0] * sent.shape[1]
-        return kept, moved[:count].reshape(sent.shape), older_kept, moved[count:].reshape(older_sent.shape)
+    gate_moved, linear_moved, down_total, nfg_send, gate_bs, linear_bs = tie(
+        gate_moved, linear_moved, down_total, nfg_send, gate_bs, linear_bs
+    )
 
     def fold_to_last(held, order, over):
         for bit in over[:-1]:
             kept, moved, order = fold_step(held, order, bit)
             held = add_low(kept, moved)
-        return held, order
-
-    gate_y, gate_yo = fold_to_last(add_low(gate_kept, gate_moved), gate_ord, bits[::-1][1:])
-    linear_y, linear_yo = fold_to_last(add_low(linear_kept, linear_moved), linear_ord, bits[1:])
+        return held
+
+    down_next = down_total
+    for j in early[1:]:
+        down_next = to_next(add_low(down_next, grad_down_a[j - 1]))
     nfg_more = rows_to_core(nfg_send)
-    gate_b, gate_bm, linear_yk, linear_ym = two_folds(
-        dg_b.reshape(1, mems, part, width), natural_order, bits[-1], linear_y, linear_yo, bits[-1]
-    )
-    linear_b, linear_bm, gate_yk, gate_ym = two_folds(
-        dl_b.reshape(1, mems, part, width), natural_order, bits[0], gate_y, gate_yo, bits[0]
-    )
-    for j in early[1:]:
-        down_total = to_next(add_low(down_total, grads_a[2][j - 1]))
+    half = mems // 2
+    if len(bits) == 2:
+        both_y = fuse(
+            lambda gk, gm, lk, lm: [
+                add_low(gk[:, 0], gm[:, 0]),
+                add_low(gk[:, 1], gm[:, 1]),
+                add_low(lk[:, 0], lm[:, 0]),
+                add_low(lk[:, 1], lm[:, 1]),
+            ],
+            gate_keep, gate_moved, linear_keep, linear_moved,
+        )
+    else:
+        gate_y = fold_to_last(add_low(gate_keep, gate_moved), gate_ord, bits[::-1][1:])
+        linear_y = fold_to_last(add_low(linear_keep, linear_moved), linear_ord, bits[1:])
+        both_y = [gate_y[:, 0], gate_y[:, 1], linear_y[:, 0], linear_y[:, 1]]
+    message_y, message_x = fuse(
+        lambda gs, ly, ls, gy: [[gs[0], ly], [ls[0], gy]], gate_bs, both_y[3], linear_bs, both_y[1]
+    )
+    message_y, message_x = to_mem(message_y, bits[-1]), to_mem(message_x, bits[0])
     kvg, (grad_gain_feed, grad_co, grad_cq, first_grad, grad_gain_cross) = cross_bwd(
         depth, length, og_low, nfg_own, nfg_more, second_sum, gain_feed, cmixed, cq, valid, oc_full,
         first_sum, gain_cross, normed_cross, qc_full, kvs,
     )
-    gate_bm, linear_bm, gate_ym, linear_ym, down_total, kvg, grad_gain_cross, res_send = tie(
-        gate_bm, linear_bm, gate_ym, linear_ym, down_total, kvg, grad_gain_cross, res_send
+    message_y, message_x, down_next, kvg, grad_gain_cross, res_send = tie(
+        message_y, message_x, down_next, kvg, grad_gain_cross, res_send
     )
 
     kvg = [to_mem(kvg[s], s) if s else kvg[s] for s in range(mems)]
-    gate_y, linear_y = add_low(gate_yk, gate_ym)[:, 0], add_low(linear_yk, linear_ym)[:, 0]
-    down_total = add_low(down_total, grads_b[2][0]).reshape(mems, part, width)
-    ring = to_next(jnp.concatenate([down_total, gate_y[:1], linear_y[:1]]))
+    shards = (mems, part, width)
+    own = last - 1
+    gate_y, linear_y, both_own, ring = fuse(
+        lambda g, x, l, y, d, b: [
+            add_low(g[:own], x[half:-1]),
+            add_low(l[:own], y[half:-1]),
+            [add_low(g[own:], x[-1:]), add_low(l[own:], y[-1:])],
+            [add_low(d, b), add_low(g[:1], x[half : half + 1]), add_low(l[:1], y[half : half + 1])],
+        ],
+        both_y[0], message_x, both_y[2], message_y, down_next.reshape(shards), grad_down_b.reshape(shards),
+    )
+    ring = to_next(ring)
     res_more = rows_to_core(res_send)
     grad_os, grad_qs, grad_ks, grad_vs, input_grad, grad_gain_self, score_sum = self_bwd(
         depth, length, first_grad, mixed, q, k, v, position_bias, os_full, qs_full, ks_full, vs_full,
         normed, tokens, gain_self,
     )
-    kvg, ring, grad_qs, res_more, gate_bm, linear_bm = tie(kvg, ring, grad_qs, res_more, gate_bm, linear_bm)
-
-    self_stack = jnp.stack(
-        [g.reshape(chips, 2, slim, width) for g in (grad_qs, grad_ks, grad_vs, grad_os)], axis=2
-    )
-    kept = lax.dynamic_index_in_dim(self_stack, core, 1, keepdims=False)
-    sent = to_core(lax.dynamic_index_in_dim(self_stack, 1 - core, 1, keepdims=False))
-    down_total, both_total = ring[:mems], ring[mems:]
-    for j in early[1:]:
-        both_total = to_next(add_low(both_total, jnp.stack([gate_y[j - 1], linear_y[j - 1]])))
-    gate_b, gate_bo = fold_to_last(add_low(gate_b, gate_bm), gate_ord, bits[::-1][1:])
-    linear_b, linear_bo = fold_to_last(add_low(linear_b, linear_bm), linear_ord, bits[1:])
-    gate_bk, gate_bm, _ = fold_step(gate_b, gate_bo, bits[0])
-    linear_bk, linear_bm, _ = fold_step(linear_b, linear_bo, bits[-1])
-    memory_grad, grad_kc, grad_vc = kv_bwd(place, source, kc_full, vc_full, jnp.stack(kvg))
-    sent, both_total, gate_bm, linear_bm, grad_kc = tie(sent, both_total, gate_bm, linear_bm, grad_kc)
-
+    kvg, ring, grad_qs, res_more = tie(kvg, ring, grad_qs, res_more)
+
+    kept, sent = core_split(
+        spot, [g.reshape(chips, 2, slim, width) for g in (grad_qs, grad_ks, grad_vs, grad_os)]
+    )
+    sent = to_core(sent)
+    for j in early[1:-1]:
+        ring_both = to_next(add_low(ring[mems:], jnp.stack([gate_y[j - 1], linear_y[j - 1]])))
+        ring = jnp.concatenate([ring[:mems], ring_both])
+    gate_b, linear_b = gate_b[0], linear_b[0]
+    gate_bm, linear_bm = message_y, message_x
+    if len(bits) > 2:
+        gate_bm, linear_bm = message_y[:half], message_x[:half]
+        gate_b = fold_to_last(add_low(gate_b, gate_bm)[None], gate_ord, bits[::-1][1:])[0]
+        linear_b = fold_to_last(add_low(linear_b, linear_bm)[None], linear_ord, bits[1:])[0]
+        gate_bm, linear_bm = jnp.zeros_like(gate_b), jnp.zeros_like(linear_b)
+    at = early[-1] - 1
+    parts = fuse(
+        lambda r, g, l, gb, gm, lb, lm, d: [
+            [add_low(r[mems : mems + 1], g[at : at + 1]), add_low(r[mems + 1 :], l[at : at + 1])],
+            add_low(gb[:1], gm[:1]),
+            add_low(lb[:1], lm[:1]),
+            [add_low(gb[1:2], gm[1:2]), add_low(r[1:2], d[1:2])],
+            [add_low(lb[1:2], lm[1:2]), add_low(r[half : half + 1], d[half : half + 1])],
+            add_low(r[:1], d[:1]),
+            *[add_low(r[k : k + 1], d[k : k + 1]) for k in range(1, mems) if k not in (1, half)],
+        ],
+        ring, gate_y, linear_y, gate_b, gate_bm, linear_b, linear_bm, grad_down_a[last - 1].reshape(shards),
+        limit=60,
+    )
+    ring_both, gate_bk, linear_bk, message_x, message_y, down_mine, *down_rest = parts
+    others = [k for k in range(1, mems) if k not in (1, half)]
+    ring_both = to_next(ring_both)
+    message_x, message_y = to_mem(message_x, bits[0]), to_mem(message_y, bits[-1])
+    down_rest = [to_mem(p, k) for p, k in zip(down_rest, others)]
+
+    def grad_sums(*grads):
+        stacked = jnp.stack([g.reshape(seqs, slim, width) for g in grads], axis=1)
+        return lax.psum_scatter(stacked.reshape(seqs, len(grads) * slim, width), "seq", scatter_dimension=0)
+
+    cross_first = grad_sums(after(grad_cq, ring), grad_co)
+    grad_kc, grad_vc = kv_weights(place, source, kvg, inner)
+    sent, ring_both, message_x, message_y, down_rest, grad_kc, kvg[0] = tie(
+        sent, ring_both, message_x, message_y, down_rest, grad_kc, kvg[0]
+    )
+
+    columns = columns_of(spot, kept, sent, mems)
+    columns = [to_mem(p, s) if s else p for s, p in enumerate(columns)]
+    ring_both, down_sum = fuse(
+        lambda r, g, x, l, y, d, *more: [
+            [add_low(r[:1], add_low(g, x[:1])), add_low(r[1:], add_low(l, y[:1]))],
+            sum_low([d, x[1:], y[1:], *more]),
+        ],
+        ring_both, gate_bk, message_x, linear_bk, message_y, down_mine, *down_rest,
+    )
+    ring_both = to_next(ring_both)
+    cross_sum = [grad_sums(grad_kc, grad_vc), cross_first]
+    memory_grad = kv_memory(place, source.shape, kc_full, vc_full, kvg)
+    score_sum, input_grad, res_more = [after(x, columns[1]) for x in (score_sum, input_grad, res_more)]
     grad_table = lax.dot_general(
         onehot.astype(f32),
         score_sum.reshape(heads, length * length),
@@ -1009,70 +1233,79 @@
         rest = (value - high.astype(f32)).astype(bf16)
         return jnp.concatenate([high, rest, jnp.zeros((16 - 2 * value.shape[0], width), bf16)])
 
-    def from_rows(value, count):
-        return value[:count].astype(f32) + value[count : 2 * count].astype(f32)
-
-    cross_stack = jnp.stack(
-        [g.reshape(seqs, slim, width) for g in (grad_kc, grad_vc, grad_cq, grad_co)], axis=1
-    ).reshape(seqs, 4 * slim, width)
-    cross_sum = lax.psum_scatter(cross_stack, "seq", scatter_dimension=0)
-    total = add_low(kept, sent).reshape(chips, mems, 4 * slim // mems, width)
+    def from_rows(value):
+        return value[:4].astype(f32) + value[4:8].astype(f32)
+
+    small_rows = to_rows(small)
+    columns, ring_both, small_rows, memory_grad = tie(columns, ring_both, small_rows, memory_grad)
+
     share = 4 * slim // mems
-    down_mine = add_low(down_total, grads_a[2][last - 1].reshape(mems, part, width))
-    columns = []
-    for s in range(mems):
-        column = lax.dynamic_index_in_dim(total, mem_index ^ s, 1, keepdims=False).reshape(-1, width)
-        columns.append(jnp.concatenate([column, down_mine[s], to_rows(small)]))
-    columns = [to_mem(p, s) if s else p for s, p in enumerate(columns)]
-    gate_b, linear_b = add_low(gate_bk, gate_bm)[0, 0], add_low(linear_bk, linear_bm)[0, 0]
-    both_total = to_next(add_low(both_total, jnp.stack([gate_b, linear_b])))
-    columns, both_total = tie(columns, both_total)
-
-    down_sum = sum_low([p[chips * share : chips * share + part] for p in columns])
-    small = tree_sum([from_rows(p[chips * share + part :], 4) for p in columns])
-    total = sum_low([p[: chips * share] for p in columns]).reshape(chips, share, width)
+    total = sum_low(columns).reshape(chips, share, width)
     pieces = [
-        jnp.concatenate(
-            [lax.dynamic_index_in_dim(total, (chip + j) % chips, 0, keepdims=False), to_rows(small)]
-        )
+        jnp.concatenate([lax.dynamic_index_in_dim(total, (chip + j) % chips, 0, keepdims=False), small_rows])
         for j in range(chips)
     ]
     pieces = [to_step(p, j) if j else p for j, p in enumerate(pieces)]
-    both_sum = add_low(both_total, jnp.stack([gate_y[last - 1], linear_y[last - 1]]))
-    gate_g = [both_sum[:1], to_mem(both_sum[:1], bits[0])]
-    linear_g = [both_sum[1:], to_mem(both_sum[1:], bits[-1])]
-    pieces, gate_g, linear_g, cross_sum = tie(pieces, gate_g, linear_g, cross_sum)
-
+    both_sum, message_x, message_y = fuse(
+        lambda r, g, d: [add_low(r, g), [add_low(r[:1], g[:1]), d], [add_low(r[1:], g[1:]), d]],
+        ring_both, both_own, down_sum,
+    )
+    message_x, message_y = to_mem(message_x, bits[0]), to_mem(message_y, bits[-1])
+    down_rest = [to_mem(down_sum, k) for k in range(1, mems) if k not in (1, half)]
+    pieces, message_x, message_y, down_rest, cross_sum = tie(pieces, message_x, message_y, down_rest, cross_sum)
+
+    down_g = [down_sum if k == 0 else message_x[1:] if k == 1 else message_y[1:] if k == half else None for k in range(mems)]
+    for k in range(mems):
+        if down_g[k] is None:
+            down_g[k] = down_rest.pop(0)
+    down_g = [p[0] for p in down_g]
     self_mine = sum_low([p[:share] for p in pieces])
-    small = jnp.stack([from_rows(p[share:], 4) for p in pieces])
+    small = jnp.stack([from_rows(p[share:]) for p in pieces])
     small = tree_sum(
         [lax.dynamic_index_in_dim(small, (chip - z) % chips, 0, keepdims=False) for z in range(chips)]
     )
-    gate_g, gate_order = spread_rest(jnp.concatenate(gate_g), [0, bits[0]], bits[1:])
-    linear_g, linear_order = spread_rest(jnp.concatenate(linear_g), [0, bits[-1]], bits[::-1][1:])
-    cross_parts = [to_mem(p, s) if s else p for s, p in enumerate(quarters(cross_sum))]
-    gate_g, linear_g, cross_parts, small, self_mine = tie(gate_g, linear_g, cross_parts, small, self_mine)
-
-    mine = jnp.concatenate([self_mine, sum_low(cross_parts), down_sum])
+    gate_g, gate_order = [both_sum[:1], message_x[:1]], [0, bits[0]]
+    linear_g, linear_order = [both_sum[1:], message_y[:1]], [0, bits[-1]]
+    gate_g, gate_order = spread_rest(jnp.concatenate(gate_g), gate_order, bits[1:-1])
+    linear_g, linear_order = spread_rest(jnp.concatenate(linear_g), linear_order, bits[::-1][1:-1])
+    gate_g, linear_g = joined(gate_g), joined(linear_g)
+    small_rows = to_rows(small)
+    cut = gate_g.shape[0] * part
+    cross_parts = list(quarters(jnp.concatenate(cross_sum)))
+    messages = fuse(
+        lambda g, l, rows_, *ps: [
+            [*([l] if k == 1 else [g] if k == half else []), p, rows_] for k, p in enumerate(ps)
+        ],
+        gate_g.reshape(cut, width), linear_g.reshape(cut, width), small_rows, *cross_parts,
+    )
+    cross_parts[0] = messages[0]
+    moved = {k: to_mem(p, k) for k, p in enumerate(messages) if k}
+    moved, small_rows, self_mine, cross_own = tie(moved, small_rows, self_mine, cross_parts[0])
+    linear_g = jnp.concatenate([linear_g, moved[1][:cut].reshape(-1, part, width)])
+    gate_g = jnp.concatenate([gate_g, moved[half][:cut].reshape(-1, part, width)])
+    gate_order = gate_order + [k | half for k in gate_order]
+    linear_order = linear_order + [k | 1 for k in linear_order]
+    cross_parts = [cross_own] + [moved[k][cut:] if k in (1, half) else moved[k] for k in range(1, mems)]
+    small = tree_sum([from_rows(p[share:]) for p in cross_parts])
+
+    mine = jnp.concatenate([self_mine, sum_low([p[:share] for p in cross_parts])])
     mine_g = [mine] + [to_mem(mine, k) for k in range(1, mems)]
     small = small + to_core(small)
 
-    def settle(parts, order):
-        flat = jnp.concatenate(parts)
-        pieces = [flat[order.index(k)] for k in range(mems)]
-        return natural(pieces, mem_index).astype(f32)
+    def settle(flat, order):
+        return natural([flat[order.index(k)] for k in range(mems)], mem_index).astype(f32)
 
     gate_out = settle(gate_g, gate_order).reshape(feed, width)
     linear_out = settle(linear_g, linear_order).reshape(feed, width)
-    mine_g, gate_out, linear_out = tie(mine_g, gate_out, linear_out)
+    down_out = natural(down_g, mem_index).astype(f32).reshape(feed, width)
     result = second_sum + res_own + res_more.astype(f32)
+    mine_g, gate_out, linear_out, down_out = tie(mine_g, gate_out, linear_out, down_out)
 
     def settled(start, rows_of):
         return natural([p[start : start + rows_of] for p in mine_g], mem_index).astype(f32)
 
     self_sum = settled(0, share).reshape(4, slim, width)
     cross_sum = settled(share, share).reshape(4, slim, width)
-    down_out = settled(2 * share, part).reshape(feed, width)
     return (
         result.reshape(inputs.shape),
         input_grad.reshape(inputs.shape),

time: 625 us -> 576 us (0.922)
  other arithmetic: 69.7 us -> 42.9 us
  waiting for transfers between devices: 175 us -> 157 us
  local copies, waits for them, and re-layouts: 84.3 us -> 67 us
  Pallas kernels: 198 us -> 210 us
    unnamed x187 -> x307, local copies, waits for them, and re-layouts: 28.6 us -> 53 us
    pallas_call x5 -> x16, Pallas kernels: 72 us -> 92 us  [the longest x2 54.3 us: feed_grad(): pl.pallas_call(functools.partial(feed_grad_kernel, places, len(weights),...]
    concatenate x7 -> x1, local copies, waits for them, and re-layouts: 19.5 us -> 0.08 us  [to_rows(): jnp.concatenate([high, rest, jnp.zeros((16 - 2 * value.shape[0], width),...]
    convert_element_type x13 -> x1, other arithmetic: 19.3 us -> 1.41 us  [add_low(): return (left.astype(f32) + right.astype(f32)).astype(bf16)]
    ppermute x11, waiting for transfers between devices: 48.9 us -> 33.2 us  [to_next(): lax.ppermute(value, 'seq', [(i, (i + 2) % count) for i in range(count)])]
    slice x14 -> x5, local copies, waits for them, and re-layouts: 12.9 us -> 0.23 us  [the longest x2 0.09 us: settle(): flat[order.index(k)]]
    another operation x13 -> x7, other arithmetic: 13.1 us -> 3.51 us  [the longest x2 3.44 us: grad_sums(): stacked = jnp.stack([g.reshape(seqs, slim, width) for g in grads], axis=1)]
  transfers between devices with their start and end apart: 63 -> 64, of which waited for: 24 -> 24; matrix products, arithmetic and copies ran while one was open for 18% -> 10% of each run, Pallas kernels for 32% -> 37%
where the time goes in v3:
time: 576 us; the launch traced here: 567 us
  Pallas kernels  210 us (36%)
  waiting for transfers between devices  157 us (27%)
  local copies, waits for them, and re-layouts  67 us (12%)
  starting transfers between devices  63.7 us (11%)
  other arithmetic  42.9 us (7%)
  between operations  16.2 us (3%)
  blocking collectives  8.17 us (1%)
    ppermute x37, waiting for transfers between devices, to_mem(): return lax.ppermute(value, 'mem', [(i, i ^ mask) for i in range(count)])  109 us
    pallas_call x2, Pallas kernels, feed_grad(): pl.pallas_call(functools.partial(feed_grad_kernel, places, len(weights),...  54.3 us
    unnamed x307, local copies, waits for them, and re-layouts  53 us
    ppermute x37, starting transfers between devices, to_mem(): return lax.ppermute(value, 'mem', [(i, i ^ mask) for i in range(count)])  41 us
    pallas_call x1, Pallas kernels, feed_out(): pl.pallas_call(functools.partial(feed_out_kernel, places, act_places, len...  34 us
    ppermute x11, waiting for transfers between devices, to_next(): lax.ppermute(value, 'seq', [(i, (i + 2) % count) for i in range(count)])  33.2 us
    pallas_call x1, Pallas kernels, cross_bwd(): pl.pallas_call(functools.partial(cross_bwd_kernel, depth, length, len(kvs...  31.6 us
    pallas_call x1, Pallas kernels, self_bwd(): pl.pallas_call(functools.partial(self_bwd_kernel, depth, length), out_sha...  18.8 us
  transfers between devices with their start and end apart: 64, of which 24 were waited for; matrix products, arithmetic and copies ran while one was open for 10% of the time, Pallas kernels for 37%

profile of v3, /device:TPU:8, one launch (start us, length us, event | category | flops | bytes accessed | tf_op | source)
XLA Modules:
  0.0 567.1 jit_solution(14112995255068593366)
XLA Ops:
  11.9 1.6 collective-permute-start
  14.5 2.0 collective-permute-start.2
  16.5 1.7 copy.96
  22.6 2.4 constant_dynamic-slice_fusion.22
  31.1 8.2 %all-gather = s32[8,1,4,256]{3,2,1,0:T(4,128)S(1)} all-gather(s32[2,1,4,256]{3,2,1,0:T(4,128)S(1)} %copy-done.133), channel_id=2, replica_groups=mesh['seq'=8,'mem'=4] {'mem'}, dimensions={0}, use_global_device_ids=true | all-gather | bytes 40960 | tf_op jit(solution)/shard_map/all_gather | solution.py:947
  40.9 1.6 collective-permute-start.4
  45.3 7.7 %collective-permute-done.4 = bf16[1,3,48,1472]{3,2,1,0:T(8,128)(2,1)S(1)} collective-permute-done((bf16[1,3,48,1472]{3,2,1,0:T(8,128)(2,1)S(1)}, bf16[1,3,48,1472]{3,2,1,0:T(8,128)(2,1)S(1)}, u32[]{:S(2)}, u32[]{:S(2)}) %collective-permute-start.4) | collective-permute-done | bytes 423968 | tf_op jit(solution)/shard_map/ppermute | solution.py:62
  54.2 4.0 collective-permute-done.6
  61.7 1.5 collective-permute-start.7
  64.1 1.8 fusion.4.bias
  65.9 13.6 %collective-permute-done.9 = bf16[2,112,1472]{2,1,0:T(8,128)(2,1)} collective-permute-done((bf16[2,112,1472]{2,1,0:T(8,128)(2,1)}, bf16[2,112,1472]{2,1,0:T(8,128)(2,1)}, u32[]{:S(2)}, u32[]{:S(2)}) %collective-permute-start.9) | collective-permute-done | bytes 659488 | tf_op jit(solution)/shard_map/ppermute | solution.py:57
  80.2 2.2 collective-permute-done.7
  87.0 1.7 collective-permute-start.12
  90.9 13.7 %collective-permute-done.12 = bf16[1,2,112,1472]{3,2,1,0:T(8,128)(2,1)S(1)} collective-permute-done((bf16[1,2,112,1472]{3,2,1,0:T(8,128)(2,1)S(1)}, bf16[1,2,112,1472]{3,2,1,0:T(8,128)(2,1)S(1)}, u32[]{:S(2)}, u32[]{:S(2)}) %collective-permute-start.12) | collective-permute-done | bytes 659488 | tf_op jit(solution)/shard_map/ppermute | solution.py:62
  110.0 10.0 %kv_fwd.1 = (bf16[2,256,768]{2,1,0:T(8,128)(2,1)S(1)}, bf16[2,256,768]{2,1,0:T(8,128)(2,1)}, bf16[2,256,768]{2,1,0:T(8,128)(2,1)S(1)}, bf16[2,256,768]{2,1,0:T(8,128)(2,1)S(1)}) custom-call(s32[4]{0:T(128)S(1)} %pad_add_fusion.place, bf16[2,4,1472,256]{3,2,1,0:T(8,128)(2,1)S(1)} %bitcast.260, bf16[384,1472]{1,0:T(8,128)(2,1)S(1)} %bitcast.266, ...), custom_call_target="tpu_custom_call" | custom-call | flops 8999999488 | bytes 27000000 | tf_op jit(solution)/shard_map/kv_fwd/pallas_call | solution.py:440
  124.6 1.6 collective-permute-start.17
  128.1 13.6 %self_fwd.1 = (bf16[512,1472]{1,0:T(8,128)(2,1)S(1)}, bf16[512,1472]{1,0:T(8,128)(2,1)S(1)}, bf16[512,384]{1,0:T(8,128)(2,1)S(1)}, bf16[512,384]{1,0:T(8,128)(2,...) custom-call(bf16[2,1472,256]{2,1,0:T(8,128)(2,1)S(1)} %bitcast.263, ...), custom_call_target="tpu_custom_call" | custom-call | flops 16000000000 | bytes 48000000 | tf_op jit(solution)/shard_map/self_fwd/pallas_call | solution.py:230
  147.6 15.1 %collective-permute-done.18.refs_2_ = bf16[2,256,768]{2,1,0:T(8,128)(2,1)S(1)} collective-permute-done((bf16[2,256,768]{2,1,0:T(8,128)(2,1)S(1)}, bf16[2,256,768]{2,1,0:T(8,128)(2,1)S(1)}, u32[]{:S(2)}, u32[]{:S(2)}) %collective-permute-start.18) | collective-permute-done | bytes 786464 | tf_op jit(solution)/shard_map/ppermute | solution.py:62
  163.1 1.7 collective-permute-start.22
  165.9 1.9 copy-done.68
  167.8 9.7 %cross_fwd.1 = (bf16[512,384]{1,0:T(8,128)(2,1)S(1)}, f32[512,1472]{1,0:T(8,128)S(1)}, bf16[512,1472]{1,0:T(8,128)(2,1)S(1)}) custom-call(bf16[512,384]{1,0:T(8,128)(2,1)S(1)} %get-tuple-element.274.cq, f32[2,1,1024]{2,1,0:T(1,128)S(1)} %and_convert_fusion.mask, bf16[384,1472]{1,0:T(8,128)(2,1)S(1)} %bitcast.280, f32[512,1472]{1,0:T(8,128)S(1)} %copy-done.68, ...), custom_call_target="tpu_custom_call" | custom-call | flops 15000000512 | bytes 45000000 | tf_op jit(solution)/shard_map/cross_fwd/pallas_call | solution.py:271
  177.6 1.7 copy-done.2
  179.2 15.0 %collective-permute-done.21.refs_5_.refs_1_ = bf16[2,2,112,1472]{3,2,1,0:T(8,128)(2,1)S(1)} collective-permute-done((bf16[2,2,112,1472]{3,2,1,0:T(8,128)(2,1)S(1)}, bf16[2,2,112,1472]{3,2,1,0:T(8,128)(2,1)S(1)}, u32[]{:S(2)}, u32[]{:S(2)}) %collective-permute-start.21) | collective-permute-done | bytes 1318944 | tf_op jit(solution)/shard_map/ppermute | solution.py:62
  194.5 1.8 collective-permute-done.23
  202.7 39.1 %feed_grad.2 = (bf16[3,2,112,1472]{3,2,1,0:T(8,128)(2,1)}, bf16[3,2,112,1472]{3,2,1,0:T(8,128)(2,1)}, bf16[3,2,112,1472]{3,2,1,0:T(8,128)(2,1)}, bf16[3,2,112,14...) custom-call(bf16[512,1472]{1,0:T(8,128)(2,1)} %copy-done.11, ...), custom_call_target="tpu_custom_call" | custom-call | flops 38999998464 | bytes 117000000 | tf_op jit(solution)/shard_map/feed_grad/pallas_call | solution.py:671
  245.8 2.7 collective-permute-start.30
  248.5 15.2 %feed_grad.3 = (bf16[1,2,112,1472]{3,2,1,0:T(8,128)(2,1)}, bf16[1,2,112,1472]{3,2,1,0:T(8,128)(2,1)}, bf16[1,2,112,1472]{3,2,1,0:T(8,128)(2,1)}, bf16[1,2,112,14...) custom-call(bf16[512,1472]{1,0:T(8,128)(2,1)} %copy-done.11, ...), custom_call_target="tpu_custom_call" | custom-call | flops 12999999488 | bytes 39000000 | tf_op jit(solution)/shard_map/feed_grad/pallas_call | solution.py:671
  263.7 34.0 %feed_out.1 = (f32[512,1472]{1,0:T(8,128)}, bf16[512,1472]{1,0:T(8,128)(2,1)}, f32[512,1472]{1,0:T(8,128)}, bf16[512,1472]{1,0:T(8,128)(2,1)}) custom-call(bf16[2,2,112,1472]{3,2,1,0:T(8,128)(2,1)} %pad_maximum_fusion.3.refs_4_.refs_0_, bf16[2,2,112,1472]{3,2,1,0:T(8,128)(2,1)} %copy-done.141, bf16[2,2,112,1472]{3,2,1,0:T(8,128)(2,1)} %pad_maximum_fusion.4.refs_6_.refs_2_, ...), custom_call_target="tpu_custom_call" | custom-call | flops 30000001024 | bytes 90000000 | tf_op jit(solution)/shard_map/feed_out/pallas_call | solution.py:738
  299.3 3.0 collective-permute-start.33
  308.1 31.6 %cross_bwd.1 = (bf16[2,256,768]{2,1,0:T(8,128)(2,1)S(1)}, bf16[2,256,768]{2,1,0:T(8,128)(2,1)}, bf16[2,256,768]{2,1,0:T(8,128)(2,1)S(1)}, bf16[2,256,768]{2,1,0:...) custom-call(bf16[512,1472]{1,0:T(8,128)(2,1)} %bitcast.301, ...), custom_call_target="tpu_custom_call" | custom-call | flops 31000000512 | bytes 93000000 | tf_op jit(solution)/shard_map/cross_bwd/pallas_call | solution.py:339
  340.6 4.2 collective-permute-done.31.refs_3_.refs_4_
  344.9 2.0 copy-done.57
  353.0 1.5 collective-permute-start.37
  354.6 18.8 %self_bwd.1 = (bf16[384,1472]{1,0:T(8,128)(2,1)S(1)}, bf16[384,1472]{1,0:T(8,128)(2,1)S(1)}, bf16[384,1472]{1,0:T(8,128)(2,1)S(1)}, bf16[384,1472]{1,0:T(8,128)(...) custom-call(f32[512,1472]{1,0:T(8,128)} %get-tuple-element.361.first_grad, ...), custom_call_target="tpu_custom_call" | custom-call | flops 20999999488 | bytes 63000000 | tf_op jit(solution)/shard_map/self_bwd/pallas_call | solution.py:405
  375.5 13.5 %collective-permute-done.37.refs_3_ = bf16[2,256,768]{2,1,0:T(8,128)(2,1)S(1)} collective-permute-done((bf16[2,256,768]{2,1,0:T(8,128)(2,1)S(1)}, bf16[2,256,768]{2,1,0:T(8,128)(2,1)S(1)}, u32[]{:S(2)}, u32[]{:S(2)}) %collective-permute-start.37) | collective-permute-done | bytes 786464 | tf_op jit(solution)/shard_map/ppermute | solution.py:62
  389.1 7.8 %collective-permute-done.38.refs_0_ = bf16[6,112,1472]{2,1,0:T(8,128)(2,1)S(1)} collective-permute-done((bf16[6,112,1472]{2,1,0:T(8,128)(2,1)S(1)}, bf16[6,112,1472]{2,1,0:T(8,128)(2,1)S(1)}, u32[]{:S(2)}, u32[]{:S(2)}) %collective-permute-start.38) | collective-permute-done | bytes 1978400 | tf_op jit(solution)/shard_map/ppermute | solution.py:57
  396.9 1.8 pad_maximum_fusion.1
  399.1 4.8 core_split.1
  404.0 5.8 %fuse.12 = (bf16[2,112,1472]{2,1,0:T(8,128)(2,1)}, bf16[1,112,1472]{2,1,0:T(8,128)(2,1)}, bf16[1,112,1472]{2,1,0:T(8,128)(2,1)}, bf16[2,112,1472]{2,1,0:T(8,128)...) custom-call(bf16[6,112,1472]{2,1,0:T(8,128)(2,1)} %copy-done.138, ...), custom_call_target="tpu_custom_call" | custom-call | flops 3000000000 | bytes 9000000 | tf_op jit(solution)/shard_map/fuse/pallas_call | solution.py:776
  412.0 1.6 collective-permute-start.44
  413.6 2.7 copy-done.8
  419.8 8.2 %kv_weights.1 = (bf16[384,1472]{1,0:T(8,128)(2,1)S(1)}, bf16[384,1472]{1,0:T(8,128)(2,1)S(1)}) custom-call(s32[4]{0:T(128)S(1)} %pad_add_fusion.place, bf16[2,4,1472,256]{3,2,1,0:T(8,128)(2,1)S(1)} %bitcast.261, bf16[2,256,768]{2,1,0:T(8,128)(2,1)S(1)} %copy-done.66, bf16[2,256,768]{2,1,0:T(8,128)(2,1)S(1)} %copy-done.14, ...), custom_call_target="tpu_custom_call" | custom-call | flops 8999999488 | bytes 27000000 | tf_op jit(solution)/shard_map/kv_weights/pallas_call | solution.py:519
  428.0 8.1 %collective-permute-done.44.refs_6_ = bf16[1,112,1472]{2,1,0:T(8,128)(2,1)S(1)} collective-permute-done((bf16[1,112,1472]{2,1,0:T(8,128)(2,1)}, bf16[1,112,1472]{2,1,0:T(8,128)(2,1)S(1)}, u32[]{:S(2)}, u32[]{:S(2)}) %collective-permute-start.44) | collective-permute-done | bytes 329760 | tf_op jit(solution)/shard_map/ppermute | solution.py:62
  436.0 5.9 %collective-permute-done.41.refs_0_ = bf16[2,112,1472]{2,1,0:T(8,128)(2,1)S(1)} collective-permute-done((bf16[2,112,1472]{2,1,0:T(8,128)(2,1)}, bf16[2,112,1472]{2,1,0:T(8,128)(2,1)S(1)}, u32[]{:S(2)}, u32[]{:S(2)}) %collective-permute-start.41) | collective-permute-done | bytes 659488 | tf_op jit(solution)/shard_map/ppermute | solution.py:57
  442.0 2.2 columns.1
  446.6 2.1 collective-permute-start.48
  448.8 1.6 collective-permute-start.47
  451.7 1.6 pad_maximum_fusion
  458.6 10.3 %kv_memory.1 = f32[2,4,1472,256]{3,2,1,0:T(8,128)} custom-call(s32[4]{0:T(128)S(1)} %pad_add_fusion.place, bf16[384,1472]{1,0:T(8,128)(2,1)S(1)} %bitcast.267, bf16[384,1472]{1,0:T(8,128)(2,1)S(1)} %bitcast.269, bf16[2,256,768]{2,1,0:T(8,128)(2,1)S(1)} %copy-done.67, bf16[2,256,768]{2,1,0:T(8,128)(2,1)S(1)} %copy-done.15, ...), custom_call_target="tpu_custom_call" | custom-call | flops 10000000000 | bytes 30000000 | tf_op jit(solution)/shard_map/kv_memory/pallas_call | solution.py:539
  471.3 3.7 copy.110
  475.0 4.8 convert_add_fusion
  479.8 3.6 copy.109
  484.9 2.1 collective-permute-start.52
  487.1 1.7 add_convert_fusion.1
  489.7 3.0 collective-permute-start.50
  492.7 1.9 collective-permute-start.51
  494.7 9.2 %collective-permute-done.49 = bf16[64,1472]{1,0:T(8,128)(2,1)S(1)} collective-permute-done((bf16[64,1472]{1,0:T(8,128)(2,1)S(1)}, bf16[64,1472]{1,0:T(8,128)(2,1)S(1)}, u32[]{:S(2)}, u32[]{:S(2)}) %collective-permute-start.49) | collective-permute-done | bytes 188448 | tf_op jit(solution)/shard_map/ppermute | solution.py:71
  503.9 2.1 collective-permute-done.50
  506.1 2.4 collective-permute-done.51
  518.6 2.0 bitcast_convert_fusion
  520.7 21.0 %collective-permute-done.57 = bf16[64,1472]{1,0:T(8,128)(2,1)S(1)} collective-permute-done((bf16[64,1472]{1,0:T(8,128)(2,1)S(1)}, bf16[64,1472]{1,0:T(8,128)(2,1)S(1)}, u32[]{:S(2)}, u32[]{:S(2)}) %collective-permute-start.57) | collective-permute-done | bytes 188448 | tf_op jit(solution)/shard_map/ppermute | solution.py:62
  546.0 2.0 bitcast_convert_fusion.1
  548.5 2.0 bitcast_convert_fusion.2
  552.0 5.2 collective-permute-done.60
  (517 shorter events, 118.2 us)
Async XLA Ops:
  7.2 502.0 %reduce-scatter.5.cloned.1.call-start = ((), (), s32[]{:S(2)}) async-start(), calls=%async_computation.3 | async-start | bytes 2654208 | tf_op jit(solution)/shard_map/reduce_scatter | solution.py:1201
  11.9 28.6 %collective-permute-start = (bf16[2,48,1472]{2,1,0:T(8,128)(2,1)}, bf16[2,48,1472]{2,1,0:T(8,128)(2,1)S(1)}, u32[]{:S(2)}, u32[]{:S(2)}) collective-permute-start(bf16[2,48,1472]{2,1,0:T(8,128)(2,1)} %pad_maximum_fusion.29), channel_id=1, source_target_pairs={{0,8},{4,12},{8,16},{12,20},{16,24},{20,28},{24,0},{28,4},{1,9},{5... | collective-permute-start | bytes 847880 | tf_op jit(solution)/shard_map/ppermute | solution.py:71
  13.5 27.0 %collective-permute-start.1 = (bf16[2,48,1472]{2,1,0:T(8,128)(2,1)}, bf16[2,48,1472]{2,1,0:T(8,128)(2,1)S(1)}, u32[]{:S(2)}, u32[]{:S(2)}) collective-permute-start(bf16[2,48,1472]{2,1,0:T(8,128)(2,1)} %pad_maximum_fusion.29), channel_id=1, source_target_pairs={{0,16},{4,20},{8,24},{12,28},{16,0},{20,4},{24,8},{28,12},{1,17},{... | collective-permute-start | bytes 847880 | tf_op jit(solution)/shard_map/ppermute | solution.py:71
  14.5 26.2 %collective-permute-start.2 = (bf16[2,48,1472]{2,1,0:T(8,128)(2,1)}, bf16[2,48,1472]{2,1,0:T(8,128)(2,1)S(1)}, u32[]{:S(2)}, u32[]{:S(2)}) collective-permute-start(bf16[2,48,1472]{2,1,0:T(8,128)(2,1)} %pad_maximum_fusion.29), channel_id=1, source_target_pairs={{0,24},{4,28},{8,0},{12,4},{16,8},{20,12},{24,16},{28,20},{1,25},{... | collective-permute-start | bytes 847880 | tf_op jit(solution)/shard_map/ppermute | solution.py:71
  18.3 22.5 %collective-permute-start.3 = (bf16[8,64,1472]{2,1,0:T(8,128)(2,1)S(1)}, bf16[8,64,1472]{2,1,0:T(8,128)(2,1)}, u32[]{:S(2)}, u32[]{:S(2)}) collective-permute-start(bf16[8,64,1472]{2,1,0:T(8,128)(2,1)S(1)} %bitcast.298), channel_id=1, source_target_pairs={{0,4},{4,0},{8,12},{12,8},{16,20},{20,16},{24,28},{28,24},{1,5},{5... | collective-permute-start | bytes 4521992 | tf_op jit(solution)/shard_map/ppermute | solution.py:48
  40.7 17.5 %collective-permute-start.6 = (bf16[2,112,1472]{2,1,0:T(8,128)(2,1)S(1)}, bf16[2,112,1472]{2,1,0:T(8,128)(2,1)}, u32[]{:S(2)}, u32[]{:S(2)}) collective-permute-start(bf16[2,112,1472]{2,1,0:T(8,128)(2,1)S(1)} %pad_maximum_fusion.15), channel_id=1, source_target_pairs={{0,8},{4,12},{8,16},{12,20},{16,24},{20,28},{24,0},{28,4},{1,9},{5... | collective-permute-start | bytes 1978376 | tf_op jit(solution)/shard_map/ppermute | solution.py:57
  40.9 12.1 %collective-permute-start.4 = (bf16[1,3,48,1472]{3,2,1,0:T(8,128)(2,1)S(1)}, bf16[1,3,48,1472]{3,2,1,0:T(8,128)(2,1)S(1)}, u32[]{:S(2)}, u32[]{:S(2)}) collective-permute-start(bf16[1,3,48,1472]{3,2,1,0:T(8,128)(2,1)S(1)} %bitcast.251), channel_id=1, source_target_pairs={{0,1},{1,0},{2,3},{3,2},{4,5},{5,4},{6,7},{7,6},{8,9},{9,8},{10,11... | collective-permute-start | bytes 1271816 | tf_op jit(solution)/shard_map/ppermute | solution.py:62
  42.5 11.7 %collective-permute-start.5 = (bf16[1,3,48,1472]{3,2,1,0:T(8,128)(2,1)S(1)}, bf16[1,3,48,1472]{3,2,1,0:T(8,128)(2,1)S(1)}, u32[]{:S(2)}, u32[]{:S(2)}) collective-permute-start(bf16[1,3,48,1472]{3,2,1,0:T(8,128)(2,1)S(1)} %bitcast.248), channel_id=1, source_target_pairs={{0,2},{1,3},{2,0},{3,1},{4,6},{5,7},{6,4},{7,5},{8,10},{9,11},{10,... | collective-permute-start | bytes 1271816 | tf_op jit(solution)/shard_map/ppermute | solution.py:62
  59.2 21.0 %collective-permute-start.8 = (bf16[2,3,48,1472]{3,2,1,0:T(8,128)(2,1)}, bf16[2,3,48,1472]{3,2,1,0:T(8,128)(2,1)}, u32[]{:S(2)}, u32[]{:S(2)}) collective-permute-start(bf16[2,3,48,1472]{3,2,1,0:T(8,128)(2,1)} %pad_maximum_fusion.14), channel_id=1, source_target_pairs={{0,1},{1,0},{2,3},{3,2},{4,5},{5,4},{6,7},{7,6},{8,9},{9,8},{10,11... | collective-permute-start | bytes 2543624 | tf_op jit(solution)/shard_map/ppermute | solution.py:62
  61.7 20.8 %collective-permute-start.7 = (bf16[2,3,48,1472]{3,2,1,0:T(8,128)(2,1)}, bf16[2,3,48,1472]{3,2,1,0:T(8,128)(2,1)}, u32[]{:S(2)}, u32[]{:S(2)}) collective-permute-start(bf16[2,3,48,1472]{3,2,1,0:T(8,128)(2,1)} %pad_maximum_fusion.13), channel_id=1, source_target_pairs={{0,2},{1,3},{2,0},{3,1},{4,6},{5,7},{6,4},{7,5},{8,10},{9,11},{10,... | collective-permute-start | bytes 2543624 | tf_op jit(solution)/shard_map/ppermute | solution.py:62
  63.2 16.3 %collective-permute-start.9 = (bf16[2,112,1472]{2,1,0:T(8,128)(2,1)}, bf16[2,112,1472]{2,1,0:T(8,128)(2,1)}, u32[]{:S(2)}, u32[]{:S(2)}) collective-permute-start(bf16[2,112,1472]{2,1,0:T(8,128)(2,1)} %collective-permute-done.6), channel_id=1, source_target_pairs={{0,8},{4,12},{8,16},{12,20},{16,24},{20,28},{24,0},{28,4},{1,9},{5... | collective-permute-start | bytes 1978376 | tf_op jit(solution)/shard_map/ppermute | solution.py:57
  84.1 22.1 %collective-permute-start.10 = (bf16[4,4,48,1472]{3,2,1,0:T(8,128)(2,1)S(1)}, bf16[4,4,48,1472]{3,2,1,0:T(8,128)(2,1)S(1)}, u32[]{:S(2)}, u32[]{:S(2)}) collective-permute-start(bf16[4,4,48,1472]{3,2,1,0:T(8,128)(2,1)S(1)} %maximum_maximum_fusion.own), channel_id=1, source_target_pairs={{0,4},{4,0},{8,12},{12,8},{16,20},{20,16},{24,28},{28,24},{1,5},{5... | collective-permute-start | bytes 6782984 | tf_op jit(solution)/shard_map/ppermute | solution.py:48
  85.3 20.9 %collective-permute-start.13 = (bf16[2,112,1472]{2,1,0:T(8,128)(2,1)}, bf16[2,112,1472]{2,1,0:T(8,128)(2,1)S(1)}, u32[]{:S(2)}, u32[]{:S(2)}) collective-permute-start(bf16[2,112,1472]{2,1,0:T(8,128)(2,1)} %collective-permute-done.9), channel_id=1, source_target_pairs={{0,8},{4,12},{8,16},{12,20},{16,24},{20,28},{24,0},{28,4},{1,9},{5... | collective-permute-start | bytes 1978376 | tf_op jit(solution)/shard_map/ppermute | solution.py:57
  87.0 17.6 %collective-permute-start.12 = (bf16[1,2,112,1472]{3,2,1,0:T(8,128)(2,1)S(1)}, bf16[1,2,112,1472]{3,2,1,0:T(8,128)(2,1)S(1)}, u32[]{:S(2)}, u32[]{:S(2)}) collective-permute-start(bf16[1,2,112,1472]{3,2,1,0:T(8,128)(2,1)S(1)} %maximum_bitcast_fusion.1), channel_id=1, source_target_pairs={{0,2},{1,3},{2,0},{3,1},{4,6},{5,7},{6,4},{7,5},{8,10},{9,11},{10,... | collective-permute-start | bytes 1978376 | tf_op jit(solution)/shard_map/ppermute | solution.py:62
  88.8 17.3 %collective-permute-start.11 = (bf16[1,2,112,1472]{3,2,1,0:T(8,128)(2,1)S(1)}, bf16[1,2,112,1472]{3,2,1,0:T(8,128)(2,1)S(1)}, u32[]{:S(2)}, u32[]{:S(2)}) collective-permute-start(bf16[1,2,112,1472]{3,2,1,0:T(8,128)(2,1)S(1)} %maximum_bitcast_fusion), channel_id=1, source_target_pairs={{0,1},{1,0},{2,3},{3,2},{4,5},{5,4},{6,7},{7,6},{8,9},{9,8},{10,11... | collective-permute-start | bytes 1978376 | tf_op jit(solution)/shard_map/ppermute | solution.py:62
  106.1 16.5 %collective-permute-start.14 = (bf16[4,4,48,1472]{3,2,1,0:T(8,128)(2,1)S(1)}, bf16[4,4,48,1472]{3,2,1,0:T(8,128)(2,1)S(1)}, u32[]{:S(2)}, u32[]{:S(2)}) collective-permute-start(bf16[4,4,48,1472]{3,2,1,0:T(8,128)(2,1)S(1)} %maximum_maximum_fusion.1.own), channel_id=1, source_target_pairs={{0,4},{4,0},{8,12},{12,8},{16,20},{20,16},{24,28},{28,24},{1,5},{5... | collective-permute-start | bytes 6782984 | tf_op jit(solution)/shard_map/ppermute | solution.py:48
  106.3 16.3 %collective-permute-start.15 = (bf16[1,112,1472]{2,1,0:T(8,128)(2,1)S(1)}, bf16[1,112,1472]{2,1,0:T(8,128)(2,1)S(1)}, u32[]{:S(2)}, u32[]{:S(2)}) collective-permute-start(bf16[1,112,1472]{2,1,0:T(8,128)(2,1)S(1)} %get-tuple-element.598), channel_id=1, source_target_pairs={{0,1},{1,0},{2,3},{3,2},{4,5},{5,4},{6,7},{7,6},{8,9},{9,8},{10,11... | collective-permute-start | bytes 989192 | tf_op jit(solution)/shard_map/ppermute | solution.py:62
  106.8 15.8 %collective-permute-start.16 = (bf16[1,112,1472]{2,1,0:T(8,128)(2,1)S(1)}, bf16[1,112,1472]{2,1,0:T(8,128)(2,1)S(1)}, u32[]{:S(2)}, u32[]{:S(2)}) collective-permute-start(bf16[1,112,1472]{2,1,0:T(8,128)(2,1)S(1)} %get-tuple-element.597), channel_id=1, source_target_pairs={{0,2},{1,3},{2,0},{3,1},{4,6},{5,7},{6,4},{7,5},{8,10},{9,11},{10,... | collective-permute-start | bytes 989192 | tf_op jit(solution)/shard_map/ppermute | solution.py:62
  124.1 38.6 %collective-permute-start.20 = (bf16[4,112,1472]{2,1,0:T(8,128)(2,1)S(1)}, bf16[4,112,1472]{2,1,0:T(8,128)(2,1)}, u32[]{:S(2)}, u32[]{:S(2)}) collective-permute-start(bf16[4,112,1472]{2,1,0:T(8,128)(2,1)S(1)} %copy-done.100), channel_id=1, source_target_pairs={{0,8},{4,12},{8,16},{12,20},{16,24},{20,28},{24,0},{28,4},{1,9},{5... | collective-permute-start | bytes 3956744 | tf_op jit(solution)/shard_map/ppermute | solution.py:57
  124.6 23.0 %collective-permute-start.17 = (bf16[2,256,768]{2,1,0:T(8,128)(2,1)}, bf16[2,256,768]{2,1,0:T(8,128)(2,1)S(1)}, u32[]{:S(2)}, u32[]{:S(2)}) collective-permute-start(bf16[2,256,768]{2,1,0:T(8,128)(2,1)} %get-tuple-element.261), channel_id=1, source_target_pairs={{0,1},{1,0},{2,3},{3,2},{4,5},{5,4},{6,7},{7,6},{8,9},{9,8},{10,11... | collective-permute-start | bytes 2359304 | tf_op jit(solution)/shard_map/ppermute | solution.py:62
  126.2 36.5 %collective-permute-start.18 = (bf16[2,256,768]{2,1,0:T(8,128)(2,1)S(1)}, bf16[2,256,768]{2,1,0:T(8,128)(2,1)S(1)}, u32[]{:S(2)}, u32[]{:S(2)}) collective-permute-start(bf16[2,256,768]{2,1,0:T(8,128)(2,1)S(1)} %get-tuple-element.262), channel_id=1, source_target_pairs={{0,2},{1,3},{2,0},{3,1},{4,6},{5,7},{6,4},{7,5},{8,10},{9,11},{10,... | collective-permute-start | bytes 2359304 | tf_op jit(solution)/shard_map/ppermute | solution.py:62
  127.0 35.7 %collective-permute-start.19 = (bf16[2,256,768]{2,1,0:T(8,128)(2,1)S(1)}, bf16[2,256,768]{2,1,0:T(8,128)(2,1)S(1)}, u32[]{:S(2)}, u32[]{:S(2)}) collective-permute-start(bf16[2,256,768]{2,1,0:T(8,128)(2,1)S(1)} %get-tuple-element.263), channel_id=1, source_target_pairs={{0,3},{1,2},{2,1},{3,0},{4,7},{5,6},{6,5},{7,4},{8,11},{9,10},{10,... | collective-permute-start | bytes 2359304 | tf_op jit(solution)/shard_map/ppermute | solution.py:62
  162.7 31.5 %collective-permute-start.21 = (bf16[2,2,112,1472]{3,2,1,0:T(8,128)(2,1)S(1)}, bf16[2,2,112,1472]{3,2,1,0:T(8,128)(2,1)S(1)}, u32[]{:S(2)}, u32[]{:S(2)}) collective-permute-start(bf16[2,2,112,1472]{3,2,1,0:T(8,128)(2,1)S(1)} %copy-done.102), channel_id=1, source_target_pairs={{0,2},{1,3},{2,0},{3,1},{4,6},{5,7},{6,4},{7,5},{8,10},{9,11},{10,... | collective-permute-start | bytes 3956744 | tf_op jit(solution)/shard_map/ppermute | solution.py:62
  163.1 31.4 %collective-permute-start.22 = (bf16[2,2,112,1472]{3,2,1,0:T(8,128)(2,1)S(1)}, bf16[2,2,112,1472]{3,2,1,0:T(8,128)(2,1)S(1)}, u32[]{:S(2)}, u32[]{:S(2)}) collective-permute-start(bf16[2,2,112,1472]{3,2,1,0:T(8,128)(2,1)S(1)} %copy-done.101), channel_id=1, source_target_pairs={{0,1},{1,0},{2,3},{3,2},{4,5},{5,4},{6,7},{7,6},{8,9},{9,8},{10,11... | collective-permute-start | bytes 3956744 | tf_op jit(solution)/shard_map/ppermute | solution.py:62
  164.7 31.5 %collective-permute-start.23 = (bf16[4,112,1472]{2,1,0:T(8,128)(2,1)}, bf16[4,112,1472]{2,1,0:T(8,128)(2,1)}, u32[]{:S(2)}, u32[]{:S(2)}) collective-permute-start(bf16[4,112,1472]{2,1,0:T(8,128)(2,1)} %collective-permute-done.20), channel_id=1, source_target_pairs={{0,8},{4,12},{8,16},{12,20},{16,24},{20,28},{24,0},{28,4},{1,9},{5... | collective-permute-start | bytes 3956744 | tf_op jit(solution)/shard_map/ppermute | solution.py:57
  196.2 5.3 collective-permute-start.24
  199.3 42.6 %collective-permute-start.27 = (bf16[4,112,1472]{2,1,0:T(8,128)(2,1)}, bf16[4,112,1472]{2,1,0:T(8,128)(2,1)S(1)}, u32[]{:S(2)}, u32[]{:S(2)}) collective-permute-start(bf16[4,112,1472]{2,1,0:T(8,128)(2,1)} %collective-permute-done.23), channel_id=1, source_target_pairs={{0,8},{4,12},{8,16},{12,20},{16,24},{20,28},{24,0},{28,4},{1,9},{5... | collective-permute-start | bytes 3956744 | tf_op jit(solution)/shard_map/ppermute | solution.py:57
  200.3 41.6 %collective-permute-start.25 = (bf16[2,112,1472]{2,1,0:T(8,128)(2,1)}, bf16[2,112,1472]{2,1,0:T(8,128)(2,1)S(1)}, u32[]{:S(2)}, u32[]{:S(2)}) collective-permute-start(bf16[2,112,1472]{2,1,0:T(8,128)(2,1)} %pad_maximum_fusion.16.refs_4_.refs_9_), channel_id=1, source_target_pairs={{0,2},{1,3},{2,0},{3,1},{4,6},{5,7},{6,4},{7,5},{8,10},{9,11},{10,... | collective-permute-start | bytes 1978376 | tf_op jit(solution)/shard_map/ppermute | solution.py:62
  200.6 41.2 %collective-permute-start.26 = (bf16[2,112,1472]{2,1,0:T(8,128)(2,1)}, bf16[2,112,1472]{2,1,0:T(8,128)(2,1)S(1)}, u32[]{:S(2)}, u32[]{:S(2)}) collective-permute-start(bf16[2,112,1472]{2,1,0:T(8,128)(2,1)} %pad_maximum_fusion.17.refs_6_.refs_11_), channel_id=1, source_target_pairs={{0,1},{1,0},{2,3},{3,2},{4,5},{5,4},{6,7},{7,6},{8,9},{9,8},{10,11... | collective-permute-start | bytes 1978376 | tf_op jit(solution)/shard_map/ppermute | solution.py:62
  243.0 54.7 %collective-permute-start.28 = (bf16[3,2,112,1472]{3,2,1,0:T(8,128)(2,1)}, bf16[3,2,112,1472]{3,2,1,0:T(8,128)(2,1)S(1)}, u32[]{:S(2)}, u32[]{:S(2)}) collective-permute-start(bf16[3,2,112,1472]{3,2,1,0:T(8,128)(2,1)} %get-tuple-element.322), channel_id=1, source_target_pairs={{0,2},{1,3},{2,0},{3,1},{4,6},{5,7},{6,4},{7,5},{8,10},{9,11},{10,... | collective-permute-start | bytes 5935112 | tf_op jit(solution)/shard_map/ppermute | solution.py:62
  244.3 53.5 %collective-permute-start.29 = (bf16[3,2,112,1472]{3,2,1,0:T(8,128)(2,1)}, bf16[3,2,112,1472]{3,2,1,0:T(8,128)(2,1)S(1)}, u32[]{:S(2)}, u32[]{:S(2)}) collective-permute-start(bf16[3,2,112,1472]{3,2,1,0:T(8,128)(2,1)} %get-tuple-element.323), channel_id=1, source_target_pairs={{0,1},{1,0},{2,3},{3,2},{4,5},{5,4},{6,7},{7,6},{8,9},{9,8},{10,11... | collective-permute-start | bytes 5935112 | tf_op jit(solution)/shard_map/ppermute | solution.py:62
  245.8 51.9 %collective-permute-start.30 = (bf16[448,1472]{1,0:T(8,128)(2,1)}, bf16[448,1472]{1,0:T(8,128)(2,1)S(1)}, u32[]{:S(2)}, u32[]{:S(2)}) collective-permute-start(bf16[448,1472]{1,0:T(8,128)(2,1)} %get-tuple-element.324), channel_id=1, source_target_pairs={{0,8},{4,12},{8,16},{12,20},{16,24},{20,28},{24,0},{28,4},{1,9},{5... | collective-permute-start | bytes 3956744 | tf_op jit(solution)/shard_map/ppermute | solution.py:57
  297.8 9.2 %collective-permute-start.34 = (bf16[8,64,1472]{2,1,0:T(8,128)(2,1)}, bf16[8,64,1472]{2,1,0:T(8,128)(2,1)S(1)}, u32[]{:S(2)}, u32[]{:S(2)}) collective-permute-start(bf16[8,64,1472]{2,1,0:T(8,128)(2,1)} %bitcast.330), channel_id=1, source_target_pairs={{0,4},{4,0},{8,12},{12,8},{16,20},{20,16},{24,28},{28,24},{1,5},{5... | collective-permute-start | bytes 4521992 | tf_op jit(solution)/shard_map/ppermute | solution.py:48
  299.3 41.3 %collective-permute-start.33 = (bf16[448,1472]{1,0:T(8,128)(2,1)}, bf16[448,1472]{1,0:T(8,128)(2,1)S(1)}, u32[]{:S(2)}, u32[]{:S(2)}) collective-permute-start(bf16[448,1472]{1,0:T(8,128)(2,1)} %add_convert_fusion), channel_id=1, source_target_pairs={{0,8},{4,12},{8,16},{12,20},{16,24},{20,28},{24,0},{28,4},{1,9},{5... | collective-permute-start | bytes 3956744 | tf_op jit(solution)/shard_map/ppermute | solution.py:57
  305.1 39.7 %collective-permute-start.31 = (bf16[5,112,1472]{2,1,0:T(8,128)(2,1)S(1)}, bf16[5,112,1472]{2,1,0:T(8,128)(2,1)S(1)}, u32[]{:S(2)}, u32[]{:S(2)}) collective-permute-start(bf16[5,112,1472]{2,1,0:T(8,128)(2,1)S(1)} %get-tuple-element.336), channel_id=1, source_target_pairs={{0,2},{1,3},{2,0},{3,1},{4,6},{5,7},{6,4},{7,5},{8,10},{9,11},{10,... | collective-permute-start | bytes 4945928 | tf_op jit(solution)/shard_map/ppermute | solution.py:62
  305.5 39.4 %collective-permute-start.32 = (bf16[5,112,1472]{2,1,0:T(8,128)(2,1)S(1)}, bf16[5,112,1472]{2,1,0:T(8,128)(2,1)S(1)}, u32[]{:S(2)}, u32[]{:S(2)}) collective-permute-start(bf16[5,112,1472]{2,1,0:T(8,128)(2,1)S(1)} %get-tuple-element.337), channel_id=1, source_target_pairs={{0,1},{1,0},{2,3},{3,2},{4,5},{5,4},{6,7},{7,6},{8,9},{9,8},{10,11... | collective-permute-start | bytes 4945928 | tf_op jit(solution)/shard_map/ppermute | solution.py:62
  350.8 46.2 %collective-permute-start.38 = (bf16[6,112,1472]{2,1,0:T(8,128)(2,1)S(1)}, bf16[6,112,1472]{2,1,0:T(8,128)(2,1)S(1)}, u32[]{:S(2)}, u32[]{:S(2)}) collective-permute-start(bf16[6,112,1472]{2,1,0:T(8,128)(2,1)S(1)} %get-tuple-element.360), channel_id=1, source_target_pairs={{0,8},{4,12},{8,16},{12,20},{16,24},{20,28},{24,0},{28,4},{1,9},{5... | collective-permute-start | bytes 5935112 | tf_op jit(solution)/shard_map/ppermute | solution.py:57
  351.1 38.0 %collective-permute-start.39 = (bf16[8,64,1472]{2,1,0:T(8,128)(2,1)}, bf16[8,64,1472]{2,1,0:T(8,128)(2,1)}, u32[]{:S(2)}, u32[]{:S(2)}) collective-permute-start(bf16[8,64,1472]{2,1,0:T(8,128)(2,1)} %bitcast.72), channel_id=1, source_target_pairs={{0,4},{4,0},{8,12},{12,8},{16,20},{20,16},{24,28},{28,24},{1,5},{5... | collective-permute-start | bytes 4521992 | tf_op jit(solution)/shard_map/ppermute | solution.py:48
  351.1 24.4 %collective-permute-start.35 = (bf16[2,256,768]{2,1,0:T(8,128)(2,1)}, bf16[2,256,768]{2,1,0:T(8,128)(2,1)S(1)}, u32[]{:S(2)}, u32[]{:S(2)}) collective-permute-start(bf16[2,256,768]{2,1,0:T(8,128)(2,1)} %get-tuple-element.351), channel_id=1, source_target_pairs={{0,1},{1,0},{2,3},{3,2},{4,5},{5,4},{6,7},{7,6},{8,9},{9,8},{10,11... | collective-permute-start | bytes 2359304 | tf_op jit(solution)/shard_map/ppermute | solution.py:62
  352.3 23.2 %collective-permute-start.36 = (bf16[2,256,768]{2,1,0:T(8,128)(2,1)}, bf16[2,256,768]{2,1,0:T(8,128)(2,1)S(1)}, u32[]{:S(2)}, u32[]{:S(2)}) collective-permute-start(bf16[2,256,768]{2,1,0:T(8,128)(2,1)} %copy-done.27), channel_id=1, source_target_pairs={{0,2},{1,3},{2,0},{3,1},{4,6},{5,7},{6,4},{7,5},{8,10},{9,11},{10,... | collective-permute-start | bytes 2359304 | tf_op jit(solution)/shard_map/ppermute | solution.py:62
  353.0 36.1 %collective-permute-start.37 = (bf16[2,256,768]{2,1,0:T(8,128)(2,1)S(1)}, bf16[2,256,768]{2,1,0:T(8,128)(2,1)S(1)}, u32[]{:S(2)}, u32[]{:S(2)}) collective-permute-start(bf16[2,256,768]{2,1,0:T(8,128)(2,1)S(1)} %copy-done.26), channel_id=1, source_target_pairs={{0,3},{1,2},{2,1},{3,0},{4,7},{5,6},{6,5},{7,4},{8,11},{9,10},{10,... | collective-permute-start | bytes 2359304 | tf_op jit(solution)/shard_map/ppermute | solution.py:62
  399.0 110.1 %reduce-scatter.3.cloned.1.call-start = ((), (), s32[]{:S(2)}) async-start(), calls=%async_computation.2 | async-start | bytes 2654208 | tf_op jit(solution)/shard_map/reduce_scatter | solution.py:1201
  403.9 38.1 %collective-permute-start.40 = (bf16[4,4,48,1472]{3,2,1,0:T(8,128)(2,1)}, bf16[4,4,48,1472]{3,2,1,0:T(8,128)(2,1)S(1)}, u32[]{:S(2)}, u32[]{:S(2)}) collective-permute-start(bf16[4,4,48,1472]{3,2,1,0:T(8,128)(2,1)} %get-tuple-element.376), channel_id=1, source_target_pairs={{0,4},{4,0},{8,12},{12,8},{16,20},{20,16},{24,28},{28,24},{1,5},{5... | collective-permute-start | bytes 6782984 | tf_op jit(solution)/shard_map/ppermute | solution.py:48
  409.8 32.2 %collective-permute-start.41 = (bf16[2,112,1472]{2,1,0:T(8,128)(2,1)}, bf16[2,112,1472]{2,1,0:T(8,128)(2,1)S(1)}, u32[]{:S(2)}, u32[]{:S(2)}) collective-permute-start(bf16[2,112,1472]{2,1,0:T(8,128)(2,1)} %get-tuple-element.383), channel_id=1, source_target_pairs={{0,8},{4,12},{8,16},{12,20},{16,24},{20,28},{24,0},{28,4},{1,9},{5... | collective-permute-start | bytes 1978376 | tf_op jit(solution)/shard_map/ppermute | solution.py:57
  410.1 31.8 %collective-permute-start.42 = (bf16[2,112,1472]{2,1,0:T(8,128)(2,1)}, bf16[2,112,1472]{2,1,0:T(8,128)(2,1)S(1)}, u32[]{:S(2)}, u32[]{:S(2)}) collective-permute-start(bf16[2,112,1472]{2,1,0:T(8,128)(2,1)} %get-tuple-element.384), channel_id=1, source_target_pairs={{0,1},{1,0},{2,3},{3,2},{4,5},{5,4},{6,7},{7,6},{8,9},{9,8},{10,11... | collective-permute-start | bytes 1978376 | tf_op jit(solution)/shard_map/ppermute | solution.py:62
  411.3 30.7 %collective-permute-start.43 = (bf16[2,112,1472]{2,1,0:T(8,128)(2,1)}, bf16[2,112,1472]{2,1,0:T(8,128)(2,1)S(1)}, u32[]{:S(2)}, u32[]{:S(2)}) collective-permute-start(bf16[2,112,1472]{2,1,0:T(8,128)(2,1)} %get-tuple-element.385), channel_id=1, source_target_pairs={{0,2},{1,3},{2,0},{3,1},{4,6},{5,7},{6,4},{7,5},{8,10},{9,11},{10,... | collective-permute-start | bytes 1978376 | tf_op jit(solution)/shard_map/ppermute | solution.py:62
  412.0 24.0 %collective-permute-start.44 = (bf16[1,112,1472]{2,1,0:T(8,128)(2,1)}, bf16[1,112,1472]{2,1,0:T(8,128)(2,1)S(1)}, u32[]{:S(2)}, u32[]{:S(2)}) collective-permute-start(bf16[1,112,1472]{2,1,0:T(8,128)(2,1)} %get-tuple-element.386), channel_id=1, source_target_pairs={{0,3},{1,2},{2,1},{3,0},{4,7},{5,6},{6,5},{7,4},{8,11},{9,10},{10,... | collective-permute-start | bytes 989192 | tf_op jit(solution)/shard_map/ppermute | solution.py:62
  444.2 24.7 %collective-permute-start.45 = (bf16[4,48,1472]{2,1,0:T(8,128)(2,1)S(1)}, bf16[4,48,1472]{2,1,0:T(8,128)(2,1)}, u32[]{:S(2)}, u32[]{:S(2)}) collective-permute-start(bf16[4,48,1472]{2,1,0:T(8,128)(2,1)S(1)} %get-tuple-element.393), channel_id=1, source_target_pairs={{0,1},{1,0},{2,3},{3,2},{4,5},{5,4},{6,7},{7,6},{8,9},{9,8},{10,11... | collective-permute-start | bytes 1695752 | tf_op jit(solution)/shard_map/ppermute | solution.py:62
  446.6 36.9 %collective-permute-start.48 = (bf16[2,112,1472]{2,1,0:T(8,128)(2,1)}, bf16[2,112,1472]{2,1,0:T(8,128)(2,1)}, u32[]{:S(2)}, u32[]{:S(2)}) collective-permute-start(bf16[2,112,1472]{2,1,0:T(8,128)(2,1)} %get-tuple-element.407), channel_id=1, source_target_pairs={{0,8},{4,12},{8,16},{12,20},{16,24},{20,28},{24,0},{28,4},{1,9},{5... | collective-permute-start | bytes 1978376 | tf_op jit(solution)/shard_map/ppermute | solution.py:57
  448.7 34.8 %collective-permute-start.46 = (bf16[4,48,1472]{2,1,0:T(8,128)(2,1)}, bf16[4,48,1472]{2,1,0:T(8,128)(2,1)}, u32[]{:S(2)}, u32[]{:S(2)}) collective-permute-start(bf16[4,48,1472]{2,1,0:T(8,128)(2,1)} %get-tuple-element.398), channel_id=1, source_target_pairs={{0,2},{1,3},{2,0},{3,1},{4,6},{5,7},{6,4},{7,5},{8,10},{9,11},{10,... | collective-permute-start | bytes 1695752 | tf_op jit(solution)/shard_map/ppermute | solution.py:62
  448.8 34.7 %collective-permute-start.47 = (bf16[4,48,1472]{2,1,0:T(8,128)(2,1)}, bf16[4,48,1472]{2,1,0:T(8,128)(2,1)}, u32[]{:S(2)}, u32[]{:S(2)}) collective-permute-start(bf16[4,48,1472]{2,1,0:T(8,128)(2,1)} %get-tuple-element.399), channel_id=1, source_target_pairs={{0,3},{1,2},{2,1},{3,0},{4,7},{5,6},{6,5},{7,4},{8,11},{9,10},{10,... | collective-permute-start | bytes 1695752 | tf_op jit(solution)/shard_map/ppermute | solution.py:62
  450.4 42.3 %collective-permute-start.54 = (bf16[1,112,1472]{2,1,0:T(8,128)(2,1)S(1)}, bf16[1,112,1472]{2,1,0:T(8,128)(2,1)}, u32[]{:S(2)}, u32[]{:S(2)}) collective-permute-start(bf16[1,112,1472]{2,1,0:T(8,128)(2,1)S(1)} %get-tuple-element.417.refs_2_), channel_id=1, source_target_pairs={{0,3},{1,2},{2,1},{3,0},{4,7},{5,6},{6,5},{7,4},{8,11},{9,10},{10,... | collective-permute-start | bytes 989192 | tf_op jit(solution)/shard_map/ppermute | solution.py:62
  484.9 23.5 %collective-permute-start.52 = (bf16[2,112,1472]{2,1,0:T(8,128)(2,1)S(1)}, bf16[2,112,1472]{2,1,0:T(8,128)(2,1)S(1)}, u32[]{:S(2)}, u32[]{:S(2)}) collective-permute-start(bf16[2,112,1472]{2,1,0:T(8,128)(2,1)S(1)} %get-tuple-element.424), channel_id=1, source_target_pairs={{0,1},{1,0},{2,3},{3,2},{4,5},{5,4},{6,7},{7,6},{8,9},{9,8},{10,11... | collective-permute-start | bytes 1978376 | tf_op jit(solution)/shard_map/ppermute | solution.py:62
  487.0 22.1 %collective-permute-start.53 = (bf16[2,112,1472]{2,1,0:T(8,128)(2,1)S(1)}, bf16[2,112,1472]{2,1,0:T(8,128)(2,1)S(1)}, u32[]{:S(2)}, u32[]{:S(2)}) collective-permute-start(bf16[2,112,1472]{2,1,0:T(8,128)(2,1)S(1)} %get-tuple-element.425), channel_id=1, source_target_pairs={{0,2},{1,3},{2,0},{3,1},{4,6},{5,7},{6,4},{7,5},{8,10},{9,11},{10,... | collective-permute-start | bytes 1978376 | tf_op jit(solution)/shard_map/ppermute | solution.py:62
  489.0 14.9 %collective-permute-start.49 = (bf16[64,1472]{1,0:T(8,128)(2,1)S(1)}, bf16[64,1472]{1,0:T(8,128)(2,1)S(1)}, u32[]{:S(2)}, u32[]{:S(2)}) collective-permute-start(bf16[64,1472]{1,0:T(8,128)(2,1)S(1)} %get-tuple-element.636), channel_id=1, source_target_pairs={{0,8},{4,12},{8,16},{12,20},{16,24},{20,28},{24,0},{28,4},{1,9},{5... | collective-permute-start | bytes 565256 | tf_op jit(solution)/shard_map/ppermute | solution.py:71
  489.7 16.4 %collective-permute-start.50 = (bf16[64,1472]{1,0:T(8,128)(2,1)S(1)}, bf16[64,1472]{1,0:T(8,128)(2,1)S(1)}, u32[]{:S(2)}, u32[]{:S(2)}) collective-permute-start(bf16[64,1472]{1,0:T(8,128)(2,1)S(1)} %get-tuple-element.637), channel_id=1, source_target_pairs={{0,16},{4,20},{8,24},{12,28},{16,0},{20,4},{24,8},{28,12},{1,17},{... | collective-permute-start | bytes 565256 | tf_op jit(solution)/shard_map/ppermute | solution.py:71
  492.7 15.8 %collective-permute-start.51 = (bf16[64,1472]{1,0:T(8,128)(2,1)S(1)}, bf16[64,1472]{1,0:T(8,128)(2,1)S(1)}, u32[]{:S(2)}, u32[]{:S(2)}) collective-permute-start(bf16[64,1472]{1,0:T(8,128)(2,1)S(1)} %get-tuple-element.635), channel_id=1, source_target_pairs={{0,24},{4,28},{8,0},{12,4},{16,8},{20,12},{24,16},{28,20},{1,25},{... | collective-permute-start | bytes 565256 | tf_op jit(solution)/shard_map/ppermute | solution.py:71
  514.9 26.8 %collective-permute-start.55 = (bf16[288,1472]{1,0:T(8,128)(2,1)S(1)}, bf16[288,1472]{1,0:T(8,128)(2,1)S(1)}, u32[]{:S(2)}, u32[]{:S(2)}) collective-permute-start(bf16[288,1472]{1,0:T(8,128)(2,1)S(1)} %get-tuple-element.439), channel_id=1, source_target_pairs={{0,1},{1,0},{2,3},{3,2},{4,5},{5,4},{6,7},{7,6},{8,9},{9,8},{10,11... | collective-permute-start | bytes 2543624 | tf_op jit(solution)/shard_map/ppermute | solution.py:62
  516.1 25.6 %collective-permute-start.56 = (bf16[288,1472]{1,0:T(8,128)(2,1)S(1)}, bf16[288,1472]{1,0:T(8,128)(2,1)S(1)}, u32[]{:S(2)}, u32[]{:S(2)}) collective-permute-start(bf16[288,1472]{1,0:T(8,128)(2,1)S(1)} %get-tuple-element.440), channel_id=1, source_target_pairs={{0,2},{1,3},{2,0},{3,1},{4,6},{5,7},{6,4},{7,5},{8,10},{9,11},{10,... | collective-permute-start | bytes 2543624 | tf_op jit(solution)/shard_map/ppermute | solution.py:62
  517.3 24.3 %collective-permute-start.57 = (bf16[64,1472]{1,0:T(8,128)(2,1)S(1)}, bf16[64,1472]{1,0:T(8,128)(2,1)S(1)}, u32[]{:S(2)}, u32[]{:S(2)}) collective-permute-start(bf16[64,1472]{1,0:T(8,128)(2,1)S(1)} %get-tuple-element.441), channel_id=1, source_target_pairs={{0,3},{1,2},{2,1},{3,0},{4,7},{5,6},{6,5},{7,4},{8,11},{9,10},{10,... | collective-permute-start | bytes 565256 | tf_op jit(solution)/shard_map/ppermute | solution.py:62
  541.9 10.1 %collective-permute-start.59 = (bf16[96,1472]{1,0:T(8,128)(2,1)S(1)}, bf16[96,1472]{1,0:T(8,128)(2,1)S(1)}, u32[]{:S(2)}, u32[]{:S(2)}) collective-permute-start(bf16[96,1472]{1,0:T(8,128)(2,1)S(1)} %pad_maximum_fusion.30), channel_id=1, source_target_pairs={{0,1},{1,0},{2,3},{3,2},{4,5},{5,4},{6,7},{7,6},{8,9},{9,8},{10,11... | collective-permute-start | bytes 847880 | tf_op jit(solution)/shard_map/ppermute | solution.py:62
  542.9 14.2 %collective-permute-start.60 = (bf16[96,1472]{1,0:T(8,128)(2,1)S(1)}, bf16[96,1472]{1,0:T(8,128)(2,1)S(1)}, u32[]{:S(2)}, u32[]{:S(2)}) collective-permute-start(bf16[96,1472]{1,0:T(8,128)(2,1)S(1)} %pad_maximum_fusion.30), channel_id=1, source_target_pairs={{0,2},{1,3},{2,0},{3,1},{4,6},{5,7},{6,4},{7,5},{8,10},{9,11},{10,... | collective-permute-start | bytes 847880 | tf_op jit(solution)/shard_map/ppermute | solution.py:62
  544.2 13.0 %collective-permute-start.61 = (bf16[96,1472]{1,0:T(8,128)(2,1)S(1)}, bf16[96,1472]{1,0:T(8,128)(2,1)S(1)}, u32[]{:S(2)}, u32[]{:S(2)}) collective-permute-start(bf16[96,1472]{1,0:T(8,128)(2,1)S(1)} %pad_maximum_fusion.30), channel_id=1, source_target_pairs={{0,3},{1,2},{2,1},{3,0},{4,7},{5,6},{6,5},{7,4},{8,11},{9,10},{10,... | collective-permute-start | bytes 847880 | tf_op jit(solution)/shard_map/ppermute | solution.py:62
  548.3 2.2 collective-permute-start.58
  (148 other events, 1338.2 us)
Sparse Core Ops, SparseCore 0:
  399.2 41.1 reduce-scatter.4
  453.5 36.3 reduce-scatter.2

commit v4 on v3

--- a/solution.py
+++ b/solution.py
@@ -654,7 +654,7 @@
             out[...] = down_grad
 
 
-def feed_grad(nf_a, nf_b, og_a, og_b, steps, block, mems):
+def feed_grad(nf_a, nf_b, og_a, og_b, steps, block, mems, price=13):
     rows, width = nf_a.shape
     weights, places = plan(steps)
     n = len(steps)
@@ -694,64 +694,59 @@
             pltpu.SemaphoreType.DMA((4,)),
         ],
         compiler_params=params(54),
-        cost_estimate=cost(13 * n),
+        cost_estimate=cost(price * n),
         name="feed_grad",
     )(nf_a, nf_b, og_a, og_b, *weights)
 
 
-def feed_out_kernel(places, act_places, count, act_count, *refs):
+def feed_sum_kernel(places, act_places, count, act_count, *refs):
     weights, acts = refs[:count], refs[count : count + act_count]
-    nfg_o, nfg_b, res_o, res_b, res_t, nfg_t, hold, acts_hold, sems, act_sems = refs[count + act_count :]
+    own_o, other_o, other, hold, acts_hold, sems, act_sems = refs[count + act_count :]
     step = pl.program_id(0)
-    rows = nfg_o.shape[0]
+    rows = own_o.shape[0]
     run_fetch(places, weights, hold, sems)
     run_fetch(act_places, acts, acts_hold, act_sems)
     slot = lax.rem(step, 2)
-    nfg = matmul(acts_hold[slot, 0], hold[slot, 0]) + matmul(acts_hold[slot, 1], hold[slot, 1])
-    res = matmul(acts_hold[slot, 2], hold[slot, 2])
+    total = matmul(acts_hold[slot, 0], hold[slot, 0])
+    for m in range(1, hold.shape[1]):
+        total = total + matmul(acts_hold[slot, m], hold[slot, m])
 
     @pl.when(step == 0)
     def first():
-        res_o[...] = res[:rows]
-        res_t[...] = res[rows:]
-        nfg_o[...] = nfg[:rows]
-        nfg_t[...] = nfg[rows:]
+        own_o[...] = total[:rows]
+        other[...] = total[rows:]
 
     @pl.when(step > 0)
     def later():
-        res_o[...] += res[:rows]
-        res_t[...] += res[rows:]
-        nfg_o[...] += nfg[:rows]
-        nfg_t[...] += nfg[rows:]
+        own_o[...] += total[:rows]
+        other[...] += total[rows:]
 
     @pl.when(step == pl.num_programs(0) - 1)
     def last():
-        res_b[...] = res_t[...].astype(bf16)
-        nfg_b[...] = nfg_t[...].astype(bf16)
-
-
-def feed_out(rows, width, steps, act_steps, block):
+        other_o[...] = other[...].astype(bf16)
+
+
+def feed_sum(rows, width, steps, act_steps, block):
     weights, places = plan(steps)
     acts, act_places = plan(act_steps)
+    count = len(steps[0])
     whole = pl.BlockSpec((rows, width), lambda i: (0, 0))
-    wide, low = jax.ShapeDtypeStruct((rows, width), f32), jax.ShapeDtypeStruct((rows, width), bf16)
     return pl.pallas_call(
-        functools.partial(feed_out_kernel, places, act_places, len(weights), len(acts)),
+        functools.partial(feed_sum_kernel, places, act_places, len(weights), len(acts)),
         grid=(len(steps),),
         in_specs=[pl.BlockSpec(memory_space=pl.ANY)] * (len(weights) + len(acts)),
-        out_specs=(whole, whole, whole, whole),
-        out_shape=(wide, low, wide, low),
+        out_specs=(whole, whole),
+        out_shape=(jax.ShapeDtypeStruct((rows, width), f32), jax.ShapeDtypeStruct((rows, width), bf16)),
         scratch_shapes=[
             pltpu.VMEM((rows, width), f32),
-            pltpu.VMEM((rows, width), f32),
-            pltpu.VMEM((2, 3, block, width), bf16),
-            pltpu.VMEM((2, 3, 2 * rows, block), bf16),
+            pltpu.VMEM((2, count, block, width), bf16),
+            pltpu.VMEM((2, count, 2 * rows, block), bf16),
             pltpu.SemaphoreType.DMA((2, max(len(p) for p in places))),
             pltpu.SemaphoreType.DMA((2, max(len(p) for p in act_places))),
         ],
-        compiler_params=params(54),
-        cost_estimate=cost(30),
-        name="feed_out",
+        compiler_params=params(48),
+        cost_estimate=cost(1 if count == 1 else 23),
+        name="feed_sum",
     )(*weights, *acts)
 
 
@@ -919,7 +914,8 @@
     )
     gate_own, linear_own, down_own = quarters(gate_feed.T), quarters(linear_feed.T), quarters(down_feed)
     both = [jnp.stack([gate_own[0], linear_own[0]])]
-    down = [down_own]
+    halved = mems // 2
+    down_a, down_b = [down_own[:halved]], [down_own[halved:]]
 
     onehot = (
         position_buckets(length).reshape(length * length, 1)
@@ -983,8 +979,8 @@
     linear_a1 = to_mem(linear_early, bits[-1])
     both.append(to_next(both[-1]))
     second_held = hold_parts(second_pack, second_parts, second_order)
-    first_more, gate_a1, linear_a1, both[last], second_held = tie(
-        first_more, gate_a1, linear_a1, both[last], second_held
+    first_more, gate_a1, linear_a1, both[last], second_held, down_a[0] = tie(
+        first_more, gate_a1, linear_a1, both[last], second_held, down_a[0]
     )
 
     second_more = to_core(second_held)
@@ -996,18 +992,22 @@
     kv_local = kv_fwd(place, source, kc_full, vc_full)
     gate_early = jnp.concatenate([gate_early, gate_a1])
     linear_early = jnp.concatenate([linear_early, linear_a1])
-    kv_local, second_more, gate_late_a1, linear_late_a1, down[0], gate_early, linear_early = tie(
-        kv_local, second_more, gate_late_a1, linear_late_a1, down[0], gate_early, linear_early
+    down_a.append(to_next(down_a[0]))
+    kv_local, second_more, gate_late_a1, linear_late_a1, down_a[1], down_b[0], gate_early, linear_early = tie(
+        kv_local, second_more, gate_late_a1, linear_late_a1, down_a[1], down_b[0], gate_early, linear_early
     )
 
     kvs = [to_mem(kv_local[s], s) if s else kv_local[s] for s in range(mems)]
-    down.append(to_next(down[0]))
+    down_b.append(to_next(down_b[0]))
+    down_a.append(to_next(down_a[1]))
     second_mats = matrices(second_held, second_more)
     vs_full, os_full, qc_full, oc_full = second_mats
     tokens, normed, q, k, v, mixed, first_sum, normed_cross, cq = self_fwd(
         depth, length, inputs.reshape(micros, length, width).swapaxes(1, 2), gain_self, qs_full, ks_full, vs_full, os_full, position_bias, gain_cross, qc_full
     )
-    kvs, down[1], cq, gate_early, linear_early = tie(kvs, down[1], cq, gate_early, linear_early)
+    kvs, down_a[2], down_b[1], cq, gate_early, linear_early = tie(
+        kvs, down_a[2], down_b[1], cq, gate_early, linear_early
+    )
 
     def spread_rest(held, order, over):
         parts = [held]
@@ -1015,17 +1015,6 @@
             parts.append(to_mem(jnp.concatenate(parts) if len(parts) > 1 else parts[0], bit))
             order = order + [k | bit for k in order]
         return parts, order
-
-    gate_parts, gate_order = spread_rest(gate_early, [0, bits[0]], bits[1:])
-    linear_parts, linear_order = spread_rest(linear_early, [0, bits[-1]], bits[::-1][1:])
-    gate_late = jnp.concatenate([gate_late, gate_late_a1])
-    linear_late = jnp.concatenate([linear_late, linear_late_a1])
-    for _ in early[1:]:
-        down.append(to_next(down[-1]))
-    cmixed, second_sum, normed_feed = cross_fwd(depth, length, cq, valid, oc_full, first_sum, gain_feed, kvs)
-    gate_parts, linear_parts, gate_late, linear_late, down[1:], normed_feed = tie(
-        gate_parts, linear_parts, gate_late, linear_late, down[1:], normed_feed
-    )
 
     def sources(parts, order, n):
         places = {}
@@ -1046,28 +1035,10 @@
             pieces.append(piece)
         return [(jnp.concatenate(pieces), (), feed)]
 
-    own_steps = [[(g.reshape(feed, width), (), feed)] for g in (gate_own, linear_own, down_own)]
-    early_steps = [
-        [
-            whole_source(None, sources(gate_parts, gate_order, n)),
-            whole_source(None, sources(linear_parts, linear_order, n)),
-            [(down[j].reshape(feed, width), (), feed)],
-        ]
-        for n, j in enumerate(early)
-    ]
-    nf_other = rows_to_core(normed_feed)
-    gate_late_parts, gate_order = spread_rest(gate_late, [0, bits[0]], bits[1:])
-    linear_late_parts, linear_order = spread_rest(linear_late, [0, bits[-1]], bits[::-1][1:])
-    down.append(to_next(down[-1]))
-    whole_bits = mems if mems == 4 and part % 16 == 0 else 0
-    grads_a = feed_grad(normed_feed, nf_other, og_low, og_other, early_steps + [own_steps], feed, whole_bits)
-    grads_a, gate_late_parts, linear_late_parts, down[last], nf_more = tie(
-        grads_a, gate_late_parts, linear_late_parts, down[last], nf_other
-    )
-
     natural_order = list(range(mems))
     gate_ord = [k for k in natural_order if not k & bits[-1]]
     linear_ord = [k for k in natural_order if not k & bits[0]]
+    whole_bits = mems if mems == 4 and part % 16 == 0 else 0
 
     def halves(grads):
         if whole_bits:
@@ -1080,7 +1051,57 @@
             *grads[-3:],
         )
 
+    middle = (len(early) + 1) // 2
+    starts = [0, middle] if middle < len(early) else [0]
+    cuts = [slice(0, middle), slice(middle, len(early))][: len(starts)]
+    gate_cuts, linear_cuts = [gate_early[:, c] for c in cuts], [linear_early[:, c] for c in cuts]
+    gate_parts, linear_parts = [None] * len(cuts), [None] * len(cuts)
+    gate_parts[0], gate_order = spread_rest(gate_cuts[0], [0, bits[0]], bits[1:])
+    linear_parts[0], linear_order = spread_rest(linear_cuts[0], [0, bits[-1]], bits[::-1][1:])
+    gate_late = jnp.concatenate([gate_late, gate_late_a1])
+    linear_late = jnp.concatenate([linear_late, linear_late_a1])
+    down_b.append(to_next(down_b[1]))
+    cmixed, second_sum, normed_feed = cross_fwd(depth, length, cq, valid, oc_full, first_sum, gain_feed, kvs)
+    gate_parts[0], linear_parts[0], gate_late, linear_late, normed_feed, gate_cuts, linear_cuts, down_b[2] = tie(
+        gate_parts[0], linear_parts[0], gate_late, linear_late, normed_feed, gate_cuts, linear_cuts, down_b[2]
+    )
+
+    nf_other = rows_to_core(normed_feed)
+    for n in range(1, len(cuts)):
+        gate_parts[n], gate_order = spread_rest(gate_cuts[n], [0, bits[0]], bits[1:])
+        linear_parts[n], linear_order = spread_rest(linear_cuts[n], [0, bits[-1]], bits[::-1][1:])
+    own_steps = [[[(g.reshape(feed, width), (), feed)] for g in (gate_own, linear_own, down_own)]]
+    grads_o = feed_grad(normed_feed, nf_other, og_low, og_other, own_steps, feed, whole_bits, 1)
+    while len(down_b) < last:
+        down_a.append(to_next(down_a[-1]))
+        down_b.append(to_next(down_b[-1]))
+    down_a.append(to_next(down_a[-1]))
+    gate_parts, linear_parts, down_a[last], down_b[1:], grads_o, nf_other = tie(
+        gate_parts, linear_parts, down_a[last], down_b[1:], grads_o, nf_other
+    )
+
+    (gate_keep_o, gate_send_o), (linear_keep_o, linear_send_o), (grad_down_o,), *acts_o = halves(grads_o)
+    gate_moved_o = to_mem(gate_send_o, bits[-1])
+    linear_moved_o = to_mem(linear_send_o, bits[0])
+    early_steps = [
+        [
+            whole_source(None, sources(gate_parts[c], gate_order, n - starts[c])),
+            whole_source(None, sources(linear_parts[c], linear_order, n - starts[c])),
+            [(p[j].reshape(feed // 2, width), (), feed // 2) for p in (down_a, down_b)],
+        ]
+        for n, j in enumerate(early)
+        for c in [len([1 for at in starts if at <= n]) - 1]
+    ]
+    gate_late_parts, gate_order = spread_rest(gate_late, [0, bits[0]], bits[1:])
+    linear_late_parts, linear_order = spread_rest(linear_late, [0, bits[-1]], bits[::-1][1:])
+    down_b.append(to_next(down_b[-1]))
+    grads_a = feed_grad(normed_feed, nf_other, og_low, og_other, early_steps, feed, whole_bits)
+    grads_a, gate_late_parts, linear_late_parts, down_b[last], nf_more, gate_moved_o, linear_moved_o = tie(
+        grads_a, gate_late_parts, linear_late_parts, down_b[last], nf_other, gate_moved_o, linear_moved_o
+    )
+
     (gate_keep, gate_send), (linear_keep, linear_send), grad_down_a, *acts_a = halves(grads_a)
+    grad_down_a = [*grad_down_a, grad_down_o]
     down_total = to_next(grad_down_a[0])
     gate_moved = to_mem(gate_send, bits[-1])
     linear_moved = to_mem(linear_send, bits[0])
@@ -1088,18 +1109,19 @@
         [
             whole_source(None, sources(gate_late_parts, gate_order, 0)),
             whole_source(None, sources(linear_late_parts, linear_order, 0)),
-            [(down[last].reshape(feed, width), (), feed)],
+            [(p[last].reshape(feed // 2, width), (), feed // 2) for p in (down_a, down_b)],
         ]
     ]
     grads_b = feed_grad(normed_feed, nf_more, og_low, og_other, late_steps, feed, whole_bits)
     (gate_b, gate_bs), (linear_b, linear_bs), (grad_down_b,), *acts_b = halves(grads_b)
-    act_steps = [
-        [[(acts[i], (n,), 2 * rows)] for i in (1, 2, 0)]
-        for acts, count in ((acts_a, last), (acts_b, 1))
-        for n in range(count)
-    ]
-    nfg_own, nfg_send, res_own, res_send = feed_out(
-        rows, width, early_steps + [own_steps] + late_steps, act_steps, feed
+    all_steps = early_steps + own_steps + late_steps
+    all_acts = [(a, n) for a, count in ((acts_a, len(early)), (acts_o, 1), (acts_b, 1)) for n in range(count)]
+    nfg_own, nfg_send = feed_sum(
+        rows,
+        width,
+        [step[:2] for step in all_steps],
+        [[[(acts[i], (n,), 2 * rows)] for i in (1, 2)] for acts, n in all_acts],
+        feed,
     )
     gate_moved, linear_moved, down_total, nfg_send, gate_bs, linear_bs = tie(
         gate_moved, linear_moved, down_total, nfg_send, gate_bs, linear_bs
@@ -1111,35 +1133,45 @@
             held = add_low(kept, moved)
         return held
 
-    down_next = down_total
-    for j in early[1:]:
-        down_next = to_next(add_low(down_next, grad_down_a[j - 1]))
     nfg_more = rows_to_core(nfg_send)
     half = mems // 2
     if len(bits) == 2:
         both_y = fuse(
-            lambda gk, gm, lk, lm: [
-                add_low(gk[:, 0], gm[:, 0]),
-                add_low(gk[:, 1], gm[:, 1]),
-                add_low(lk[:, 0], lm[:, 0]),
-                add_low(lk[:, 1], lm[:, 1]),
+            lambda gk, gm, lk, lm, gko, gmo, lko, lmo: [
+                [add_low(gk[:, 0], gm[:, 0]), add_low(gko[:, 0], gmo[:, 0])],
+                [add_low(gk[:, 1], gm[:, 1]), add_low(gko[:, 1], gmo[:, 1])],
+                [add_low(lk[:, 0], lm[:, 0]), add_low(lko[:, 0], lmo[:, 0])],
+                [add_low(lk[:, 1], lm[:, 1]), add_low(lko[:, 1], lmo[:, 1])],
             ],
             gate_keep, gate_moved, linear_keep, linear_moved,
+            gate_keep_o, gate_moved_o, linear_keep_o, linear_moved_o,
         )
     else:
+        gate_keep, gate_moved, linear_keep, linear_moved = [
+            jnp.concatenate(pair)
+            for pair in (
+                (gate_keep, gate_keep_o),
+                (gate_moved, gate_moved_o),
+                (linear_keep, linear_keep_o),
+                (linear_moved, linear_moved_o),
+            )
+        ]
         gate_y = fold_to_last(add_low(gate_keep, gate_moved), gate_ord, bits[::-1][1:])
         linear_y = fold_to_last(add_low(linear_keep, linear_moved), linear_ord, bits[1:])
         both_y = [gate_y[:, 0], gate_y[:, 1], linear_y[:, 0], linear_y[:, 1]]
     message_y, message_x = fuse(
         lambda gs, ly, ls, gy: [[gs[0], ly], [ls[0], gy]], gate_bs, both_y[3], linear_bs, both_y[1]
     )
+    down_next = after(down_total, message_y, message_x)
+    for j in early[1:]:
+        down_next = to_next(add_low(down_next, grad_down_a[j - 1]))
     message_y, message_x = to_mem(message_y, bits[-1]), to_mem(message_x, bits[0])
     kvg, (grad_gain_feed, grad_co, grad_cq, first_grad, grad_gain_cross) = cross_bwd(
         depth, length, og_low, nfg_own, nfg_more, second_sum, gain_feed, cmixed, cq, valid, oc_full,
         first_sum, gain_cross, normed_cross, qc_full, kvs,
     )
-    message_y, message_x, down_next, kvg, grad_gain_cross, res_send = tie(
-        message_y, message_x, down_next, kvg, grad_gain_cross, res_send
+    message_y, message_x, down_next, kvg, grad_gain_cross, hid_b = tie(
+        message_y, message_x, down_next, kvg, grad_gain_cross, acts_b[0]
     )
 
     kvg = [to_mem(kvg[s], s) if s else kvg[s] for s in range(mems)]
@@ -1155,13 +1187,28 @@
         both_y[0], message_x, both_y[2], message_y, down_next.reshape(shards), grad_down_b.reshape(shards),
     )
     ring = to_next(ring)
-    res_more = rows_to_core(res_send)
+    hid_acts = [(hid_b if a is acts_b else a[0], n) for a, n in all_acts]
+    res_own, res_send = feed_sum(
+        rows,
+        width,
+        [step[2:] for step in all_steps],
+        [[[(hid, (n,), 2 * rows)]] for hid, n in hid_acts],
+        feed,
+    )
     grad_os, grad_qs, grad_ks, grad_vs, input_grad, grad_gain_self, score_sum = self_bwd(
         depth, length, first_grad, mixed, q, k, v, position_bias, os_full, qs_full, ks_full, vs_full,
         normed, tokens, gain_self,
     )
-    kvg, ring, grad_qs, res_more = tie(kvg, ring, grad_qs, res_more)
-
+    kvg, ring, grad_qs, res_send = tie(kvg, ring, grad_qs, res_send)
+
+    at = early[-1] - 1
+    if len(early) == 2:
+        (ring_both,) = fuse(
+            lambda r, g, l: [[add_low(r[:1], g[at : at + 1]), add_low(r[1:], l[at : at + 1])]],
+            ring[mems:], gate_y, linear_y,
+        )
+        ring_both = to_next(ring_both)
+        grad_qs = after(grad_qs, gate_y)
     kept, sent = core_split(
         spot, [g.reshape(chips, 2, slim, width) for g in (grad_qs, grad_ks, grad_vs, grad_os)]
     )
@@ -1176,10 +1223,10 @@
         gate_b = fold_to_last(add_low(gate_b, gate_bm)[None], gate_ord, bits[::-1][1:])[0]
         linear_b = fold_to_last(add_low(linear_b, linear_bm)[None], linear_ord, bits[1:])[0]
         gate_bm, linear_bm = jnp.zeros_like(gate_b), jnp.zeros_like(linear_b)
-    at = early[-1] - 1
+    if len(early) != 2:
+        ring_both = to_next(add_low(ring[mems:], jnp.stack([gate_y[at], linear_y[at]])))
     parts = fuse(
-        lambda r, g, l, gb, gm, lb, lm, d: [
-            [add_low(r[mems : mems + 1], g[at : at + 1]), add_low(r[mems + 1 :], l[at : at + 1])],
+        lambda r, gb, gm, lb, lm, d: [
             add_low(gb[:1], gm[:1]),
             add_low(lb[:1], lm[:1]),
             [add_low(gb[1:2], gm[1:2]), add_low(r[1:2], d[1:2])],
@@ -1187,12 +1234,11 @@
             add_low(r[:1], d[:1]),
             *[add_low(r[k : k + 1], d[k : k + 1]) for k in range(1, mems) if k not in (1, half)],
         ],
-        ring, gate_y, linear_y, gate_b, gate_bm, linear_b, linear_bm, grad_down_a[last - 1].reshape(shards),
+        ring[:mems], gate_b, gate_bm, linear_b, linear_bm, grad_down_a[last - 1].reshape(shards),
         limit=60,
     )
-    ring_both, gate_bk, linear_bk, message_x, message_y, down_mine, *down_rest = parts
+    gate_bk, linear_bk, message_x, message_y, down_mine, *down_rest = parts
     others = [k for k in range(1, mems) if k not in (1, half)]
-    ring_both = to_next(ring_both)
     message_x, message_y = to_mem(message_x, bits[0]), to_mem(message_y, bits[-1])
     down_rest = [to_mem(p, k) for p, k in zip(down_rest, others)]
 
@@ -1218,7 +1264,7 @@
     ring_both = to_next(ring_both)
     cross_sum = [grad_sums(grad_kc, grad_vc), cross_first]
     memory_grad = kv_memory(place, source.shape, kc_full, vc_full, kvg)
-    score_sum, input_grad, res_more = [after(x, columns[1]) for x in (score_sum, input_grad, res_more)]
+    score_sum, input_grad = [after(x, columns[1]) for x in (score_sum, input_grad)]
     grad_table = lax.dot_general(
         onehot.astype(f32),
         score_sum.reshape(heads, length * length),
@@ -1252,7 +1298,9 @@
     )
     message_x, message_y = to_mem(message_x, bits[0]), to_mem(message_y, bits[-1])
     down_rest = [to_mem(down_sum, k) for k in range(1, mems) if k not in (1, half)]
-    pieces, message_x, message_y, down_rest, cross_sum = tie(pieces, message_x, message_y, down_rest, cross_sum)
+    pieces, message_x, message_y, down_rest, cross_sum, res_send = tie(
+        pieces, message_x, message_y, down_rest, cross_sum, res_send
+    )
 
     down_g = [down_sum if k == 0 else message_x[1:] if k == 1 else message_y[1:] if k == half else None for k in range(mems)]
     for k in range(mems):
@@ -1280,6 +1328,7 @@
     )
     cross_parts[0] = messages[0]
     moved = {k: to_mem(p, k) for k, p in enumerate(messages) if k}
+    res_more = rows_to_core(res_send)
     moved, small_rows, self_mine, cross_own = tie(moved, small_rows, self_mine, cross_parts[0])
     linear_g = jnp.concatenate([linear_g, moved[1][:cut].reshape(-1, part, width)])
     gate_g = jnp.concatenate([gate_g, moved[half][:cut].reshape(-1, part, width)])

time: 576 us -> 571 us (level)
  waiting for transfers between devices: 157 us -> 141 us
  Pallas kernels: 210 us -> 216 us
  starting transfers between devices: 63.7 us -> 69.5 us
    ppermute x37 -> x41, waiting for transfers between devices: 109 us -> 80.5 us  [to_mem(): return lax.ppermute(value, 'mem', [(i, i ^ mask) for i in range(count)])]
    ppermute x11 -> x14, waiting for transfers between devices: 33.2 us -> 47.7 us  [to_next(): lax.ppermute(value, 'seq', [(i, (i + 2) % count) for i in range(count)])]
    unnamed x307 -> x399, local copies, waits for them, and re-layouts: 53 us -> 48.1 us
    pallas_call x2 -> x3, Pallas kernels: 54.3 us -> 59.1 us  [feed_grad(): pl.pallas_call(functools.partial(feed_grad_kernel, places, len(weights),...]
    ppermute x37 -> x41, starting transfers between devices: 41 us -> 45.5 us  [to_mem(): return lax.ppermute(value, 'mem', [(i, i ^ mask) for i in range(count)])]
    pallas_call x1 -> x2, Pallas kernels: 34 us -> 38.2 us  [feed_sum(): pl.pallas_call(functools.partial(feed_sum_kernel, places, act_places, len...]
    ppermute x11 -> x14, starting transfers between devices: 12.1 us -> 13.5 us  [to_next(): lax.ppermute(value, 'seq', [(i, (i + 2) % count) for i in range(count)])]
  transfers between devices with their start and end apart: 64 -> 71, of which waited for: 24 -> 25; matrix products, arithmetic and copies ran while one was open for 10% -> 10% of each run, Pallas kernels for 37% -> 38%
where the time goes in v4:
time: 571 us; the launch traced here: 562 us
  Pallas kernels  216 us (38%)
  waiting for transfers between devices  141 us (25%)
  starting transfers between devices  69.5 us (12%)
  local copies, waits for them, and re-layouts  66 us (12%)
  other arithmetic  41.7 us (7%)
  between operations  16.7 us (3%)
  blocking collectives  8.17 us (1%)
    ppermute x41, waiting for transfers between devices, to_mem(): return lax.ppermute(value, 'mem', [(i, i ^ mask) for i in range(count)])  80.5 us
    pallas_call x3, Pallas kernels, feed_grad(): pl.pallas_call(functools.partial(feed_grad_kernel, places, len(weights),...  59.1 us
    unnamed x399, local copies, waits for them, and re-layouts  48.1 us
    ppermute x14, waiting for transfers between devices, to_next(): lax.ppermute(value, 'seq', [(i, (i + 2) % count) for i in range(count)])  47.7 us
    ppermute x41, starting transfers between devices, to_mem(): return lax.ppermute(value, 'mem', [(i, i ^ mask) for i in range(count)])  45.5 us
    pallas_call x2, Pallas kernels, feed_sum(): pl.pallas_call(functools.partial(feed_sum_kernel, places, act_places, len...  38.2 us
    pallas_call x1, Pallas kernels, cross_bwd(): pl.pallas_call(functools.partial(cross_bwd_kernel, depth, length, len(kvs...  32.4 us
    pallas_call x1, Pallas kernels, self_bwd(): pl.pallas_call(functools.partial(self_bwd_kernel, depth, length), out_sha...  19.1 us
  transfers between devices with their start and end apart: 71, of which 25 were waited for; matrix products, arithmetic and copies ran while one was open for 10% of the time, Pallas kernels for 38%

profile of v4, /device:TPU:8, one launch (start us, length us, event | category | flops | bytes accessed | tf_op | source)
XLA Modules:
  0.0 562.1 jit_solution(96364726908327940)
XLA Ops:
  14.5 2.0 collective-permute-start.2
  16.5 1.7 copy.96
  22.5 2.4 constant_dynamic-slice_fusion.22
  32.4 8.2 %all-gather = s32[8,1,4,256]{3,2,1,0:T(4,128)S(1)} all-gather(s32[2,1,4,256]{3,2,1,0:T(4,128)S(1)} %copy-done.184), channel_id=2, replica_groups=mesh['seq'=8,'mem'=4] {'mem'}, dimensions={0}, use_global_device_ids=true | all-gather | bytes 40960 | tf_op jit(solution)/shard_map/all_gather | solution.py:943
  45.3 7.7 %collective-permute-done.4 = bf16[1,3,48,1472]{3,2,1,0:T(8,128)(2,1)S(1)} collective-permute-done((bf16[1,3,48,1472]{3,2,1,0:T(8,128)(2,1)S(1)}, bf16[1,3,48,1472]{3,2,1,0:T(8,128)(2,1)S(1)}, u32[]{:S(2)}, u32[]{:S(2)}) %collective-permute-start.4) | collective-permute-done | bytes 423968 | tf_op jit(solution)/shard_map/ppermute | solution.py:62
  54.2 4.0 collective-permute-done.6
  64.1 1.8 fusion.4.bias
  65.9 13.6 %collective-permute-done.9 = bf16[2,112,1472]{2,1,0:T(8,128)(2,1)} collective-permute-done((bf16[2,112,1472]{2,1,0:T(8,128)(2,1)}, bf16[2,112,1472]{2,1,0:T(8,128)(2,1)}, u32[]{:S(2)}, u32[]{:S(2)}) %collective-permute-start.9) | collective-permute-done | bytes 659488 | tf_op jit(solution)/shard_map/ppermute | solution.py:57
  79.5 2.7 collective-permute-done.7
  86.9 1.8 collective-permute-start.12
  90.7 13.8 %collective-permute-done.12 = bf16[1,2,112,1472]{3,2,1,0:T(8,128)(2,1)S(1)} collective-permute-done((bf16[1,2,112,1472]{3,2,1,0:T(8,128)(2,1)S(1)}, bf16[1,2,112,1472]{3,2,1,0:T(8,128)(2,1)S(1)}, u32[]{:S(2)}, u32[]{:S(2)}) %collective-permute-start.12) | collective-permute-done | bytes 659488 | tf_op jit(solution)/shard_map/ppermute | solution.py:62
  109.8 9.2 %kv_fwd.1 = (bf16[2,256,768]{2,1,0:T(8,128)(2,1)S(1)}, bf16[2,256,768]{2,1,0:T(8,128)(2,1)S(1)}, bf16[2,256,768]{2,1,0:T(8,128)(2,1)S(1)}, bf16[2,256,768]{2,1,0:T(8,128)(2,1)S(1)}) custom-call(s32[4]{0:T(128)S(1)} %pad_add_fusion.place, bf16[2,4,1472,256]{3,2,1,0:T(8,128)(2,1)S(1)} %bitcast.278, bf16[384,1472]{1,0:T(8,128)(2,1)S(1)} %bitcast.283, ...), custom_call_target="tpu_custom_call" | custom-call | flops 8999999488 | bytes 27000000 | tf_op jit(solution)/shard_map/kv_fwd/pallas_call | solution.py:440
  120.4 3.9 collective-permute-done.17
  126.3 1.6 collective-permute-start.18
  127.9 1.7 collective-permute-start.19
  130.2 2.7 collective-permute-start.22
  132.9 13.5 %self_fwd.1 = (bf16[512,1472]{1,0:T(8,128)(2,1)S(1)}, bf16[512,1472]{1,0:T(8,128)(2,1)S(1)}, bf16[512,384]{1,0:T(8,128)(2,1)S(1)}, bf16[512,384]{1,0:T(8,128)(2,...) custom-call(bf16[2,1472,256]{2,1,0:T(8,128)(2,1)S(1)} %bitcast.280, ...), custom_call_target="tpu_custom_call" | custom-call | flops 16000000000 | bytes 48000000 | tf_op jit(solution)/shard_map/self_fwd/pallas_call | solution.py:230
  150.6 11.2 %collective-permute-done.22 = bf16[2,112,1472]{2,1,0:T(8,128)(2,1)S(1)} collective-permute-done((bf16[2,112,1472]{2,1,0:T(8,128)(2,1)}, bf16[2,112,1472]{2,1,0:T(8,128)(2,1)S(1)}, u32[]{:S(2)}, u32[]{:S(2)}) %collective-permute-start.22) | collective-permute-done | bytes 659488 | tf_op jit(solution)/shard_map/ppermute | solution.py:57
  164.4 1.7 collective-permute-start.23
  167.2 9.7 %cross_fwd.1 = (bf16[512,384]{1,0:T(8,128)(2,1)S(1)}, f32[512,1472]{1,0:T(8,128)S(1)}, bf16[512,1472]{1,0:T(8,128)(2,1)S(1)}) custom-call(bf16[512,384]{1,0:T(8,128)(2,1)S(1)} %get-tuple-element.309.cq, f32[2,1,1024]{2,1,0:T(1,128)S(1)} %and_convert_fusion.mask, bf16[384,1472]{1,0:T(8,128)(2,1)S(1)} %bitcast.298, f32[512,1472]{1,0:T(8,128)S(1)} %copy-done.112, ...), custom_call_target="tpu_custom_call" | custom-call | flops 15000000512 | bytes 45000000 | tf_op jit(solution)/shard_map/cross_fwd/pallas_call | solution.py:271
  180.4 2.6 collective-permute-done.25
  193.2 15.1 %feed_grad.3 = (bf16[1,2,112,1472]{3,2,1,0:T(8,128)(2,1)}, bf16[1,2,112,1472]{3,2,1,0:T(8,128)(2,1)}, bf16[1,2,112,1472]{3,2,1,0:T(8,128)(2,1)}, bf16[1,2,112,14...) custom-call(bf16[512,1472]{1,0:T(8,128)(2,1)} %copy-done.4, ...), custom_call_target="tpu_custom_call" | custom-call | flops 1000000000 | bytes 3000000 | tf_op jit(solution)/shard_map/feed_grad/pallas_call | solution.py:671
  208.3 2.6 collective-permute-start.32
  212.8 28.7 %feed_grad.4 = (bf16[2,2,112,1472]{3,2,1,0:T(8,128)(2,1)}, bf16[2,2,112,1472]{3,2,1,0:T(8,128)(2,1)}, bf16[2,2,112,1472]{3,2,1,0:T(8,128)(2,1)}, bf16[2,2,112,14...) custom-call(bf16[512,1472]{1,0:T(8,128)(2,1)} %copy-done.4, ...), custom_call_target="tpu_custom_call" | custom-call | flops 25999998976 | bytes 78000000 | tf_op jit(solution)/shard_map/feed_grad/pallas_call | solution.py:671
  245.6 4.4 collective-permute-start.37
  250.2 15.3 %feed_grad.5 = (bf16[1,2,112,1472]{3,2,1,0:T(8,128)(2,1)}, bf16[1,2,112,1472]{3,2,1,0:T(8,128)(2,1)}, bf16[1,2,112,1472]{3,2,1,0:T(8,128)(2,1)}, bf16[1,2,112,14...) custom-call(bf16[512,1472]{1,0:T(8,128)(2,1)} %copy-done.4, ...), custom_call_target="tpu_custom_call" | custom-call | flops 12999999488 | bytes 39000000 | tf_op jit(solution)/shard_map/feed_grad/pallas_call | solution.py:671
  266.7 22.9 %feed_sum.2 = (f32[512,1472]{1,0:T(8,128)}, bf16[512,1472]{1,0:T(8,128)(2,1)}) custom-call(bf16[2,1,112,1472]{3,2,1,0:T(8,128)(2,1)S(1)} %copy-done.12, bf16[2,1,112,1472]{3,2,1,0:T(8,128)(2,1)S(1)} %copy-done.51, bf16[2,1,112,1472]{3,2,1,0:T(8,128)(2,1)S(1)} %copy-done.16, bf16[2,1,112,1472]{3,2,1,0:T(8,128)(2,1)S(1)} %copy-done.53, ...), custom_call_target="tpu_custom_call" | custom-call | flops 23000000512 | bytes 69000000 | tf_op jit(solution)/shard_map/feed_sum/pallas_call | solution.py:734
  293.5 2.8 add_convert_fusion
  297.5 32.4 %cross_bwd.1 = (bf16[2,256,768]{2,1,0:T(8,128)(2,1)S(1)}, bf16[2,256,768]{2,1,0:T(8,128)(2,1)}, bf16[2,256,768]{2,1,0:T(8,128)(2,1)}, bf16[2,256,768]{2,1,0:T(8,...) custom-call(bf16[512,1472]{1,0:T(8,128)(2,1)} %bitcast.313, ...), custom_call_target="tpu_custom_call" | custom-call | flops 31000000512 | bytes 93000000 | tf_op jit(solution)/shard_map/cross_bwd/pallas_call | solution.py:339
  329.9 1.7 collective-permute-done.38.refs_3_.refs_2_
  332.6 2.0 copy-done.72
  340.8 2.0 collective-permute-start.44
  342.9 19.1 %self_bwd.1 = (bf16[384,1472]{1,0:T(8,128)(2,1)S(1)}, bf16[384,1472]{1,0:T(8,128)(2,1)S(1)}, bf16[384,1472]{1,0:T(8,128)(2,1)S(1)}, bf16[384,1472]{1,0:T(8,128)(...) custom-call(f32[512,1472]{1,0:T(8,128)} %get-tuple-element.427.first_grad, ...), custom_call_target="tpu_custom_call" | custom-call | flops 20999999488 | bytes 63000000 | tf_op jit(solution)/shard_map/self_bwd/pallas_call | solution.py:405
  362.1 15.3 %feed_sum.3 = (f32[512,1472]{1,0:T(8,128)}, bf16[512,1472]{1,0:T(8,128)(2,1)}) custom-call(bf16[224,1472]{1,0:T(8,128)(2,1)S(1)} %bitcast.265, bf16[224,1472]{1,0:T(8,128)(2,1)S(1)} %bitcast.269, bf16[224,1472]{1,0:T(8,128)(2,1)S(1)} %bitcast.267, bf16[224,1472]{1,0:T(8,128)(2,1)S(1)} %bitcast.271, bf16[448,1472]{1,0:T(8,128)(2,1)} %bitcast.306, ...), custom_call_target="tpu_custom_call" | custom-call | flops 1000000000 | bytes 3000000 | tf_op jit(solution)/shard_map/feed_sum/pallas_call | solution.py:734
  377.6 8.0 %collective-permute-done.45 = bf16[6,112,1472]{2,1,0:T(8,128)(2,1)} collective-permute-done((bf16[6,112,1472]{2,1,0:T(8,128)(2,1)S(1)}, bf16[6,112,1472]{2,1,0:T(8,128)(2,1)}, u32[]{:S(2)}, u32[]{:S(2)}) %collective-permute-start.45) | collective-permute-done | bytes 1978400 | tf_op jit(solution)/shard_map/ppermute | solution.py:57
  385.5 3.2 pad_maximum_fusion.1
  388.9 4.8 core_split.1
  393.8 2.5 slice.279.refs_0_
  397.5 5.0 fuse.14
  404.3 1.7 collective-permute-start.50
  410.0 2.7 copy-done.33
  412.8 8.2 %kv_weights.1 = (bf16[384,1472]{1,0:T(8,128)(2,1)S(1)}, bf16[384,1472]{1,0:T(8,128)(2,1)S(1)}) custom-call(s32[4]{0:T(128)S(1)} %copy-done.30, bf16[2,4,1472,256]{3,2,1,0:T(8,128)(2,1)S(1)} %bitcast.279, bf16[2,256,768]{2,1,0:T(8,128)(2,1)S(1)} %copy-done.110, bf16[2,256,768]{2,1,0:T(8,128)(2,1)S(1)} %copy-done.38, bf16[2,256,768]{2,1,0:T(8,128)(2,1)S(1)} %copy-done.41, ...), custom_call_target="tpu_custom_call" | custom-call | flops 8999999488 | bytes 27000000 | tf_op jit(solution)/shard_map/kv_weights/pallas_call | solution.py:519
  421.0 7.5 %collective-permute-done.50.refs_6_ = bf16[1,112,1472]{2,1,0:T(8,128)(2,1)S(1)} collective-permute-done((bf16[1,112,1472]{2,1,0:T(8,128)(2,1)}, bf16[1,112,1472]{2,1,0:T(8,128)(2,1)S(1)}, u32[]{:S(2)}, u32[]{:S(2)}) %collective-permute-start.50) | collective-permute-done | bytes 329760 | tf_op jit(solution)/shard_map/ppermute | solution.py:62
  430.1 4.2 collective-permute-done.47.refs_0_
  434.4 1.6 pad_maximum_fusion
  436.7 1.7 copy-done.106
  438.4 2.0 columns.1
  445.8 1.7 collective-permute-start.60
  447.6 10.1 %kv_memory.1 = f32[2,4,1472,256]{3,2,1,0:T(8,128)} custom-call(s32[4]{0:T(128)S(1)} %copy-done.30, bf16[384,1472]{1,0:T(8,128)(2,1)S(1)} %bitcast.284, bf16[384,1472]{1,0:T(8,128)(2,1)S(1)} %bitcast.286, bf16[2,256,768]{2,1,0:T(8,128)(2,1)S(1)} %copy-done.111, bf16[2,256,768]{2,1,0:T(8,128)(2,1)S(1)} %copy-done.39, bf16[2,256,768]{2,1,0:T(8,128)(2,1)S(1)} %copy-done.42, ...), custom_call_target="tpu_custom_call" | custom-call | flops 10000000000 | bytes 30000000 | tf_op jit(solution)/shard_map/kv_memory/pallas_call | solution.py:539
  460.1 3.6 copy.110
  463.8 14.2 %collective-permute-done.52 = bf16[4,48,1472]{2,1,0:T(8,128)(2,1)} collective-permute-done((bf16[4,48,1472]{2,1,0:T(8,128)(2,1)}, bf16[4,48,1472]{2,1,0:T(8,128)(2,1)}, u32[]{:S(2)}, u32[]{:S(2)}) %collective-permute-start.52) | collective-permute-done | bytes 565280 | tf_op jit(solution)/shard_map/ppermute | solution.py:62
  483.2 2.3 collective-permute-start.56
  485.4 1.9 collective-permute-start.57
  487.3 8.3 %collective-permute-done.55 = bf16[64,1472]{1,0:T(8,128)(2,1)S(1)} collective-permute-done((bf16[64,1472]{1,0:T(8,128)(2,1)S(1)}, bf16[64,1472]{1,0:T(8,128)(2,1)S(1)}, u32[]{:S(2)}, u32[]{:S(2)}) %collective-permute-start.55) | collective-permute-done | bytes 188448 | tf_op jit(solution)/shard_map/ppermute | solution.py:71
  495.6 2.1 collective-permute-done.56
  497.7 2.6 collective-permute-done.57
  507.7 2.0 bitcast_convert_fusion
  509.8 20.4 %collective-permute-done.64 = bf16[64,1472]{1,0:T(8,128)(2,1)S(1)} collective-permute-done((bf16[64,1472]{1,0:T(8,128)(2,1)S(1)}, bf16[64,1472]{1,0:T(8,128)(2,1)S(1)}, u32[]{:S(2)}, u32[]{:S(2)}) %collective-permute-start.64) | collective-permute-done | bytes 188448 | tf_op jit(solution)/shard_map/ppermute | solution.py:62
  532.8 1.7 collective-permute-start.68
  535.1 2.0 bitcast_convert_fusion.1
  537.7 2.0 bitcast_convert_fusion.2
  541.1 5.1 collective-permute-done.67
  550.5 2.3 convert_add_fusion
  552.8 2.3 copy.109
  (632 shorter events, 125.9 us)
Async XLA Ops:
  7.2 493.8 %reduce-scatter.5.cloned.1.call-start = ((), (), s32[]{:S(2)}) async-start(), calls=%async_computation.3 | async-start | bytes 2654208 | tf_op jit(solution)/shard_map/reduce_scatter | solution.py:1247
  11.9 29.5 %collective-permute-start = (bf16[2,48,1472]{2,1,0:T(8,128)(2,1)}, bf16[2,48,1472]{2,1,0:T(8,128)(2,1)S(1)}, u32[]{:S(2)}, u32[]{:S(2)}) collective-permute-start(bf16[2,48,1472]{2,1,0:T(8,128)(2,1)} %pad_maximum_fusion.31), channel_id=1, source_target_pairs={{0,8},{4,12},{8,16},{12,20},{16,24},{20,28},{24,0},{28,4},{1,9},{5... | collective-permute-start | bytes 847880 | tf_op jit(solution)/shard_map/ppermute | solution.py:71
  13.5 28.0 %collective-permute-start.1 = (bf16[2,48,1472]{2,1,0:T(8,128)(2,1)}, bf16[2,48,1472]{2,1,0:T(8,128)(2,1)S(1)}, u32[]{:S(2)}, u32[]{:S(2)}) collective-permute-start(bf16[2,48,1472]{2,1,0:T(8,128)(2,1)} %pad_maximum_fusion.31), channel_id=1, source_target_pairs={{0,16},{4,20},{8,24},{12,28},{16,0},{20,4},{24,8},{28,12},{1,17},{... | collective-permute-start | bytes 847880 | tf_op jit(solution)/shard_map/ppermute | solution.py:71
  14.5 26.9 %collective-permute-start.2 = (bf16[2,48,1472]{2,1,0:T(8,128)(2,1)}, bf16[2,48,1472]{2,1,0:T(8,128)(2,1)S(1)}, u32[]{:S(2)}, u32[]{:S(2)}) collective-permute-start(bf16[2,48,1472]{2,1,0:T(8,128)(2,1)} %pad_maximum_fusion.31), channel_id=1, source_target_pairs={{0,24},{4,28},{8,0},{12,4},{16,8},{20,12},{24,16},{28,20},{1,25},{... | collective-permute-start | bytes 847880 | tf_op jit(solution)/shard_map/ppermute | solution.py:71
  18.3 23.2 %collective-permute-start.3 = (bf16[8,64,1472]{2,1,0:T(8,128)(2,1)S(1)}, bf16[8,64,1472]{2,1,0:T(8,128)(2,1)}, u32[]{:S(2)}, u32[]{:S(2)}) collective-permute-start(bf16[8,64,1472]{2,1,0:T(8,128)(2,1)S(1)} %bitcast.309), channel_id=1, source_target_pairs={{0,4},{4,0},{8,12},{12,8},{16,20},{20,16},{24,28},{28,24},{1,5},{5... | collective-permute-start | bytes 4521992 | tf_op jit(solution)/shard_map/ppermute | solution.py:48
  41.5 16.7 %collective-permute-start.6 = (bf16[2,112,1472]{2,1,0:T(8,128)(2,1)S(1)}, bf16[2,112,1472]{2,1,0:T(8,128)(2,1)}, u32[]{:S(2)}, u32[]{:S(2)}) collective-permute-start(bf16[2,112,1472]{2,1,0:T(8,128)(2,1)S(1)} %pad_maximum_fusion.15), channel_id=1, source_target_pairs={{0,8},{4,12},{8,16},{12,20},{16,24},{20,28},{24,0},{28,4},{1,9},{5... | collective-permute-start | bytes 1978376 | tf_op jit(solution)/shard_map/ppermute | solution.py:57
  59.2 20.3 %collective-permute-start.8 = (bf16[2,3,48,1472]{3,2,1,0:T(8,128)(2,1)}, bf16[2,3,48,1472]{3,2,1,0:T(8,128)(2,1)}, u32[]{:S(2)}, u32[]{:S(2)}) collective-permute-start(bf16[2,3,48,1472]{3,2,1,0:T(8,128)(2,1)} %pad_maximum_fusion.14), channel_id=1, source_target_pairs={{0,1},{1,0},{2,3},{3,2},{4,5},{5,4},{6,7},{7,6},{8,9},{9,8},{10,11... | collective-permute-start | bytes 2543624 | tf_op jit(solution)/shard_map/ppermute | solution.py:62
  61.7 20.5 %collective-permute-start.7 = (bf16[2,3,48,1472]{3,2,1,0:T(8,128)(2,1)}, bf16[2,3,48,1472]{3,2,1,0:T(8,128)(2,1)}, u32[]{:S(2)}, u32[]{:S(2)}) collective-permute-start(bf16[2,3,48,1472]{3,2,1,0:T(8,128)(2,1)} %pad_maximum_fusion.13), channel_id=1, source_target_pairs={{0,2},{1,3},{2,0},{3,1},{4,6},{5,7},{6,4},{7,5},{8,10},{9,11},{10,... | collective-permute-start | bytes 2543624 | tf_op jit(solution)/shard_map/ppermute | solution.py:62
  63.2 16.3 %collective-permute-start.9 = (bf16[2,112,1472]{2,1,0:T(8,128)(2,1)}, bf16[2,112,1472]{2,1,0:T(8,128)(2,1)}, u32[]{:S(2)}, u32[]{:S(2)}) collective-permute-start(bf16[2,112,1472]{2,1,0:T(8,128)(2,1)} %collective-permute-done.6), channel_id=1, source_target_pairs={{0,8},{4,12},{8,16},{12,20},{16,24},{20,28},{24,0},{28,4},{1,9},{5... | collective-permute-start | bytes 1978376 | tf_op jit(solution)/shard_map/ppermute | solution.py:57
  83.8 22.3 %collective-permute-start.10 = (bf16[4,4,48,1472]{3,2,1,0:T(8,128)(2,1)S(1)}, bf16[4,4,48,1472]{3,2,1,0:T(8,128)(2,1)S(1)}, u32[]{:S(2)}, u32[]{:S(2)}) collective-permute-start(bf16[4,4,48,1472]{3,2,1,0:T(8,128)(2,1)S(1)} %maximum_maximum_fusion.own), channel_id=1, source_target_pairs={{0,4},{4,0},{8,12},{12,8},{16,20},{20,16},{24,28},{28,24},{1,5},{5... | collective-permute-start | bytes 6782984 | tf_op jit(solution)/shard_map/ppermute | solution.py:48
  85.0 21.0 %collective-permute-start.13 = (bf16[2,112,1472]{2,1,0:T(8,128)(2,1)}, bf16[2,112,1472]{2,1,0:T(8,128)(2,1)S(1)}, u32[]{:S(2)}, u32[]{:S(2)}) collective-permute-start(bf16[2,112,1472]{2,1,0:T(8,128)(2,1)} %collective-permute-done.9), channel_id=1, source_target_pairs={{0,8},{4,12},{8,16},{12,20},{16,24},{20,28},{24,0},{28,4},{1,9},{5... | collective-permute-start | bytes 1978376 | tf_op jit(solution)/shard_map/ppermute | solution.py:57
  86.9 17.6 %collective-permute-start.12 = (bf16[1,2,112,1472]{3,2,1,0:T(8,128)(2,1)S(1)}, bf16[1,2,112,1472]{3,2,1,0:T(8,128)(2,1)S(1)}, u32[]{:S(2)}, u32[]{:S(2)}) collective-permute-start(bf16[1,2,112,1472]{3,2,1,0:T(8,128)(2,1)S(1)} %maximum_bitcast_fusion.1), channel_id=1, source_target_pairs={{0,2},{1,3},{2,0},{3,1},{4,6},{5,7},{6,4},{7,5},{8,10},{9,11},{10,... | collective-permute-start | bytes 1978376 | tf_op jit(solution)/shard_map/ppermute | solution.py:62
  88.7 17.3 %collective-permute-start.11 = (bf16[1,2,112,1472]{3,2,1,0:T(8,128)(2,1)S(1)}, bf16[1,2,112,1472]{3,2,1,0:T(8,128)(2,1)S(1)}, u32[]{:S(2)}, u32[]{:S(2)}) collective-permute-start(bf16[1,2,112,1472]{3,2,1,0:T(8,128)(2,1)S(1)} %maximum_bitcast_fusion), channel_id=1, source_target_pairs={{0,1},{1,0},{2,3},{3,2},{4,5},{5,4},{6,7},{7,6},{8,9},{9,8},{10,11... | collective-permute-start | bytes 1978376 | tf_op jit(solution)/shard_map/ppermute | solution.py:62
  106.1 18.2 %collective-permute-start.14 = (bf16[4,4,48,1472]{3,2,1,0:T(8,128)(2,1)S(1)}, bf16[4,4,48,1472]{3,2,1,0:T(8,128)(2,1)S(1)}, u32[]{:S(2)}, u32[]{:S(2)}) collective-permute-start(bf16[4,4,48,1472]{3,2,1,0:T(8,128)(2,1)S(1)} %maximum_maximum_fusion.1.own), channel_id=1, source_target_pairs={{0,4},{4,0},{8,12},{12,8},{16,20},{20,16},{24,28},{28,24},{1,5},{5... | collective-permute-start | bytes 6782984 | tf_op jit(solution)/shard_map/ppermute | solution.py:48
  106.2 14.2 %collective-permute-start.15 = (bf16[1,112,1472]{2,1,0:T(8,128)(2,1)S(1)}, bf16[1,112,1472]{2,1,0:T(8,128)(2,1)S(1)}, u32[]{:S(2)}, u32[]{:S(2)}) collective-permute-start(bf16[1,112,1472]{2,1,0:T(8,128)(2,1)S(1)} %get-tuple-element.668), channel_id=1, source_target_pairs={{0,1},{1,0},{2,3},{3,2},{4,5},{5,4},{6,7},{7,6},{8,9},{9,8},{10,11... | collective-permute-start | bytes 989192 | tf_op jit(solution)/shard_map/ppermute | solution.py:62
  106.6 13.8 %collective-permute-start.16 = (bf16[1,112,1472]{2,1,0:T(8,128)(2,1)S(1)}, bf16[1,112,1472]{2,1,0:T(8,128)(2,1)S(1)}, u32[]{:S(2)}, u32[]{:S(2)}) collective-permute-start(bf16[1,112,1472]{2,1,0:T(8,128)(2,1)S(1)} %get-tuple-element.667), channel_id=1, source_target_pairs={{0,2},{1,3},{2,0},{3,1},{4,6},{5,7},{6,4},{7,5},{8,10},{9,11},{10,... | collective-permute-start | bytes 989192 | tf_op jit(solution)/shard_map/ppermute | solution.py:62
  106.9 17.4 %collective-permute-start.17 = (bf16[2,112,1472]{2,1,0:T(8,128)(2,1)S(1)}, bf16[2,112,1472]{2,1,0:T(8,128)(2,1)S(1)}, u32[]{:S(2)}, u32[]{:S(2)}) collective-permute-start(bf16[2,112,1472]{2,1,0:T(8,128)(2,1)S(1)} %copy-done.165), channel_id=1, source_target_pairs={{0,8},{4,12},{8,16},{12,20},{16,24},{20,28},{24,0},{28,4},{1,9},{5... | collective-permute-start | bytes 1978376 | tf_op jit(solution)/shard_map/ppermute | solution.py:57
  126.3 35.5 %collective-permute-start.18 = (bf16[2,256,768]{2,1,0:T(8,128)(2,1)S(1)}, bf16[2,256,768]{2,1,0:T(8,128)(2,1)S(1)}, u32[]{:S(2)}, u32[]{:S(2)}) collective-permute-start(bf16[2,256,768]{2,1,0:T(8,128)(2,1)S(1)} %get-tuple-element.295), channel_id=1, source_target_pairs={{0,1},{1,0},{2,3},{3,2},{4,5},{5,4},{6,7},{7,6},{8,9},{9,8},{10,11... | collective-permute-start | bytes 2359304 | tf_op jit(solution)/shard_map/ppermute | solution.py:62
  127.9 35.1 %collective-permute-start.19 = (bf16[2,256,768]{2,1,0:T(8,128)(2,1)S(1)}, bf16[2,256,768]{2,1,0:T(8,128)(2,1)S(1)}, u32[]{:S(2)}, u32[]{:S(2)}) collective-permute-start(bf16[2,256,768]{2,1,0:T(8,128)(2,1)S(1)} %get-tuple-element.296), channel_id=1, source_target_pairs={{0,2},{1,3},{2,0},{3,1},{4,6},{5,7},{6,4},{7,5},{8,10},{9,11},{10,... | collective-permute-start | bytes 2359304 | tf_op jit(solution)/shard_map/ppermute | solution.py:62
  129.6 33.4 %collective-permute-start.20 = (bf16[2,256,768]{2,1,0:T(8,128)(2,1)S(1)}, bf16[2,256,768]{2,1,0:T(8,128)(2,1)S(1)}, u32[]{:S(2)}, u32[]{:S(2)}) collective-permute-start(bf16[2,256,768]{2,1,0:T(8,128)(2,1)S(1)} %get-tuple-element.297), channel_id=1, source_target_pairs={{0,3},{1,2},{2,1},{3,0},{4,7},{5,6},{6,5},{7,4},{8,11},{9,10},{10,... | collective-permute-start | bytes 2359304 | tf_op jit(solution)/shard_map/ppermute | solution.py:62
  129.7 20.8 %collective-permute-start.21 = (bf16[2,112,1472]{2,1,0:T(8,128)(2,1)S(1)}, bf16[2,112,1472]{2,1,0:T(8,128)(2,1)S(1)}, u32[]{:S(2)}, u32[]{:S(2)}) collective-permute-start(bf16[2,112,1472]{2,1,0:T(8,128)(2,1)S(1)} %collective-permute-done.17), channel_id=1, source_target_pairs={{0,8},{4,12},{8,16},{12,20},{16,24},{20,28},{24,0},{28,4},{1,9},{5... | collective-permute-start | bytes 1978376 | tf_op jit(solution)/shard_map/ppermute | solution.py:57
  130.2 31.6 %collective-permute-start.22 = (bf16[2,112,1472]{2,1,0:T(8,128)(2,1)}, bf16[2,112,1472]{2,1,0:T(8,128)(2,1)S(1)}, u32[]{:S(2)}, u32[]{:S(2)}) collective-permute-start(bf16[2,112,1472]{2,1,0:T(8,128)(2,1)} %pad_maximum_fusion.17), channel_id=1, source_target_pairs={{0,8},{4,12},{8,16},{12,20},{16,24},{20,28},{24,0},{28,4},{1,9},{5... | collective-permute-start | bytes 1978376 | tf_op jit(solution)/shard_map/ppermute | solution.py:57
  164.4 15.3 %collective-permute-start.23 = (bf16[2,1,112,1472]{3,2,1,0:T(8,128)(2,1)S(1)}, bf16[2,1,112,1472]{3,2,1,0:T(8,128)(2,1)S(1)}, u32[]{:S(2)}, u32[]{:S(2)}) collective-permute-start(bf16[2,1,112,1472]{3,2,1,0:T(8,128)(2,1)S(1)} %get-tuple-element.346.refs_4_.refs_0_), channel_id=1, source_target_pairs={{0,2},{1,3},{2,0},{3,1},{4,6},{5,7},{6,4},{7,5},{8,10},{9,11},{10,... | collective-permute-start | bytes 1978376 | tf_op jit(solution)/shard_map/ppermute | solution.py:62
  166.2 14.2 %collective-permute-start.24 = (bf16[2,1,112,1472]{3,2,1,0:T(8,128)(2,1)S(1)}, bf16[2,1,112,1472]{3,2,1,0:T(8,128)(2,1)S(1)}, u32[]{:S(2)}, u32[]{:S(2)}) collective-permute-start(bf16[2,1,112,1472]{3,2,1,0:T(8,128)(2,1)S(1)} %get-tuple-element.348.refs_6_.refs_2_), channel_id=1, source_target_pairs={{0,1},{1,0},{2,3},{3,2},{4,5},{5,4},{6,7},{7,6},{8,9},{9,8},{10,11... | collective-permute-start | bytes 1978376 | tf_op jit(solution)/shard_map/ppermute | solution.py:62
  167.0 16.0 %collective-permute-start.25 = (bf16[2,112,1472]{2,1,0:T(8,128)(2,1)S(1)}, bf16[2,112,1472]{2,1,0:T(8,128)(2,1)S(1)}, u32[]{:S(2)}, u32[]{:S(2)}) collective-permute-start(bf16[2,112,1472]{2,1,0:T(8,128)(2,1)S(1)} %collective-permute-done.22), channel_id=1, source_target_pairs={{0,8},{4,12},{8,16},{12,20},{16,24},{20,28},{24,0},{28,4},{1,9},{5... | collective-permute-start | bytes 1978376 | tf_op jit(solution)/shard_map/ppermute | solution.py:57
  183.2 25.1 %collective-permute-start.28 = (bf16[2,112,1472]{2,1,0:T(8,128)(2,1)S(1)}, bf16[2,112,1472]{2,1,0:T(8,128)(2,1)S(1)}, u32[]{:S(2)}, u32[]{:S(2)}) collective-permute-start(bf16[2,112,1472]{2,1,0:T(8,128)(2,1)S(1)} %collective-permute-done.21), channel_id=1, source_target_pairs={{0,8},{4,12},{8,16},{12,20},{16,24},{20,28},{24,0},{28,4},{1,9},{5... | collective-permute-start | bytes 1978376 | tf_op jit(solution)/shard_map/ppermute | solution.py:57
  183.5 24.8 %collective-permute-start.26 = (bf16[2,1,112,1472]{3,2,1,0:T(8,128)(2,1)S(1)}, bf16[2,1,112,1472]{3,2,1,0:T(8,128)(2,1)S(1)}, u32[]{:S(2)}, u32[]{:S(2)}) collective-permute-start(bf16[2,1,112,1472]{3,2,1,0:T(8,128)(2,1)S(1)} %get-tuple-element.350.refs_10_.refs_4_), channel_id=1, source_target_pairs={{0,2},{1,3},{2,0},{3,1},{4,6},{5,7},{6,4},{7,5},{8,10},{9,11},{10,... | collective-permute-start | bytes 1978376 | tf_op jit(solution)/shard_map/ppermute | solution.py:62
  184.7 23.6 %collective-permute-start.27 = (bf16[2,1,112,1472]{3,2,1,0:T(8,128)(2,1)S(1)}, bf16[2,1,112,1472]{3,2,1,0:T(8,128)(2,1)S(1)}, u32[]{:S(2)}, u32[]{:S(2)}) collective-permute-start(bf16[2,1,112,1472]{3,2,1,0:T(8,128)(2,1)S(1)} %get-tuple-element.352.refs_12_.refs_6_), channel_id=1, source_target_pairs={{0,1},{1,0},{2,3},{3,2},{4,5},{5,4},{6,7},{7,6},{8,9},{9,8},{10,11... | collective-permute-start | bytes 1978376 | tf_op jit(solution)/shard_map/ppermute | solution.py:62
  189.8 51.7 %collective-permute-start.30 = (bf16[2,112,1472]{2,1,0:T(8,128)(2,1)S(1)}, bf16[2,112,1472]{2,1,0:T(8,128)(2,1)S(1)}, u32[]{:S(2)}, u32[]{:S(2)}) collective-permute-start(bf16[2,112,1472]{2,1,0:T(8,128)(2,1)S(1)} %pad_maximum_fusion.18.refs_4_.refs_10_), channel_id=1, source_target_pairs={{0,2},{1,3},{2,0},{3,1},{4,6},{5,7},{6,4},{7,5},{8,10},{9,11},{10,... | collective-permute-start | bytes 1978376 | tf_op jit(solution)/shard_map/ppermute | solution.py:62
  191.8 49.8 %collective-permute-start.31 = (bf16[2,112,1472]{2,1,0:T(8,128)(2,1)}, bf16[2,112,1472]{2,1,0:T(8,128)(2,1)S(1)}, u32[]{:S(2)}, u32[]{:S(2)}) collective-permute-start(bf16[2,112,1472]{2,1,0:T(8,128)(2,1)} %pad_maximum_fusion.19.refs_6_.refs_12_), channel_id=1, source_target_pairs={{0,1},{1,0},{2,3},{3,2},{4,5},{5,4},{6,7},{7,6},{8,9},{9,8},{10,11... | collective-permute-start | bytes 1978376 | tf_op jit(solution)/shard_map/ppermute | solution.py:62
  208.3 33.2 %collective-permute-start.32 = (bf16[2,112,1472]{2,1,0:T(8,128)(2,1)S(1)}, bf16[2,112,1472]{2,1,0:T(8,128)(2,1)S(1)}, u32[]{:S(2)}, u32[]{:S(2)}) collective-permute-start(bf16[2,112,1472]{2,1,0:T(8,128)(2,1)S(1)} %collective-permute-done.25), channel_id=1, source_target_pairs={{0,8},{4,12},{8,16},{12,20},{16,24},{20,28},{24,0},{28,4},{1,9},{5... | collective-permute-start | bytes 1978376 | tf_op jit(solution)/shard_map/ppermute | solution.py:57
  210.9 30.6 %collective-permute-start.33 = (bf16[1,2,112,1472]{3,2,1,0:T(8,128)(2,1)}, bf16[1,2,112,1472]{3,2,1,0:T(8,128)(2,1)S(1)}, u32[]{:S(2)}, u32[]{:S(2)}) collective-permute-start(bf16[1,2,112,1472]{3,2,1,0:T(8,128)(2,1)} %get-tuple-element.365), channel_id=1, source_target_pairs={{0,2},{1,3},{2,0},{3,1},{4,6},{5,7},{6,4},{7,5},{8,10},{9,11},{10,... | collective-permute-start | bytes 1978376 | tf_op jit(solution)/shard_map/ppermute | solution.py:62
  212.1 30.4 %collective-permute-start.34 = (bf16[1,2,112,1472]{3,2,1,0:T(8,128)(2,1)}, bf16[1,2,112,1472]{3,2,1,0:T(8,128)(2,1)S(1)}, u32[]{:S(2)}, u32[]{:S(2)}) collective-permute-start(bf16[1,2,112,1472]{3,2,1,0:T(8,128)(2,1)} %get-tuple-element.366), channel_id=1, source_target_pairs={{0,1},{1,0},{2,3},{3,2},{4,5},{5,4},{6,7},{7,6},{8,9},{9,8},{10,11... | collective-permute-start | bytes 1978376 | tf_op jit(solution)/shard_map/ppermute | solution.py:62
  243.4 46.2 %collective-permute-start.35 = (bf16[2,2,112,1472]{3,2,1,0:T(8,128)(2,1)}, bf16[2,2,112,1472]{3,2,1,0:T(8,128)(2,1)S(1)}, u32[]{:S(2)}, u32[]{:S(2)}) collective-permute-start(bf16[2,2,112,1472]{3,2,1,0:T(8,128)(2,1)} %get-tuple-element.370), channel_id=1, source_target_pairs={{0,2},{1,3},{2,0},{3,1},{4,6},{5,7},{6,4},{7,5},{8,10},{9,11},{10,... | collective-permute-start | bytes 3956744 | tf_op jit(solution)/shard_map/ppermute | solution.py:62
  244.4 45.2 %collective-permute-start.36 = (bf16[2,2,112,1472]{3,2,1,0:T(8,128)(2,1)}, bf16[2,2,112,1472]{3,2,1,0:T(8,128)(2,1)S(1)}, u32[]{:S(2)}, u32[]{:S(2)}) collective-permute-start(bf16[2,2,112,1472]{3,2,1,0:T(8,128)(2,1)} %get-tuple-element.371), channel_id=1, source_target_pairs={{0,1},{1,0},{2,3},{3,2},{4,5},{5,4},{6,7},{7,6},{8,9},{9,8},{10,11... | collective-permute-start | bytes 3956744 | tf_op jit(solution)/shard_map/ppermute | solution.py:62
  245.6 44.0 %collective-permute-start.37 = (bf16[448,1472]{1,0:T(8,128)(2,1)}, bf16[448,1472]{1,0:T(8,128)(2,1)}, u32[]{:S(2)}, u32[]{:S(2)}) collective-permute-start(bf16[448,1472]{1,0:T(8,128)(2,1)} %get-tuple-element.372), channel_id=1, source_target_pairs={{0,8},{4,12},{8,16},{12,20},{16,24},{20,28},{24,0},{28,4},{1,9},{5... | collective-permute-start | bytes 3956744 | tf_op jit(solution)/shard_map/ppermute | solution.py:57
  291.7 39.9 %collective-permute-start.38 = (bf16[5,112,1472]{2,1,0:T(8,128)(2,1)S(1)}, bf16[5,112,1472]{2,1,0:T(8,128)(2,1)S(1)}, u32[]{:S(2)}, u32[]{:S(2)}) collective-permute-start(bf16[5,112,1472]{2,1,0:T(8,128)(2,1)S(1)} %get-tuple-element.399), channel_id=1, source_target_pairs={{0,2},{1,3},{2,0},{3,1},{4,6},{5,7},{6,4},{7,5},{8,10},{9,11},{10,... | collective-permute-start | bytes 4945928 | tf_op jit(solution)/shard_map/ppermute | solution.py:62
  292.9 39.6 %collective-permute-start.39 = (bf16[5,112,1472]{2,1,0:T(8,128)(2,1)S(1)}, bf16[5,112,1472]{2,1,0:T(8,128)(2,1)S(1)}, u32[]{:S(2)}, u32[]{:S(2)}) collective-permute-start(bf16[5,112,1472]{2,1,0:T(8,128)(2,1)S(1)} %get-tuple-element.400), channel_id=1, source_target_pairs={{0,1},{1,0},{2,3},{3,2},{4,5},{5,4},{6,7},{7,6},{8,9},{9,8},{10,11... | collective-permute-start | bytes 4945928 | tf_op jit(solution)/shard_map/ppermute | solution.py:62
  296.3 33.6 %collective-permute-start.40 = (bf16[448,1472]{1,0:T(8,128)(2,1)}, bf16[448,1472]{1,0:T(8,128)(2,1)S(1)}, u32[]{:S(2)}, u32[]{:S(2)}) collective-permute-start(bf16[448,1472]{1,0:T(8,128)(2,1)} %add_convert_fusion), channel_id=1, source_target_pairs={{0,8},{4,12},{8,16},{12,20},{16,24},{20,28},{24,0},{28,4},{1,9},{5... | collective-permute-start | bytes 3956744 | tf_op jit(solution)/shard_map/ppermute | solution.py:57
  339.2 46.3 %collective-permute-start.45 = (bf16[6,112,1472]{2,1,0:T(8,128)(2,1)S(1)}, bf16[6,112,1472]{2,1,0:T(8,128)(2,1)}, u32[]{:S(2)}, u32[]{:S(2)}) collective-permute-start(bf16[6,112,1472]{2,1,0:T(8,128)(2,1)S(1)} %get-tuple-element.426), channel_id=1, source_target_pairs={{0,8},{4,12},{8,16},{12,20},{16,24},{20,28},{24,0},{28,4},{1,9},{5... | collective-permute-start | bytes 5935112 | tf_op jit(solution)/shard_map/ppermute | solution.py:57
  339.3 38.2 %collective-permute-start.42 = (bf16[2,256,768]{2,1,0:T(8,128)(2,1)}, bf16[2,256,768]{2,1,0:T(8,128)(2,1)S(1)}, u32[]{:S(2)}, u32[]{:S(2)}) collective-permute-start(bf16[2,256,768]{2,1,0:T(8,128)(2,1)} %get-tuple-element.417), channel_id=1, source_target_pairs={{0,1},{1,0},{2,3},{3,2},{4,5},{5,4},{6,7},{7,6},{8,9},{9,8},{10,11... | collective-permute-start | bytes 2359304 | tf_op jit(solution)/shard_map/ppermute | solution.py:62
  340.0 37.6 %collective-permute-start.43 = (bf16[2,256,768]{2,1,0:T(8,128)(2,1)}, bf16[2,256,768]{2,1,0:T(8,128)(2,1)S(1)}, u32[]{:S(2)}, u32[]{:S(2)}) collective-permute-start(bf16[2,256,768]{2,1,0:T(8,128)(2,1)} %get-tuple-element.418), channel_id=1, source_target_pairs={{0,2},{1,3},{2,0},{3,1},{4,6},{5,7},{6,4},{7,5},{8,10},{9,11},{10,... | collective-permute-start | bytes 2359304 | tf_op jit(solution)/shard_map/ppermute | solution.py:62
  340.8 36.7 %collective-permute-start.44 = (bf16[2,256,768]{2,1,0:T(8,128)(2,1)}, bf16[2,256,768]{2,1,0:T(8,128)(2,1)S(1)}, u32[]{:S(2)}, u32[]{:S(2)}) collective-permute-start(bf16[2,256,768]{2,1,0:T(8,128)(2,1)} %get-tuple-element.419), channel_id=1, source_target_pairs={{0,3},{1,2},{2,1},{3,0},{4,7},{5,6},{6,5},{7,4},{8,11},{9,10},{10,... | collective-permute-start | bytes 2359304 | tf_op jit(solution)/shard_map/ppermute | solution.py:62
  388.8 112.2 %reduce-scatter.3.cloned.1.call-start = ((), (), s32[]{:S(2)}) async-start(), calls=%async_computation.2 | async-start | bytes 2654208 | tf_op jit(solution)/shard_map/reduce_scatter | solution.py:1247
  393.7 40.7 %collective-permute-start.46 = (bf16[4,4,48,1472]{3,2,1,0:T(8,128)(2,1)}, bf16[4,4,48,1472]{3,2,1,0:T(8,128)(2,1)S(1)}, u32[]{:S(2)}, u32[]{:S(2)}) collective-permute-start(bf16[4,4,48,1472]{3,2,1,0:T(8,128)(2,1)} %get-tuple-element.443), channel_id=1, source_target_pairs={{0,4},{4,0},{8,12},{12,8},{16,20},{20,16},{24,28},{28,24},{1,5},{5... | collective-permute-start | bytes 6782984 | tf_op jit(solution)/shard_map/ppermute | solution.py:48
  402.5 26.8 %collective-permute-start.48 = (bf16[2,112,1472]{2,1,0:T(8,128)(2,1)}, bf16[2,112,1472]{2,1,0:T(8,128)(2,1)S(1)}, u32[]{:S(2)}, u32[]{:S(2)}) collective-permute-start(bf16[2,112,1472]{2,1,0:T(8,128)(2,1)} %get-tuple-element.449), channel_id=1, source_target_pairs={{0,1},{1,0},{2,3},{3,2},{4,5},{5,4},{6,7},{7,6},{8,9},{9,8},{10,11... | collective-permute-start | bytes 1978376 | tf_op jit(solution)/shard_map/ppermute | solution.py:62
  403.2 27.0 %collective-permute-start.49 = (bf16[2,112,1472]{2,1,0:T(8,128)(2,1)}, bf16[2,112,1472]{2,1,0:T(8,128)(2,1)S(1)}, u32[]{:S(2)}, u32[]{:S(2)}) collective-permute-start(bf16[2,112,1472]{2,1,0:T(8,128)(2,1)} %get-tuple-element.450), channel_id=1, source_target_pairs={{0,2},{1,3},{2,0},{3,1},{4,6},{5,7},{6,4},{7,5},{8,10},{9,11},{10,... | collective-permute-start | bytes 1978376 | tf_op jit(solution)/shard_map/ppermute | solution.py:62
  404.3 24.2 %collective-permute-start.50 = (bf16[1,112,1472]{2,1,0:T(8,128)(2,1)}, bf16[1,112,1472]{2,1,0:T(8,128)(2,1)S(1)}, u32[]{:S(2)}, u32[]{:S(2)}) collective-permute-start(bf16[1,112,1472]{2,1,0:T(8,128)(2,1)} %get-tuple-element.451), channel_id=1, source_target_pairs={{0,3},{1,2},{2,1},{3,0},{4,7},{5,6},{6,5},{7,4},{8,11},{9,10},{10,... | collective-permute-start | bytes 989192 | tf_op jit(solution)/shard_map/ppermute | solution.py:62
  408.4 26.0 %collective-permute-start.47 = (bf16[2,112,1472]{2,1,0:T(8,128)(2,1)S(1)}, bf16[2,112,1472]{2,1,0:T(8,128)(2,1)S(1)}, u32[]{:S(2)}, u32[]{:S(2)}) collective-permute-start(bf16[2,112,1472]{2,1,0:T(8,128)(2,1)S(1)} %fuse.13), channel_id=1, source_target_pairs={{0,8},{4,12},{8,16},{12,20},{16,24},{20,28},{24,0},{28,4},{1,9},{5... | collective-permute-start | bytes 1978376 | tf_op jit(solution)/shard_map/ppermute | solution.py:57
  440.4 17.2 %collective-permute-start.51 = (bf16[4,48,1472]{2,1,0:T(8,128)(2,1)S(1)}, bf16[4,48,1472]{2,1,0:T(8,128)(2,1)S(1)}, u32[]{:S(2)}, u32[]{:S(2)}) collective-permute-start(bf16[4,48,1472]{2,1,0:T(8,128)(2,1)S(1)} %get-tuple-element.459), channel_id=1, source_target_pairs={{0,1},{1,0},{2,3},{3,2},{4,5},{5,4},{6,7},{7,6},{8,9},{9,8},{10,11... | collective-permute-start | bytes 1695752 | tf_op jit(solution)/shard_map/ppermute | solution.py:62
  442.4 35.7 %collective-permute-start.54 = (bf16[2,112,1472]{2,1,0:T(8,128)(2,1)S(1)}, bf16[2,112,1472]{2,1,0:T(8,128)(2,1)S(1)}, u32[]{:S(2)}, u32[]{:S(2)}) collective-permute-start(bf16[2,112,1472]{2,1,0:T(8,128)(2,1)S(1)} %get-tuple-element.469), channel_id=1, source_target_pairs={{0,8},{4,12},{8,16},{12,20},{16,24},{20,28},{24,0},{28,4},{1,9},{5... | collective-permute-start | bytes 1978376 | tf_op jit(solution)/shard_map/ppermute | solution.py:57
  443.4 34.7 %collective-permute-start.52 = (bf16[4,48,1472]{2,1,0:T(8,128)(2,1)}, bf16[4,48,1472]{2,1,0:T(8,128)(2,1)}, u32[]{:S(2)}, u32[]{:S(2)}) collective-permute-start(bf16[4,48,1472]{2,1,0:T(8,128)(2,1)} %get-tuple-element.460), channel_id=1, source_target_pairs={{0,2},{1,3},{2,0},{3,1},{4,6},{5,7},{6,4},{7,5},{8,10},{9,11},{10,... | collective-permute-start | bytes 1695752 | tf_op jit(solution)/shard_map/ppermute | solution.py:62
  444.6 33.5 %collective-permute-start.53 = (bf16[4,48,1472]{2,1,0:T(8,128)(2,1)}, bf16[4,48,1472]{2,1,0:T(8,128)(2,1)}, u32[]{:S(2)}, u32[]{:S(2)}) collective-permute-start(bf16[4,48,1472]{2,1,0:T(8,128)(2,1)} %get-tuple-element.461), channel_id=1, source_target_pairs={{0,3},{1,2},{2,1},{3,0},{4,7},{5,6},{6,5},{7,4},{8,11},{9,10},{10,... | collective-permute-start | bytes 1695752 | tf_op jit(solution)/shard_map/ppermute | solution.py:62
  445.8 39.6 %collective-permute-start.60 = (bf16[1,112,1472]{2,1,0:T(8,128)(2,1)S(1)}, bf16[1,112,1472]{2,1,0:T(8,128)(2,1)S(1)}, u32[]{:S(2)}, u32[]{:S(2)}) collective-permute-start(bf16[1,112,1472]{2,1,0:T(8,128)(2,1)S(1)} %get-tuple-element.483.refs_2_), channel_id=1, source_target_pairs={{0,3},{1,2},{2,1},{3,0},{4,7},{5,6},{6,5},{7,4},{8,11},{9,10},{10,... | collective-permute-start | bytes 989192 | tf_op jit(solution)/shard_map/ppermute | solution.py:62
  478.3 22.0 %collective-permute-start.58 = (bf16[2,112,1472]{2,1,0:T(8,128)(2,1)S(1)}, bf16[2,112,1472]{2,1,0:T(8,128)(2,1)S(1)}, u32[]{:S(2)}, u32[]{:S(2)}) collective-permute-start(bf16[2,112,1472]{2,1,0:T(8,128)(2,1)S(1)} %get-tuple-element.484), channel_id=1, source_target_pairs={{0,1},{1,0},{2,3},{3,2},{4,5},{5,4},{6,7},{7,6},{8,9},{9,8},{10,11... | collective-permute-start | bytes 1978376 | tf_op jit(solution)/shard_map/ppermute | solution.py:62
  479.4 21.7 %collective-permute-start.59 = (bf16[2,112,1472]{2,1,0:T(8,128)(2,1)S(1)}, bf16[2,112,1472]{2,1,0:T(8,128)(2,1)S(1)}, u32[]{:S(2)}, u32[]{:S(2)}) collective-permute-start(bf16[2,112,1472]{2,1,0:T(8,128)(2,1)S(1)} %get-tuple-element.485), channel_id=1, source_target_pairs={{0,2},{1,3},{2,0},{3,1},{4,6},{5,7},{6,4},{7,5},{8,10},{9,11},{10,... | collective-permute-start | bytes 1978376 | tf_op jit(solution)/shard_map/ppermute | solution.py:62
  482.0 13.6 %collective-permute-start.55 = (bf16[64,1472]{1,0:T(8,128)(2,1)S(1)}, bf16[64,1472]{1,0:T(8,128)(2,1)S(1)}, u32[]{:S(2)}, u32[]{:S(2)}) collective-permute-start(bf16[64,1472]{1,0:T(8,128)(2,1)S(1)} %get-tuple-element.706), channel_id=1, source_target_pairs={{0,8},{4,12},{8,16},{12,20},{16,24},{20,28},{24,0},{28,4},{1,9},{5... | collective-permute-start | bytes 565256 | tf_op jit(solution)/shard_map/ppermute | solution.py:71
  483.2 14.5 %collective-permute-start.56 = (bf16[64,1472]{1,0:T(8,128)(2,1)S(1)}, bf16[64,1472]{1,0:T(8,128)(2,1)S(1)}, u32[]{:S(2)}, u32[]{:S(2)}) collective-permute-start(bf16[64,1472]{1,0:T(8,128)(2,1)S(1)} %get-tuple-element.707), channel_id=1, source_target_pairs={{0,16},{4,20},{8,24},{12,28},{16,0},{20,4},{24,8},{28,12},{1,17},{... | collective-permute-start | bytes 565256 | tf_op jit(solution)/shard_map/ppermute | solution.py:71
  485.4 14.9 %collective-permute-start.57 = (bf16[64,1472]{1,0:T(8,128)(2,1)S(1)}, bf16[64,1472]{1,0:T(8,128)(2,1)S(1)}, u32[]{:S(2)}, u32[]{:S(2)}) collective-permute-start(bf16[64,1472]{1,0:T(8,128)(2,1)S(1)} %get-tuple-element.705), channel_id=1, source_target_pairs={{0,24},{4,28},{8,0},{12,4},{16,8},{20,12},{24,16},{28,20},{1,25},{... | collective-permute-start | bytes 565256 | tf_op jit(solution)/shard_map/ppermute | solution.py:71
  504.0 26.3 %collective-permute-start.62 = (bf16[288,1472]{1,0:T(8,128)(2,1)S(1)}, bf16[288,1472]{1,0:T(8,128)(2,1)S(1)}, u32[]{:S(2)}, u32[]{:S(2)}) collective-permute-start(bf16[288,1472]{1,0:T(8,128)(2,1)S(1)} %get-tuple-element.505), channel_id=1, source_target_pairs={{0,1},{1,0},{2,3},{3,2},{4,5},{5,4},{6,7},{7,6},{8,9},{9,8},{10,11... | collective-permute-start | bytes 2543624 | tf_op jit(solution)/shard_map/ppermute | solution.py:62
  505.3 25.5 %collective-permute-start.63 = (bf16[288,1472]{1,0:T(8,128)(2,1)S(1)}, bf16[288,1472]{1,0:T(8,128)(2,1)S(1)}, u32[]{:S(2)}, u32[]{:S(2)}) collective-permute-start(bf16[288,1472]{1,0:T(8,128)(2,1)S(1)} %get-tuple-element.506), channel_id=1, source_target_pairs={{0,2},{1,3},{2,0},{3,1},{4,6},{5,7},{6,4},{7,5},{8,10},{9,11},{10,... | collective-permute-start | bytes 2543624 | tf_op jit(solution)/shard_map/ppermute | solution.py:62
  506.6 23.6 %collective-permute-start.64 = (bf16[64,1472]{1,0:T(8,128)(2,1)S(1)}, bf16[64,1472]{1,0:T(8,128)(2,1)S(1)}, u32[]{:S(2)}, u32[]{:S(2)}) collective-permute-start(bf16[64,1472]{1,0:T(8,128)(2,1)S(1)} %get-tuple-element.507), channel_id=1, source_target_pairs={{0,3},{1,2},{2,1},{3,0},{4,7},{5,6},{6,5},{7,4},{8,11},{9,10},{10,... | collective-permute-start | bytes 565256 | tf_op jit(solution)/shard_map/ppermute | solution.py:62
  509.8 39.2 %collective-permute-start.61 = (bf16[8,64,1472]{2,1,0:T(8,128)(2,1)}, bf16[8,64,1472]{2,1,0:T(8,128)(2,1)}, u32[]{:S(2)}, u32[]{:S(2)}) collective-permute-start(bf16[8,64,1472]{2,1,0:T(8,128)(2,1)} %bitcast.99), channel_id=1, source_target_pairs={{0,4},{4,0},{8,12},{12,8},{16,20},{20,16},{24,28},{28,24},{1,5},{5... | collective-permute-start | bytes 4521992 | tf_op jit(solution)/shard_map/ppermute | solution.py:48
  532.1 14.1 %collective-permute-start.67 = (bf16[96,1472]{1,0:T(8,128)(2,1)S(1)}, bf16[96,1472]{1,0:T(8,128)(2,1)S(1)}, u32[]{:S(2)}, u32[]{:S(2)}) collective-permute-start(bf16[96,1472]{1,0:T(8,128)(2,1)S(1)} %pad_maximum_fusion.32), channel_id=1, source_target_pairs={{0,2},{1,3},{2,0},{3,1},{4,6},{5,7},{6,4},{7,5},{8,10},{9,11},{10,... | collective-permute-start | bytes 847880 | tf_op jit(solution)/shard_map/ppermute | solution.py:62
  (201 other events, 1752.4 us)
Sparse Core Ops, SparseCore 0:
  388.9 37.8 reduce-scatter.4
  436.2 43.8 reduce-scatter.2

commit v5 on v4

--- a/solution.py
+++ b/solution.py
@@ -1329,7 +1329,11 @@
     cross_parts[0] = messages[0]
     moved = {k: to_mem(p, k) for k, p in enumerate(messages) if k}
     res_more = rows_to_core(res_send)
-    moved, small_rows, self_mine, cross_own = tie(moved, small_rows, self_mine, cross_parts[0])
+    result = (second_sum + res_own + res_more.astype(f32)).reshape(micros, length, width).swapaxes(1, 2)
+    moved, small_rows, self_mine, cross_own, result = tie(
+        moved, small_rows, self_mine, cross_parts[0], result
+    )
+    result = result.swapaxes(1, 2)
     linear_g = jnp.concatenate([linear_g, moved[1][:cut].reshape(-1, part, width)])
     gate_g = jnp.concatenate([gate_g, moved[half][:cut].reshape(-1, part, width)])
     gate_order = gate_order + [k | half for k in gate_order]
@@ -1347,7 +1351,6 @@
     gate_out = settle(gate_g, gate_order).reshape(feed, width)
     linear_out = settle(linear_g, linear_order).reshape(feed, width)
     down_out = natural(down_g, mem_index).astype(f32).reshape(feed, width)
-    result = second_sum + res_own + res_more.astype(f32)
     mine_g, gate_out, linear_out, down_out = tie(mine_g, gate_out, linear_out, down_out)
 
     def settled(start, rows_of):

time: 571 us -> 571 us (level)
  waiting for transfers between devices: 141 us -> 135 us
    ppermute x41, waiting for transfers between devices: 80.5 us -> 73.7 us  [to_mem(): return lax.ppermute(value, 'mem', [(i, i ^ mask) for i in range(count)])]
    unnamed x399 -> x420, local copies, waits for them, and re-layouts: 48.1 us -> 44.3 us
  transfers between devices with their start and end apart: 71 -> 71, of which waited for: 25 -> 25; matrix products, arithmetic and copies ran while one was open for 10% -> 11% of each run, Pallas kernels for 38% -> 38%
where the time goes in v5:
time: 571 us; the launch traced here: 562 us
  Pallas kernels  216 us (38%)
  waiting for transfers between devices  135 us (24%)
  local copies, waits for them, and re-layouts  70 us (12%)
  starting transfers between devices  69.6 us (12%)
  other arithmetic  43.9 us (8%)
  between operations  16.9 us (3%)
  blocking collectives  8.17 us (1%)
    ppermute x41, waiting for transfers between devices, to_mem(): return lax.ppermute(value, 'mem', [(i, i ^ mask) for i in range(count)])  73.7 us
    pallas_call x3, Pallas kernels, feed_grad(): pl.pallas_call(functools.partial(feed_grad_kernel, places, len(weights),...  59.1 us
    ppermute x14, waiting for transfers between devices, to_next(): lax.ppermute(value, 'seq', [(i, (i + 2) % count) for i in range(count)])  47.7 us
    ppermute x41, starting transfers between devices, to_mem(): return lax.ppermute(value, 'mem', [(i, i ^ mask) for i in range(count)])  46 us
    unnamed x420, local copies, waits for them, and re-layouts  44.3 us
    pallas_call x2, Pallas kernels, feed_sum(): pl.pallas_call(functools.partial(feed_sum_kernel, places, act_places, len...  38.2 us
    pallas_call x1, Pallas kernels, cross_bwd(): pl.pallas_call(functools.partial(cross_bwd_kernel, depth, length, len(kvs...  32.4 us
    pallas_call x1, Pallas kernels, self_bwd(): pl.pallas_call(functools.partial(self_bwd_kernel, depth, length), out_sha...  19.1 us
  transfers between devices with their start and end apart: 71, of which 25 were waited for; matrix products, arithmetic and copies ran while one was open for 11% of the time, Pallas kernels for 38%

profile of v5, /device:TPU:8, one launch (start us, length us, event | category | flops | bytes accessed | tf_op | source)
XLA Modules:
  0.0 562.0 jit_solution(2208476964237447790)
XLA Ops:
  14.5 2.0 collective-permute-start.2
  16.5 1.7 copy.96
  22.5 2.4 constant_dynamic-slice_fusion.22
  32.4 8.2 %all-gather = s32[8,1,4,256]{3,2,1,0:T(4,128)S(1)} all-gather(s32[2,1,4,256]{3,2,1,0:T(4,128)S(1)} %copy-done.194), channel_id=2, replica_groups=mesh['seq'=8,'mem'=4] {'mem'}, dimensions={0}, use_global_device_ids=true | all-gather | bytes 40960 | tf_op jit(solution)/shard_map/all_gather | solution.py:943
  45.3 7.6 %collective-permute-done.4 = bf16[1,3,48,1472]{3,2,1,0:T(8,128)(2,1)S(1)} collective-permute-done((bf16[1,3,48,1472]{3,2,1,0:T(8,128)(2,1)S(1)}, bf16[1,3,48,1472]{3,2,1,0:T(8,128)(2,1)S(1)}, u32[]{:S(2)}, u32[]{:S(2)}) %collective-permute-start.4) | collective-permute-done | bytes 423968 | tf_op jit(solution)/shard_map/ppermute | solution.py:62
  54.2 4.0 collective-permute-done.6
  64.1 1.8 fusion.4.bias
  65.9 13.6 %collective-permute-done.9 = bf16[2,112,1472]{2,1,0:T(8,128)(2,1)} collective-permute-done((bf16[2,112,1472]{2,1,0:T(8,128)(2,1)}, bf16[2,112,1472]{2,1,0:T(8,128)(2,1)}, u32[]{:S(2)}, u32[]{:S(2)}) %collective-permute-start.9) | collective-permute-done | bytes 659488 | tf_op jit(solution)/shard_map/ppermute | solution.py:57
  79.5 2.7 collective-permute-done.7
  86.8 1.8 collective-permute-start.12
  90.7 13.8 %collective-permute-done.12 = bf16[1,2,112,1472]{3,2,1,0:T(8,128)(2,1)S(1)} collective-permute-done((bf16[1,2,112,1472]{3,2,1,0:T(8,128)(2,1)S(1)}, bf16[1,2,112,1472]{3,2,1,0:T(8,128)(2,1)S(1)}, u32[]{:S(2)}, u32[]{:S(2)}) %collective-permute-start.12) | collective-permute-done | bytes 659488 | tf_op jit(solution)/shard_map/ppermute | solution.py:62
  109.8 9.2 %kv_fwd.1 = (bf16[2,256,768]{2,1,0:T(8,128)(2,1)S(1)}, bf16[2,256,768]{2,1,0:T(8,128)(2,1)S(1)}, bf16[2,256,768]{2,1,0:T(8,128)(2,1)S(1)}, bf16[2,256,768]{2,1,0:T(8,128)(2,1)S(1)}) custom-call(s32[4]{0:T(128)S(1)} %pad_add_fusion.place, bf16[2,4,1472,256]{3,2,1,0:T(8,128)(2,1)S(1)} %bitcast.282, bf16[384,1472]{1,0:T(8,128)(2,1)S(1)} %bitcast.287, ...), custom_call_target="tpu_custom_call" | custom-call | flops 8999999488 | bytes 27000000 | tf_op jit(solution)/shard_map/kv_fwd/pallas_call | solution.py:440
  120.4 3.9 collective-permute-done.17
  126.2 1.6 collective-permute-start.18
  127.9 1.7 collective-permute-start.19
  130.2 2.7 collective-permute-start.22
  132.9 13.5 %self_fwd.1 = (bf16[512,1472]{1,0:T(8,128)(2,1)S(1)}, bf16[512,1472]{1,0:T(8,128)(2,1)S(1)}, bf16[512,384]{1,0:T(8,128)(2,1)S(1)}, bf16[512,384]{1,0:T(8,128)(2,...) custom-call(bf16[2,1472,256]{2,1,0:T(8,128)(2,1)S(1)} %bitcast.284, ...), custom_call_target="tpu_custom_call" | custom-call | flops 16000000000 | bytes 48000000 | tf_op jit(solution)/shard_map/self_fwd/pallas_call | solution.py:230
  150.5 11.3 %collective-permute-done.22 = bf16[2,112,1472]{2,1,0:T(8,128)(2,1)S(1)} collective-permute-done((bf16[2,112,1472]{2,1,0:T(8,128)(2,1)}, bf16[2,112,1472]{2,1,0:T(8,128)(2,1)S(1)}, u32[]{:S(2)}, u32[]{:S(2)}) %collective-permute-start.22) | collective-permute-done | bytes 659488 | tf_op jit(solution)/shard_map/ppermute | solution.py:57
  164.4 1.7 collective-permute-start.23
  167.2 9.7 %cross_fwd.1 = (bf16[512,384]{1,0:T(8,128)(2,1)S(1)}, f32[512,1472]{1,0:T(8,128)S(1)}, bf16[512,1472]{1,0:T(8,128)(2,1)S(1)}) custom-call(bf16[512,384]{1,0:T(8,128)(2,1)S(1)} %get-tuple-element.314.cq, f32[2,1,1024]{2,1,0:T(1,128)S(1)} %and_convert_fusion.mask, bf16[384,1472]{1,0:T(8,128)(2,1)S(1)} %bitcast.302, f32[512,1472]{1,0:T(8,128)S(1)} %copy-done.112, ...), custom_call_target="tpu_custom_call" | custom-call | flops 15000000512 | bytes 45000000 | tf_op jit(solution)/shard_map/cross_fwd/pallas_call | solution.py:271
  176.9 1.6 copy-done.2
  180.4 2.7 collective-permute-done.25
  193.1 15.1 %feed_grad.3 = (bf16[1,2,112,1472]{3,2,1,0:T(8,128)(2,1)}, bf16[1,2,112,1472]{3,2,1,0:T(8,128)(2,1)}, bf16[1,2,112,1472]{3,2,1,0:T(8,128)(2,1)}, bf16[1,2,112,14...) custom-call(bf16[512,1472]{1,0:T(8,128)(2,1)} %copy-done.4, ...), custom_call_target="tpu_custom_call" | custom-call | flops 1000000000 | bytes 3000000 | tf_op jit(solution)/shard_map/feed_grad/pallas_call | solution.py:671
  208.3 2.6 collective-permute-start.32
  212.7 28.7 %feed_grad.4 = (bf16[2,2,112,1472]{3,2,1,0:T(8,128)(2,1)}, bf16[2,2,112,1472]{3,2,1,0:T(8,128)(2,1)}, bf16[2,2,112,1472]{3,2,1,0:T(8,128)(2,1)}, bf16[2,2,112,14...) custom-call(bf16[512,1472]{1,0:T(8,128)(2,1)} %copy-done.4, ...), custom_call_target="tpu_custom_call" | custom-call | flops 25999998976 | bytes 78000000 | tf_op jit(solution)/shard_map/feed_grad/pallas_call | solution.py:671
  245.6 4.4 collective-permute-start.37
  250.1 15.3 %feed_grad.5 = (bf16[1,2,112,1472]{3,2,1,0:T(8,128)(2,1)}, bf16[1,2,112,1472]{3,2,1,0:T(8,128)(2,1)}, bf16[1,2,112,1472]{3,2,1,0:T(8,128)(2,1)}, bf16[1,2,112,14...) custom-call(bf16[512,1472]{1,0:T(8,128)(2,1)} %copy-done.4, ...), custom_call_target="tpu_custom_call" | custom-call | flops 12999999488 | bytes 39000000 | tf_op jit(solution)/shard_map/feed_grad/pallas_call | solution.py:671
  266.6 22.9 %feed_sum.2 = (f32[512,1472]{1,0:T(8,128)}, bf16[512,1472]{1,0:T(8,128)(2,1)}) custom-call(bf16[2,1,112,1472]{3,2,1,0:T(8,128)(2,1)S(1)} %copy-done.12, bf16[2,1,112,1472]{3,2,1,0:T(8,128)(2,1)S(1)} %copy-done.51, bf16[2,1,112,1472]{3,2,1,0:T(8,128)(2,1)S(1)} %copy-done.16, bf16[2,1,112,1472]{3,2,1,0:T(8,128)(2,1)S(1)} %copy-done.53, ...), custom_call_target="tpu_custom_call" | custom-call | flops 23000000512 | bytes 69000000 | tf_op jit(solution)/shard_map/feed_sum/pallas_call | solution.py:734
  293.5 2.8 add_convert_fusion
  297.5 32.4 %cross_bwd.1 = (bf16[2,256,768]{2,1,0:T(8,128)(2,1)S(1)}, bf16[2,256,768]{2,1,0:T(8,128)(2,1)}, bf16[2,256,768]{2,1,0:T(8,128)(2,1)}, bf16[2,256,768]{2,1,0:T(8,...) custom-call(bf16[512,1472]{1,0:T(8,128)(2,1)} %bitcast.317, ...), custom_call_target="tpu_custom_call" | custom-call | flops 31000000512 | bytes 93000000 | tf_op jit(solution)/shard_map/cross_bwd/pallas_call | solution.py:339
  329.9 1.7 collective-permute-done.38.refs_3_.refs_2_
  332.5 2.0 copy-done.72
  340.8 2.0 collective-permute-start.44
  342.9 19.1 %self_bwd.1 = (bf16[384,1472]{1,0:T(8,128)(2,1)S(1)}, bf16[384,1472]{1,0:T(8,128)(2,1)S(1)}, bf16[384,1472]{1,0:T(8,128)(2,1)S(1)}, bf16[384,1472]{1,0:T(8,128)(...) custom-call(f32[512,1472]{1,0:T(8,128)} %get-tuple-element.424.first_grad, ...), custom_call_target="tpu_custom_call" | custom-call | flops 20999999488 | bytes 63000000 | tf_op jit(solution)/shard_map/self_bwd/pallas_call | solution.py:405
  362.1 15.4 %feed_sum.3 = (f32[512,1472]{1,0:T(8,128)}, bf16[512,1472]{1,0:T(8,128)(2,1)}) custom-call(bf16[224,1472]{1,0:T(8,128)(2,1)S(1)} %bitcast.269, bf16[224,1472]{1,0:T(8,128)(2,1)S(1)} %bitcast.273, bf16[224,1472]{1,0:T(8,128)(2,1)S(1)} %bitcast.271, bf16[224,1472]{1,0:T(8,128)(2,1)S(1)} %bitcast.275, bf16[448,1472]{1,0:T(8,128)(2,1)} %bitcast.310, ...), custom_call_target="tpu_custom_call" | custom-call | flops 1000000000 | bytes 3000000 | tf_op jit(solution)/shard_map/feed_sum/pallas_call | solution.py:734
  377.6 7.9 %collective-permute-done.45 = bf16[6,112,1472]{2,1,0:T(8,128)(2,1)} collective-permute-done((bf16[6,112,1472]{2,1,0:T(8,128)(2,1)S(1)}, bf16[6,112,1472]{2,1,0:T(8,128)(2,1)}, u32[]{:S(2)}, u32[]{:S(2)}) %collective-permute-start.45) | collective-permute-done | bytes 1978400 | tf_op jit(solution)/shard_map/ppermute | solution.py:57
  385.5 3.2 pad_maximum_fusion.1
  388.8 4.8 core_split.1
  393.7 2.5 slice.279.refs_0_
  397.4 5.0 fuse.14
  409.9 2.7 copy-done.33
  412.7 8.2 %kv_weights.1 = (bf16[384,1472]{1,0:T(8,128)(2,1)S(1)}, bf16[384,1472]{1,0:T(8,128)(2,1)S(1)}) custom-call(s32[4]{0:T(128)S(1)} %copy-done.30, bf16[2,4,1472,256]{3,2,1,0:T(8,128)(2,1)S(1)} %bitcast.283, bf16[2,256,768]{2,1,0:T(8,128)(2,1)S(1)} %copy-done.110, bf16[2,256,768]{2,1,0:T(8,128)(2,1)S(1)} %copy-done.38, bf16[2,256,768]{2,1,0:T(8,128)(2,1)S(1)} %copy-done.41, ...), custom_call_target="tpu_custom_call" | custom-call | flops 8999999488 | bytes 27000000 | tf_op jit(solution)/shard_map/kv_weights/pallas_call | solution.py:519
  420.9 7.5 %collective-permute-done.50.refs_6_ = bf16[1,112,1472]{2,1,0:T(8,128)(2,1)S(1)} collective-permute-done((bf16[1,112,1472]{2,1,0:T(8,128)(2,1)}, bf16[1,112,1472]{2,1,0:T(8,128)(2,1)S(1)}, u32[]{:S(2)}, u32[]{:S(2)}) %collective-permute-start.50) | collective-permute-done | bytes 329760 | tf_op jit(solution)/shard_map/ppermute | solution.py:62
  430.0 4.3 collective-permute-done.47.refs_0_
  434.3 1.6 pad_maximum_fusion
  436.6 1.7 copy-done.106
  438.3 2.0 columns.1
  445.8 1.7 collective-permute-start.60
  447.6 10.1 %kv_memory.1 = f32[2,4,1472,256]{3,2,1,0:T(8,128)} custom-call(s32[4]{0:T(128)S(1)} %copy-done.30, bf16[384,1472]{1,0:T(8,128)(2,1)S(1)} %bitcast.288, bf16[384,1472]{1,0:T(8,128)(2,1)S(1)} %bitcast.290, bf16[2,256,768]{2,1,0:T(8,128)(2,1)S(1)} %copy-done.111, bf16[2,256,768]{2,1,0:T(8,128)(2,1)S(1)} %copy-done.39, bf16[2,256,768]{2,1,0:T(8,128)(2,1)S(1)} %copy-done.42, ...), custom_call_target="tpu_custom_call" | custom-call | flops 10000000000 | bytes 30000000 | tf_op jit(solution)/shard_map/kv_memory/pallas_call | solution.py:539
  460.1 3.6 copy.110
  463.9 14.0 %collective-permute-done.52 = bf16[4,48,1472]{2,1,0:T(8,128)(2,1)} collective-permute-done((bf16[4,48,1472]{2,1,0:T(8,128)(2,1)}, bf16[4,48,1472]{2,1,0:T(8,128)(2,1)}, u32[]{:S(2)}, u32[]{:S(2)}) %collective-permute-start.52) | collective-permute-done | bytes 565280 | tf_op jit(solution)/shard_map/ppermute | solution.py:62
  483.1 2.3 collective-permute-start.56
  485.4 1.7 collective-permute-start.57
  487.1 8.6 %collective-permute-done.55 = bf16[64,1472]{1,0:T(8,128)(2,1)S(1)} collective-permute-done((bf16[64,1472]{1,0:T(8,128)(2,1)S(1)}, bf16[64,1472]{1,0:T(8,128)(2,1)S(1)}, u32[]{:S(2)}, u32[]{:S(2)}) %collective-permute-start.55) | collective-permute-done | bytes 188448 | tf_op jit(solution)/shard_map/ppermute | solution.py:71
  495.7 2.1 collective-permute-done.56
  497.8 2.6 collective-permute-done.57
  503.5 1.7 collective-permute-start.61
  506.3 2.0 bitcast_convert_fusion
  510.0 2.6 convert_add_fusion
  512.7 3.7 copy.109
  516.3 13.9 %collective-permute-done.63 = bf16[64,1472]{1,0:T(8,128)(2,1)S(1)} collective-permute-done((bf16[64,1472]{1,0:T(8,128)(2,1)S(1)}, bf16[64,1472]{1,0:T(8,128)(2,1)S(1)}, u32[]{:S(2)}, u32[]{:S(2)}) %collective-permute-start.63) | collective-permute-done | bytes 188448 | tf_op jit(solution)/shard_map/ppermute | solution.py:62
  539.6 2.0 bitcast_convert_fusion.1
  542.2 2.0 bitcast_convert_fusion.2
  545.6 4.7 collective-permute-done.67
  (654 shorter events, 130.9 us)
Async XLA Ops:
  7.2 493.2 %reduce-scatter.5.cloned.1.call-start = ((), (), s32[]{:S(2)}) async-start(), calls=%async_computation.3 | async-start | bytes 2654208 | tf_op jit(solution)/shard_map/reduce_scatter | solution.py:1247
  11.9 29.6 %collective-permute-start = (bf16[2,48,1472]{2,1,0:T(8,128)(2,1)}, bf16[2,48,1472]{2,1,0:T(8,128)(2,1)S(1)}, u32[]{:S(2)}, u32[]{:S(2)}) collective-permute-start(bf16[2,48,1472]{2,1,0:T(8,128)(2,1)} %pad_maximum_fusion.31), channel_id=1, source_target_pairs={{0,8},{4,12},{8,16},{12,20},{16,24},{20,28},{24,0},{28,4},{1,9},{5... | collective-permute-start | bytes 847880 | tf_op jit(solution)/shard_map/ppermute | solution.py:71
  13.5 28.0 %collective-permute-start.1 = (bf16[2,48,1472]{2,1,0:T(8,128)(2,1)}, bf16[2,48,1472]{2,1,0:T(8,128)(2,1)S(1)}, u32[]{:S(2)}, u32[]{:S(2)}) collective-permute-start(bf16[2,48,1472]{2,1,0:T(8,128)(2,1)} %pad_maximum_fusion.31), channel_id=1, source_target_pairs={{0,16},{4,20},{8,24},{12,28},{16,0},{20,4},{24,8},{28,12},{1,17},{... | collective-permute-start | bytes 847880 | tf_op jit(solution)/shard_map/ppermute | solution.py:71
  14.5 27.0 %collective-permute-start.2 = (bf16[2,48,1472]{2,1,0:T(8,128)(2,1)}, bf16[2,48,1472]{2,1,0:T(8,128)(2,1)S(1)}, u32[]{:S(2)}, u32[]{:S(2)}) collective-permute-start(bf16[2,48,1472]{2,1,0:T(8,128)(2,1)} %pad_maximum_fusion.31), channel_id=1, source_target_pairs={{0,24},{4,28},{8,0},{12,4},{16,8},{20,12},{24,16},{28,20},{1,25},{... | collective-permute-start | bytes 847880 | tf_op jit(solution)/shard_map/ppermute | solution.py:71
  18.3 23.2 %collective-permute-start.3 = (bf16[8,64,1472]{2,1,0:T(8,128)(2,1)S(1)}, bf16[8,64,1472]{2,1,0:T(8,128)(2,1)}, u32[]{:S(2)}, u32[]{:S(2)}) collective-permute-start(bf16[8,64,1472]{2,1,0:T(8,128)(2,1)S(1)} %bitcast.313), channel_id=1, source_target_pairs={{0,4},{4,0},{8,12},{12,8},{16,20},{20,16},{24,28},{28,24},{1,5},{5... | collective-permute-start | bytes 4521992 | tf_op jit(solution)/shard_map/ppermute | solution.py:48
  41.5 16.7 %collective-permute-start.6 = (bf16[2,112,1472]{2,1,0:T(8,128)(2,1)S(1)}, bf16[2,112,1472]{2,1,0:T(8,128)(2,1)}, u32[]{:S(2)}, u32[]{:S(2)}) collective-permute-start(bf16[2,112,1472]{2,1,0:T(8,128)(2,1)S(1)} %pad_maximum_fusion.15), channel_id=1, source_target_pairs={{0,8},{4,12},{8,16},{12,20},{16,24},{20,28},{24,0},{28,4},{1,9},{5... | collective-permute-start | bytes 1978376 | tf_op jit(solution)/shard_map/ppermute | solution.py:57
  59.2 20.3 %collective-permute-start.8 = (bf16[2,3,48,1472]{3,2,1,0:T(8,128)(2,1)}, bf16[2,3,48,1472]{3,2,1,0:T(8,128)(2,1)}, u32[]{:S(2)}, u32[]{:S(2)}) collective-permute-start(bf16[2,3,48,1472]{3,2,1,0:T(8,128)(2,1)} %pad_maximum_fusion.14), channel_id=1, source_target_pairs={{0,1},{1,0},{2,3},{3,2},{4,5},{5,4},{6,7},{7,6},{8,9},{9,8},{10,11... | collective-permute-start | bytes 2543624 | tf_op jit(solution)/shard_map/ppermute | solution.py:62
  61.7 20.5 %collective-permute-start.7 = (bf16[2,3,48,1472]{3,2,1,0:T(8,128)(2,1)}, bf16[2,3,48,1472]{3,2,1,0:T(8,128)(2,1)}, u32[]{:S(2)}, u32[]{:S(2)}) collective-permute-start(bf16[2,3,48,1472]{3,2,1,0:T(8,128)(2,1)} %pad_maximum_fusion.13), channel_id=1, source_target_pairs={{0,2},{1,3},{2,0},{3,1},{4,6},{5,7},{6,4},{7,5},{8,10},{9,11},{10,... | collective-permute-start | bytes 2543624 | tf_op jit(solution)/shard_map/ppermute | solution.py:62
  63.2 16.3 %collective-permute-start.9 = (bf16[2,112,1472]{2,1,0:T(8,128)(2,1)}, bf16[2,112,1472]{2,1,0:T(8,128)(2,1)}, u32[]{:S(2)}, u32[]{:S(2)}) collective-permute-start(bf16[2,112,1472]{2,1,0:T(8,128)(2,1)} %collective-permute-done.6), channel_id=1, source_target_pairs={{0,8},{4,12},{8,16},{12,20},{16,24},{20,28},{24,0},{28,4},{1,9},{5... | collective-permute-start | bytes 1978376 | tf_op jit(solution)/shard_map/ppermute | solution.py:57
  83.8 22.2 %collective-permute-start.10 = (bf16[4,4,48,1472]{3,2,1,0:T(8,128)(2,1)S(1)}, bf16[4,4,48,1472]{3,2,1,0:T(8,128)(2,1)S(1)}, u32[]{:S(2)}, u32[]{:S(2)}) collective-permute-start(bf16[4,4,48,1472]{3,2,1,0:T(8,128)(2,1)S(1)} %maximum_maximum_fusion.own), channel_id=1, source_target_pairs={{0,4},{4,0},{8,12},{12,8},{16,20},{20,16},{24,28},{28,24},{1,5},{5... | collective-permute-start | bytes 6782984 | tf_op jit(solution)/shard_map/ppermute | solution.py:48
  85.0 21.0 %collective-permute-start.13 = (bf16[2,112,1472]{2,1,0:T(8,128)(2,1)}, bf16[2,112,1472]{2,1,0:T(8,128)(2,1)S(1)}, u32[]{:S(2)}, u32[]{:S(2)}) collective-permute-start(bf16[2,112,1472]{2,1,0:T(8,128)(2,1)} %collective-permute-done.9), channel_id=1, source_target_pairs={{0,8},{4,12},{8,16},{12,20},{16,24},{20,28},{24,0},{28,4},{1,9},{5... | collective-permute-start | bytes 1978376 | tf_op jit(solution)/shard_map/ppermute | solution.py:57
  86.8 17.6 %collective-permute-start.12 = (bf16[1,2,112,1472]{3,2,1,0:T(8,128)(2,1)S(1)}, bf16[1,2,112,1472]{3,2,1,0:T(8,128)(2,1)S(1)}, u32[]{:S(2)}, u32[]{:S(2)}) collective-permute-start(bf16[1,2,112,1472]{3,2,1,0:T(8,128)(2,1)S(1)} %maximum_bitcast_fusion.1), channel_id=1, source_target_pairs={{0,2},{1,3},{2,0},{3,1},{4,6},{5,7},{6,4},{7,5},{8,10},{9,11},{10,... | collective-permute-start | bytes 1978376 | tf_op jit(solution)/shard_map/ppermute | solution.py:62
  88.7 17.3 %collective-permute-start.11 = (bf16[1,2,112,1472]{3,2,1,0:T(8,128)(2,1)S(1)}, bf16[1,2,112,1472]{3,2,1,0:T(8,128)(2,1)S(1)}, u32[]{:S(2)}, u32[]{:S(2)}) collective-permute-start(bf16[1,2,112,1472]{3,2,1,0:T(8,128)(2,1)S(1)} %maximum_bitcast_fusion), channel_id=1, source_target_pairs={{0,1},{1,0},{2,3},{3,2},{4,5},{5,4},{6,7},{7,6},{8,9},{9,8},{10,11... | collective-permute-start | bytes 1978376 | tf_op jit(solution)/shard_map/ppermute | solution.py:62
  106.1 18.2 %collective-permute-start.14 = (bf16[4,4,48,1472]{3,2,1,0:T(8,128)(2,1)S(1)}, bf16[4,4,48,1472]{3,2,1,0:T(8,128)(2,1)S(1)}, u32[]{:S(2)}, u32[]{:S(2)}) collective-permute-start(bf16[4,4,48,1472]{3,2,1,0:T(8,128)(2,1)S(1)} %maximum_maximum_fusion.1.own), channel_id=1, source_target_pairs={{0,4},{4,0},{8,12},{12,8},{16,20},{20,16},{24,28},{28,24},{1,5},{5... | collective-permute-start | bytes 6782984 | tf_op jit(solution)/shard_map/ppermute | solution.py:48
  106.2 14.1 %collective-permute-start.15 = (bf16[1,112,1472]{2,1,0:T(8,128)(2,1)S(1)}, bf16[1,112,1472]{2,1,0:T(8,128)(2,1)S(1)}, u32[]{:S(2)}, u32[]{:S(2)}) collective-permute-start(bf16[1,112,1472]{2,1,0:T(8,128)(2,1)S(1)} %get-tuple-element.670), channel_id=1, source_target_pairs={{0,1},{1,0},{2,3},{3,2},{4,5},{5,4},{6,7},{7,6},{8,9},{9,8},{10,11... | collective-permute-start | bytes 989192 | tf_op jit(solution)/shard_map/ppermute | solution.py:62
  106.6 13.8 %collective-permute-start.16 = (bf16[1,112,1472]{2,1,0:T(8,128)(2,1)S(1)}, bf16[1,112,1472]{2,1,0:T(8,128)(2,1)S(1)}, u32[]{:S(2)}, u32[]{:S(2)}) collective-permute-start(bf16[1,112,1472]{2,1,0:T(8,128)(2,1)S(1)} %get-tuple-element.669), channel_id=1, source_target_pairs={{0,2},{1,3},{2,0},{3,1},{4,6},{5,7},{6,4},{7,5},{8,10},{9,11},{10,... | collective-permute-start | bytes 989192 | tf_op jit(solution)/shard_map/ppermute | solution.py:62
  106.9 17.4 %collective-permute-start.17 = (bf16[2,112,1472]{2,1,0:T(8,128)(2,1)S(1)}, bf16[2,112,1472]{2,1,0:T(8,128)(2,1)S(1)}, u32[]{:S(2)}, u32[]{:S(2)}) collective-permute-start(bf16[2,112,1472]{2,1,0:T(8,128)(2,1)S(1)} %copy-done.171), channel_id=1, source_target_pairs={{0,8},{4,12},{8,16},{12,20},{16,24},{20,28},{24,0},{28,4},{1,9},{5... | collective-permute-start | bytes 1978376 | tf_op jit(solution)/shard_map/ppermute | solution.py:57
  126.2 35.5 %collective-permute-start.18 = (bf16[2,256,768]{2,1,0:T(8,128)(2,1)S(1)}, bf16[2,256,768]{2,1,0:T(8,128)(2,1)S(1)}, u32[]{:S(2)}, u32[]{:S(2)}) collective-permute-start(bf16[2,256,768]{2,1,0:T(8,128)(2,1)S(1)} %get-tuple-element.296), channel_id=1, source_target_pairs={{0,1},{1,0},{2,3},{3,2},{4,5},{5,4},{6,7},{7,6},{8,9},{9,8},{10,11... | collective-permute-start | bytes 2359304 | tf_op jit(solution)/shard_map/ppermute | solution.py:62
  127.9 35.1 %collective-permute-start.19 = (bf16[2,256,768]{2,1,0:T(8,128)(2,1)S(1)}, bf16[2,256,768]{2,1,0:T(8,128)(2,1)S(1)}, u32[]{:S(2)}, u32[]{:S(2)}) collective-permute-start(bf16[2,256,768]{2,1,0:T(8,128)(2,1)S(1)} %get-tuple-element.297), channel_id=1, source_target_pairs={{0,2},{1,3},{2,0},{3,1},{4,6},{5,7},{6,4},{7,5},{8,10},{9,11},{10,... | collective-permute-start | bytes 2359304 | tf_op jit(solution)/shard_map/ppermute | solution.py:62
  129.6 33.4 %collective-permute-start.20 = (bf16[2,256,768]{2,1,0:T(8,128)(2,1)S(1)}, bf16[2,256,768]{2,1,0:T(8,128)(2,1)S(1)}, u32[]{:S(2)}, u32[]{:S(2)}) collective-permute-start(bf16[2,256,768]{2,1,0:T(8,128)(2,1)S(1)} %get-tuple-element.298), channel_id=1, source_target_pairs={{0,3},{1,2},{2,1},{3,0},{4,7},{5,6},{6,5},{7,4},{8,11},{9,10},{10,... | collective-permute-start | bytes 2359304 | tf_op jit(solution)/shard_map/ppermute | solution.py:62
  129.7 20.8 %collective-permute-start.21 = (bf16[2,112,1472]{2,1,0:T(8,128)(2,1)S(1)}, bf16[2,112,1472]{2,1,0:T(8,128)(2,1)S(1)}, u32[]{:S(2)}, u32[]{:S(2)}) collective-permute-start(bf16[2,112,1472]{2,1,0:T(8,128)(2,1)S(1)} %collective-permute-done.17), channel_id=1, source_target_pairs={{0,8},{4,12},{8,16},{12,20},{16,24},{20,28},{24,0},{28,4},{1,9},{5... | collective-permute-start | bytes 1978376 | tf_op jit(solution)/shard_map/ppermute | solution.py:57
  130.2 31.6 %collective-permute-start.22 = (bf16[2,112,1472]{2,1,0:T(8,128)(2,1)}, bf16[2,112,1472]{2,1,0:T(8,128)(2,1)S(1)}, u32[]{:S(2)}, u32[]{:S(2)}) collective-permute-start(bf16[2,112,1472]{2,1,0:T(8,128)(2,1)} %pad_maximum_fusion.17), channel_id=1, source_target_pairs={{0,8},{4,12},{8,16},{12,20},{16,24},{20,28},{24,0},{28,4},{1,9},{5... | collective-permute-start | bytes 1978376 | tf_op jit(solution)/shard_map/ppermute | solution.py:57
  164.4 15.2 %collective-permute-start.23 = (bf16[2,1,112,1472]{3,2,1,0:T(8,128)(2,1)S(1)}, bf16[2,1,112,1472]{3,2,1,0:T(8,128)(2,1)S(1)}, u32[]{:S(2)}, u32[]{:S(2)}) collective-permute-start(bf16[2,1,112,1472]{3,2,1,0:T(8,128)(2,1)S(1)} %get-tuple-element.343.refs_4_.refs_0_), channel_id=1, source_target_pairs={{0,2},{1,3},{2,0},{3,1},{4,6},{5,7},{6,4},{7,5},{8,10},{9,11},{10,... | collective-permute-start | bytes 1978376 | tf_op jit(solution)/shard_map/ppermute | solution.py:62
  166.2 14.1 %collective-permute-start.24 = (bf16[2,1,112,1472]{3,2,1,0:T(8,128)(2,1)S(1)}, bf16[2,1,112,1472]{3,2,1,0:T(8,128)(2,1)S(1)}, u32[]{:S(2)}, u32[]{:S(2)}) collective-permute-start(bf16[2,1,112,1472]{3,2,1,0:T(8,128)(2,1)S(1)} %get-tuple-element.345.refs_6_.refs_2_), channel_id=1, source_target_pairs={{0,1},{1,0},{2,3},{3,2},{4,5},{5,4},{6,7},{7,6},{8,9},{9,8},{10,11... | collective-permute-start | bytes 1978376 | tf_op jit(solution)/shard_map/ppermute | solution.py:62
  167.1 16.0 %collective-permute-start.25 = (bf16[2,112,1472]{2,1,0:T(8,128)(2,1)S(1)}, bf16[2,112,1472]{2,1,0:T(8,128)(2,1)S(1)}, u32[]{:S(2)}, u32[]{:S(2)}) collective-permute-start(bf16[2,112,1472]{2,1,0:T(8,128)(2,1)S(1)} %collective-permute-done.22), channel_id=1, source_target_pairs={{0,8},{4,12},{8,16},{12,20},{16,24},{20,28},{24,0},{28,4},{1,9},{5... | collective-permute-start | bytes 1978376 | tf_op jit(solution)/shard_map/ppermute | solution.py:57
  183.1 25.1 %collective-permute-start.28 = (bf16[2,112,1472]{2,1,0:T(8,128)(2,1)S(1)}, bf16[2,112,1472]{2,1,0:T(8,128)(2,1)S(1)}, u32[]{:S(2)}, u32[]{:S(2)}) collective-permute-start(bf16[2,112,1472]{2,1,0:T(8,128)(2,1)S(1)} %collective-permute-done.21), channel_id=1, source_target_pairs={{0,8},{4,12},{8,16},{12,20},{16,24},{20,28},{24,0},{28,4},{1,9},{5... | collective-permute-start | bytes 1978376 | tf_op jit(solution)/shard_map/ppermute | solution.py:57
  183.5 24.8 %collective-permute-start.26 = (bf16[2,1,112,1472]{3,2,1,0:T(8,128)(2,1)S(1)}, bf16[2,1,112,1472]{3,2,1,0:T(8,128)(2,1)S(1)}, u32[]{:S(2)}, u32[]{:S(2)}) collective-permute-start(bf16[2,1,112,1472]{3,2,1,0:T(8,128)(2,1)S(1)} %get-tuple-element.348.refs_10_.refs_4_), channel_id=1, source_target_pairs={{0,2},{1,3},{2,0},{3,1},{4,6},{5,7},{6,4},{7,5},{8,10},{9,11},{10,... | collective-permute-start | bytes 1978376 | tf_op jit(solution)/shard_map/ppermute | solution.py:62
  184.7 23.5 %collective-permute-start.27 = (bf16[2,1,112,1472]{3,2,1,0:T(8,128)(2,1)S(1)}, bf16[2,1,112,1472]{3,2,1,0:T(8,128)(2,1)S(1)}, u32[]{:S(2)}, u32[]{:S(2)}) collective-permute-start(bf16[2,1,112,1472]{3,2,1,0:T(8,128)(2,1)S(1)} %get-tuple-element.350.refs_12_.refs_6_), channel_id=1, source_target_pairs={{0,1},{1,0},{2,3},{3,2},{4,5},{5,4},{6,7},{7,6},{8,9},{9,8},{10,11... | collective-permute-start | bytes 1978376 | tf_op jit(solution)/shard_map/ppermute | solution.py:62
  189.8 51.7 %collective-permute-start.30 = (bf16[2,112,1472]{2,1,0:T(8,128)(2,1)S(1)}, bf16[2,112,1472]{2,1,0:T(8,128)(2,1)S(1)}, u32[]{:S(2)}, u32[]{:S(2)}) collective-permute-start(bf16[2,112,1472]{2,1,0:T(8,128)(2,1)S(1)} %pad_maximum_fusion.18.refs_4_.refs_10_), channel_id=1, source_target_pairs={{0,2},{1,3},{2,0},{3,1},{4,6},{5,7},{6,4},{7,5},{8,10},{9,11},{10,... | collective-permute-start | bytes 1978376 | tf_op jit(solution)/shard_map/ppermute | solution.py:62
  191.7 49.8 %collective-permute-start.31 = (bf16[2,112,1472]{2,1,0:T(8,128)(2,1)}, bf16[2,112,1472]{2,1,0:T(8,128)(2,1)S(1)}, u32[]{:S(2)}, u32[]{:S(2)}) collective-permute-start(bf16[2,112,1472]{2,1,0:T(8,128)(2,1)} %pad_maximum_fusion.19.refs_6_.refs_12_), channel_id=1, source_target_pairs={{0,1},{1,0},{2,3},{3,2},{4,5},{5,4},{6,7},{7,6},{8,9},{9,8},{10,11... | collective-permute-start | bytes 1978376 | tf_op jit(solution)/shard_map/ppermute | solution.py:62
  208.3 33.3 %collective-permute-start.32 = (bf16[2,112,1472]{2,1,0:T(8,128)(2,1)S(1)}, bf16[2,112,1472]{2,1,0:T(8,128)(2,1)S(1)}, u32[]{:S(2)}, u32[]{:S(2)}) collective-permute-start(bf16[2,112,1472]{2,1,0:T(8,128)(2,1)S(1)} %collective-permute-done.25), channel_id=1, source_target_pairs={{0,8},{4,12},{8,16},{12,20},{16,24},{20,28},{24,0},{28,4},{1,9},{5... | collective-permute-start | bytes 1978376 | tf_op jit(solution)/shard_map/ppermute | solution.py:57
  210.9 30.7 %collective-permute-start.33 = (bf16[1,2,112,1472]{3,2,1,0:T(8,128)(2,1)}, bf16[1,2,112,1472]{3,2,1,0:T(8,128)(2,1)S(1)}, u32[]{:S(2)}, u32[]{:S(2)}) collective-permute-start(bf16[1,2,112,1472]{3,2,1,0:T(8,128)(2,1)} %get-tuple-element.364), channel_id=1, source_target_pairs={{0,2},{1,3},{2,0},{3,1},{4,6},{5,7},{6,4},{7,5},{8,10},{9,11},{10,... | collective-permute-start | bytes 1978376 | tf_op jit(solution)/shard_map/ppermute | solution.py:62
  212.1 30.4 %collective-permute-start.34 = (bf16[1,2,112,1472]{3,2,1,0:T(8,128)(2,1)}, bf16[1,2,112,1472]{3,2,1,0:T(8,128)(2,1)S(1)}, u32[]{:S(2)}, u32[]{:S(2)}) collective-permute-start(bf16[1,2,112,1472]{3,2,1,0:T(8,128)(2,1)} %get-tuple-element.365), channel_id=1, source_target_pairs={{0,1},{1,0},{2,3},{3,2},{4,5},{5,4},{6,7},{7,6},{8,9},{9,8},{10,11... | collective-permute-start | bytes 1978376 | tf_op jit(solution)/shard_map/ppermute | solution.py:62
  243.4 46.1 %collective-permute-start.35 = (bf16[2,2,112,1472]{3,2,1,0:T(8,128)(2,1)}, bf16[2,2,112,1472]{3,2,1,0:T(8,128)(2,1)S(1)}, u32[]{:S(2)}, u32[]{:S(2)}) collective-permute-start(bf16[2,2,112,1472]{3,2,1,0:T(8,128)(2,1)} %get-tuple-element.366), channel_id=1, source_target_pairs={{0,2},{1,3},{2,0},{3,1},{4,6},{5,7},{6,4},{7,5},{8,10},{9,11},{10,... | collective-permute-start | bytes 3956744 | tf_op jit(solution)/shard_map/ppermute | solution.py:62
  244.4 45.1 %collective-permute-start.36 = (bf16[2,2,112,1472]{3,2,1,0:T(8,128)(2,1)}, bf16[2,2,112,1472]{3,2,1,0:T(8,128)(2,1)S(1)}, u32[]{:S(2)}, u32[]{:S(2)}) collective-permute-start(bf16[2,2,112,1472]{3,2,1,0:T(8,128)(2,1)} %get-tuple-element.367), channel_id=1, source_target_pairs={{0,1},{1,0},{2,3},{3,2},{4,5},{5,4},{6,7},{7,6},{8,9},{9,8},{10,11... | collective-permute-start | bytes 3956744 | tf_op jit(solution)/shard_map/ppermute | solution.py:62
  245.6 43.9 %collective-permute-start.37 = (bf16[448,1472]{1,0:T(8,128)(2,1)}, bf16[448,1472]{1,0:T(8,128)(2,1)}, u32[]{:S(2)}, u32[]{:S(2)}) collective-permute-start(bf16[448,1472]{1,0:T(8,128)(2,1)} %get-tuple-element.368), channel_id=1, source_target_pairs={{0,8},{4,12},{8,16},{12,20},{16,24},{20,28},{24,0},{28,4},{1,9},{5... | collective-permute-start | bytes 3956744 | tf_op jit(solution)/shard_map/ppermute | solution.py:57
  291.7 39.9 %collective-permute-start.38 = (bf16[5,112,1472]{2,1,0:T(8,128)(2,1)S(1)}, bf16[5,112,1472]{2,1,0:T(8,128)(2,1)S(1)}, u32[]{:S(2)}, u32[]{:S(2)}) collective-permute-start(bf16[5,112,1472]{2,1,0:T(8,128)(2,1)S(1)} %get-tuple-element.397), channel_id=1, source_target_pairs={{0,2},{1,3},{2,0},{3,1},{4,6},{5,7},{6,4},{7,5},{8,10},{9,11},{10,... | collective-permute-start | bytes 4945928 | tf_op jit(solution)/shard_map/ppermute | solution.py:62
  292.9 39.6 %collective-permute-start.39 = (bf16[5,112,1472]{2,1,0:T(8,128)(2,1)S(1)}, bf16[5,112,1472]{2,1,0:T(8,128)(2,1)S(1)}, u32[]{:S(2)}, u32[]{:S(2)}) collective-permute-start(bf16[5,112,1472]{2,1,0:T(8,128)(2,1)S(1)} %get-tuple-element.398), channel_id=1, source_target_pairs={{0,1},{1,0},{2,3},{3,2},{4,5},{5,4},{6,7},{7,6},{8,9},{9,8},{10,11... | collective-permute-start | bytes 4945928 | tf_op jit(solution)/shard_map/ppermute | solution.py:62
  296.3 33.6 %collective-permute-start.40 = (bf16[448,1472]{1,0:T(8,128)(2,1)}, bf16[448,1472]{1,0:T(8,128)(2,1)S(1)}, u32[]{:S(2)}, u32[]{:S(2)}) collective-permute-start(bf16[448,1472]{1,0:T(8,128)(2,1)} %add_convert_fusion), channel_id=1, source_target_pairs={{0,8},{4,12},{8,16},{12,20},{16,24},{20,28},{24,0},{28,4},{1,9},{5... | collective-permute-start | bytes 3956744 | tf_op jit(solution)/shard_map/ppermute | solution.py:57
  339.2 46.3 %collective-permute-start.45 = (bf16[6,112,1472]{2,1,0:T(8,128)(2,1)S(1)}, bf16[6,112,1472]{2,1,0:T(8,128)(2,1)}, u32[]{:S(2)}, u32[]{:S(2)}) collective-permute-start(bf16[6,112,1472]{2,1,0:T(8,128)(2,1)S(1)} %get-tuple-element.423), channel_id=1, source_target_pairs={{0,8},{4,12},{8,16},{12,20},{16,24},{20,28},{24,0},{28,4},{1,9},{5... | collective-permute-start | bytes 5935112 | tf_op jit(solution)/shard_map/ppermute | solution.py:57
  339.3 38.2 %collective-permute-start.42 = (bf16[2,256,768]{2,1,0:T(8,128)(2,1)}, bf16[2,256,768]{2,1,0:T(8,128)(2,1)S(1)}, u32[]{:S(2)}, u32[]{:S(2)}) collective-permute-start(bf16[2,256,768]{2,1,0:T(8,128)(2,1)} %get-tuple-element.414), channel_id=1, source_target_pairs={{0,1},{1,0},{2,3},{3,2},{4,5},{5,4},{6,7},{7,6},{8,9},{9,8},{10,11... | collective-permute-start | bytes 2359304 | tf_op jit(solution)/shard_map/ppermute | solution.py:62
  339.9 37.6 %collective-permute-start.43 = (bf16[2,256,768]{2,1,0:T(8,128)(2,1)}, bf16[2,256,768]{2,1,0:T(8,128)(2,1)S(1)}, u32[]{:S(2)}, u32[]{:S(2)}) collective-permute-start(bf16[2,256,768]{2,1,0:T(8,128)(2,1)} %get-tuple-element.415), channel_id=1, source_target_pairs={{0,2},{1,3},{2,0},{3,1},{4,6},{5,7},{6,4},{7,5},{8,10},{9,11},{10,... | collective-permute-start | bytes 2359304 | tf_op jit(solution)/shard_map/ppermute | solution.py:62
  340.8 36.8 %collective-permute-start.44 = (bf16[2,256,768]{2,1,0:T(8,128)(2,1)}, bf16[2,256,768]{2,1,0:T(8,128)(2,1)S(1)}, u32[]{:S(2)}, u32[]{:S(2)}) collective-permute-start(bf16[2,256,768]{2,1,0:T(8,128)(2,1)} %get-tuple-element.416), channel_id=1, source_target_pairs={{0,3},{1,2},{2,1},{3,0},{4,7},{5,6},{6,5},{7,4},{8,11},{9,10},{10,... | collective-permute-start | bytes 2359304 | tf_op jit(solution)/shard_map/ppermute | solution.py:62
  388.8 111.7 %reduce-scatter.3.cloned.1.call-start = ((), (), s32[]{:S(2)}) async-start(), calls=%async_computation.2 | async-start | bytes 2654208 | tf_op jit(solution)/shard_map/reduce_scatter | solution.py:1247
  393.6 40.7 %collective-permute-start.46 = (bf16[4,4,48,1472]{3,2,1,0:T(8,128)(2,1)}, bf16[4,4,48,1472]{3,2,1,0:T(8,128)(2,1)S(1)}, u32[]{:S(2)}, u32[]{:S(2)}) collective-permute-start(bf16[4,4,48,1472]{3,2,1,0:T(8,128)(2,1)} %get-tuple-element.443), channel_id=1, source_target_pairs={{0,4},{4,0},{8,12},{12,8},{16,20},{20,16},{24,28},{28,24},{1,5},{5... | collective-permute-start | bytes 6782984 | tf_op jit(solution)/shard_map/ppermute | solution.py:48
  402.4 26.8 %collective-permute-start.48 = (bf16[2,112,1472]{2,1,0:T(8,128)(2,1)}, bf16[2,112,1472]{2,1,0:T(8,128)(2,1)S(1)}, u32[]{:S(2)}, u32[]{:S(2)}) collective-permute-start(bf16[2,112,1472]{2,1,0:T(8,128)(2,1)} %get-tuple-element.449), channel_id=1, source_target_pairs={{0,1},{1,0},{2,3},{3,2},{4,5},{5,4},{6,7},{7,6},{8,9},{9,8},{10,11... | collective-permute-start | bytes 1978376 | tf_op jit(solution)/shard_map/ppermute | solution.py:62
  403.1 26.9 %collective-permute-start.49 = (bf16[2,112,1472]{2,1,0:T(8,128)(2,1)}, bf16[2,112,1472]{2,1,0:T(8,128)(2,1)S(1)}, u32[]{:S(2)}, u32[]{:S(2)}) collective-permute-start(bf16[2,112,1472]{2,1,0:T(8,128)(2,1)} %get-tuple-element.450), channel_id=1, source_target_pairs={{0,2},{1,3},{2,0},{3,1},{4,6},{5,7},{6,4},{7,5},{8,10},{9,11},{10,... | collective-permute-start | bytes 1978376 | tf_op jit(solution)/shard_map/ppermute | solution.py:62
  404.2 24.2 %collective-permute-start.50 = (bf16[1,112,1472]{2,1,0:T(8,128)(2,1)}, bf16[1,112,1472]{2,1,0:T(8,128)(2,1)S(1)}, u32[]{:S(2)}, u32[]{:S(2)}) collective-permute-start(bf16[1,112,1472]{2,1,0:T(8,128)(2,1)} %get-tuple-element.451), channel_id=1, source_target_pairs={{0,3},{1,2},{2,1},{3,0},{4,7},{5,6},{6,5},{7,4},{8,11},{9,10},{10,... | collective-permute-start | bytes 989192 | tf_op jit(solution)/shard_map/ppermute | solution.py:62
  408.3 26.0 %collective-permute-start.47 = (bf16[2,112,1472]{2,1,0:T(8,128)(2,1)S(1)}, bf16[2,112,1472]{2,1,0:T(8,128)(2,1)S(1)}, u32[]{:S(2)}, u32[]{:S(2)}) collective-permute-start(bf16[2,112,1472]{2,1,0:T(8,128)(2,1)S(1)} %fuse.13), channel_id=1, source_target_pairs={{0,8},{4,12},{8,16},{12,20},{16,24},{20,28},{24,0},{28,4},{1,9},{5... | collective-permute-start | bytes 1978376 | tf_op jit(solution)/shard_map/ppermute | solution.py:57
  440.3 17.3 %collective-permute-start.51 = (bf16[4,48,1472]{2,1,0:T(8,128)(2,1)S(1)}, bf16[4,48,1472]{2,1,0:T(8,128)(2,1)S(1)}, u32[]{:S(2)}, u32[]{:S(2)}) collective-permute-start(bf16[4,48,1472]{2,1,0:T(8,128)(2,1)S(1)} %get-tuple-element.459), channel_id=1, source_target_pairs={{0,1},{1,0},{2,3},{3,2},{4,5},{5,4},{6,7},{7,6},{8,9},{9,8},{10,11... | collective-permute-start | bytes 1695752 | tf_op jit(solution)/shard_map/ppermute | solution.py:62
  442.3 35.6 %collective-permute-start.54 = (bf16[2,112,1472]{2,1,0:T(8,128)(2,1)S(1)}, bf16[2,112,1472]{2,1,0:T(8,128)(2,1)S(1)}, u32[]{:S(2)}, u32[]{:S(2)}) collective-permute-start(bf16[2,112,1472]{2,1,0:T(8,128)(2,1)S(1)} %get-tuple-element.469), channel_id=1, source_target_pairs={{0,8},{4,12},{8,16},{12,20},{16,24},{20,28},{24,0},{28,4},{1,9},{5... | collective-permute-start | bytes 1978376 | tf_op jit(solution)/shard_map/ppermute | solution.py:57
  443.2 34.6 %collective-permute-start.52 = (bf16[4,48,1472]{2,1,0:T(8,128)(2,1)}, bf16[4,48,1472]{2,1,0:T(8,128)(2,1)}, u32[]{:S(2)}, u32[]{:S(2)}) collective-permute-start(bf16[4,48,1472]{2,1,0:T(8,128)(2,1)} %get-tuple-element.460), channel_id=1, source_target_pairs={{0,2},{1,3},{2,0},{3,1},{4,6},{5,7},{6,4},{7,5},{8,10},{9,11},{10,... | collective-permute-start | bytes 1695752 | tf_op jit(solution)/shard_map/ppermute | solution.py:62
  444.6 33.2 %collective-permute-start.53 = (bf16[4,48,1472]{2,1,0:T(8,128)(2,1)}, bf16[4,48,1472]{2,1,0:T(8,128)(2,1)}, u32[]{:S(2)}, u32[]{:S(2)}) collective-permute-start(bf16[4,48,1472]{2,1,0:T(8,128)(2,1)} %get-tuple-element.461), channel_id=1, source_target_pairs={{0,3},{1,2},{2,1},{3,0},{4,7},{5,6},{6,5},{7,4},{8,11},{9,10},{10,... | collective-permute-start | bytes 1695752 | tf_op jit(solution)/shard_map/ppermute | solution.py:62
  445.8 39.6 %collective-permute-start.60 = (bf16[1,112,1472]{2,1,0:T(8,128)(2,1)S(1)}, bf16[1,112,1472]{2,1,0:T(8,128)(2,1)S(1)}, u32[]{:S(2)}, u32[]{:S(2)}) collective-permute-start(bf16[1,112,1472]{2,1,0:T(8,128)(2,1)S(1)} %get-tuple-element.478.refs_2_), channel_id=1, source_target_pairs={{0,3},{1,2},{2,1},{3,0},{4,7},{5,6},{6,5},{7,4},{8,11},{9,10},{10,... | collective-permute-start | bytes 989192 | tf_op jit(solution)/shard_map/ppermute | solution.py:62
  478.1 22.3 %collective-permute-start.58 = (bf16[2,112,1472]{2,1,0:T(8,128)(2,1)S(1)}, bf16[2,112,1472]{2,1,0:T(8,128)(2,1)S(1)}, u32[]{:S(2)}, u32[]{:S(2)}) collective-permute-start(bf16[2,112,1472]{2,1,0:T(8,128)(2,1)S(1)} %get-tuple-element.485), channel_id=1, source_target_pairs={{0,1},{1,0},{2,3},{3,2},{4,5},{5,4},{6,7},{7,6},{8,9},{9,8},{10,11... | collective-permute-start | bytes 1978376 | tf_op jit(solution)/shard_map/ppermute | solution.py:62
  479.3 21.0 %collective-permute-start.59 = (bf16[2,112,1472]{2,1,0:T(8,128)(2,1)S(1)}, bf16[2,112,1472]{2,1,0:T(8,128)(2,1)S(1)}, u32[]{:S(2)}, u32[]{:S(2)}) collective-permute-start(bf16[2,112,1472]{2,1,0:T(8,128)(2,1)S(1)} %get-tuple-element.486), channel_id=1, source_target_pairs={{0,2},{1,3},{2,0},{3,1},{4,6},{5,7},{6,4},{7,5},{8,10},{9,11},{10,... | collective-permute-start | bytes 1978376 | tf_op jit(solution)/shard_map/ppermute | solution.py:62
  481.9 13.7 %collective-permute-start.55 = (bf16[64,1472]{1,0:T(8,128)(2,1)S(1)}, bf16[64,1472]{1,0:T(8,128)(2,1)S(1)}, u32[]{:S(2)}, u32[]{:S(2)}) collective-permute-start(bf16[64,1472]{1,0:T(8,128)(2,1)S(1)} %get-tuple-element.708), channel_id=1, source_target_pairs={{0,8},{4,12},{8,16},{12,20},{16,24},{20,28},{24,0},{28,4},{1,9},{5... | collective-permute-start | bytes 565256 | tf_op jit(solution)/shard_map/ppermute | solution.py:71
  483.1 14.7 %collective-permute-start.56 = (bf16[64,1472]{1,0:T(8,128)(2,1)S(1)}, bf16[64,1472]{1,0:T(8,128)(2,1)S(1)}, u32[]{:S(2)}, u32[]{:S(2)}) collective-permute-start(bf16[64,1472]{1,0:T(8,128)(2,1)S(1)} %get-tuple-element.709), channel_id=1, source_target_pairs={{0,16},{4,20},{8,24},{12,28},{16,0},{20,4},{24,8},{28,12},{1,17},{... | collective-permute-start | bytes 565256 | tf_op jit(solution)/shard_map/ppermute | solution.py:71
  485.4 15.0 %collective-permute-start.57 = (bf16[64,1472]{1,0:T(8,128)(2,1)S(1)}, bf16[64,1472]{1,0:T(8,128)(2,1)S(1)}, u32[]{:S(2)}, u32[]{:S(2)}) collective-permute-start(bf16[64,1472]{1,0:T(8,128)(2,1)S(1)} %get-tuple-element.707), channel_id=1, source_target_pairs={{0,24},{4,28},{8,0},{12,4},{16,8},{20,12},{24,16},{28,20},{1,25},{... | collective-permute-start | bytes 565256 | tf_op jit(solution)/shard_map/ppermute | solution.py:71
  503.5 26.8 %collective-permute-start.61 = (bf16[288,1472]{1,0:T(8,128)(2,1)S(1)}, bf16[288,1472]{1,0:T(8,128)(2,1)}, u32[]{:S(2)}, u32[]{:S(2)}) collective-permute-start(bf16[288,1472]{1,0:T(8,128)(2,1)S(1)} %get-tuple-element.501), channel_id=1, source_target_pairs={{0,1},{1,0},{2,3},{3,2},{4,5},{5,4},{6,7},{7,6},{8,9},{9,8},{10,11... | collective-permute-start | bytes 2543624 | tf_op jit(solution)/shard_map/ppermute | solution.py:62
  505.2 26.0 %collective-permute-start.62 = (bf16[288,1472]{1,0:T(8,128)(2,1)S(1)}, bf16[288,1472]{1,0:T(8,128)(2,1)}, u32[]{:S(2)}, u32[]{:S(2)}) collective-permute-start(bf16[288,1472]{1,0:T(8,128)(2,1)S(1)} %get-tuple-element.502), channel_id=1, source_target_pairs={{0,2},{1,3},{2,0},{3,1},{4,6},{5,7},{6,4},{7,5},{8,10},{9,11},{10,... | collective-permute-start | bytes 2543624 | tf_op jit(solution)/shard_map/ppermute | solution.py:62
  508.3 21.9 %collective-permute-start.63 = (bf16[64,1472]{1,0:T(8,128)(2,1)S(1)}, bf16[64,1472]{1,0:T(8,128)(2,1)S(1)}, u32[]{:S(2)}, u32[]{:S(2)}) collective-permute-start(bf16[64,1472]{1,0:T(8,128)(2,1)S(1)} %get-tuple-element.503), channel_id=1, source_target_pairs={{0,3},{1,2},{2,1},{3,0},{4,7},{5,6},{6,5},{7,4},{8,11},{9,10},{10,... | collective-permute-start | bytes 565256 | tf_op jit(solution)/shard_map/ppermute | solution.py:62
  535.7 14.6 %collective-permute-start.67 = (bf16[96,1472]{1,0:T(8,128)(2,1)S(1)}, bf16[96,1472]{1,0:T(8,128)(2,1)}, u32[]{:S(2)}, u32[]{:S(2)}) collective-permute-start(bf16[96,1472]{1,0:T(8,128)(2,1)S(1)} %pad_maximum_fusion.32), channel_id=1, source_target_pairs={{0,2},{1,3},{2,0},{3,1},{4,6},{5,7},{6,4},{7,5},{8,10},{9,11},{10,... | collective-permute-start | bytes 847880 | tf_op jit(solution)/shard_map/ppermute | solution.py:62
  537.1 13.3 %collective-permute-start.68 = (bf16[96,1472]{1,0:T(8,128)(2,1)S(1)}, bf16[96,1472]{1,0:T(8,128)(2,1)}, u32[]{:S(2)}, u32[]{:S(2)}) collective-permute-start(bf16[96,1472]{1,0:T(8,128)(2,1)S(1)} %pad_maximum_fusion.32), channel_id=1, source_target_pairs={{0,3},{1,2},{2,1},{3,0},{4,7},{5,6},{6,5},{7,4},{8,11},{9,10},{10,... | collective-permute-start | bytes 847880 | tf_op jit(solution)/shard_map/ppermute | solution.py:62
  (212 other events, 1795.1 us)
Sparse Core Ops, SparseCore 0:
  388.9 37.8 reduce-scatter.4
  436.1 43.8 reduce-scatter.2
